TPU v7x, 32 devices: a whole 2x2x4 slice. The times are simulated.
32 devices in a mesh: dp: 4 (over y, x), ctx: 8 (over z, core).
Axes of the slice: x: 2, y: 2, z: 4, core: 2. Of those that a mesh axis runs over, the one named last changes fastest.
Arguments:
- queries: bfloat16 [4, 1024, 4096], P('dp', 'ctx'), may hold values from -80 to 80
- key_tokens: bfloat16 [4, 1024, 1024], P('dp', 'ctx'), may hold values from -80 to 80
- value_tokens: bfloat16 [4, 1024, 1024], P('dp', 'ctx'), may hold values from -6 to 6
- cotangent: bfloat16 [4, 1024, 4096], P('dp', 'ctx'), may hold values from -6 to 6
- query_map: bfloat16 [32, 128, 64], replicated, may hold values from -4 to 4
- key_map: bfloat16 [32, 128, 64], replicated, may hold values from -4 to 4
Outputs:
- attended: bfloat16 [4, 1024, 4096], P('dp', 'ctx')
- grad_query_map: float32 [32, 128, 64], replicated
- grad_key_map: float32 [32, 128, 64], replicated
All inputs are finite; a program needn't handle non-finite values.
Results may differ from a plain program's by a relative error of at most 0.015.
Values sent between devices are 32-bit elements; how exact they have to be, the bound alone decides.
No kernel may reach another device: no remote copies, remote signals or barrier semaphores. Data moves between devices by JAX's collectives and lax.ppermute only.
A program may use at most 320 MiB of HBM per device.

v0:
```python
import jax
import jax.numpy as jnp
from jax import lax
from jax.experimental import pallas as pl
from jax.experimental.pallas import tpu as pltpu
from jax.sharding import PartitionSpec as P

BF = jnp.bfloat16
F32 = jnp.float32
VMEM_LIMIT = 40 * 1024 * 1024


def mm(a, b):
    return jnp.dot(a, b, preferred_element_type=F32)


def mm_nt(a, b):
    return lax.dot_general(a, b, (((1,), (1,)), ((), ())), preferred_element_type=F32)


def mm_tn(a, b):
    return lax.dot_general(a, b, (((0,), (0,)), ((), ())), preferred_element_type=F32)


def split(x):
    high = x.astype(BF)
    return high, (x - high.astype(F32)).astype(BF)


def soft(scores):
    top = jnp.max(scores, axis=0, keepdims=True)
    raised = jnp.exp(scores - top)
    return raised * (1.0 / jnp.sum(raised, axis=0, keepdims=True))


def both_soft(scores):
    return jnp.concatenate([soft(scores), soft(-scores)], axis=0)


def soft_back(probs, upstream):
    half = probs.shape[0] // 2
    p, n = probs[:half], probs[half:]
    gp, gn = upstream[:half], upstream[half:]
    result = p * (gp - jnp.sum(p * gp, axis=0, keepdims=True))
    result = result - n * (gn - jnp.sum(n * gn, axis=0, keepdims=True))
    return result.astype(BF)


def causal_mask(length):
    rows = lax.broadcasted_iota(jnp.int32, (length, length), 0)
    cols = lax.broadcasted_iota(jnp.int32, (length, length), 1)
    return rows >= cols


def outer(row_a, row_b):
    ah, al = split(row_a)
    bh, bl = split(row_b)
    zero_a = jnp.zeros((13, row_a.shape[1]), F32)
    zero_b = jnp.zeros((13, row_b.shape[1]), F32)
    a = jnp.concatenate([ah.astype(F32), al.astype(F32), ah.astype(F32), zero_a], axis=0).astype(BF)
    b = jnp.concatenate([bh.astype(F32), bh.astype(F32), bl.astype(F32), zero_b], axis=0).astype(BF)
    return mm_tn(a, b)


def denominators(weights, query_rows, norm_row):
    lanes = weights.shape[1]
    high, low = split(jnp.broadcast_to(norm_row, (lanes, norm_row.shape[1])))
    ones = jnp.ones((lanes, lanes), BF)
    return mm(weights, ones) + mm_nt(query_rows, high) + mm_nt(query_rows, low)


def put_half(own_ref, other_ref, value):
    half = pl.program_id(1)

    @pl.when(half == 0)
    def _():
        own_ref[...] = value

    @pl.when(half == 1)
    def _():
        other_ref[...] = value


def key_kernel(order, k_ref, v_ref, w_ref, kp_ref, own_ref, other_ref, norm_ref):
    group, dim, width = w_ref.shape
    length = k_ref.shape[0]
    maps = jnp.concatenate([w_ref[i].T for i in range(group)], axis=0)
    scores = mm_nt(maps, k_ref[...])
    probs = jnp.concatenate(
        [both_soft(scores[i * width : (i + 1) * width]) for i in range(group)], axis=0
    )
    kp_ref[0, 0] = probs
    features = probs.astype(BF)
    put_half(own_ref, other_ref, mm(features, v_ref[...]))
    norm_ref[0, 0] = mm_nt(jnp.ones((16, length), BF), features)[:1]


def query_kernel(order, q_ref, c_ref, w_ref, kp_ref, pn_ref, qp_ref, wt_ref, own_ref, other_ref):
    group, dim, width = w_ref.shape
    length = q_ref.shape[0]
    causal = causal_mask(length)
    sums = []
    for i in range(group):
        cols = slice(i * dim, (i + 1) * dim)
        rows = slice(i * 2 * width, (i + 1) * 2 * width)
        probs = both_soft(mm_nt(w_ref[i].T, q_ref[:, cols]))
        qp_ref[0, 0, rows] = probs
        query_t = probs.astype(BF)
        query_rows = query_t.T
        key_t = kp_ref[0, 0, rows].astype(BF)
        weights = jnp.where(causal, mm(query_rows, key_t), 0.0).astype(BF)
        wt_ref[0, 0, i] = weights
        den = denominators(weights, query_rows, pn_ref[0, 0, :, rows])
        scaled = (c_ref[:, cols].astype(F32) * (1.0 / den)).astype(BF)
        sums.append(mm(query_t, scaled))
    put_half(own_ref, other_ref, jnp.concatenate(sums, axis=0))


def middle_kernel(
    order, q_ref, c_ref, v_ref, kp_ref, qp_ref, wt_ref, pn_ref, so_ref, st_ref,
    att_ref, own_ref, other_ref, gk_ref, sn_ref,
):
    group, length = wt_ref.shape[2], wt_ref.shape[3]
    dim = v_ref.shape[1]
    causal = causal_mask(length)
    half = pl.program_id(1)
    values = v_ref[...]
    ones = jnp.ones((2 * dim, length), BF)
    ones_rows = jnp.ones((16, 2 * dim), BF)
    feats = qp_ref.shape[2] // group
    grads = []
    for i in range(group):
        cols = slice(i * dim, (i + 1) * dim)
        rows = slice(i * feats, (i + 1) * feats)
        state = jnp.where(half == 0, so_ref[rows], st_ref[rows])
        high, low = split(state)
        norm_row = pn_ref[0, 0, :, rows]
        probs = qp_ref[0, 0, rows]
        query_t = probs.astype(BF)
        query_rows = query_t.T
        key_t = kp_ref[0, 0, rows].astype(BF)
        weights = wt_ref[0, 0, i]
        inverse = 1.0 / denominators(weights, query_rows, norm_row)
        numerator = mm(
            jnp.concatenate([weights, query_rows], axis=1),
            jnp.concatenate([values, high], axis=0),
        ) + mm(query_rows, low)
        att_ref[:, cols] = (numerator * inverse).astype(BF)
        upstream = c_ref[:, cols].astype(F32)
        scaled_wide = upstream * inverse
        scaled = scaled_wide.astype(BF)
        product = jnp.concatenate(split(-(scaled_wide * inverse) * numerator), axis=1)
        norm_grad = mm(product, ones)
        norm_grad_row = mm_nt(ones_rows, product)[:1]
        mixed = mm_nt(scaled, values) + norm_grad
        block = jnp.where(causal, mixed, 0.0).astype(BF)
        upstream_q = mm_nt(
            jnp.concatenate([key_t, high], axis=1), jnp.concatenate([block, scaled], axis=1)
        )
        upstream_q = upstream_q + mm_nt(low, scaled) + outer(norm_row, norm_grad_row)
        grads.append(mm(soft_back(probs, upstream_q), q_ref[:, cols]))
        gk_ref[0, 0, rows] = mm(query_t, block)
        grad_high, grad_low = split(jnp.broadcast_to(norm_grad_row, (16, length)))
        sn_ref[0, 0, :, rows] = (mm(grad_high, query_rows) + mm(grad_low, query_rows))[:1]
    put_half(own_ref, other_ref, jnp.concatenate(grads, axis=0))


def last_kernel(
    order, k_ref, v_ref, kp_ref, gk_ref, sn_ref, to_ref, tt_ref, own_ref, other_ref
):
    half = pl.program_id(1)
    rows = kp_ref.shape[2]
    length = k_ref.shape[0]
    state = jnp.where(half == 0, to_ref[...], tt_ref[...])
    high, low = split(state)
    values = v_ref[...]
    upstream = gk_ref[0, 0] + mm_nt(
        jnp.concatenate([high, low], axis=1), jnp.concatenate([values, values], axis=1)
    )
    upstream = upstream + outer(sn_ref[0, 0], jnp.ones((1, length), F32))
    probs = kp_ref[0, 0]
    dim = k_ref.shape[1]
    feats = dim
    back = [
        soft_back(probs[a : a + feats], upstream[a : a + feats]) for a in range(0, rows, feats)
    ]
    put_half(own_ref, other_ref, mm(jnp.concatenate(back, axis=0), k_ref[...]))


def out_kernel(order, x_ref, o_ref):
    group, dim, width = o_ref.shape
    for i in range(group):
        o_ref[i] = x_ref[0, i * width : (i + 1) * width].T


def core_swap(x):
    size = lax.axis_size("ctx")
    return lax.ppermute(x, "ctx", [(i, i ^ 1) for i in range(size)])


def chip_move(x, pairs):
    return lax.ppermute(x, "ctx", [(2 * a + c, 2 * b + c) for a, b in pairs for c in (0, 1)])


def chip_before(x, chip, chips, forward):
    turn = (lambda a: a) if forward else (lambda a: chips - 1 - a)
    place = chip if forward else chips - 1 - chip

    def move(y, pairs):
        return chip_move(y, [(turn(a), turn(b)) for a, b in pairs])

    if chips == 4:
        rows = x.shape[0] // 2
        a, b = x[:rows], x[rows:]
        near = move(jnp.where(place == 1, b, a), [(0, 1), (1, 2), (2, 3)])
        far = move(b, [(0, 2)])
        second = jnp.where(place == 1, a + near, jnp.where(place == 2, b + near + far, b))
        near2 = move(second, [(0, 1), (1, 2), (2, 3)])
        far2 = move(second, [(1, 3)])
        first_half = jnp.where(place == 2, near2, near + far2)
        second_half = jnp.where(place == 2, near + far, near2)
        return jnp.concatenate([first_half, second_half], axis=0)
    total = move(x, [(i, i + 1) for i in range(chips - 1)])
    step = 1
    while step < chips:
        total = total + move(total, [(i, i + step) for i in range(chips - step)])
        step *= 2
    return total


def scan_states(own, other, chip, core, chips, forward):
    got = core_swap(other)
    before = chip_before(own + got, chip, chips, forward)
    second = core == 1 if forward else core == 0
    mine = before + jnp.where(second, got, 0.0)
    sent = before + jnp.where(second, 0.0, own)
    return mine, core_swap(sent)


def scan_norms(norm, chip, core, chips, forward):
    got = core_swap(norm)[:, ::-1]
    second = core == 1 if forward else core == 0
    base = jnp.where(second, got, 0.0)
    total = norm + got
    if chips & (chips - 1):
        before = chip_before(total.reshape(-1, total.shape[-1]), chip, chips, forward)
        return base + before.reshape(total.shape)
    bit = 1
    while bit < chips:
        moved = chip_move(total, [(i, i ^ bit) for i in range(chips)])
        upper = (chip & bit) != 0 if forward else (chip & bit) == 0
        base = base + jnp.where(upper, moved, 0.0)
        total = total + moved
        bit *= 2
    return base


def sum_all(own, other, chips):
    mine = own + core_swap(other)
    dp = lax.axis_size("dp")
    parts = mine.shape[0]
    if dp & (dp - 1) or parts % dp or chips & (chips - 1) or parts & (parts - 1):
        mine = lax.psum(mine, "dp")
        total = sum_chips(mine, chips)
        return jnp.concatenate([total, core_swap(total)], axis=0)
    share = parts // dp
    got = [
        lax.ppermute(mine[k * share : (k + 1) * share], "dp", [(i, i ^ k) for i in range(dp)])
        for k in range(1, dp)
    ]
    total = mine[:share]
    for piece in got:
        total = total + piece
    total = sum_chips(total, chips)
    pieces = [total] + [
        lax.ppermute(total, "dp", [(i, i ^ k) for i in range(dp)]) for k in range(1, dp)
    ]
    full = jnp.concatenate(pieces, axis=0)
    return jnp.concatenate([full, core_swap(full)], axis=0)


def sum_chips(total, chips):
    if chips & (chips - 1):
        size = 2 * chips
        return lax.psum(
            total, "ctx", axis_index_groups=[list(range(c, size, 2)) for c in (0, 1)]
        )
    bit = 1
    while bit < chips:
        total = total + chip_move(total, [(i, i ^ bit) for i in range(chips)])
        bit *= 2
    return total


def shards(queries, key_tokens, value_tokens, cotangent, query_map, key_map):
    length = queries.shape[1]
    head_count, dim, width = query_map.shape
    shared = key_tokens.shape[2] // dim
    group = head_count // shared
    feats = 2 * width
    n = shared // 2
    wide = group * feats
    queries = queries.reshape(length, head_count * dim)
    cotangent = cotangent.reshape(length, head_count * dim)
    keys = key_tokens.reshape(length, shared * dim)
    values = value_tokens.reshape(length, shared * dim)

    ctx = lax.axis_index("ctx")
    chips = lax.axis_size("ctx") // 2
    chip, core = ctx // 2, ctx % 2
    dp = lax.axis_size("dp")
    turn = lax.axis_index("dp") * (n // dp) if n % dp == 0 and n & (n - 1) == 0 else 0
    part = jnp.arange(n, dtype=jnp.int32) ^ turn
    order = jnp.concatenate([part + n * core, part + n * (1 - core)]).astype(jnp.int32)
    heads = jnp.arange(shared, dtype=jnp.int32)
    back = jnp.where(heads // n == core, 0, n) + ((heads % n) ^ turn)
    back = back.astype(jnp.int32)

    def head_cols(rows, cols):
        return pl.BlockSpec((rows, cols), lambda i, s, order: (0, order[s * n + i]))

    map_spec = pl.BlockSpec((group, dim, width), lambda i, s, order: (order[s * n + i], 0, 0))
    kept_spec = pl.BlockSpec((1, 1, wide, length), lambda i, s, order: (i, s, 0, 0))
    kept = jax.ShapeDtypeStruct((n, 2, wide, length), F32)
    row_spec = pl.BlockSpec((1, 1, 1, wide), lambda i, s, order: (i, s, 0, 0))
    row = jax.ShapeDtypeStruct((n, 2, 1, wide), F32)
    weight_spec = pl.BlockSpec((1, 1, group, length, length), lambda i, s, order: (i, s, 0, 0, 0))
    weight = jax.ShapeDtypeStruct((n, 2, group, length, length), BF)

    def half_spec(rows):
        return pl.BlockSpec((rows, dim), lambda i, s, order: (i, 0))

    def call(name, body, in_specs, out_specs, out_shape):
        return pl.pallas_call(
            body,
            name=name,
            out_shape=out_shape,
            grid_spec=pltpu.PrefetchScalarGridSpec(
                num_scalar_prefetch=1, grid=(n, 2), in_specs=in_specs, out_specs=out_specs
            ),
            compiler_params=pltpu.CompilerParams(vmem_limit_bytes=VMEM_LIMIT),
        )

    state = jax.ShapeDtypeStruct((n * wide, dim), F32)
    grad = jax.ShapeDtypeStruct((n * group * width, dim), F32)
    token = head_cols(length, dim)
    wide_token = head_cols(length, group * dim)

    key_probs, own, other, norm = call(
        "key_features",
        key_kernel,
        [token, token, map_spec],
        [kept_spec, half_spec(wide), half_spec(wide), row_spec],
        [kept, state, state, row],
    )(order, keys, values, key_map)
    prefix_norm = scan_norms(norm, chip, core, chips, True)
    prefix_own, prefix_other = scan_states(own, other, chip, core, chips, True)

    query_probs, weights, own, other = call(
        "query_features",
        query_kernel,
        [wide_token, wide_token, map_spec, kept_spec, row_spec],
        [kept_spec, weight_spec, half_spec(wide), half_spec(wide)],
        [kept, weight, state, state],
    )(order, queries, cotangent, query_map, key_probs, prefix_norm)
    suffix_own, suffix_other = scan_states(own, other, chip, core, chips, False)

    attended, query_own, query_other, key_up, norm = call(
        "attend",
        middle_kernel,
        [wide_token, wide_token, token, kept_spec, kept_spec, weight_spec, row_spec]
        + [half_spec(wide)] * 2,
        [wide_token, half_spec(group * width), half_spec(group * width), kept_spec, row_spec],
        [jax.ShapeDtypeStruct((length, head_count * dim), BF), grad, grad, kept, row],
    )(order, queries, cotangent, values, key_probs, query_probs, weights, prefix_norm, prefix_own, prefix_other)
    suffix_norm = scan_norms(norm, chip, core, chips, False)

    key_own, key_other = call(
        "key_grads",
        last_kernel,
        [token, token, kept_spec, kept_spec, row_spec] + [half_spec(wide)] * 2,
        [half_spec(group * width)] * 2,
        [grad, grad],
    )(order, keys, values, key_probs, key_up, suffix_norm, suffix_own, suffix_other)

    def finish(name, own, other):
        shape = (n, group * width, dim)
        total = sum_all(own.reshape(shape), other.reshape(shape), chips)
        return pl.pallas_call(
            out_kernel,
            name=name,
            out_shape=jax.ShapeDtypeStruct((head_count, dim, width), F32),
            grid_spec=pltpu.PrefetchScalarGridSpec(
                num_scalar_prefetch=1,
                grid=(shared,),
                in_specs=[pl.BlockSpec((1, group * width, dim), lambda i, back: (back[i], 0, 0))],
                out_specs=pl.BlockSpec((group, dim, width), lambda i, back: (i, 0, 0)),
            ),
            compiler_params=pltpu.CompilerParams(vmem_limit_bytes=VMEM_LIMIT),
        )(back, total)

    query_grad = finish("query_out", query_own, query_other)
    key_grad = finish("key_out", key_own, key_other)
    return attended.reshape(1, length, head_count * dim), query_grad, key_grad


def solution(mesh):
    in_specs = (
        P("dp", "ctx", None),
        P("dp", "ctx", None),
        P("dp", "ctx", None),
        P("dp", "ctx", None),
        P(),
        P(),
    )
    out_specs = (P("dp", "ctx", None), P(), P())
    return jax.shard_map(shards, mesh=mesh, in_specs=in_specs, out_specs=out_specs, check_vma=False)
```

profile of v0, /device:TPU:1, one launch (start us, length us, event | category | flops | bytes accessed | tf_op | source)
XLA Modules:
  0.0 219.8 jit_solution(4362668960751917094)
XLA Ops:
  0.7 2.4 %copy.9.w_ref = bf16[32,128,64]{2,1,0:T(8,128)(2,1)} copy(bf16[32,128,64]{1,2,0:T(8,128)(2,1)} %param.11) | data formatting | bytes 1048576 | tf_op args[5]
  6.3 6.1 %key_features.1 = (f32[4,2,512,128]{3,2,1,0:T(8,128)S(1)}, f32[2048,128]{1,0:T(8,128)S(1)}, f32[2048,128]{1,0:T(8,128)}, f32[4,2,1,512]{3,2,1,0:T(1,128)S(1)}) custom-call(s32[8]{0:T(128)S(1)} %pad_add_fusion.order, bf16[128,1024]{1,0:T(8,128)(2,1)S(1)} %bitcast.16, bf16[128,1024]{1,0:T(8,128)(2,1)S(1)} %bitcast.13, bf16[32,128,64]{2,1,0:T(8,128)(2,1)S(1)} %copy-done.7), custom_call_target="tpu_custom_call" | custom-call | tf_op jit(solution)/shard_map/key_features/pallas_call | solution.py:349
  15.8 2.7 %collective-permute-start.1 = (f32[4,2,1,512]{3,2,1,0:T(1,128)S(1)}, f32[4,2,1,512]{3,2,1,0:T(1,128)S(1)}, u32[]{:S(2)}, u32[]{:S(2)}) collective-permute-start(f32[4,2,1,512]{3,2,1,0:T(1,128)S(1)} %reverse_add_fusion.1), channel_id=1, source_target_pairs={{0,2},{1,3},{2,0},{3,1},{4,6},{5,7},{6,4},{7,5},{8,10},{9,11},{10,... | collective-permute-start | bytes 49160 | tf_op jit(solution)/shard_map/ppermute | solution.py:202
  19.6 2.5 %collective-permute-start.2 = (f32[4,2,1,512]{3,2,1,0:T(1,128)S(1)}, f32[4,2,1,512]{3,2,1,0:T(1,128)S(1)}, u32[]{:S(2)}, u32[]{:S(2)}) collective-permute-start(f32[4,2,1,512]{3,2,1,0:T(1,128)S(1)} %add.142), channel_id=1, source_target_pairs={{0,4},{1,5},{2,6},{3,7},{4,0},{5,1},{6,2},{7,3},{8,12},{9,13},{10,... | collective-permute-start | bytes 49160 | tf_op jit(solution)/shard_map/ppermute | solution.py:202
  22.2 2.4 %copy.10.w_ref = bf16[32,128,64]{2,1,0:T(8,128)(2,1)} copy(bf16[32,128,64]{1,2,0:T(8,128)(2,1)} %param.10) | data formatting | bytes 1048576 | tf_op args[4]
  27.0 20.4 %query_features.1 = (f32[4,2,512,128]{3,2,1,0:T(8,128)S(1)}, bf16[4,2,4,128,128]{4,3,2,1,0:T(8,128)(2,1)S(1)}, f32[2048,128]{1,0:T(8,128)S(1)}, f32[2048,128]{1,0:T(8,128)}) custom-call(s32[8]{0:T(128)S(1)} %pad_add_fusion.order, bf16[128,4096]{1,0:T(8,128)(2,1)S(1)} %bitcast.9, bf16[128,4096]{1,0:T(8,128)(2,1)S(1)} %bitcast.11, ...), custom_call_target="tpu_custom_call" | custom-call | tf_op jit(solution)/shard_map/query_features/pallas_call | solution.py:359
  56.0 4.0 %collective-permute-start.4 = (f32[1024,128]{1,0:T(8,128)}, f32[1024,128]{1,0:T(8,128)}, u32[]{:S(2)}, u32[]{:S(2)}) collective-permute-start(f32[1024,128]{1,0:T(8,128)} %get-tuple-element.50), channel_id=1, source_target_pairs={{0,2},{1,3},{2,4},{3,5},{4,6},{5,7},{8,10},{9,11},{10,12},{11,13},... | collective-permute-start | bytes 1572872 | tf_op jit(solution)/shard_map/ppermute | solution.py:202
  60.0 4.0 %collective-permute-start.5 = (f32[1024,128]{1,0:T(8,128)}, f32[1024,128]{1,0:T(8,128)}, u32[]{:S(2)}, u32[]{:S(2)}) collective-permute-start(f32[1024,128]{1,0:T(8,128)} %get-tuple-element.51), channel_id=1, source_target_pairs={{0,4},{1,5},{8,12},{9,13},{16,20},{17,21},{24,28},{25,29}} | collective-permute-start | bytes 1572872 | tf_op jit(solution)/shard_map/ppermute | solution.py:202
  70.8 11.2 %collective-permute-done.5 = f32[1024,128]{1,0:T(8,128)} collective-permute-done((f32[1024,128]{1,0:T(8,128)}, f32[1024,128]{1,0:T(8,128)}, u32[]{:S(2)}, u32[]{:S(2)}) %collective-permute-start.5) | collective-permute-done | bytes 524320 | tf_op jit(solution)/shard_map/ppermute | solution.py:202
  92.1 4.5 %collective-permute-done.6 = f32[1024,128]{1,0:T(8,128)} collective-permute-done((f32[1024,128]{1,0:T(8,128)}, f32[1024,128]{1,0:T(8,128)}, u32[]{:S(2)}, u32[]{:S(2)}) %collective-permute-start.6) | collective-permute-done | bytes 524320 | tf_op jit(solution)/shard_map/ppermute | solution.py:202
  99.8 7.2 %collective-permute-done.25 = f32[1024,128]{1,0:T(8,128)S(1)} collective-permute-done((f32[1024,128]{1,0:T(8,128)S(1)}, f32[1024,128]{1,0:T(8,128)S(1)}, u32[]{:S(2)}, u32[]{:S(2)}) %collective-permute-start.25) | collective-permute-done | bytes 524320 | tf_op jit(solution)/shard_map/ppermute | solution.py:202
  107.0 12.1 %collective-permute-done.26 = f32[1024,128]{1,0:T(8,128)S(1)} collective-permute-done((f32[1024,128]{1,0:T(8,128)S(1)}, f32[1024,128]{1,0:T(8,128)S(1)}, u32[]{:S(2)}, u32[]{:S(2)}) %collective-permute-start.26) | collective-permute-done | bytes 524320 | tf_op jit(solution)/shard_map/ppermute | solution.py:202
  121.9 3.4 %collective-permute-start.27 = (f32[2048,128]{1,0:T(8,128)}, f32[2048,128]{1,0:T(8,128)}, u32[]{:S(2)}, u32[]{:S(2)}) collective-permute-start(f32[2048,128]{1,0:T(8,128)} %get-tuple-element.40), channel_id=1, source_target_pairs={{0,1},{1,0},{2,3},{3,2},{4,5},{5,4},{6,7},{7,6},{8,9},{9,8},{10,11... | collective-permute-start | bytes 3145736 | tf_op jit(solution)/shard_map/ppermute | solution.py:198
  125.3 20.9 %attend.1 = (bf16[128,4096]{1,0:T(8,128)(2,1)}, f32[1024,128]{1,0:T(8,128)S(1)}, f32[1024,128]{1,0:T(8,128)}, f32[4,2,512,128]{3,2,1,0:T(8,128)S(1)}, f32[4,2,1,512]{3,2,1,0:T(1,128)S(1)}) custom-call(s32[8]{0:T(128)S(1)} %pad_add_fusion.order, bf16[128,4096]{1,0:T(8,128)(2,1)S(1)} %bitcast.10, bf16[128,4096]{1,0:T(8,128)(2,1)S(1)} %bitcast.12, ...), custom_call_target="tpu_custom_call" | custom-call | tf_op jit(solution)/shard_map/attend/pallas_call | solution.py:368
  149.6 2.6 %collective-permute-done.20 = f32[4,2,1,512]{3,2,1,0:T(1,128)S(1)} collective-permute-done((f32[4,2,1,512]{3,2,1,0:T(1,128)S(1)}, f32[4,2,1,512]{3,2,1,0:T(1,128)S(1)}, u32[]{:S(2)}, u32[]{:S(2)}) %collective-permute-start.20) | collective-permute-done | bytes 16416 | tf_op jit(solution)/shard_map/ppermute | solution.py:202
  153.7 2.1 collective-permute-done.21
  159.6 6.7 %key_grads.1 = (f32[1024,128]{1,0:T(8,128)S(1)}, f32[1024,128]{1,0:T(8,128)S(1)}) custom-call(s32[8]{0:T(128)S(1)} %pad_add_fusion.order, bf16[128,1024]{1,0:T(8,128)(2,1)S(1)} %bitcast.17, bf16[128,1024]{1,0:T(8,128)(2,1)S(1)} %bitcast.15, f32[4,2,512,128]{3,2,1,0:T(8,128)S(1)} %get-tuple-element.18.kp_ref, f32[4,2,512,128]{3,2,1,0:T(8,128)S(1)} %copy-done.15, ...), custom_call_target="tpu_custom_call" | custom-call | tf_op jit(solution)/shard_map/key_grads/pallas_call | solution.py:378
  166.2 2.5 %collective-permute-start.28 = (f32[4,256,128]{2,1,0:T(8,128)S(1)}, f32[4,256,128]{2,1,0:T(8,128)S(1)}, u32[]{:S(2)}, u32[]{:S(2)}) collective-permute-start(f32[4,256,128]{2,1,0:T(8,128)S(1)} %bitcast.20), channel_id=1, source_target_pairs={{0,1},{1,0},{2,3},{3,2},{4,5},{5,4},{6,7},{7,6},{8,9},{9,8},{10,11... | collective-permute-start | bytes 1572872 | tf_op jit(solution)/shard_map/ppermute | solution.py:198
  180.5 2.8 %collective-permute-done.30 = f32[1,256,128]{2,1,0:T(8,128)S(1)} collective-permute-done((f32[1,256,128]{2,1,0:T(8,128)S(1)}, f32[1,256,128]{2,1,0:T(8,128)S(1)}, u32[]{:S(2)}, u32[]{:S(2)}) %collective-permute-start.30) | collective-permute-done | bytes 131104 | tf_op jit(solution)/shard_map/ppermute | solution.py:268
  184.6 5.8 %collective-permute-done.32 = f32[1,256,128]{2,1,0:T(8,128)S(1)} collective-permute-done((f32[1,256,128]{2,1,0:T(8,128)S(1)}, f32[1,256,128]{2,1,0:T(8,128)S(1)}, u32[]{:S(2)}, u32[]{:S(2)}) %collective-permute-start.32) | collective-permute-done | bytes 131104 | tf_op jit(solution)/shard_map/ppermute | solution.py:202
  190.4 3.6 %collective-permute-start.15 = (f32[1,256,128]{2,1,0:T(8,128)S(1)}, f32[1,256,128]{2,1,0:T(8,128)S(1)}, u32[]{:S(2)}, u32[]{:S(2)}) collective-permute-start(f32[1,256,128]{2,1,0:T(8,128)S(1)} %get-tuple-element.39), channel_id=1, source_target_pairs={{0,8},{8,0},{16,24},{24,16},{1,9},{9,1},{17,25},{25,17},{2,10},{10... | collective-permute-start | bytes 393224 | tf_op jit(solution)/shard_map/ppermute | solution.py:276
  195.3 3.0 %collective-permute-done.33 = f32[1,256,128]{2,1,0:T(8,128)S(1)} collective-permute-done((f32[1,256,128]{2,1,0:T(8,128)S(1)}, f32[1,256,128]{2,1,0:T(8,128)S(1)}, u32[]{:S(2)}, u32[]{:S(2)}) %collective-permute-start.33) | collective-permute-done | bytes 131104 | tf_op jit(solution)/shard_map/ppermute | solution.py:202
  201.0 7.5 %collective-permute-start.18 = (f32[4,256,128]{2,1,0:T(8,128)S(1)}, f32[4,256,128]{2,1,0:T(8,128)S(1)}, u32[]{:S(2)}, u32[]{:S(2)}) collective-permute-start(f32[4,256,128]{2,1,0:T(8,128)S(1)} %pad_maximum_fusion.2), channel_id=1, source_target_pairs={{0,1},{1,0},{2,3},{3,2},{4,5},{5,4},{6,7},{7,6},{8,9},{9,8},{10,11... | collective-permute-start | bytes 1572872 | tf_op jit(solution)/shard_map/ppermute | solution.py:198
  209.4 2.6 %collective-permute-start.37 = (f32[4,256,128]{2,1,0:T(8,128)}, f32[4,256,128]{2,1,0:T(8,128)}, u32[]{:S(2)}, u32[]{:S(2)}) collective-permute-start(f32[4,256,128]{2,1,0:T(8,128)} %pad_maximum_fusion.3), channel_id=1, source_target_pairs={{0,1},{1,0},{2,3},{3,2},{4,5},{5,4},{6,7},{7,6},{8,9},{9,8},{10,11... | collective-permute-start | bytes 1572872 | tf_op jit(solution)/shard_map/ppermute | solution.py:198
  (151 shorter events, 75.9 us)
Async XLA Ops:
  13.4 38.9 %collective-permute-start.3 = (f32[2048,128]{1,0:T(8,128)}, f32[2048,128]{1,0:T(8,128)}, u32[]{:S(2)}, u32[]{:S(2)}) collective-permute-start(f32[2048,128]{1,0:T(8,128)} %get-tuple-element.23), channel_id=1, source_target_pairs={{0,1},{1,0},{2,3},{3,2},{4,5},{5,4},{6,7},{7,6},{8,9},{9,8},{10,11... | collective-permute-start | bytes 3145736 | tf_op jit(solution)/shard_map/ppermute | solution.py:198
  50.7 13.3 %collective-permute-start.22 = (f32[2048,128]{1,0:T(8,128)}, f32[2048,128]{1,0:T(8,128)}, u32[]{:S(2)}, u32[]{:S(2)}) collective-permute-start(f32[2048,128]{1,0:T(8,128)} %get-tuple-element.30), channel_id=1, source_target_pairs={{0,1},{1,0},{2,3},{3,2},{4,5},{5,4},{6,7},{7,6},{8,9},{9,8},{10,11... | collective-permute-start | bytes 3145736 | tf_op jit(solution)/shard_map/ppermute | solution.py:198
  56.0 14.9 %collective-permute-start.4 = (f32[1024,128]{1,0:T(8,128)}, f32[1024,128]{1,0:T(8,128)}, u32[]{:S(2)}, u32[]{:S(2)}) collective-permute-start(f32[1024,128]{1,0:T(8,128)} %get-tuple-element.50), channel_id=1, source_target_pairs={{0,2},{1,3},{2,4},{3,5},{4,6},{5,7},{8,10},{9,11},{10,12},{11,13},... | collective-permute-start | bytes 1572872 | tf_op jit(solution)/shard_map/ppermute | solution.py:202
  60.0 22.1 %collective-permute-start.5 = (f32[1024,128]{1,0:T(8,128)}, f32[1024,128]{1,0:T(8,128)}, u32[]{:S(2)}, u32[]{:S(2)}) collective-permute-start(f32[1024,128]{1,0:T(8,128)} %get-tuple-element.51), channel_id=1, source_target_pairs={{0,4},{1,5},{8,12},{9,13},{16,20},{17,21},{24,28},{25,29}} | collective-permute-start | bytes 1572872 | tf_op jit(solution)/shard_map/ppermute | solution.py:202
  66.9 20.8 %collective-permute-start.23 = (f32[1024,128]{1,0:T(8,128)}, f32[1024,128]{1,0:T(8,128)}, u32[]{:S(2)}, u32[]{:S(2)}) collective-permute-start(f32[1024,128]{1,0:T(8,128)} %get-tuple-element.44), channel_id=1, source_target_pairs={{6,4},{7,5},{4,2},{5,3},{2,0},{3,1},{14,12},{15,13},{12,10},{13,11... | collective-permute-start | bytes 1572872 | tf_op jit(solution)/shard_map/ppermute | solution.py:202
  68.2 19.5 %collective-permute-start.24 = (f32[1024,128]{1,0:T(8,128)}, f32[1024,128]{1,0:T(8,128)}, u32[]{:S(2)}, u32[]{:S(2)}) collective-permute-start(f32[1024,128]{1,0:T(8,128)} %get-tuple-element.45), channel_id=1, source_target_pairs={{6,2},{7,3},{14,10},{15,11},{22,18},{23,19},{30,26},{31,27}} | collective-permute-start | bytes 1572872 | tf_op jit(solution)/shard_map/ppermute | solution.py:202
  84.2 12.4 %collective-permute-start.6 = (f32[1024,128]{1,0:T(8,128)}, f32[1024,128]{1,0:T(8,128)}, u32[]{:S(2)}, u32[]{:S(2)}) collective-permute-start(f32[1024,128]{1,0:T(8,128)} %select_select_fusion.1), channel_id=1, source_target_pairs={{0,2},{1,3},{2,4},{3,5},{4,6},{5,7},{8,10},{9,11},{10,12},{11,13},... | collective-permute-start | bytes 1572872 | tf_op jit(solution)/shard_map/ppermute | solution.py:202
  86.3 10.3 %collective-permute-start.7 = (f32[1024,128]{1,0:T(8,128)}, f32[1024,128]{1,0:T(8,128)}, u32[]{:S(2)}, u32[]{:S(2)}) collective-permute-start(f32[1024,128]{1,0:T(8,128)} %select_select_fusion.1), channel_id=1, source_target_pairs={{2,6},{3,7},{10,14},{11,15},{18,22},{19,23},{26,30},{27,31}} | collective-permute-start | bytes 1572872 | tf_op jit(solution)/shard_map/ppermute | solution.py:202
  89.3 17.6 %collective-permute-start.25 = (f32[1024,128]{1,0:T(8,128)S(1)}, f32[1024,128]{1,0:T(8,128)S(1)}, u32[]{:S(2)}, u32[]{:S(2)}) collective-permute-start(f32[1024,128]{1,0:T(8,128)S(1)} %select_select_fusion), channel_id=1, source_target_pairs={{6,4},{7,5},{4,2},{5,3},{2,0},{3,1},{14,12},{15,13},{12,10},{13,11... | collective-permute-start | bytes 1572872 | tf_op jit(solution)/shard_map/ppermute | solution.py:202
  90.8 28.3 %collective-permute-start.26 = (f32[1024,128]{1,0:T(8,128)S(1)}, f32[1024,128]{1,0:T(8,128)S(1)}, u32[]{:S(2)}, u32[]{:S(2)}) collective-permute-start(f32[1024,128]{1,0:T(8,128)S(1)} %select_select_fusion), channel_id=1, source_target_pairs={{4,0},{5,1},{12,8},{13,9},{20,16},{21,17},{28,24},{29,25}} | collective-permute-start | bytes 1572872 | tf_op jit(solution)/shard_map/ppermute | solution.py:202
  99.6 25.7 %collective-permute-start.8 = (f32[2048,128]{1,0:T(8,128)S(1)}, f32[2048,128]{1,0:T(8,128)S(1)}, u32[]{:S(2)}, u32[]{:S(2)}) collective-permute-start(f32[2048,128]{1,0:T(8,128)S(1)} %get-tuple-element.46), channel_id=1, source_target_pairs={{0,1},{1,0},{2,3},{3,2},{4,5},{5,4},{6,7},{7,6},{8,9},{9,8},{10,11... | collective-permute-start | bytes 3145736 | tf_op jit(solution)/shard_map/ppermute | solution.py:198
  121.9 33.9 %collective-permute-start.27 = (f32[2048,128]{1,0:T(8,128)}, f32[2048,128]{1,0:T(8,128)}, u32[]{:S(2)}, u32[]{:S(2)}) collective-permute-start(f32[2048,128]{1,0:T(8,128)} %get-tuple-element.40), channel_id=1, source_target_pairs={{0,1},{1,0},{2,3},{3,2},{4,5},{5,4},{6,7},{7,6},{8,9},{9,8},{10,11... | collective-permute-start | bytes 3145736 | tf_op jit(solution)/shard_map/ppermute | solution.py:198
  152.3 16.5 %collective-permute-start.9 = (f32[4,256,128]{2,1,0:T(8,128)}, f32[4,256,128]{2,1,0:T(8,128)}, u32[]{:S(2)}, u32[]{:S(2)}) collective-permute-start(f32[4,256,128]{2,1,0:T(8,128)} %bitcast.6), channel_id=1, source_target_pairs={{0,1},{1,0},{2,3},{3,2},{4,5},{5,4},{6,7},{7,6},{8,9},{9,8},{10,11... | collective-permute-start | bytes 1572872 | tf_op jit(solution)/shard_map/ppermute | solution.py:198
  172.7 7.8 %collective-permute-start.29 = (f32[1,256,128]{2,1,0:T(8,128)S(1)}, f32[1,256,128]{2,1,0:T(8,128)S(1)}, u32[]{:S(2)}, u32[]{:S(2)}) collective-permute-start(f32[1,256,128]{2,1,0:T(8,128)S(1)} %get-tuple-element.52), channel_id=1, source_target_pairs={{0,8},{8,0},{16,24},{24,16},{1,9},{9,1},{17,25},{25,17},{2,10},{10... | collective-permute-start | bytes 393224 | tf_op jit(solution)/shard_map/ppermute | solution.py:268
  174.0 9.3 %collective-permute-start.30 = (f32[1,256,128]{2,1,0:T(8,128)S(1)}, f32[1,256,128]{2,1,0:T(8,128)S(1)}, u32[]{:S(2)}, u32[]{:S(2)}) collective-permute-start(f32[1,256,128]{2,1,0:T(8,128)S(1)} %get-tuple-element.54), channel_id=1, source_target_pairs={{0,16},{8,24},{16,0},{24,8},{1,17},{9,25},{17,1},{25,9},{2,18},{10... | collective-permute-start | bytes 393224 | tf_op jit(solution)/shard_map/ppermute | solution.py:268
  175.3 9.1 %collective-permute-start.31 = (f32[1,256,128]{2,1,0:T(8,128)S(1)}, f32[1,256,128]{2,1,0:T(8,128)S(1)}, u32[]{:S(2)}, u32[]{:S(2)}) collective-permute-start(f32[1,256,128]{2,1,0:T(8,128)S(1)} %get-tuple-element.53), channel_id=1, source_target_pairs={{0,24},{8,16},{16,8},{24,0},{1,25},{9,17},{17,9},{25,1},{2,26},{10... | collective-permute-start | bytes 393224 | tf_op jit(solution)/shard_map/ppermute | solution.py:268
  190.3 7.9 %collective-permute-start.33 = (f32[1,256,128]{2,1,0:T(8,128)S(1)}, f32[1,256,128]{2,1,0:T(8,128)S(1)}, u32[]{:S(2)}, u32[]{:S(2)}) collective-permute-start(f32[1,256,128]{2,1,0:T(8,128)S(1)} %add.176), channel_id=1, source_target_pairs={{0,4},{1,5},{2,6},{3,7},{4,0},{5,1},{6,2},{7,3},{8,12},{9,13},{10,... | collective-permute-start | bytes 393224 | tf_op jit(solution)/shard_map/ppermute | solution.py:202
  190.4 9.6 %collective-permute-start.15 = (f32[1,256,128]{2,1,0:T(8,128)S(1)}, f32[1,256,128]{2,1,0:T(8,128)S(1)}, u32[]{:S(2)}, u32[]{:S(2)}) collective-permute-start(f32[1,256,128]{2,1,0:T(8,128)S(1)} %get-tuple-element.39), channel_id=1, source_target_pairs={{0,8},{8,0},{16,24},{24,16},{1,9},{9,1},{17,25},{25,17},{2,10},{10... | collective-permute-start | bytes 393224 | tf_op jit(solution)/shard_map/ppermute | solution.py:276
  194.0 7.0 %collective-permute-start.16 = (f32[1,256,128]{2,1,0:T(8,128)S(1)}, f32[1,256,128]{2,1,0:T(8,128)S(1)}, u32[]{:S(2)}, u32[]{:S(2)}) collective-permute-start(f32[1,256,128]{2,1,0:T(8,128)S(1)} %get-tuple-element.39), channel_id=1, source_target_pairs={{0,16},{8,24},{16,0},{24,8},{1,17},{9,25},{17,1},{25,9},{2,18},{10... | collective-permute-start | bytes 393224 | tf_op jit(solution)/shard_map/ppermute | solution.py:276
  194.0 7.0 %collective-permute-start.17 = (f32[1,256,128]{2,1,0:T(8,128)S(1)}, f32[1,256,128]{2,1,0:T(8,128)S(1)}, u32[]{:S(2)}, u32[]{:S(2)}) collective-permute-start(f32[1,256,128]{2,1,0:T(8,128)S(1)} %get-tuple-element.39), channel_id=1, source_target_pairs={{0,24},{8,16},{16,8},{24,0},{1,25},{9,17},{17,9},{25,1},{2,26},{10... | collective-permute-start | bytes 393224 | tf_op jit(solution)/shard_map/ppermute | solution.py:276
  198.3 10.3 %collective-permute-start.34 = (f32[1,256,128]{2,1,0:T(8,128)S(1)}, f32[1,256,128]{2,1,0:T(8,128)S(1)}, u32[]{:S(2)}, u32[]{:S(2)}) collective-permute-start(f32[1,256,128]{2,1,0:T(8,128)S(1)} %get-tuple-element.37), channel_id=1, source_target_pairs={{0,8},{8,0},{16,24},{24,16},{1,9},{9,1},{17,25},{25,17},{2,10},{10... | collective-permute-start | bytes 393224 | tf_op jit(solution)/shard_map/ppermute | solution.py:276
  199.7 8.9 %collective-permute-start.35 = (f32[1,256,128]{2,1,0:T(8,128)S(1)}, f32[1,256,128]{2,1,0:T(8,128)S(1)}, u32[]{:S(2)}, u32[]{:S(2)}) collective-permute-start(f32[1,256,128]{2,1,0:T(8,128)S(1)} %get-tuple-element.37), channel_id=1, source_target_pairs={{0,16},{8,24},{16,0},{24,8},{1,17},{9,25},{17,1},{25,9},{2,18},{10... | collective-permute-start | bytes 393224 | tf_op jit(solution)/shard_map/ppermute | solution.py:276
  200.1 8.5 %collective-permute-start.36 = (f32[1,256,128]{2,1,0:T(8,128)S(1)}, f32[1,256,128]{2,1,0:T(8,128)S(1)}, u32[]{:S(2)}, u32[]{:S(2)}) collective-permute-start(f32[1,256,128]{2,1,0:T(8,128)S(1)} %get-tuple-element.37), channel_id=1, source_target_pairs={{0,24},{8,16},{16,8},{24,0},{1,25},{9,17},{17,9},{25,1},{2,26},{10... | collective-permute-start | bytes 393224 | tf_op jit(solution)/shard_map/ppermute | solution.py:276
  201.0 11.1 %collective-permute-start.18 = (f32[4,256,128]{2,1,0:T(8,128)S(1)}, f32[4,256,128]{2,1,0:T(8,128)S(1)}, u32[]{:S(2)}, u32[]{:S(2)}) collective-permute-start(f32[4,256,128]{2,1,0:T(8,128)S(1)} %pad_maximum_fusion.2), channel_id=1, source_target_pairs={{0,1},{1,0},{2,3},{3,2},{4,5},{5,4},{6,7},{7,6},{8,9},{9,8},{10,11... | collective-permute-start | bytes 1572872 | tf_op jit(solution)/shard_map/ppermute | solution.py:198
  (39 other events, 201.8 us)
where the time goes:
time: 221 us; the launch traced here: 220 us
  waiting for transfers between devices  60.7 us (27%)
  Pallas kernels  57.4 us (26%)
  starting transfers between devices  57.1 us (26%)
  local copies, waits for them, and re-layouts  25.9 us (12%)
  other arithmetic  17.5 us (8%)
    ppermute x16, waiting for transfers between devices, chip_move(): lax.ppermute(x, 'ctx', [(2 * a + c, 2 * b + c) for a, b in pairs for c in...  50.7 us
    unnamed x60, local copies, waits for them, and re-layouts  24.7 us
    ppermute x16, starting transfers between devices, chip_move(): lax.ppermute(x, 'ctx', [(2 * a + c, 2 * b + c) for a, b in pairs for c in...  22.7 us
    pallas_call x1, Pallas kernels, shards(): call('attend', middle_kernel, [wide_token, wide_token, token, kept_spec,...  20.9 us
    pallas_call x1, Pallas kernels, shards(): call('query_features', query_kernel, [wide_token, wide_token, map_spec, k...  20.4 us
    ppermute x10, starting transfers between devices, core_swap(): return lax.ppermute(x, 'ctx', [(i, i ^ 1) for i in range(size)])  19.7 us
    ppermute x6, starting transfers between devices, sum_all(): lax.ppermute(total, 'dp', [(i, i ^ k) for i in range(dp)])  7.55 us
    ppermute x6, starting transfers between devices, sum_all(): lax.ppermute(mine[k * share:(k + 1) * share], 'dp', [(i, i ^ k) for i in...  7.2 us
  transfers between devices with their start and end apart: 38, of which 16 were waited for; matrix products, arithmetic and copies ran while one was open for 10% of the time, Pallas kernels for 23%

commit v1 on v0

--- a/solution.py
+++ b/solution.py
@@ -7,7 +7,7 @@
 
 BF = jnp.bfloat16
 F32 = jnp.float32
-VMEM_LIMIT = 40 * 1024 * 1024
+VMEM_LIMIT = 16 * 1024 * 1024
 
 
 def mm(a, b):
@@ -16,10 +16,6 @@
 
 def mm_nt(a, b):
     return lax.dot_general(a, b, (((1,), (1,)), ((), ())), preferred_element_type=F32)
-
-
-def mm_tn(a, b):
-    return lax.dot_general(a, b, (((0,), (0,)), ((), ())), preferred_element_type=F32)
 
 
 def split(x):
@@ -52,21 +48,25 @@
     return rows >= cols
 
 
-def outer(row_a, row_b):
-    ah, al = split(row_a)
-    bh, bl = split(row_b)
-    zero_a = jnp.zeros((13, row_a.shape[1]), F32)
-    zero_b = jnp.zeros((13, row_b.shape[1]), F32)
-    a = jnp.concatenate([ah.astype(F32), al.astype(F32), ah.astype(F32), zero_a], axis=0).astype(BF)
-    b = jnp.concatenate([bh.astype(F32), bh.astype(F32), bl.astype(F32), zero_b], axis=0).astype(BF)
-    return mm_tn(a, b)
-
-
-def denominators(weights, query_rows, norm_row):
-    lanes = weights.shape[1]
-    high, low = split(jnp.broadcast_to(norm_row, (lanes, norm_row.shape[1])))
-    ones = jnp.ones((lanes, lanes), BF)
-    return mm(weights, ones) + mm_nt(query_rows, high) + mm_nt(query_rows, low)
+def column(row):
+    return jnp.broadcast_to(row, (8, row.shape[1])).T[:, :1]
+
+
+def three_lanes(wide, order):
+    lane = lax.broadcasted_iota(jnp.int32, wide.shape, 1)
+    high = wide.astype(BF).astype(F32)
+    parts = {"h": high, "l": wide - high}
+    result = jnp.where(lane == 2, parts[order[2]], 0.0)
+    result = jnp.where(lane == 1, parts[order[1]], result)
+    return jnp.where(lane == 0, parts[order[0]], result).astype(BF)
+
+
+def cat(*pieces):
+    return jnp.concatenate(pieces, axis=1)
+
+
+def stack(*pieces):
+    return jnp.concatenate(pieces, axis=0)
 
 
 def put_half(own_ref, other_ref, value):
@@ -82,115 +82,126 @@
 
 
 def key_kernel(order, k_ref, v_ref, w_ref, kp_ref, own_ref, other_ref, norm_ref):
-    group, dim, width = w_ref.shape
+    group, width, dim = w_ref.shape
     length = k_ref.shape[0]
-    maps = jnp.concatenate([w_ref[i].T for i in range(group)], axis=0)
-    scores = mm_nt(maps, k_ref[...])
-    probs = jnp.concatenate(
-        [both_soft(scores[i * width : (i + 1) * width]) for i in range(group)], axis=0
-    )
+    scores = mm_nt(w_ref[...].reshape(group * width, dim), k_ref[...])
+    probs = stack(*[both_soft(scores[i * width : (i + 1) * width]) for i in range(group)])
     kp_ref[0, 0] = probs
     features = probs.astype(BF)
     put_half(own_ref, other_ref, mm(features, v_ref[...]))
     norm_ref[0, 0] = mm_nt(jnp.ones((16, length), BF), features)[:1]
 
 
-def query_kernel(order, q_ref, c_ref, w_ref, kp_ref, pn_ref, qp_ref, wt_ref, own_ref, other_ref):
-    group, dim, width = w_ref.shape
+def query_kernel(
+    order, q_ref, c_ref, w_ref, kp_ref, pn_ref, qp_ref, qr_ref, wt_ref, inv_ref, own_ref, other_ref
+):
+    group, width, dim = w_ref.shape
     length = q_ref.shape[0]
     causal = causal_mask(length)
-    sums = []
-    for i in range(group):
-        cols = slice(i * dim, (i + 1) * dim)
-        rows = slice(i * 2 * width, (i + 1) * 2 * width)
-        probs = both_soft(mm_nt(w_ref[i].T, q_ref[:, cols]))
-        qp_ref[0, 0, rows] = probs
-        query_t = probs.astype(BF)
-        query_rows = query_t.T
-        key_t = kp_ref[0, 0, rows].astype(BF)
-        weights = jnp.where(causal, mm(query_rows, key_t), 0.0).astype(BF)
-        wt_ref[0, 0, i] = weights
-        den = denominators(weights, query_rows, pn_ref[0, 0, :, rows])
-        scaled = (c_ref[:, cols].astype(F32) * (1.0 / den)).astype(BF)
-        sums.append(mm(query_t, scaled))
-    put_half(own_ref, other_ref, jnp.concatenate(sums, axis=0))
+    heads = range(group)
+    cols = [slice(i * dim, (i + 1) * dim) for i in heads]
+    rows = [slice(i * 2 * width, (i + 1) * 2 * width) for i in heads]
+    scores = [mm_nt(w_ref[i], q_ref[:, cols[i]]) for i in heads]
+    probs = [both_soft(x) for x in scores]
+    query_t = [x.astype(BF) for x in probs]
+    query_rows = [x.T for x in query_t]
+    weights = [mm(query_rows[i], kp_ref[0, 0, rows[i]].astype(BF)) for i in heads]
+    weights = [jnp.where(causal, x, 0.0).astype(BF) for x in weights]
+    norms = split(jnp.broadcast_to(pn_ref[0, 0], (length, group * 2 * width)))
+    ones = jnp.ones((length, length), BF)
+    den = [
+        mm_nt(
+            cat(weights[i], query_rows[i], query_rows[i]),
+            cat(ones, norms[0][:, rows[i]], norms[1][:, rows[i]]),
+        )
+        for i in heads
+    ]
+    inverse = [1.0 / x for x in den]
+    scaled = [(c_ref[:, cols[i]].astype(F32) * inverse[i]).astype(BF) for i in heads]
+    sums = [mm(query_t[i], scaled[i]) for i in heads]
+    for i in heads:
+        qp_ref[0, 0, rows[i]] = probs[i]
+        qr_ref[0, 0, i] = query_rows[i]
+        wt_ref[0, 0, i] = weights[i]
+        inv_ref[0, 0, i] = inverse[i]
+    put_half(own_ref, other_ref, stack(*sums))
 
 
 def middle_kernel(
-    order, q_ref, c_ref, v_ref, kp_ref, qp_ref, wt_ref, pn_ref, so_ref, st_ref,
+    order, q_ref, c_ref, v_ref, kp_ref, qp_ref, qr_ref, wt_ref, inv_ref, pn_ref, so_ref, st_ref,
     att_ref, own_ref, other_ref, gk_ref, sn_ref,
 ):
     group, length = wt_ref.shape[2], wt_ref.shape[3]
     dim = v_ref.shape[1]
+    feats = qp_ref.shape[2] // group
     causal = causal_mask(length)
     half = pl.program_id(1)
+    heads = range(group)
+    cols = [slice(i * dim, (i + 1) * dim) for i in heads]
+    rows = [slice(i * feats, (i + 1) * feats) for i in heads]
     values = v_ref[...]
-    ones = jnp.ones((2 * dim, length), BF)
-    ones_rows = jnp.ones((16, 2 * dim), BF)
-    feats = qp_ref.shape[2] // group
-    grads = []
-    for i in range(group):
-        cols = slice(i * dim, (i + 1) * dim)
-        rows = slice(i * feats, (i + 1) * feats)
-        state = jnp.where(half == 0, so_ref[rows], st_ref[rows])
-        high, low = split(state)
-        norm_row = pn_ref[0, 0, :, rows]
-        probs = qp_ref[0, 0, rows]
-        query_t = probs.astype(BF)
-        query_rows = query_t.T
-        key_t = kp_ref[0, 0, rows].astype(BF)
-        weights = wt_ref[0, 0, i]
-        inverse = 1.0 / denominators(weights, query_rows, norm_row)
-        numerator = mm(
-            jnp.concatenate([weights, query_rows], axis=1),
-            jnp.concatenate([values, high], axis=0),
-        ) + mm(query_rows, low)
-        att_ref[:, cols] = (numerator * inverse).astype(BF)
-        upstream = c_ref[:, cols].astype(F32)
-        scaled_wide = upstream * inverse
-        scaled = scaled_wide.astype(BF)
-        product = jnp.concatenate(split(-(scaled_wide * inverse) * numerator), axis=1)
-        norm_grad = mm(product, ones)
-        norm_grad_row = mm_nt(ones_rows, product)[:1]
-        mixed = mm_nt(scaled, values) + norm_grad
-        block = jnp.where(causal, mixed, 0.0).astype(BF)
-        upstream_q = mm_nt(
-            jnp.concatenate([key_t, high], axis=1), jnp.concatenate([block, scaled], axis=1)
-        )
-        upstream_q = upstream_q + mm_nt(low, scaled) + outer(norm_row, norm_grad_row)
-        grads.append(mm(soft_back(probs, upstream_q), q_ref[:, cols]))
-        gk_ref[0, 0, rows] = mm(query_t, block)
-        grad_high, grad_low = split(jnp.broadcast_to(norm_grad_row, (16, length)))
-        sn_ref[0, 0, :, rows] = (mm(grad_high, query_rows) + mm(grad_low, query_rows))[:1]
-    put_half(own_ref, other_ref, jnp.concatenate(grads, axis=0))
+    ones = jnp.ones((2 * dim, dim), BF)
+    lane = lax.broadcasted_iota(jnp.int32, (length, dim), 1)
+    values_wide = cat(values, jnp.where(lane < 2, 1.0, 0.0).astype(BF))
+    states = [split(jnp.where(half == 0, so_ref[r], st_ref[r])) for r in rows]
+    norm_cols = column(pn_ref[0, 0])
+    norm_cols = [
+        three_lanes(jnp.broadcast_to(norm_cols[r], (feats, dim)), "hhl") for r in rows
+    ]
+    query_rows = [qr_ref[0, 0, i] for i in heads]
+    numerator = [
+        mm(
+            cat(wt_ref[0, 0, i], query_rows[i], query_rows[i]),
+            stack(values, states[i][0], states[i][1]),
+        )
+        for i in heads
+    ]
+    inverse = [inv_ref[0, 0, i] for i in heads]
+    scaled_wide = [c_ref[:, cols[i]].astype(F32) * inverse[i] for i in heads]
+    scaled = [x.astype(BF) for x in scaled_wide]
+    products = [cat(*split(-(scaled_wide[i] * inverse[i]) * numerator[i])) for i in heads]
+    norm_grad = [mm(x, ones) for x in products]
+    norm_lanes = [three_lanes(x, "hlh") for x in norm_grad]
+    mixed = [mm_nt(cat(scaled[i], norm_lanes[i]), values_wide) for i in heads]
+    block = [jnp.where(causal, x, 0.0).astype(BF) for x in mixed]
+    upstream = [
+        mm_nt(
+            cat(kp_ref[0, 0, rows[i]].astype(BF), states[i][0], norm_cols[i], states[i][1]),
+            cat(block[i], scaled[i], norm_lanes[i], scaled[i]),
+        )
+        for i in heads
+    ]
+    probs = [qp_ref[0, 0, r] for r in rows]
+    back = [soft_back(probs[i], upstream[i]) for i in heads]
+    grads = [mm(back[i], q_ref[:, cols[i]]) for i in heads]
+    for i in heads:
+        att_ref[:, cols[i]] = (numerator[i] * inverse[i]).astype(BF)
+        sn_ref[0, 0, :, rows[i]] = jnp.sum(
+            query_rows[i].astype(F32) * norm_grad[i], axis=0, keepdims=True
+        )
+        gk_ref[0, 0, rows[i]] = mm(probs[i].astype(BF), block[i])
+    put_half(own_ref, other_ref, stack(*grads))
 
 
 def last_kernel(
     order, k_ref, v_ref, kp_ref, gk_ref, sn_ref, to_ref, tt_ref, own_ref, other_ref
 ):
     half = pl.program_id(1)
-    rows = kp_ref.shape[2]
-    length = k_ref.shape[0]
-    state = jnp.where(half == 0, to_ref[...], tt_ref[...])
-    high, low = split(state)
+    rows, length = kp_ref.shape[2:]
+    feats = k_ref.shape[1]
+    high, low = split(jnp.where(half == 0, to_ref[...], tt_ref[...]))
     values = v_ref[...]
-    upstream = gk_ref[0, 0] + mm_nt(
-        jnp.concatenate([high, low], axis=1), jnp.concatenate([values, values], axis=1)
-    )
-    upstream = upstream + outer(sn_ref[0, 0], jnp.ones((1, length), F32))
+    upstream = gk_ref[0, 0] + mm_nt(cat(high, low), cat(values, values))
+    upstream = upstream + jnp.broadcast_to(column(sn_ref[0, 0]), (rows, length))
     probs = kp_ref[0, 0]
-    dim = k_ref.shape[1]
-    feats = dim
     back = [
         soft_back(probs[a : a + feats], upstream[a : a + feats]) for a in range(0, rows, feats)
     ]
-    put_half(own_ref, other_ref, mm(jnp.concatenate(back, axis=0), k_ref[...]))
+    put_half(own_ref, other_ref, mm(stack(*back), k_ref[...]))
 
 
 def out_kernel(order, x_ref, o_ref):
-    group, dim, width = o_ref.shape
-    for i in range(group):
-        o_ref[i] = x_ref[0, i * width : (i + 1) * width].T
+    o_ref[...] = x_ref[...]
 
 
 def core_swap(x):
@@ -304,6 +315,8 @@
     cotangent = cotangent.reshape(length, head_count * dim)
     keys = key_tokens.reshape(length, shared * dim)
     values = value_tokens.reshape(length, shared * dim)
+    query_map = jnp.swapaxes(query_map, 1, 2)
+    key_map = jnp.swapaxes(key_map, 1, 2)
 
     ctx = lax.axis_index("ctx")
     chips = lax.axis_size("ctx") // 2
@@ -319,13 +332,14 @@
     def head_cols(rows, cols):
         return pl.BlockSpec((rows, cols), lambda i, s, order: (0, order[s * n + i]))
 
-    map_spec = pl.BlockSpec((group, dim, width), lambda i, s, order: (order[s * n + i], 0, 0))
+    map_spec = pl.BlockSpec((group, width, dim), lambda i, s, order: (order[s * n + i], 0, 0))
     kept_spec = pl.BlockSpec((1, 1, wide, length), lambda i, s, order: (i, s, 0, 0))
     kept = jax.ShapeDtypeStruct((n, 2, wide, length), F32)
     row_spec = pl.BlockSpec((1, 1, 1, wide), lambda i, s, order: (i, s, 0, 0))
     row = jax.ShapeDtypeStruct((n, 2, 1, wide), F32)
     weight_spec = pl.BlockSpec((1, 1, group, length, length), lambda i, s, order: (i, s, 0, 0, 0))
     weight = jax.ShapeDtypeStruct((n, 2, group, length, length), BF)
+    inverse = jax.ShapeDtypeStruct((n, 2, group, length, dim), F32)
 
     def half_spec(rows):
         return pl.BlockSpec((rows, dim), lambda i, s, order: (i, 0))
@@ -356,23 +370,28 @@
     prefix_norm = scan_norms(norm, chip, core, chips, True)
     prefix_own, prefix_other = scan_states(own, other, chip, core, chips, True)
 
-    query_probs, weights, own, other = call(
+    query_probs, query_rows, weights, inverse, own, other = call(
         "query_features",
         query_kernel,
         [wide_token, wide_token, map_spec, kept_spec, row_spec],
-        [kept_spec, weight_spec, half_spec(wide), half_spec(wide)],
-        [kept, weight, state, state],
+        [kept_spec, weight_spec, weight_spec, weight_spec, half_spec(wide), half_spec(wide)],
+        [kept, weight, weight, inverse, state, state],
     )(order, queries, cotangent, query_map, key_probs, prefix_norm)
     suffix_own, suffix_other = scan_states(own, other, chip, core, chips, False)
 
     attended, query_own, query_other, key_up, norm = call(
         "attend",
         middle_kernel,
-        [wide_token, wide_token, token, kept_spec, kept_spec, weight_spec, row_spec]
+        [wide_token, wide_token, token, kept_spec, kept_spec]
+        + [weight_spec] * 3
+        + [row_spec]
         + [half_spec(wide)] * 2,
         [wide_token, half_spec(group * width), half_spec(group * width), kept_spec, row_spec],
         [jax.ShapeDtypeStruct((length, head_count * dim), BF), grad, grad, kept, row],
-    )(order, queries, cotangent, values, key_probs, query_probs, weights, prefix_norm, prefix_own, prefix_other)
+    )(
+        order, queries, cotangent, values, key_probs, query_probs, query_rows, weights, inverse,
+        prefix_norm, prefix_own, prefix_other,
+    )
     suffix_norm = scan_norms(norm, chip, core, chips, False)
 
     key_own, key_other = call(
@@ -386,18 +405,20 @@
     def finish(name, own, other):
         shape = (n, group * width, dim)
         total = sum_all(own.reshape(shape), other.reshape(shape), chips)
-        return pl.pallas_call(
+        rows = pl.BlockSpec((1, group * width, dim), lambda i, back: (back[i], 0, 0))
+        natural = pl.pallas_call(
             out_kernel,
             name=name,
-            out_shape=jax.ShapeDtypeStruct((head_count, dim, width), F32),
+            out_shape=jax.ShapeDtypeStruct((shared, group * width, dim), F32),
             grid_spec=pltpu.PrefetchScalarGridSpec(
                 num_scalar_prefetch=1,
                 grid=(shared,),
-                in_specs=[pl.BlockSpec((1, group * width, dim), lambda i, back: (back[i], 0, 0))],
-                out_specs=pl.BlockSpec((group, dim, width), lambda i, back: (i, 0, 0)),
+                in_specs=[rows],
+                out_specs=pl.BlockSpec((1, group * width, dim), lambda i, back: (i, 0, 0)),
             ),
             compiler_params=pltpu.CompilerParams(vmem_limit_bytes=VMEM_LIMIT),
         )(back, total)
+        return jnp.swapaxes(natural.reshape(head_count, width, dim), 1, 2)
 
     query_grad = finish("query_out", query_own, query_other)
     key_grad = finish("key_out", key_own, key_other)

time: 221 us -> 193 us (0.87)
  Pallas kernels: 57.4 us -> 37 us
  local copies, waits for them, and re-layouts: 25.9 us -> 17.9 us
    pallas_call x1, Pallas kernels: 20.4 us -> 8.13 us  [shards(): call('query_features', query_kernel, [wide_token, wide_token, map_spec, k...]
    pallas_call x1, Pallas kernels: 20.9 us -> 9.79 us  [shards(): call('attend', middle_kernel, [wide_token, wide_token, token, kept_spec,...]
    unnamed x60, local copies, waits for them, and re-layouts: 24.7 us -> 17.8 us
    pallas_call x2, Pallas kernels: 3.37 us -> 6.53 us  [finish(): pl.pallas_call(out_kernel, name=name, out_shape=jax.ShapeDtypeStruct((sha...]
  transfers between devices with their start and end apart: 38 -> 38, of which waited for: 16 -> 17; matrix products, arithmetic and copies ran while one was open for 10% -> 9% of each run, Pallas kernels for 23% -> 14%
where the time goes in v1:
time: 193 us
  waiting for transfers between devices  61.8 us (32%)
  starting transfers between devices  58.1 us (30%)
  Pallas kernels  37 us (19%)
  local copies, waits for them, and re-layouts  17.9 us (9%)
  other arithmetic  16.5 us (9%)
    ppermute x16, waiting for transfers between devices, chip_move(): lax.ppermute(x, 'ctx', [(2 * a + c, 2 * b + c) for a, b in pairs for c in...  51.8 us
    ppermute x16, starting transfers between devices, chip_move(): lax.ppermute(x, 'ctx', [(2 * a + c, 2 * b + c) for a, b in pairs for c in...  23.1 us
    ppermute x10, starting transfers between devices, core_swap(): return lax.ppermute(x, 'ctx', [(i, i ^ 1) for i in range(size)])  20.3 us
    unnamed x60, local copies, waits for them, and re-layouts  17.8 us
    pallas_call x1, Pallas kernels, shards(): call('attend', middle_kernel, [wide_token, wide_token, token, kept_spec,...  9.79 us
    pallas_call x1, Pallas kernels, shards(): call('query_features', query_kernel, [wide_token, wide_token, map_spec, k...  8.13 us
    ppermute x6, starting transfers between devices, sum_all(): lax.ppermute(total, 'dp', [(i, i ^ k) for i in range(dp)])  7.55 us
    ppermute x6, starting transfers between devices, sum_all(): lax.ppermute(mine[k * share:(k + 1) * share], 'dp', [(i, i ^ k) for i in...  7.2 us
  transfers between devices with their start and end apart: 38, of which 17 were waited for; matrix products, arithmetic and copies ran while one was open for 9% of the time, Pallas kernels for 14%

profile of v1, /device:TPU:1, one launch (start us, length us, event | category | flops | bytes accessed | tf_op | source)
XLA Modules:
  0.0 192.6 jit_solution(3589671207034585176)
XLA Ops:
  3.7 5.9 %key_features.1 = (f32[4,2,512,128]{3,2,1,0:T(8,128)S(1)}, f32[2048,128]{1,0:T(8,128)S(1)}, f32[2048,128]{1,0:T(8,128)}, f32[4,2,1,512]{3,2,1,0:T(1,128)S(1)}) custom-call(s32[8]{0:T(128)S(1)} %pad_add_fusion.order, bf16[128,1024]{1,0:T(8,128)(2,1)S(1)} %bitcast.24, bf16[128,1024]{1,0:T(8,128)(2,1)S(1)} %bitcast.21, bf16[32,64,128]{2,1,0:T(8,128)(2,1)S(1)} %bitcast.29), custom_call_target="tpu_custom_call" | custom-call | tf_op jit(solution)/shard_map/key_features/pallas_call | solution.py:363
  11.9 2.7 %collective-permute-start.1 = (f32[4,2,1,512]{3,2,1,0:T(1,128)S(1)}, f32[4,2,1,512]{3,2,1,0:T(1,128)S(1)}, u32[]{:S(2)}, u32[]{:S(2)}) collective-permute-start(f32[4,2,1,512]{3,2,1,0:T(1,128)S(1)} %reverse_add_fusion.1), channel_id=1, source_target_pairs={{0,2},{1,3},{2,0},{3,1},{4,6},{5,7},{6,4},{7,5},{8,10},{9,11},{10,... | collective-permute-start | bytes 49160 | tf_op jit(solution)/shard_map/ppermute | solution.py:213
  15.8 2.5 %collective-permute-start.2 = (f32[4,2,1,512]{3,2,1,0:T(1,128)S(1)}, f32[4,2,1,512]{3,2,1,0:T(1,128)S(1)}, u32[]{:S(2)}, u32[]{:S(2)}) collective-permute-start(f32[4,2,1,512]{3,2,1,0:T(1,128)S(1)} %add.142), channel_id=1, source_target_pairs={{0,4},{1,5},{2,6},{3,7},{4,0},{5,1},{6,2},{7,3},{8,12},{9,13},{10,... | collective-permute-start | bytes 49160 | tf_op jit(solution)/shard_map/ppermute | solution.py:213
  23.0 8.1 %query_features.1 = (f32[4,2,512,128]{3,2,1,0:T(8,128)S(1)}, bf16[4,2,4,128,128]{4,3,2,1,0:T(8,128)(2,1)S(1)}, bf16[4,2,4,128,128]{4,3,2,1,0:T(8,128)(2,1)S(1)},...) custom-call(s32[8]{0:T(128)S(1)} %pad_add_fusion.order, ...), custom_call_target="tpu_custom_call" | custom-call | tf_op jit(solution)/shard_map/query_features/pallas_call | solution.py:373
  36.8 2.2 %collective-permute-start.22 = (f32[2048,128]{1,0:T(8,128)}, f32[2048,128]{1,0:T(8,128)}, u32[]{:S(2)}, u32[]{:S(2)}) collective-permute-start(f32[2048,128]{1,0:T(8,128)} %get-tuple-element.34), channel_id=1, source_target_pairs={{0,1},{1,0},{2,3},{3,2},{4,5},{5,4},{6,7},{7,6},{8,9},{9,8},{10,11... | collective-permute-start | bytes 3145736 | tf_op jit(solution)/shard_map/ppermute | solution.py:209
  42.3 4.3 %collective-permute-start.4 = (f32[1024,128]{1,0:T(8,128)}, f32[1024,128]{1,0:T(8,128)}, u32[]{:S(2)}, u32[]{:S(2)}) collective-permute-start(f32[1024,128]{1,0:T(8,128)} %get-tuple-element.51), channel_id=1, source_target_pairs={{0,2},{1,3},{2,4},{3,5},{4,6},{5,7},{8,10},{9,11},{10,12},{11,13},... | collective-permute-start | bytes 1572872 | tf_op jit(solution)/shard_map/ppermute | solution.py:213
  46.6 4.3 %collective-permute-start.5 = (f32[1024,128]{1,0:T(8,128)}, f32[1024,128]{1,0:T(8,128)}, u32[]{:S(2)}, u32[]{:S(2)}) collective-permute-start(f32[1024,128]{1,0:T(8,128)} %get-tuple-element.52), channel_id=1, source_target_pairs={{0,4},{1,5},{8,12},{9,13},{16,20},{17,21},{24,28},{25,29}} | collective-permute-start | bytes 1572872 | tf_op jit(solution)/shard_map/ppermute | solution.py:213
  57.5 11.3 %collective-permute-done.5 = f32[1024,128]{1,0:T(8,128)} collective-permute-done((f32[1024,128]{1,0:T(8,128)}, f32[1024,128]{1,0:T(8,128)}, u32[]{:S(2)}, u32[]{:S(2)}) %collective-permute-start.5) | collective-permute-done | bytes 524320 | tf_op jit(solution)/shard_map/ppermute | solution.py:213
  78.6 4.6 %collective-permute-done.6 = f32[1024,128]{1,0:T(8,128)} collective-permute-done((f32[1024,128]{1,0:T(8,128)}, f32[1024,128]{1,0:T(8,128)}, u32[]{:S(2)}, u32[]{:S(2)}) %collective-permute-start.6) | collective-permute-done | bytes 524320 | tf_op jit(solution)/shard_map/ppermute | solution.py:213
  86.6 7.3 %collective-permute-done.25 = f32[1024,128]{1,0:T(8,128)S(1)} collective-permute-done((f32[1024,128]{1,0:T(8,128)S(1)}, f32[1024,128]{1,0:T(8,128)S(1)}, u32[]{:S(2)}, u32[]{:S(2)}) %collective-permute-start.25) | collective-permute-done | bytes 524320 | tf_op jit(solution)/shard_map/ppermute | solution.py:213
  93.8 12.1 %collective-permute-done.26 = f32[1024,128]{1,0:T(8,128)S(1)} collective-permute-done((f32[1024,128]{1,0:T(8,128)S(1)}, f32[1024,128]{1,0:T(8,128)S(1)}, u32[]{:S(2)}, u32[]{:S(2)}) %collective-permute-start.26) | collective-permute-done | bytes 524320 | tf_op jit(solution)/shard_map/ppermute | solution.py:213
  108.6 3.4 %collective-permute-start.27 = (f32[2048,128]{1,0:T(8,128)}, f32[2048,128]{1,0:T(8,128)}, u32[]{:S(2)}, u32[]{:S(2)}) collective-permute-start(f32[2048,128]{1,0:T(8,128)} %get-tuple-element.41), channel_id=1, source_target_pairs={{0,1},{1,0},{2,3},{3,2},{4,5},{5,4},{6,7},{7,6},{8,9},{9,8},{10,11... | collective-permute-start | bytes 3145736 | tf_op jit(solution)/shard_map/ppermute | solution.py:209
  112.1 9.8 %attend.1 = (bf16[128,4096]{1,0:T(8,128)(2,1)}, f32[1024,128]{1,0:T(8,128)S(1)}, f32[1024,128]{1,0:T(8,128)}, f32[4,2,512,128]{3,2,1,0:T(8,128)S(1)}, f32[4,2,1,512]{3,2,1,0:T(1,128)S(1)}) custom-call(s32[8]{0:T(128)S(1)} %pad_add_fusion.order, bf16[128,4096]{1,0:T(8,128)(2,1)S(1)} %bitcast.18, bf16[128,4096]{1,0:T(8,128)(2,1)S(1)} %bitcast.20, ...), custom_call_target="tpu_custom_call" | custom-call | tf_op jit(solution)/shard_map/attend/pallas_call | solution.py:382
  125.3 2.6 %collective-permute-done.20 = f32[4,2,1,512]{3,2,1,0:T(1,128)S(1)} collective-permute-done((f32[4,2,1,512]{3,2,1,0:T(1,128)S(1)}, f32[4,2,1,512]{3,2,1,0:T(1,128)S(1)}, u32[]{:S(2)}, u32[]{:S(2)}) %collective-permute-start.20) | collective-permute-done | bytes 16416 | tf_op jit(solution)/shard_map/ppermute | solution.py:213
  134.0 6.7 %key_grads.1 = (f32[1024,128]{1,0:T(8,128)S(1)}, f32[1024,128]{1,0:T(8,128)S(1)}) custom-call(s32[8]{0:T(128)S(1)} %pad_add_fusion.order, bf16[128,1024]{1,0:T(8,128)(2,1)S(1)} %bitcast.25, bf16[128,1024]{1,0:T(8,128)(2,1)S(1)} %bitcast.23, f32[4,2,512,128]{3,2,1,0:T(8,128)S(1)} %get-tuple-element.20.kp_ref, f32[4,2,512,128]{3,2,1,0:T(8,128)S(1)} %copy-done.13, ...), custom_call_target="tpu_custom_call" | custom-call | tf_op jit(solution)/shard_map/key_grads/pallas_call | solution.py:397
  140.8 2.5 %collective-permute-start.28 = (f32[4,256,128]{2,1,0:T(8,128)S(1)}, f32[4,256,128]{2,1,0:T(8,128)S(1)}, u32[]{:S(2)}, u32[]{:S(2)}) collective-permute-start(f32[4,256,128]{2,1,0:T(8,128)S(1)} %bitcast.30), channel_id=1, source_target_pairs={{0,1},{1,0},{2,3},{3,2},{4,5},{5,4},{6,7},{7,6},{8,9},{9,8},{10,11... | collective-permute-start | bytes 1572872 | tf_op jit(solution)/shard_map/ppermute | solution.py:209
  155.0 2.8 %collective-permute-done.30 = f32[1,256,128]{2,1,0:T(8,128)S(1)} collective-permute-done((f32[1,256,128]{2,1,0:T(8,128)S(1)}, f32[1,256,128]{2,1,0:T(8,128)S(1)}, u32[]{:S(2)}, u32[]{:S(2)}) %collective-permute-start.30) | collective-permute-done | bytes 131104 | tf_op jit(solution)/shard_map/ppermute | solution.py:279
  159.1 5.8 %collective-permute-done.32 = f32[1,256,128]{2,1,0:T(8,128)S(1)} collective-permute-done((f32[1,256,128]{2,1,0:T(8,128)S(1)}, f32[1,256,128]{2,1,0:T(8,128)S(1)}, u32[]{:S(2)}, u32[]{:S(2)}) %collective-permute-start.32) | collective-permute-done | bytes 131104 | tf_op jit(solution)/shard_map/ppermute | solution.py:213
  165.0 3.6 %collective-permute-start.15 = (f32[1,256,128]{2,1,0:T(8,128)S(1)}, f32[1,256,128]{2,1,0:T(8,128)S(1)}, u32[]{:S(2)}, u32[]{:S(2)}) collective-permute-start(f32[1,256,128]{2,1,0:T(8,128)S(1)} %get-tuple-element.40), channel_id=1, source_target_pairs={{0,8},{8,0},{16,24},{24,16},{1,9},{9,1},{17,25},{25,17},{2,10},{10... | collective-permute-start | bytes 393224 | tf_op jit(solution)/shard_map/ppermute | solution.py:287
  169.8 3.0 %collective-permute-done.33 = f32[1,256,128]{2,1,0:T(8,128)S(1)} collective-permute-done((f32[1,256,128]{2,1,0:T(8,128)S(1)}, f32[1,256,128]{2,1,0:T(8,128)S(1)}, u32[]{:S(2)}, u32[]{:S(2)}) %collective-permute-start.33) | collective-permute-done | bytes 131104 | tf_op jit(solution)/shard_map/ppermute | solution.py:213
  175.6 7.5 %collective-permute-start.18 = (f32[4,256,128]{2,1,0:T(8,128)S(1)}, f32[4,256,128]{2,1,0:T(8,128)S(1)}, u32[]{:S(2)}, u32[]{:S(2)}) collective-permute-start(f32[4,256,128]{2,1,0:T(8,128)S(1)} %pad_maximum_fusion.2), channel_id=1, source_target_pairs={{0,1},{1,0},{2,3},{3,2},{4,5},{5,4},{6,7},{7,6},{8,9},{9,8},{10,11... | collective-permute-start | bytes 1572872 | tf_op jit(solution)/shard_map/ppermute | solution.py:209
  183.2 2.7 %collective-permute-start.37 = (f32[4,256,128]{2,1,0:T(8,128)S(1)}, f32[4,256,128]{2,1,0:T(8,128)S(1)}, u32[]{:S(2)}, u32[]{:S(2)}) collective-permute-start(f32[4,256,128]{2,1,0:T(8,128)S(1)} %pad_maximum_fusion.3), channel_id=1, source_target_pairs={{0,1},{1,0},{2,3},{3,2},{4,5},{5,4},{6,7},{7,6},{8,9},{9,8},{10,11... | collective-permute-start | bytes 1572872 | tf_op jit(solution)/shard_map/ppermute | solution.py:209
  186.0 3.3 %query_out.1 = f32[8,256,128]{2,1,0:T(8,128)} custom-call(s32[8]{0:T(128)S(1)} %fusion.9.order, f32[8,256,128]{2,1,0:T(8,128)S(1)} %constant_dynamic-update-slice_fusion.x_ref), custom_call_target="tpu_custom_call" | custom-call | tf_op jit(solution)/shard_map/query_out/pallas_call | solution.py:409
  189.3 3.3 %key_out.1 = f32[8,256,128]{2,1,0:T(8,128)} custom-call(s32[8]{0:T(128)S(1)} %fusion.9.order, f32[8,256,128]{2,1,0:T(8,128)S(1)} %constant_dynamic-update-slice_fusion.5.x_ref), custom_call_target="tpu_custom_call" | custom-call | tf_op jit(solution)/shard_map/key_out/pallas_call | solution.py:409
  (151 shorter events, 69.4 us)
Async XLA Ops:
  9.5 29.4 %collective-permute-start.3 = (f32[2048,128]{1,0:T(8,128)}, f32[2048,128]{1,0:T(8,128)}, u32[]{:S(2)}, u32[]{:S(2)}) collective-permute-start(f32[2048,128]{1,0:T(8,128)} %get-tuple-element.27), channel_id=1, source_target_pairs={{0,1},{1,0},{2,3},{3,2},{4,5},{5,4},{6,7},{7,6},{8,9},{9,8},{10,11... | collective-permute-start | bytes 3145736 | tf_op jit(solution)/shard_map/ppermute | solution.py:209
  36.8 14.2 %collective-permute-start.22 = (f32[2048,128]{1,0:T(8,128)}, f32[2048,128]{1,0:T(8,128)}, u32[]{:S(2)}, u32[]{:S(2)}) collective-permute-start(f32[2048,128]{1,0:T(8,128)} %get-tuple-element.34), channel_id=1, source_target_pairs={{0,1},{1,0},{2,3},{3,2},{4,5},{5,4},{6,7},{7,6},{8,9},{9,8},{10,11... | collective-permute-start | bytes 3145736 | tf_op jit(solution)/shard_map/ppermute | solution.py:209
  42.3 15.2 %collective-permute-start.4 = (f32[1024,128]{1,0:T(8,128)}, f32[1024,128]{1,0:T(8,128)}, u32[]{:S(2)}, u32[]{:S(2)}) collective-permute-start(f32[1024,128]{1,0:T(8,128)} %get-tuple-element.51), channel_id=1, source_target_pairs={{0,2},{1,3},{2,4},{3,5},{4,6},{5,7},{8,10},{9,11},{10,12},{11,13},... | collective-permute-start | bytes 1572872 | tf_op jit(solution)/shard_map/ppermute | solution.py:213
  46.6 22.1 %collective-permute-start.5 = (f32[1024,128]{1,0:T(8,128)}, f32[1024,128]{1,0:T(8,128)}, u32[]{:S(2)}, u32[]{:S(2)}) collective-permute-start(f32[1024,128]{1,0:T(8,128)} %get-tuple-element.52), channel_id=1, source_target_pairs={{0,4},{1,5},{8,12},{9,13},{16,20},{17,21},{24,28},{25,29}} | collective-permute-start | bytes 1572872 | tf_op jit(solution)/shard_map/ppermute | solution.py:213
  53.9 20.6 %collective-permute-start.23 = (f32[1024,128]{1,0:T(8,128)}, f32[1024,128]{1,0:T(8,128)}, u32[]{:S(2)}, u32[]{:S(2)}) collective-permute-start(f32[1024,128]{1,0:T(8,128)} %get-tuple-element.45), channel_id=1, source_target_pairs={{6,4},{7,5},{4,2},{5,3},{2,0},{3,1},{14,12},{15,13},{12,10},{13,11... | collective-permute-start | bytes 1572872 | tf_op jit(solution)/shard_map/ppermute | solution.py:213
  55.2 19.3 %collective-permute-start.24 = (f32[1024,128]{1,0:T(8,128)}, f32[1024,128]{1,0:T(8,128)}, u32[]{:S(2)}, u32[]{:S(2)}) collective-permute-start(f32[1024,128]{1,0:T(8,128)} %get-tuple-element.46), channel_id=1, source_target_pairs={{6,2},{7,3},{14,10},{15,11},{22,18},{23,19},{30,26},{31,27}} | collective-permute-start | bytes 1572872 | tf_op jit(solution)/shard_map/ppermute | solution.py:213
  70.9 12.4 %collective-permute-start.6 = (f32[1024,128]{1,0:T(8,128)}, f32[1024,128]{1,0:T(8,128)}, u32[]{:S(2)}, u32[]{:S(2)}) collective-permute-start(f32[1024,128]{1,0:T(8,128)} %select_select_fusion.1), channel_id=1, source_target_pairs={{0,2},{1,3},{2,4},{3,5},{4,6},{5,7},{8,10},{9,11},{10,12},{11,13},... | collective-permute-start | bytes 1572872 | tf_op jit(solution)/shard_map/ppermute | solution.py:213
  73.0 10.3 %collective-permute-start.7 = (f32[1024,128]{1,0:T(8,128)}, f32[1024,128]{1,0:T(8,128)}, u32[]{:S(2)}, u32[]{:S(2)}) collective-permute-start(f32[1024,128]{1,0:T(8,128)} %select_select_fusion.1), channel_id=1, source_target_pairs={{2,6},{3,7},{10,14},{11,15},{18,22},{19,23},{26,30},{27,31}} | collective-permute-start | bytes 1572872 | tf_op jit(solution)/shard_map/ppermute | solution.py:213
  76.0 17.8 %collective-permute-start.25 = (f32[1024,128]{1,0:T(8,128)S(1)}, f32[1024,128]{1,0:T(8,128)S(1)}, u32[]{:S(2)}, u32[]{:S(2)}) collective-permute-start(f32[1024,128]{1,0:T(8,128)S(1)} %select_select_fusion), channel_id=1, source_target_pairs={{6,4},{7,5},{4,2},{5,3},{2,0},{3,1},{14,12},{15,13},{12,10},{13,11... | collective-permute-start | bytes 1572872 | tf_op jit(solution)/shard_map/ppermute | solution.py:213
  77.3 28.6 %collective-permute-start.26 = (f32[1024,128]{1,0:T(8,128)S(1)}, f32[1024,128]{1,0:T(8,128)S(1)}, u32[]{:S(2)}, u32[]{:S(2)}) collective-permute-start(f32[1024,128]{1,0:T(8,128)S(1)} %select_select_fusion), channel_id=1, source_target_pairs={{4,0},{5,1},{12,8},{13,9},{20,16},{21,17},{28,24},{29,25}} | collective-permute-start | bytes 1572872 | tf_op jit(solution)/shard_map/ppermute | solution.py:213
  86.5 25.6 %collective-permute-start.8 = (f32[2048,128]{1,0:T(8,128)S(1)}, f32[2048,128]{1,0:T(8,128)S(1)}, u32[]{:S(2)}, u32[]{:S(2)}) collective-permute-start(f32[2048,128]{1,0:T(8,128)S(1)} %get-tuple-element.47), channel_id=1, source_target_pairs={{0,1},{1,0},{2,3},{3,2},{4,5},{5,4},{6,7},{7,6},{8,9},{9,8},{10,11... | collective-permute-start | bytes 3145736 | tf_op jit(solution)/shard_map/ppermute | solution.py:209
  108.6 22.8 %collective-permute-start.27 = (f32[2048,128]{1,0:T(8,128)}, f32[2048,128]{1,0:T(8,128)}, u32[]{:S(2)}, u32[]{:S(2)}) collective-permute-start(f32[2048,128]{1,0:T(8,128)} %get-tuple-element.41), channel_id=1, source_target_pairs={{0,1},{1,0},{2,3},{3,2},{4,5},{5,4},{6,7},{7,6},{8,9},{9,8},{10,11... | collective-permute-start | bytes 3145736 | tf_op jit(solution)/shard_map/ppermute | solution.py:209
  128.0 15.3 %collective-permute-start.9 = (f32[4,256,128]{2,1,0:T(8,128)}, f32[4,256,128]{2,1,0:T(8,128)}, u32[]{:S(2)}, u32[]{:S(2)}) collective-permute-start(f32[4,256,128]{2,1,0:T(8,128)} %bitcast.8), channel_id=1, source_target_pairs={{0,1},{1,0},{2,3},{3,2},{4,5},{5,4},{6,7},{7,6},{8,9},{9,8},{10,11... | collective-permute-start | bytes 1572872 | tf_op jit(solution)/shard_map/ppermute | solution.py:209
  147.3 7.8 %collective-permute-start.29 = (f32[1,256,128]{2,1,0:T(8,128)S(1)}, f32[1,256,128]{2,1,0:T(8,128)S(1)}, u32[]{:S(2)}, u32[]{:S(2)}) collective-permute-start(f32[1,256,128]{2,1,0:T(8,128)S(1)} %get-tuple-element.53), channel_id=1, source_target_pairs={{0,8},{8,0},{16,24},{24,16},{1,9},{9,1},{17,25},{25,17},{2,10},{10... | collective-permute-start | bytes 393224 | tf_op jit(solution)/shard_map/ppermute | solution.py:279
  148.6 9.3 %collective-permute-start.30 = (f32[1,256,128]{2,1,0:T(8,128)S(1)}, f32[1,256,128]{2,1,0:T(8,128)S(1)}, u32[]{:S(2)}, u32[]{:S(2)}) collective-permute-start(f32[1,256,128]{2,1,0:T(8,128)S(1)} %get-tuple-element.55), channel_id=1, source_target_pairs={{0,16},{8,24},{16,0},{24,8},{1,17},{9,25},{17,1},{25,9},{2,18},{10... | collective-permute-start | bytes 393224 | tf_op jit(solution)/shard_map/ppermute | solution.py:279
  149.8 9.1 %collective-permute-start.31 = (f32[1,256,128]{2,1,0:T(8,128)S(1)}, f32[1,256,128]{2,1,0:T(8,128)S(1)}, u32[]{:S(2)}, u32[]{:S(2)}) collective-permute-start(f32[1,256,128]{2,1,0:T(8,128)S(1)} %get-tuple-element.54), channel_id=1, source_target_pairs={{0,24},{8,16},{16,8},{24,0},{1,25},{9,17},{17,9},{25,1},{2,26},{10... | collective-permute-start | bytes 393224 | tf_op jit(solution)/shard_map/ppermute | solution.py:279
  164.9 7.9 %collective-permute-start.33 = (f32[1,256,128]{2,1,0:T(8,128)S(1)}, f32[1,256,128]{2,1,0:T(8,128)S(1)}, u32[]{:S(2)}, u32[]{:S(2)}) collective-permute-start(f32[1,256,128]{2,1,0:T(8,128)S(1)} %add.176), channel_id=1, source_target_pairs={{0,4},{1,5},{2,6},{3,7},{4,0},{5,1},{6,2},{7,3},{8,12},{9,13},{10,... | collective-permute-start | bytes 393224 | tf_op jit(solution)/shard_map/ppermute | solution.py:213
  165.0 9.6 %collective-permute-start.15 = (f32[1,256,128]{2,1,0:T(8,128)S(1)}, f32[1,256,128]{2,1,0:T(8,128)S(1)}, u32[]{:S(2)}, u32[]{:S(2)}) collective-permute-start(f32[1,256,128]{2,1,0:T(8,128)S(1)} %get-tuple-element.40), channel_id=1, source_target_pairs={{0,8},{8,0},{16,24},{24,16},{1,9},{9,1},{17,25},{25,17},{2,10},{10... | collective-permute-start | bytes 393224 | tf_op jit(solution)/shard_map/ppermute | solution.py:287
  168.6 7.0 %collective-permute-start.16 = (f32[1,256,128]{2,1,0:T(8,128)S(1)}, f32[1,256,128]{2,1,0:T(8,128)S(1)}, u32[]{:S(2)}, u32[]{:S(2)}) collective-permute-start(f32[1,256,128]{2,1,0:T(8,128)S(1)} %get-tuple-element.40), channel_id=1, source_target_pairs={{0,16},{8,24},{16,0},{24,8},{1,17},{9,25},{17,1},{25,9},{2,18},{10... | collective-permute-start | bytes 393224 | tf_op jit(solution)/shard_map/ppermute | solution.py:287
  168.6 7.0 %collective-permute-start.17 = (f32[1,256,128]{2,1,0:T(8,128)S(1)}, f32[1,256,128]{2,1,0:T(8,128)S(1)}, u32[]{:S(2)}, u32[]{:S(2)}) collective-permute-start(f32[1,256,128]{2,1,0:T(8,128)S(1)} %get-tuple-element.40), channel_id=1, source_target_pairs={{0,24},{8,16},{16,8},{24,0},{1,25},{9,17},{17,9},{25,1},{2,26},{10... | collective-permute-start | bytes 393224 | tf_op jit(solution)/shard_map/ppermute | solution.py:287
  172.8 10.3 %collective-permute-start.34 = (f32[1,256,128]{2,1,0:T(8,128)S(1)}, f32[1,256,128]{2,1,0:T(8,128)S(1)}, u32[]{:S(2)}, u32[]{:S(2)}) collective-permute-start(f32[1,256,128]{2,1,0:T(8,128)S(1)} %get-tuple-element.38), channel_id=1, source_target_pairs={{0,8},{8,0},{16,24},{24,16},{1,9},{9,1},{17,25},{25,17},{2,10},{10... | collective-permute-start | bytes 393224 | tf_op jit(solution)/shard_map/ppermute | solution.py:287
  174.2 8.9 %collective-permute-start.35 = (f32[1,256,128]{2,1,0:T(8,128)S(1)}, f32[1,256,128]{2,1,0:T(8,128)S(1)}, u32[]{:S(2)}, u32[]{:S(2)}) collective-permute-start(f32[1,256,128]{2,1,0:T(8,128)S(1)} %get-tuple-element.38), channel_id=1, source_target_pairs={{0,16},{8,24},{16,0},{24,8},{1,17},{9,25},{17,1},{25,9},{2,18},{10... | collective-permute-start | bytes 393224 | tf_op jit(solution)/shard_map/ppermute | solution.py:287
  174.6 8.5 %collective-permute-start.36 = (f32[1,256,128]{2,1,0:T(8,128)S(1)}, f32[1,256,128]{2,1,0:T(8,128)S(1)}, u32[]{:S(2)}, u32[]{:S(2)}) collective-permute-start(f32[1,256,128]{2,1,0:T(8,128)S(1)} %get-tuple-element.38), channel_id=1, source_target_pairs={{0,24},{8,16},{16,8},{24,0},{1,25},{9,17},{17,9},{25,1},{2,26},{10... | collective-permute-start | bytes 393224 | tf_op jit(solution)/shard_map/ppermute | solution.py:287
  175.6 10.4 %collective-permute-start.18 = (f32[4,256,128]{2,1,0:T(8,128)S(1)}, f32[4,256,128]{2,1,0:T(8,128)S(1)}, u32[]{:S(2)}, u32[]{:S(2)}) collective-permute-start(f32[4,256,128]{2,1,0:T(8,128)S(1)} %pad_maximum_fusion.2), channel_id=1, source_target_pairs={{0,1},{1,0},{2,3},{3,2},{4,5},{5,4},{6,7},{7,6},{8,9},{9,8},{10,11... | collective-permute-start | bytes 1572872 | tf_op jit(solution)/shard_map/ppermute | solution.py:209
  (41 other events, 228.0 us)

commit v2 on v1

--- a/solution.py
+++ b/solution.py
@@ -81,15 +81,21 @@
         other_ref[...] = value
 
 
-def key_kernel(order, k_ref, v_ref, w_ref, kp_ref, own_ref, other_ref, norm_ref):
-    group, width, dim = w_ref.shape
-    length = k_ref.shape[0]
-    scores = mm_nt(w_ref[...].reshape(group * width, dim), k_ref[...])
-    probs = stack(*[both_soft(scores[i * width : (i + 1) * width]) for i in range(group)])
-    kp_ref[0, 0] = probs
-    features = probs.astype(BF)
-    put_half(own_ref, other_ref, mm(features, v_ref[...]))
-    norm_ref[0, 0] = mm_nt(jnp.ones((16, length), BF), features)[:1]
+def key_kernel(
+    order, ko_ref, vo_ref, wo_ref, kt_ref, vt_ref, wt_ref, kp_ref, own_ref, other_ref, norm_ref
+):
+    group, width, dim = wo_ref.shape
+    length = ko_ref.shape[0]
+    halves = ((ko_ref, vo_ref, wo_ref, own_ref), (kt_ref, vt_ref, wt_ref, other_ref))
+    scores = [mm_nt(w[...].reshape(group * width, dim), k[...]) for k, _, w, _ in halves]
+    probs = [
+        stack(*[both_soft(x[i * width : (i + 1) * width]) for i in range(group)]) for x in scores
+    ]
+    features = [x.astype(BF) for x in probs]
+    for s, (_, v_ref, _, out_ref) in enumerate(halves):
+        kp_ref[0, s] = probs[s]
+        out_ref[...] = mm(features[s], v_ref[...])
+        norm_ref[0, s] = mm_nt(jnp.ones((16, length), BF), features[s])[:1]
 
 
 def query_kernel(
@@ -184,24 +190,31 @@
 
 
 def last_kernel(
-    order, k_ref, v_ref, kp_ref, gk_ref, sn_ref, to_ref, tt_ref, own_ref, other_ref
+    order, ko_ref, vo_ref, kt_ref, vt_ref, kp_ref, gk_ref, sn_ref, to_ref, tt_ref, own_ref, other_ref
 ):
-    half = pl.program_id(1)
     rows, length = kp_ref.shape[2:]
-    feats = k_ref.shape[1]
-    high, low = split(jnp.where(half == 0, to_ref[...], tt_ref[...]))
-    values = v_ref[...]
-    upstream = gk_ref[0, 0] + mm_nt(cat(high, low), cat(values, values))
-    upstream = upstream + jnp.broadcast_to(column(sn_ref[0, 0]), (rows, length))
-    probs = kp_ref[0, 0]
+    feats = ko_ref.shape[1]
+    halves = ((ko_ref, vo_ref, to_ref, own_ref), (kt_ref, vt_ref, tt_ref, other_ref))
+    states = [cat(*split(t[...])) for _, _, t, _ in halves]
+    upstream = [
+        gk_ref[0, s] + mm_nt(states[s], cat(v[...], v[...]))
+        for s, (_, v, _, _) in enumerate(halves)
+    ]
+    upstream = [
+        upstream[s] + jnp.broadcast_to(column(sn_ref[0, s]), (rows, length)) for s in (0, 1)
+    ]
     back = [
-        soft_back(probs[a : a + feats], upstream[a : a + feats]) for a in range(0, rows, feats)
-    ]
-    put_half(own_ref, other_ref, mm(stack(*back), k_ref[...]))
-
-
-def out_kernel(order, x_ref, o_ref):
-    o_ref[...] = x_ref[...]
+        stack(*[soft_back(kp_ref[0, s, a : a + feats], upstream[s][a : a + feats]) for a in range(0, rows, feats)])
+        for s in (0, 1)
+    ]
+    for s, (k_ref, _, _, out_ref) in enumerate(halves):
+        out_ref[...] = mm(back[s], k_ref[...])
+
+
+def out_kernel(order, *refs):
+    out_ref = refs[-1]
+    for i, ref in enumerate(refs[:-1]):
+        out_ref[order[i]] = ref[...]
 
 
 def core_swap(x):
@@ -213,49 +226,83 @@
     return lax.ppermute(x, "ctx", [(2 * a + c, 2 * b + c) for a, b in pairs for c in (0, 1)])
 
 
-def chip_before(x, chip, chips, forward):
-    turn = (lambda a: a) if forward else (lambda a: chips - 1 - a)
-    place = chip if forward else chips - 1 - chip
-
-    def move(y, pairs):
-        return chip_move(y, [(turn(a), turn(b)) for a, b in pairs])
-
-    if chips == 4:
-        rows = x.shape[0] // 2
-        a, b = x[:rows], x[rows:]
-        near = move(jnp.where(place == 1, b, a), [(0, 1), (1, 2), (2, 3)])
-        far = move(b, [(0, 2)])
-        second = jnp.where(place == 1, a + near, jnp.where(place == 2, b + near + far, b))
-        near2 = move(second, [(0, 1), (1, 2), (2, 3)])
-        far2 = move(second, [(1, 3)])
-        first_half = jnp.where(place == 2, near2, near + far2)
-        second_half = jnp.where(place == 2, near + far, near2)
-        return jnp.concatenate([first_half, second_half], axis=0)
-    total = move(x, [(i, i + 1) for i in range(chips - 1)])
-    step = 1
-    while step < chips:
-        total = total + move(total, [(i, i + step) for i in range(chips - step)])
-        step *= 2
-    return total
-
-
-def scan_states(own, other, chip, core, chips, forward):
-    got = core_swap(other)
-    before = chip_before(own + got, chip, chips, forward)
-    second = core == 1 if forward else core == 0
-    mine = before + jnp.where(second, got, 0.0)
-    sent = before + jnp.where(second, 0.0, own)
-    return mine, core_swap(sent)
-
-
-def scan_norms(norm, chip, core, chips, forward):
+def after(values, *earlier):
+    return lax.optimization_barrier((values, earlier))[0]
+
+
+class Scan:
+    def __init__(self, own, other, forward):
+        ctx = lax.axis_index("ctx")
+        self.chips = lax.axis_size("ctx") // 2
+        chip, core = ctx // 2, ctx % 2
+        self.forward = forward
+        self.place = chip if forward else self.chips - 1 - chip
+        self.second = core == 1 if forward else core == 0
+        self.own = own
+        self.got = core_swap(other)
+        rows = own.shape[0] // 2
+        self.a = own[:rows] + self.got[:rows]
+        self.b = own[rows:] + self.got[rows:]
+        if self.chips == 4:
+            self.payload = (jnp.where(self.place == 1, self.b, self.a), self.b)
+        else:
+            self.payload = (jnp.concatenate([self.a, self.b], axis=0),)
+
+    def move(self, x, pairs):
+        last = self.chips - 1
+        turn = (lambda p: p) if self.forward else (lambda p: last - p)
+        return chip_move(x, [(turn(p), turn(q)) for p, q in pairs])
+
+    def first(self):
+        if self.chips == 4:
+            near, far = self.payload
+            self.near = self.move(near, [(0, 1), (1, 2), (2, 3)])
+            self.far = self.move(far, [(0, 2)])
+
+    def turn_around(self, *earlier):
+        if self.chips == 4:
+            a, b = after((self.a, self.b), *earlier) if earlier else (self.a, self.b)
+            self.payload = (
+                jnp.where(
+                    self.place == 1,
+                    a + self.near,
+                    jnp.where(self.place == 2, b + self.near + self.far, b),
+                ),
+            )
+
+    def second_move(self):
+        if self.chips == 4:
+            (second,) = self.payload
+            self.near2 = self.move(second, [(0, 1), (1, 2), (2, 3)])
+            self.far2 = self.move(second, [(1, 3)])
+
+    def finish(self, *earlier):
+        own, got = after((self.own, self.got), *earlier) if earlier else (self.own, self.got)
+        if self.chips == 4:
+            near = after(self.near, *earlier) if earlier else self.near
+            first_half = jnp.where(self.place == 2, self.near2, near + self.far2)
+            second_half = jnp.where(self.place == 2, near + self.far, self.near2)
+            before = jnp.concatenate([first_half, second_half], axis=0)
+        else:
+            (total,) = self.payload
+            before = self.move(total, [(i, i + 1) for i in range(self.chips - 1)])
+            step = 1
+            while step < self.chips:
+                pairs = [(i, i + step) for i in range(self.chips - step)]
+                before = before + self.move(before, pairs)
+                step *= 2
+        mine = before + jnp.where(self.second, got, 0.0)
+        sent = before + jnp.where(self.second, 0.0, own)
+        return mine, core_swap(sent)
+
+
+def scan_norms(norm, chip, core, chips, forward, *earlier):
     got = core_swap(norm)[:, ::-1]
     second = core == 1 if forward else core == 0
     base = jnp.where(second, got, 0.0)
     total = norm + got
-    if chips & (chips - 1):
-        before = chip_before(total.reshape(-1, total.shape[-1]), chip, chips, forward)
-        return base + before.reshape(total.shape)
+    if earlier:
+        total = after(total, *earlier)
     bit = 1
     while bit < chips:
         moved = chip_move(total, [(i, i ^ bit) for i in range(chips)])
@@ -269,11 +316,7 @@
 def sum_all(own, other, chips):
     mine = own + core_swap(other)
     dp = lax.axis_size("dp")
-    parts = mine.shape[0]
-    if dp & (dp - 1) or parts % dp or chips & (chips - 1) or parts & (parts - 1):
-        mine = lax.psum(mine, "dp")
-        total = sum_chips(mine, chips)
-        return jnp.concatenate([total, core_swap(total)], axis=0)
+    parts = own.shape[0]
     share = parts // dp
     got = [
         lax.ppermute(mine[k * share : (k + 1) * share], "dp", [(i, i ^ k) for i in range(dp)])
@@ -282,25 +325,15 @@
     total = mine[:share]
     for piece in got:
         total = total + piece
-    total = sum_chips(total, chips)
-    pieces = [total] + [
-        lax.ppermute(total, "dp", [(i, i ^ k) for i in range(dp)]) for k in range(1, dp)
-    ]
-    full = jnp.concatenate(pieces, axis=0)
-    return jnp.concatenate([full, core_swap(full)], axis=0)
-
-
-def sum_chips(total, chips):
-    if chips & (chips - 1):
-        size = 2 * chips
-        return lax.psum(
-            total, "ctx", axis_index_groups=[list(range(c, size, 2)) for c in (0, 1)]
-        )
     bit = 1
     while bit < chips:
         total = total + chip_move(total, [(i, i ^ bit) for i in range(chips)])
         bit *= 2
-    return total
+    pieces = [total] + [
+        lax.ppermute(total, "dp", [(i, i ^ k) for i in range(dp)]) for k in range(1, dp)
+    ]
+    pieces = pieces + [core_swap(x) for x in pieces]
+    return [x[i] for x in pieces for i in range(share)]
 
 
 def shards(queries, key_tokens, value_tokens, cotangent, query_map, key_map):
@@ -322,12 +355,8 @@
     chips = lax.axis_size("ctx") // 2
     chip, core = ctx // 2, ctx % 2
     dp = lax.axis_size("dp")
-    turn = lax.axis_index("dp") * (n // dp) if n % dp == 0 and n & (n - 1) == 0 else 0
-    part = jnp.arange(n, dtype=jnp.int32) ^ turn
+    part = jnp.arange(n, dtype=jnp.int32) ^ (lax.axis_index("dp") * (n // dp))
     order = jnp.concatenate([part + n * core, part + n * (1 - core)]).astype(jnp.int32)
-    heads = jnp.arange(shared, dtype=jnp.int32)
-    back = jnp.where(heads // n == core, 0, n) + ((heads % n) ^ turn)
-    back = back.astype(jnp.int32)
 
     def head_cols(rows, cols):
         return pl.BlockSpec((rows, cols), lambda i, s, order: (0, order[s * n + i]))
@@ -344,44 +373,65 @@
     def half_spec(rows):
         return pl.BlockSpec((rows, dim), lambda i, s, order: (i, 0))
 
-    def call(name, body, in_specs, out_specs, out_shape):
-        return pl.pallas_call(
+    def side(spec, s):
+        return pl.BlockSpec(spec.block_shape, lambda i, order: spec.index_map(i, s, order))
+
+    def call(name, body, grid, in_specs, out_specs, out_shape):
+        run = pl.pallas_call(
             body,
             name=name,
-            out_shape=out_shape,
+            out_shape=[pltpu.HBM(x.shape, x.dtype) for x in out_shape],
             grid_spec=pltpu.PrefetchScalarGridSpec(
-                num_scalar_prefetch=1, grid=(n, 2), in_specs=in_specs, out_specs=out_specs
+                num_scalar_prefetch=1, grid=grid, in_specs=in_specs, out_specs=out_specs
             ),
             compiler_params=pltpu.CompilerParams(vmem_limit_bytes=VMEM_LIMIT),
+        )
+        return lambda order, *arrays: run(
+            order, *[pltpu.with_memory_space_constraint(x, pltpu.HBM) for x in arrays]
         )
 
     state = jax.ShapeDtypeStruct((n * wide, dim), F32)
     grad = jax.ShapeDtypeStruct((n * group * width, dim), F32)
     token = head_cols(length, dim)
     wide_token = head_cols(length, group * dim)
+    half_state = pl.BlockSpec((wide, dim), lambda i, order: (i, 0))
+    half_grad = pl.BlockSpec((group * width, dim), lambda i, order: (i, 0))
+    both_kept = pl.BlockSpec((1, 2, wide, length), lambda i, order: (i, 0, 0, 0))
+    both_rows = pl.BlockSpec((1, 2, 1, wide), lambda i, order: (i, 0, 0, 0))
+    pair = (n, 2)
 
     key_probs, own, other, norm = call(
         "key_features",
         key_kernel,
-        [token, token, map_spec],
-        [kept_spec, half_spec(wide), half_spec(wide), row_spec],
+        (n,),
+        [side(x, s) for s in (0, 1) for x in (token, token, map_spec)],
+        [both_kept, half_state, half_state, both_rows],
         [kept, state, state, row],
-    )(order, keys, values, key_map)
-    prefix_norm = scan_norms(norm, chip, core, chips, True)
-    prefix_own, prefix_other = scan_states(own, other, chip, core, chips, True)
+    )(order, keys, values, key_map, keys, values, key_map)
+    prefix = Scan(own, other, True)
+    prefix.first()
+    prefix_norm = scan_norms(norm, chip, core, chips, True, *prefix.payload)
 
     query_probs, query_rows, weights, inverse, own, other = call(
         "query_features",
         query_kernel,
+        pair,
         [wide_token, wide_token, map_spec, kept_spec, row_spec],
         [kept_spec, weight_spec, weight_spec, weight_spec, half_spec(wide), half_spec(wide)],
         [kept, weight, weight, inverse, state, state],
     )(order, queries, cotangent, query_map, key_probs, prefix_norm)
-    suffix_own, suffix_other = scan_states(own, other, chip, core, chips, False)
+    suffix = Scan(own, other, False)
+    suffix.first()
+    prefix.turn_around(*suffix.payload)
+    prefix.second_move()
+    suffix.turn_around()
+    suffix.second_move()
+    prefix_own, prefix_other = after(prefix.finish(), *suffix.payload)
 
     attended, query_own, query_other, key_up, norm = call(
         "attend",
         middle_kernel,
+        pair,
         [wide_token, wide_token, token, kept_spec, kept_spec]
         + [weight_spec] * 3
         + [row_spec]
@@ -393,31 +443,29 @@
         prefix_norm, prefix_own, prefix_other,
     )
     suffix_norm = scan_norms(norm, chip, core, chips, False)
+    suffix_own, suffix_other = suffix.finish(suffix_norm)
 
     key_own, key_other = call(
         "key_grads",
         last_kernel,
-        [token, token, kept_spec, kept_spec, row_spec] + [half_spec(wide)] * 2,
-        [half_spec(group * width)] * 2,
+        (n,),
+        [side(token, 0)] * 2 + [side(token, 1)] * 2 + [both_kept] * 2 + [both_rows] + [half_state] * 2,
+        [half_grad] * 2,
         [grad, grad],
-    )(order, keys, values, key_probs, key_up, suffix_norm, suffix_own, suffix_other)
+    )(order, keys, values, keys, values, key_probs, key_up, suffix_norm, suffix_own, suffix_other)
 
     def finish(name, own, other):
         shape = (n, group * width, dim)
-        total = sum_all(own.reshape(shape), other.reshape(shape), chips)
-        rows = pl.BlockSpec((1, group * width, dim), lambda i, back: (back[i], 0, 0))
+        pieces = sum_all(own.reshape(shape), other.reshape(shape), chips)
+        whole = pl.BlockSpec(memory_space=pltpu.VMEM)
         natural = pl.pallas_call(
             out_kernel,
             name=name,
             out_shape=jax.ShapeDtypeStruct((shared, group * width, dim), F32),
-            grid_spec=pltpu.PrefetchScalarGridSpec(
-                num_scalar_prefetch=1,
-                grid=(shared,),
-                in_specs=[rows],
-                out_specs=pl.BlockSpec((1, group * width, dim), lambda i, back: (i, 0, 0)),
-            ),
+            in_specs=[pl.BlockSpec(memory_space=pltpu.SMEM)] + [whole] * shared,
+            out_specs=whole,
             compiler_params=pltpu.CompilerParams(vmem_limit_bytes=VMEM_LIMIT),
-        )(back, total)
+        )(order, *pieces)
         return jnp.swapaxes(natural.reshape(head_count, width, dim), 1, 2)
 
     query_grad = finish("query_out", query_own, query_other)

time: 193 us -> 214 us (1.11)
  waiting for transfers between devices: 61.8 us -> 85.8 us
  local copies, waits for them, and re-layouts: 17.9 us -> 1.04 us
  starting transfers between devices: 58.1 us -> 68.5 us
    ppermute x16, waiting for transfers between devices: 51.8 us -> 68.6 us  [chip_move(): lax.ppermute(x, 'ctx', [(2 * a + c, 2 * b + c) for a, b in pairs for c in...]
    unnamed x60 -> x10, local copies, waits for them, and re-layouts: 17.8 us -> 0.99 us
    ppermute x16, starting transfers between devices: 23.1 us -> 36.7 us  [chip_move(): lax.ppermute(x, 'ctx', [(2 * a + c, 2 * b + c) for a, b in pairs for c in...]
    pallas_call x4, Pallas kernels: 30.5 us -> 35.5 us  [call(): run(order, *[pltpu.with_memory_space_constraint(x, pltpu.HBM) for x in ar...]
    ppermute x6, waiting for transfers between devices: 6.98 us -> 10.7 us  [sum_all(): lax.ppermute(mine[k * share:(k + 1) * share], 'dp', [(i, i ^ k) for i in...]
    ppermute x10 -> x16, waiting for transfers between devices: 3.04 us -> 6.5 us  [core_swap(): return lax.ppermute(x, 'ctx', [(i, i ^ 1) for i in range(size)])]
    pallas_call x2, Pallas kernels: 6.53 us -> 3.17 us  [finish(): pl.pallas_call(out_kernel, name=name, out_shape=jax.ShapeDtypeStruct((sha...]
    add x7 -> x6, other arithmetic: 5.88 us -> 2.7 us  [the longest x2 2.64 us: finish(): sent = before + jnp.where(self.second, 0.0, own)]
  transfers between devices with their start and end apart: 38 -> 44, of which waited for: 17 -> 19; matrix products, arithmetic and copies ran while one was open for 9% -> 4% of each run, Pallas kernels for 14% -> 7%
where the time goes in v2:
time: 214 us; the launch traced here: 212 us
  waiting for transfers between devices  85.8 us (40%)
  starting transfers between devices  68.5 us (32%)
  Pallas kernels  38.7 us (18%)
  other arithmetic  17.5 us (8%)
    ppermute x16, waiting for transfers between devices, chip_move(): lax.ppermute(x, 'ctx', [(2 * a + c, 2 * b + c) for a, b in pairs for c in...  68.6 us
    ppermute x16, starting transfers between devices, chip_move(): lax.ppermute(x, 'ctx', [(2 * a + c, 2 * b + c) for a, b in pairs for c in...  36.7 us
    pallas_call x4, Pallas kernels, call(): run(order, *[pltpu.with_memory_space_constraint(x, pltpu.HBM) for x in ar...  35.5 us
    ppermute x16, starting transfers between devices, core_swap(): return lax.ppermute(x, 'ctx', [(i, i ^ 1) for i in range(size)])  20.5 us
    ppermute x6, waiting for transfers between devices, sum_all(): lax.ppermute(mine[k * share:(k + 1) * share], 'dp', [(i, i ^ k) for i in...  10.7 us
    ppermute x16, waiting for transfers between devices, core_swap(): return lax.ppermute(x, 'ctx', [(i, i ^ 1) for i in range(size)])  6.5 us
    ppermute x6, starting transfers between devices, sum_all(): lax.ppermute(total, 'dp', [(i, i ^ k) for i in range(dp)])  5.85 us
    ppermute x6, starting transfers between devices, sum_all(): lax.ppermute(mine[k * share:(k + 1) * share], 'dp', [(i, i ^ k) for i in...  5.43 us
  transfers between devices with their start and end apart: 44, of which 19 were waited for; matrix products, arithmetic and copies ran while one was open for 4% of the time, Pallas kernels for 7%

profile of v2, /device:TPU:1, one launch (start us, length us, event | category | flops | bytes accessed | tf_op | source)
XLA Modules:
  0.0 212.4 jit_solution(357275058405711011)
XLA Ops:
  0.7 5.2 %key_features.1 = (f32[4,2,512,128]{3,2,1,0:T(8,128)}, f32[2048,128]{1,0:T(8,128)}, f32[2048,128]{1,0:T(8,128)}, f32[4,2,1,512]{3,2,1,0:T(1,128)}) custom-call(s32[8]{0:T(128)S(1)} %pad_add_fusion.order, bf16[128,1024]{1,0:T(8,128)(2,1)} %bitcast.58, bf16[128,1024]{1,0:T(8,128)(2,1)} %bitcast.49, bf16[32,64,128]{2,1,0:T(8,128)(2,1)} %bitcast.62, ...), custom_call_target="tpu_custom_call" | custom-call | tf_op jit(solution)/shard_map/key_features/pallas_call | solution.py:389
  6.5 2.4 %collective-permute-done = f32[4,2,1,512]{3,2,1,0:T(1,128)S(1)} collective-permute-done((f32[4,2,1,512]{3,2,1,0:T(1,128)}, f32[4,2,1,512]{3,2,1,0:T(1,128)S(1)}, u32[]{:S(2)}, u32[]{:S(2)}) %collective-permute-start) | collective-permute-done | bytes 16416 | tf_op jit(solution)/shard_map/ppermute | solution.py:222
  9.6 2.2 %broadcast_select_fusion.1 = (f32[1024,128]{1,0:T(8,128)}, f32[1024,128]{1,0:T(8,128)S(1)}, f32[1024,128]{1,0:T(8,128)S(1)}) fusion(pred[]{:T(512)S(6)} %eq.37, f32[2048,128]{1,0:T(8,128)S(1)} %collective-permute-done.1, f32[2048,128]{1,0:T(8,128)} %get-tuple-element.30), kind=kLoop, calls=%fused_computation.17 | loop fusion | flops 393216 | bytes 3670017 | tf_op jit(solution)/shard_map/jit(_where)/select_n | solution.py:247
  11.8 2.4 %collective-permute-start.2 = (f32[4,2,1,512]{3,2,1,0:T(1,128)S(1)}, f32[4,2,1,512]{3,2,1,0:T(1,128)S(1)}, u32[]{:S(2)}, u32[]{:S(2)}) collective-permute-start(f32[4,2,1,512]{3,2,1,0:T(1,128)S(1)} %reverse_add_fusion.1), channel_id=1, source_target_pairs={{0,2},{1,3},{2,0},{3,1},{4,6},{5,7},{6,4},{7,5},{8,10},{9,11},{10,... | collective-permute-start | bytes 49160 | tf_op jit(solution)/shard_map/ppermute | solution.py:226
  15.4 2.5 %collective-permute-start.3 = (f32[4,2,1,512]{3,2,1,0:T(1,128)S(1)}, f32[4,2,1,512]{3,2,1,0:T(1,128)S(1)}, u32[]{:S(2)}, u32[]{:S(2)}) collective-permute-start(f32[4,2,1,512]{3,2,1,0:T(1,128)S(1)} %add.142), channel_id=1, source_target_pairs={{0,4},{1,5},{2,6},{3,7},{4,0},{5,1},{6,2},{7,3},{8,12},{9,13},{10,... | collective-permute-start | bytes 49160 | tf_op jit(solution)/shard_map/ppermute | solution.py:226
  19.7 11.5 %query_features.1 = (f32[4,2,512,128]{3,2,1,0:T(8,128)}, bf16[4,2,4,128,128]{4,3,2,1,0:T(8,128)(2,1)}, bf16[4,2,4,128,128]{4,3,2,1,0:T(8,128)(2,1)}, f32[4,2,4,1...) custom-call(s32[8]{0:T(128)S(1)} %pad_add_fusion.order, bf16[128,4096]{1,0:T(8,128)(2,1)} %bitcast.54, ...), custom_call_target="tpu_custom_call" | custom-call | tf_op jit(solution)/shard_map/query_features/pallas_call | solution.py:389
  31.2 2.4 %collective-permute-start.4 = (f32[2048,128]{1,0:T(8,128)}, f32[2048,128]{1,0:T(8,128)S(1)}, u32[]{:S(2)}, u32[]{:S(2)}) collective-permute-start(f32[2048,128]{1,0:T(8,128)} %get-tuple-element.38), channel_id=1, source_target_pairs={{0,1},{1,0},{2,3},{3,2},{4,5},{5,4},{6,7},{7,6},{8,9},{9,8},{10,11... | collective-permute-start | bytes 3145736 | tf_op jit(solution)/shard_map/ppermute | solution.py:222
  33.6 4.3 %collective-permute-start.5 = (f32[1024,128]{1,0:T(8,128)}, f32[1024,128]{1,0:T(8,128)}, u32[]{:S(2)}, u32[]{:S(2)}) collective-permute-start(f32[1024,128]{1,0:T(8,128)} %get-tuple-element.55), channel_id=1, source_target_pairs={{0,2},{1,3},{2,4},{3,5},{4,6},{5,7},{8,10},{9,11},{10,12},{11,13},... | collective-permute-start | bytes 1572872 | tf_op jit(solution)/shard_map/ppermute | solution.py:226
  38.0 4.3 %collective-permute-start.6 = (f32[1024,128]{1,0:T(8,128)S(1)}, f32[1024,128]{1,0:T(8,128)}, u32[]{:S(2)}, u32[]{:S(2)}) collective-permute-start(f32[1024,128]{1,0:T(8,128)S(1)} %get-tuple-element.40), channel_id=1, source_target_pairs={{0,4},{1,5},{8,12},{9,13},{16,20},{17,21},{24,28},{25,29}} | collective-permute-start | bytes 1572872 | tf_op jit(solution)/shard_map/ppermute | solution.py:226
  42.3 2.4 %broadcast_select_fusion = (f32[1024,128]{1,0:T(8,128)}, f32[1024,128]{1,0:T(8,128)}) fusion(pred[]{:T(512)S(6)} %eq.39, f32[2048,128]{1,0:T(8,128)S(1)} %collective-permute-done.4, f32[2048,128]{1,0:T(8,128)} %get-tuple-element.50), kind=kLoop, calls=%fused_computation.16 | loop fusion | flops 393216 | bytes 3145729 | tf_op jit(solution)/shard_map/jit(_where)/select_n | solution.py:247
  44.7 4.2 %collective-permute-done.5 = f32[1024,128]{1,0:T(8,128)} collective-permute-done((f32[1024,128]{1,0:T(8,128)}, f32[1024,128]{1,0:T(8,128)}, u32[]{:S(2)}, u32[]{:S(2)}) %collective-permute-start.5) | collective-permute-done | bytes 524320 | tf_op jit(solution)/shard_map/ppermute | solution.py:226
  48.8 11.2 %collective-permute-done.6 = f32[1024,128]{1,0:T(8,128)} collective-permute-done((f32[1024,128]{1,0:T(8,128)S(1)}, f32[1024,128]{1,0:T(8,128)}, u32[]{:S(2)}, u32[]{:S(2)}) %collective-permute-start.6) | collective-permute-done | bytes 524320 | tf_op jit(solution)/shard_map/ppermute | solution.py:226
  63.5 10.0 %collective-permute-done.7 = f32[1024,128]{1,0:T(8,128)S(1)} collective-permute-done((f32[1024,128]{1,0:T(8,128)S(1)}, f32[1024,128]{1,0:T(8,128)S(1)}, u32[]{:S(2)}, u32[]{:S(2)}) %collective-permute-start.7) | collective-permute-done | bytes 524320 | tf_op jit(solution)/shard_map/ppermute | solution.py:226
  79.8 27.7 %collective-permute-done.10 = f32[1024,128]{1,0:T(8,128)S(1)} collective-permute-done((f32[1024,128]{1,0:T(8,128)}, f32[1024,128]{1,0:T(8,128)S(1)}, u32[]{:S(2)}, u32[]{:S(2)}) %collective-permute-start.10) | collective-permute-done | bytes 524320 | tf_op jit(solution)/shard_map/ppermute | solution.py:226
  112.1 12.7 %attend.1 = (bf16[128,4096]{1,0:T(8,128)(2,1)}, f32[1024,128]{1,0:T(8,128)}, f32[1024,128]{1,0:T(8,128)}, f32[4,2,512,128]{3,2,1,0:T(8,128)}, f32[4,2,1,512]{3,2,1,0:T(1,128)}) custom-call(s32[8]{0:T(128)S(1)} %pad_add_fusion.order, bf16[128,4096]{1,0:T(8,128)(2,1)} %bitcast.55, bf16[128,4096]{1,0:T(8,128)(2,1)} %bitcast.57, bf16[128,1024]{1,0:T(8,128)(2,1)} %bitcast.51, ...), custom_call_target="tpu_custom_call" | custom-call | tf_op jit(solution)/shard_map/attend/pallas_call | solution.py:389
  127.3 14.6 %collective-permute-start.26 = (f32[4,2,1,512]{3,2,1,0:T(1,128)S(1)}, f32[4,2,1,512]{3,2,1,0:T(1,128)S(1)}, u32[]{:S(2)}, u32[]{:S(2)}) collective-permute-start(f32[4,2,1,512]{3,2,1,0:T(1,128)S(1)} %reverse_add_fusion), channel_id=1, source_target_pairs={{0,2},{1,3},{2,0},{3,1},{4,6},{5,7},{6,4},{7,5},{8,10},{9,11},{10,... | collective-permute-start | bytes 49160 | tf_op jit(solution)/shard_map/ppermute | solution.py:226
  141.8 8.7 %collective-permute-done.26 = f32[4,2,1,512]{3,2,1,0:T(1,128)S(1)} collective-permute-done((f32[4,2,1,512]{3,2,1,0:T(1,128)S(1)}, f32[4,2,1,512]{3,2,1,0:T(1,128)S(1)}, u32[]{:S(2)}, u32[]{:S(2)}) %collective-permute-start.26) | collective-permute-done | bytes 16416 | tf_op jit(solution)/shard_map/ppermute | solution.py:226
  150.6 3.5 %collective-permute-done.27 = f32[4,2,1,512]{3,2,1,0:T(1,128)S(1)} collective-permute-done((f32[4,2,1,512]{3,2,1,0:T(1,128)S(1)}, f32[4,2,1,512]{3,2,1,0:T(1,128)S(1)}, u32[]{:S(2)}, u32[]{:S(2)}) %collective-permute-start.27) | collective-permute-done | bytes 16416 | tf_op jit(solution)/shard_map/ppermute | solution.py:226
  158.9 3.0 %collective-permute-done.12 = f32[4,256,128]{2,1,0:T(8,128)S(1)} collective-permute-done((f32[4,256,128]{2,1,0:T(8,128)S(1)}, f32[4,256,128]{2,1,0:T(8,128)S(1)}, u32[]{:S(2)}, u32[]{:S(2)}) %collective-permute-start.12) | collective-permute-done | bytes 524320 | tf_op jit(solution)/shard_map/ppermute | solution.py:222
  163.0 6.1 %key_grads.1 = (f32[1024,128]{1,0:T(8,128)}, f32[1024,128]{1,0:T(8,128)}) custom-call(s32[8]{0:T(128)S(1)} %pad_add_fusion.order, bf16[128,1024]{1,0:T(8,128)(2,1)} %bitcast.60, bf16[128,1024]{1,0:T(8,128)(2,1)} %bitcast.52, bf16[128,1024]{1,0:T(8,128)(2,1)} %bitcast.61, bf16[128,1024]{1,0:T(8,128)(2,1)} %bitcast.53, ...), custom_call_target="tpu_custom_call" | custom-call | tf_op jit(solution)/shard_map/key_grads/pallas_call | solution.py:389
  172.2 2.3 %collective-permute-done.13 = f32[1,256,128]{2,1,0:T(8,128)S(1)} collective-permute-done((f32[1,256,128]{2,1,0:T(8,128)S(1)}, f32[1,256,128]{2,1,0:T(8,128)S(1)}, u32[]{:S(2)}, u32[]{:S(2)}) %collective-permute-start.13) | collective-permute-done | bytes 131104 | tf_op jit(solution)/shard_map/ppermute | solution.py:322
  175.4 2.7 %collective-permute-done.15 = f32[1,256,128]{2,1,0:T(8,128)S(1)} collective-permute-done((f32[1,256,128]{2,1,0:T(8,128)S(1)}, f32[1,256,128]{2,1,0:T(8,128)S(1)}, u32[]{:S(2)}, u32[]{:S(2)}) %collective-permute-start.15) | collective-permute-done | bytes 131104 | tf_op jit(solution)/shard_map/ppermute | solution.py:322
  192.9 4.0 %collective-permute-start.21 = (f32[1,256,128]{2,1,0:T(8,128)S(1)}, f32[1,256,128]{2,1,0:T(8,128)S(1)}, u32[]{:S(2)}, u32[]{:S(2)}) collective-permute-start(f32[1,256,128]{2,1,0:T(8,128)S(1)} %add.161), channel_id=1, source_target_pairs={{0,1},{1,0},{2,3},{3,2},{4,5},{5,4},{6,7},{7,6},{8,9},{9,8},{10,11... | collective-permute-start | bytes 393224 | tf_op jit(solution)/shard_map/ppermute | solution.py:222
  201.4 3.4 %collective-permute-start.24 = (f32[1,256,128]{2,1,0:T(8,128)S(1)}, f32[1,256,128]{2,1,0:T(8,128)S(1)}, u32[]{:S(2)}, u32[]{:S(2)}) collective-permute-start(f32[1,256,128]{2,1,0:T(8,128)S(1)} %collective-permute-done.20), channel_id=1, source_target_pairs={{0,1},{1,0},{2,3},{3,2},{4,5},{5,4},{6,7},{7,6},{8,9},{9,8},{10,11... | collective-permute-start | bytes 393224 | tf_op jit(solution)/shard_map/ppermute | solution.py:222
  (106 shorter events, 57.8 us)
Async XLA Ops:
  31.2 11.1 %collective-permute-start.4 = (f32[2048,128]{1,0:T(8,128)}, f32[2048,128]{1,0:T(8,128)S(1)}, u32[]{:S(2)}, u32[]{:S(2)}) collective-permute-start(f32[2048,128]{1,0:T(8,128)} %get-tuple-element.38), channel_id=1, source_target_pairs={{0,1},{1,0},{2,3},{3,2},{4,5},{5,4},{6,7},{7,6},{8,9},{9,8},{10,11... | collective-permute-start | bytes 3145736 | tf_op jit(solution)/shard_map/ppermute | solution.py:222
  33.6 15.2 %collective-permute-start.5 = (f32[1024,128]{1,0:T(8,128)}, f32[1024,128]{1,0:T(8,128)}, u32[]{:S(2)}, u32[]{:S(2)}) collective-permute-start(f32[1024,128]{1,0:T(8,128)} %get-tuple-element.55), channel_id=1, source_target_pairs={{0,2},{1,3},{2,4},{3,5},{4,6},{5,7},{8,10},{9,11},{10,12},{11,13},... | collective-permute-start | bytes 1572872 | tf_op jit(solution)/shard_map/ppermute | solution.py:226
  38.0 22.0 %collective-permute-start.6 = (f32[1024,128]{1,0:T(8,128)S(1)}, f32[1024,128]{1,0:T(8,128)}, u32[]{:S(2)}, u32[]{:S(2)}) collective-permute-start(f32[1024,128]{1,0:T(8,128)S(1)} %get-tuple-element.40), channel_id=1, source_target_pairs={{0,4},{1,5},{8,12},{9,13},{16,20},{17,21},{24,28},{25,29}} | collective-permute-start | bytes 1572872 | tf_op jit(solution)/shard_map/ppermute | solution.py:226
  61.3 12.2 %collective-permute-start.7 = (f32[1024,128]{1,0:T(8,128)S(1)}, f32[1024,128]{1,0:T(8,128)S(1)}, u32[]{:S(2)}, u32[]{:S(2)}) collective-permute-start(f32[1024,128]{1,0:T(8,128)S(1)} %select_select_fusion.1), channel_id=1, source_target_pairs={{0,2},{1,3},{2,4},{3,5},{4,6},{5,7},{8,10},{9,11},{10,12},{11,13},... | collective-permute-start | bytes 1572872 | tf_op jit(solution)/shard_map/ppermute | solution.py:226
  62.8 10.7 %collective-permute-start.8 = (f32[1024,128]{1,0:T(8,128)S(1)}, f32[1024,128]{1,0:T(8,128)S(1)}, u32[]{:S(2)}, u32[]{:S(2)}) collective-permute-start(f32[1024,128]{1,0:T(8,128)S(1)} %select_select_fusion.1), channel_id=1, source_target_pairs={{2,6},{3,7},{10,14},{11,15},{18,22},{19,23},{26,30},{27,31}} | collective-permute-start | bytes 1572872 | tf_op jit(solution)/shard_map/ppermute | solution.py:226
  76.4 35.7 %collective-permute-start.9 = (f32[2048,128]{1,0:T(8,128)}, f32[2048,128]{1,0:T(8,128)}, u32[]{:S(2)}, u32[]{:S(2)}) collective-permute-start(f32[2048,128]{1,0:T(8,128)} %get-tuple-element.62), channel_id=1, source_target_pairs={{0,1},{1,0},{2,3},{3,2},{4,5},{5,4},{6,7},{7,6},{8,9},{9,8},{10,11... | collective-permute-start | bytes 3145736 | tf_op jit(solution)/shard_map/ppermute | solution.py:222
  77.8 29.7 %collective-permute-start.10 = (f32[1024,128]{1,0:T(8,128)}, f32[1024,128]{1,0:T(8,128)S(1)}, u32[]{:S(2)}, u32[]{:S(2)}) collective-permute-start(f32[1024,128]{1,0:T(8,128)} %get-tuple-element.53), channel_id=1, source_target_pairs={{6,4},{7,5},{4,2},{5,3},{2,0},{3,1},{14,12},{15,13},{12,10},{13,11... | collective-permute-start | bytes 1572872 | tf_op jit(solution)/shard_map/ppermute | solution.py:226
  79.1 28.4 %collective-permute-start.11 = (f32[1024,128]{1,0:T(8,128)}, f32[1024,128]{1,0:T(8,128)S(1)}, u32[]{:S(2)}, u32[]{:S(2)}) collective-permute-start(f32[1024,128]{1,0:T(8,128)} %get-tuple-element.54), channel_id=1, source_target_pairs={{6,2},{7,3},{14,10},{15,11},{22,18},{23,19},{30,26},{31,27}} | collective-permute-start | bytes 1572872 | tf_op jit(solution)/shard_map/ppermute | solution.py:226
  109.5 45.2 %collective-permute-start.28 = (f32[1024,128]{1,0:T(8,128)}, f32[1024,128]{1,0:T(8,128)}, u32[]{:S(2)}, u32[]{:S(2)}) collective-permute-start(f32[1024,128]{1,0:T(8,128)} %select_select_fusion), channel_id=1, source_target_pairs={{6,4},{7,5},{4,2},{5,3},{2,0},{3,1},{14,12},{15,13},{12,10},{13,11... | collective-permute-start | bytes 1572872 | tf_op jit(solution)/shard_map/ppermute | solution.py:226
  110.8 43.9 %collective-permute-start.29 = (f32[1024,128]{1,0:T(8,128)}, f32[1024,128]{1,0:T(8,128)}, u32[]{:S(2)}, u32[]{:S(2)}) collective-permute-start(f32[1024,128]{1,0:T(8,128)} %select_select_fusion), channel_id=1, source_target_pairs={{4,0},{5,1},{12,8},{13,9},{20,16},{21,17},{28,24},{29,25}} | collective-permute-start | bytes 1572872 | tf_op jit(solution)/shard_map/ppermute | solution.py:226
  127.3 23.3 %collective-permute-start.26 = (f32[4,2,1,512]{3,2,1,0:T(1,128)S(1)}, f32[4,2,1,512]{3,2,1,0:T(1,128)S(1)}, u32[]{:S(2)}, u32[]{:S(2)}) collective-permute-start(f32[4,2,1,512]{3,2,1,0:T(1,128)S(1)} %reverse_add_fusion), channel_id=1, source_target_pairs={{0,2},{1,3},{2,0},{3,1},{4,6},{5,7},{6,4},{7,5},{8,10},{9,11},{10,... | collective-permute-start | bytes 49160 | tf_op jit(solution)/shard_map/ppermute | solution.py:226
  169.1 9.2 %collective-permute-start.31 = (f32[4,256,128]{2,1,0:T(8,128)}, f32[4,256,128]{2,1,0:T(8,128)S(1)}, u32[]{:S(2)}, u32[]{:S(2)}) collective-permute-start(f32[4,256,128]{2,1,0:T(8,128)} %bitcast.71), channel_id=1, source_target_pairs={{0,1},{1,0},{2,3},{3,2},{4,5},{5,4},{6,7},{7,6},{8,9},{9,8},{10,11... | collective-permute-start | bytes 1572872 | tf_op jit(solution)/shard_map/ppermute | solution.py:222
  172.0 6.1 %collective-permute-start.15 = (f32[1,256,128]{2,1,0:T(8,128)S(1)}, f32[1,256,128]{2,1,0:T(8,128)S(1)}, u32[]{:S(2)}, u32[]{:S(2)}) collective-permute-start(f32[1,256,128]{2,1,0:T(8,128)S(1)} %get-tuple-element.70), channel_id=1, source_target_pairs={{0,24},{8,16},{16,8},{24,0},{1,25},{9,17},{17,9},{25,1},{2,26},{10... | collective-permute-start | bytes 393224 | tf_op jit(solution)/shard_map/ppermute | solution.py:322
  182.1 6.5 %collective-permute-start.17 = (f32[1,256,128]{2,1,0:T(8,128)S(1)}, f32[1,256,128]{2,1,0:T(8,128)S(1)}, u32[]{:S(2)}, u32[]{:S(2)}) collective-permute-start(f32[1,256,128]{2,1,0:T(8,128)S(1)} %add.160), channel_id=1, source_target_pairs={{0,4},{1,5},{2,6},{3,7},{4,0},{5,1},{6,2},{7,3},{8,12},{9,13},{10,... | collective-permute-start | bytes 393224 | tf_op jit(solution)/shard_map/ppermute | solution.py:226
  188.6 8.3 %collective-permute-start.18 = (f32[1,256,128]{2,1,0:T(8,128)S(1)}, f32[1,256,128]{2,1,0:T(8,128)S(1)}, u32[]{:S(2)}, u32[]{:S(2)}) collective-permute-start(f32[1,256,128]{2,1,0:T(8,128)S(1)} %add.161), channel_id=1, source_target_pairs={{0,8},{8,0},{16,24},{24,16},{1,9},{9,1},{17,25},{25,17},{2,10},{10... | collective-permute-start | bytes 393224 | tf_op jit(solution)/shard_map/ppermute | solution.py:333
  190.2 6.8 %collective-permute-start.19 = (f32[1,256,128]{2,1,0:T(8,128)S(1)}, f32[1,256,128]{2,1,0:T(8,128)S(1)}, u32[]{:S(2)}, u32[]{:S(2)}) collective-permute-start(f32[1,256,128]{2,1,0:T(8,128)S(1)} %add.161), channel_id=1, source_target_pairs={{0,16},{8,24},{16,0},{24,8},{1,17},{9,25},{17,1},{25,9},{2,18},{10... | collective-permute-start | bytes 393224 | tf_op jit(solution)/shard_map/ppermute | solution.py:333
  191.3 7.4 %collective-permute-start.36 = (f32[1,256,128]{2,1,0:T(8,128)S(1)}, f32[1,256,128]{2,1,0:T(8,128)S(1)}, u32[]{:S(2)}, u32[]{:S(2)}) collective-permute-start(f32[1,256,128]{2,1,0:T(8,128)S(1)} %add.174), channel_id=1, source_target_pairs={{0,4},{1,5},{2,6},{3,7},{4,0},{5,1},{6,2},{7,3},{8,12},{9,13},{10,... | collective-permute-start | bytes 393224 | tf_op jit(solution)/shard_map/ppermute | solution.py:226
  191.5 8.2 %collective-permute-start.20 = (f32[1,256,128]{2,1,0:T(8,128)S(1)}, f32[1,256,128]{2,1,0:T(8,128)S(1)}, u32[]{:S(2)}, u32[]{:S(2)}) collective-permute-start(f32[1,256,128]{2,1,0:T(8,128)S(1)} %add.161), channel_id=1, source_target_pairs={{0,24},{8,16},{16,8},{24,0},{1,25},{9,17},{17,9},{25,1},{2,26},{10... | collective-permute-start | bytes 393224 | tf_op jit(solution)/shard_map/ppermute | solution.py:333
  192.9 7.5 %collective-permute-start.21 = (f32[1,256,128]{2,1,0:T(8,128)S(1)}, f32[1,256,128]{2,1,0:T(8,128)S(1)}, u32[]{:S(2)}, u32[]{:S(2)}) collective-permute-start(f32[1,256,128]{2,1,0:T(8,128)S(1)} %add.161), channel_id=1, source_target_pairs={{0,1},{1,0},{2,3},{3,2},{4,5},{5,4},{6,7},{7,6},{8,9},{9,8},{10,11... | collective-permute-start | bytes 393224 | tf_op jit(solution)/shard_map/ppermute | solution.py:222
  197.0 7.9 %collective-permute-start.23 = (f32[1,256,128]{2,1,0:T(8,128)S(1)}, f32[1,256,128]{2,1,0:T(8,128)S(1)}, u32[]{:S(2)}, u32[]{:S(2)}) collective-permute-start(f32[1,256,128]{2,1,0:T(8,128)S(1)} %collective-permute-done.19), channel_id=1, source_target_pairs={{0,1},{1,0},{2,3},{3,2},{4,5},{5,4},{6,7},{7,6},{8,9},{9,8},{10,11... | collective-permute-start | bytes 393224 | tf_op jit(solution)/shard_map/ppermute | solution.py:222
  198.7 6.2 %collective-permute-start.37 = (f32[1,256,128]{2,1,0:T(8,128)S(1)}, f32[1,256,128]{2,1,0:T(8,128)S(1)}, u32[]{:S(2)}, u32[]{:S(2)}) collective-permute-start(f32[1,256,128]{2,1,0:T(8,128)S(1)} %add.175), channel_id=1, source_target_pairs={{0,8},{8,0},{16,24},{24,16},{1,9},{9,1},{17,25},{25,17},{2,10},{10... | collective-permute-start | bytes 393224 | tf_op jit(solution)/shard_map/ppermute | solution.py:333
  199.7 7.1 %collective-permute-start.38 = (f32[1,256,128]{2,1,0:T(8,128)S(1)}, f32[1,256,128]{2,1,0:T(8,128)S(1)}, u32[]{:S(2)}, u32[]{:S(2)}) collective-permute-start(f32[1,256,128]{2,1,0:T(8,128)S(1)} %add.175), channel_id=1, source_target_pairs={{0,16},{8,24},{16,0},{24,8},{1,17},{9,25},{17,1},{25,9},{2,18},{10... | collective-permute-start | bytes 393224 | tf_op jit(solution)/shard_map/ppermute | solution.py:333
  200.4 7.1 %collective-permute-start.39 = (f32[1,256,128]{2,1,0:T(8,128)S(1)}, f32[1,256,128]{2,1,0:T(8,128)S(1)}, u32[]{:S(2)}, u32[]{:S(2)}) collective-permute-start(f32[1,256,128]{2,1,0:T(8,128)S(1)} %add.175), channel_id=1, source_target_pairs={{0,24},{8,16},{16,8},{24,0},{1,25},{9,17},{17,9},{25,1},{2,26},{10... | collective-permute-start | bytes 393224 | tf_op jit(solution)/shard_map/ppermute | solution.py:333
  201.4 7.9 %collective-permute-start.24 = (f32[1,256,128]{2,1,0:T(8,128)S(1)}, f32[1,256,128]{2,1,0:T(8,128)S(1)}, u32[]{:S(2)}, u32[]{:S(2)}) collective-permute-start(f32[1,256,128]{2,1,0:T(8,128)S(1)} %collective-permute-done.20), channel_id=1, source_target_pairs={{0,1},{1,0},{2,3},{3,2},{4,5},{5,4},{6,7},{7,6},{8,9},{9,8},{10,11... | collective-permute-start | bytes 393224 | tf_op jit(solution)/shard_map/ppermute | solution.py:222
  (25 other events, 138.7 us)

commit v3 on v2

--- a/solution.py
+++ b/solution.py
@@ -313,10 +313,9 @@
     return base
 
 
-def sum_all(own, other, chips):
-    mine = own + core_swap(other)
+def sum_all(mine, chips):
     dp = lax.axis_size("dp")
-    parts = own.shape[0]
+    parts = mine.shape[0]
     share = parts // dp
     got = [
         lax.ppermute(mine[k * share : (k + 1) * share], "dp", [(i, i ^ k) for i in range(dp)])
@@ -411,7 +410,6 @@
     prefix = Scan(own, other, True)
     prefix.first()
     prefix_norm = scan_norms(norm, chip, core, chips, True, *prefix.payload)
-
     query_probs, query_rows, weights, inverse, own, other = call(
         "query_features",
         query_kernel,
@@ -420,13 +418,13 @@
         [kept_spec, weight_spec, weight_spec, weight_spec, half_spec(wide), half_spec(wide)],
         [kept, weight, weight, inverse, state, state],
     )(order, queries, cotangent, query_map, key_probs, prefix_norm)
-    suffix = Scan(own, other, False)
+    prefix.turn_around(own)
+    prefix.second_move()
+    suffix = Scan(*after((own, other), prefix.payload), False)
     suffix.first()
-    prefix.turn_around(*suffix.payload)
-    prefix.second_move()
     suffix.turn_around()
     suffix.second_move()
-    prefix_own, prefix_other = after(prefix.finish(), *suffix.payload)
+    prefix_own, prefix_other = prefix.finish(*suffix.payload)
 
     attended, query_own, query_other, key_up, norm = call(
         "attend",
@@ -443,6 +441,7 @@
         prefix_norm, prefix_own, prefix_other,
     )
     suffix_norm = scan_norms(norm, chip, core, chips, False)
+    query_mine = query_own + core_swap(query_other)
     suffix_own, suffix_other = suffix.finish(suffix_norm)
 
     key_own, key_other = call(
@@ -454,9 +453,8 @@
         [grad, grad],
     )(order, keys, values, keys, values, key_probs, key_up, suffix_norm, suffix_own, suffix_other)
 
-    def finish(name, own, other):
-        shape = (n, group * width, dim)
-        pieces = sum_all(own.reshape(shape), other.reshape(shape), chips)
+    def finish(name, mine):
+        pieces = sum_all(mine.reshape(n, group * width, dim), chips)
         whole = pl.BlockSpec(memory_space=pltpu.VMEM)
         natural = pl.pallas_call(
             out_kernel,
@@ -468,8 +466,8 @@
         )(order, *pieces)
         return jnp.swapaxes(natural.reshape(head_count, width, dim), 1, 2)
 
-    query_grad = finish("query_out", query_own, query_other)
-    key_grad = finish("key_out", key_own, key_other)
+    query_grad = finish("query_out", query_mine)
+    key_grad = finish("key_out", key_own + core_swap(key_other))
     return attended.reshape(1, length, head_count * dim), query_grad, key_grad
 
 

time: 214 us -> 191 us (0.89)
  waiting for transfers between devices: 85.8 us -> 62.8 us
    ppermute x16, waiting for transfers between devices: 68.6 us -> 41.6 us  [chip_move(): lax.ppermute(x, 'ctx', [(2 * a + c, 2 * b + c) for a, b in pairs for c in...]
    ppermute x16, waiting for transfers between devices: 6.5 us -> 10.5 us  [core_swap(): return lax.ppermute(x, 'ctx', [(i, i ^ 1) for i in range(size)])]
  transfers between devices with their start and end apart: 44 -> 44, of which waited for: 19 -> 19; matrix products, arithmetic and copies ran while one was open for 4% -> 3% of each run, Pallas kernels for 7% -> 14%
where the time goes in v3:
time: 191 us; the launch traced here: 190 us
  starting transfers between devices  68.7 us (36%)
  waiting for transfers between devices  62.8 us (33%)
  Pallas kernels  38.7 us (20%)
  other arithmetic  16.7 us (9%)
  local copies, waits for them, and re-layouts  2.03 us (1%)
    ppermute x16, waiting for transfers between devices, chip_move(): lax.ppermute(x, 'ctx', [(2 * a + c, 2 * b + c) for a, b in pairs for c in...  41.6 us
    ppermute x16, starting transfers between devices, chip_move(): lax.ppermute(x, 'ctx', [(2 * a + c, 2 * b + c) for a, b in pairs for c in...  36.3 us
    pallas_call x4, Pallas kernels, call(): run(order, *[pltpu.with_memory_space_constraint(x, pltpu.HBM) for x in ar...  35.5 us
    ppermute x16, starting transfers between devices, core_swap(): return lax.ppermute(x, 'ctx', [(i, i ^ 1) for i in range(size)])  21.2 us
    ppermute x6, waiting for transfers between devices, sum_all(): lax.ppermute(mine[k * share:(k + 1) * share], 'dp', [(i, i ^ k) for i in...  10.7 us
    ppermute x16, waiting for transfers between devices, core_swap(): return lax.ppermute(x, 'ctx', [(i, i ^ 1) for i in range(size)])  10.5 us
    ppermute x6, starting transfers between devices, sum_all(): lax.ppermute(total, 'dp', [(i, i ^ k) for i in range(dp)])  5.84 us
    ppermute x6, starting transfers between devices, sum_all(): lax.ppermute(mine[k * share:(k + 1) * share], 'dp', [(i, i ^ k) for i in...  5.44 us
  transfers between devices with their start and end apart: 44, of which 19 were waited for; matrix products, arithmetic and copies ran while one was open for 3% of the time, Pallas kernels for 14%

profile of v3, /device:TPU:1, one launch (start us, length us, event | category | flops | bytes accessed | tf_op | source)
XLA Modules:
  0.0 190.0 jit_solution(7544771563170101607)
XLA Ops:
  0.7 5.2 %key_features.1 = (f32[4,2,512,128]{3,2,1,0:T(8,128)}, f32[2048,128]{1,0:T(8,128)}, f32[2048,128]{1,0:T(8,128)}, f32[4,2,1,512]{3,2,1,0:T(1,128)}) custom-call(s32[8]{0:T(128)S(1)} %pad_add_fusion.order, bf16[128,1024]{1,0:T(8,128)(2,1)} %bitcast.82, bf16[128,1024]{1,0:T(8,128)(2,1)} %bitcast.73, bf16[32,64,128]{2,1,0:T(8,128)(2,1)} %bitcast.86, ...), custom_call_target="tpu_custom_call" | custom-call | tf_op jit(solution)/shard_map/key_features/pallas_call | solution.py:388
  6.0 2.8 %collective-permute-done.1 = f32[2048,128]{1,0:T(8,128)S(1)} collective-permute-done((f32[2048,128]{1,0:T(8,128)}, f32[2048,128]{1,0:T(8,128)S(1)}, u32[]{:S(2)}, u32[]{:S(2)}) %collective-permute-start.1) | collective-permute-done | bytes 1048608 | tf_op jit(solution)/shard_map/ppermute | solution.py:222
  8.8 2.5 %broadcast_select_fusion.1 = (f32[1024,128]{1,0:T(8,128)}, f32[1024,128]{1,0:T(8,128)}, f32[1024,128]{1,0:T(8,128)}) fusion(pred[]{:T(512)S(6)} %eq.37, f32[2048,128]{1,0:T(8,128)S(1)} %collective-permute-done.1, f32[2048,128]{1,0:T(8,128)} %get-tuple-element.48), kind=kLoop, calls=%fused_computation.17 | loop fusion | flops 393216 | bytes 3670017 | tf_op jit(solution)/shard_map/jit(_where)/select_n | solution.py:247
  11.3 4.4 %collective-permute-start.4 = (f32[1024,128]{1,0:T(8,128)}, f32[1024,128]{1,0:T(8,128)S(1)}, u32[]{:S(2)}, u32[]{:S(2)}) collective-permute-start(f32[1024,128]{1,0:T(8,128)} %get-tuple-element.61), channel_id=1, source_target_pairs={{0,2},{1,3},{2,4},{3,5},{4,6},{5,7},{8,10},{9,11},{10,12},{11,13},... | collective-permute-start | bytes 1572872 | tf_op jit(solution)/shard_map/ppermute | solution.py:226
  15.7 4.2 %collective-permute-start.5 = (f32[1024,128]{1,0:T(8,128)}, f32[1024,128]{1,0:T(8,128)S(1)}, u32[]{:S(2)}, u32[]{:S(2)}) collective-permute-start(f32[1024,128]{1,0:T(8,128)} %get-tuple-element.42), channel_id=1, source_target_pairs={{0,4},{1,5},{8,12},{9,13},{16,20},{17,21},{24,28},{25,29}} | collective-permute-start | bytes 1572872 | tf_op jit(solution)/shard_map/ppermute | solution.py:226
  21.9 16.6 %collective-permute-done.2 = f32[4,2,1,512]{3,2,1,0:T(1,128)S(1)} collective-permute-done((f32[4,2,1,512]{3,2,1,0:T(1,128)S(1)}, f32[4,2,1,512]{3,2,1,0:T(1,128)S(1)}, u32[]{:S(2)}, u32[]{:S(2)}) %collective-permute-start.2) | collective-permute-done | bytes 16416 | tf_op jit(solution)/shard_map/ppermute | solution.py:226
  38.5 3.5 %collective-permute-done.3 = f32[4,2,1,512]{3,2,1,0:T(1,128)S(1)} collective-permute-done((f32[4,2,1,512]{3,2,1,0:T(1,128)S(1)}, f32[4,2,1,512]{3,2,1,0:T(1,128)S(1)}, u32[]{:S(2)}, u32[]{:S(2)}) %collective-permute-start.3) | collective-permute-done | bytes 16416 | tf_op jit(solution)/shard_map/ppermute | solution.py:226
  42.6 11.6 %query_features.1 = (f32[4,2,512,128]{3,2,1,0:T(8,128)}, bf16[4,2,4,128,128]{4,3,2,1,0:T(8,128)(2,1)}, bf16[4,2,4,128,128]{4,3,2,1,0:T(8,128)(2,1)}, f32[4,2,4,1...) custom-call(s32[8]{0:T(128)S(1)} %pad_add_fusion.order, bf16[128,4096]{1,0:T(8,128)(2,1)} %bitcast.78, ...), custom_call_target="tpu_custom_call" | custom-call | tf_op jit(solution)/shard_map/query_features/pallas_call | solution.py:388
  54.3 2.4 %select_select_fusion.1 = f32[1024,128]{1,0:T(8,128)} fusion(f32[1024,128]{1,0:T(8,128)} %get-tuple-element.42, f32[1024,128]{1,0:T(8,128)S(1)} %collective-permute-done.5, f32[1024,128]{1,0:T(8,128)S(1)} %collective-permute-done.4, f32[1024,128]{1,0:T(8,128)S(1)} %copy-done.6, pred[]{:T(512)S(6)} %eq.38, pred[]{:T(512)S(6)} %eq.37), kind=kLoop, calls=%fused_computation.15 | loop fusion | flops 655360 | bytes 2621442 | tf_op jit(solution)/shard_map/jit(_where)/select_n | solution.py:266
  56.7 2.5 %collective-permute-start.7 = (f32[2048,128]{1,0:T(8,128)}, f32[2048,128]{1,0:T(8,128)S(1)}, u32[]{:S(2)}, u32[]{:S(2)}) collective-permute-start(f32[2048,128]{1,0:T(8,128)} %get-tuple-element.45), channel_id=1, source_target_pairs={{0,1},{1,0},{2,3},{3,2},{4,5},{5,4},{6,7},{7,6},{8,9},{9,8},{10,11... | collective-permute-start | bytes 3145736 | tf_op jit(solution)/shard_map/ppermute | solution.py:222
  59.2 2.5 %collective-permute-done.7 = f32[2048,128]{1,0:T(8,128)S(1)} collective-permute-done((f32[2048,128]{1,0:T(8,128)}, f32[2048,128]{1,0:T(8,128)S(1)}, u32[]{:S(2)}, u32[]{:S(2)}) %collective-permute-start.7) | collective-permute-done | bytes 1048608 | tf_op jit(solution)/shard_map/ppermute | solution.py:222
  66.9 10.4 %collective-permute-start.6 = (f32[1024,128]{1,0:T(8,128)}, f32[1024,128]{1,0:T(8,128)}, u32[]{:S(2)}, u32[]{:S(2)}) collective-permute-start(f32[1024,128]{1,0:T(8,128)} %select_select_fusion.1), channel_id=1, source_target_pairs={{0,2},{1,3},{2,4},{3,5},{4,6},{5,7},{8,10},{9,11},{10,12},{11,13},... | collective-permute-start | bytes 1572872 | tf_op jit(solution)/shard_map/ppermute | solution.py:226
  79.2 2.3 %select_select_fusion = f32[1024,128]{1,0:T(8,128)} fusion(f32[1024,128]{1,0:T(8,128)} %get-tuple-element.60, f32[1024,128]{1,0:T(8,128)} %collective-permute-done.9, f32[1024,128]{1,0:T(8,128)} %collective-permute-done.8, pred[]{:T(512)S(6)} %eq.40, pred[]{:T(512)S(6)} %eq.39, f32[2048,128]{1,0:T(8,128)S(1)} %collective-permute-done.7, ...), kind=kLoop, calls=%fused_computation.14 | loop fusion | flops 786432 | bytes 3145730 | tf_op jit(solution)/shard_map/jit(_where)/select_n | solution.py:266
  81.4 5.6 %collective-permute-done.6 = f32[1024,128]{1,0:T(8,128)} collective-permute-done((f32[1024,128]{1,0:T(8,128)}, f32[1024,128]{1,0:T(8,128)}, u32[]{:S(2)}, u32[]{:S(2)}) %collective-permute-start.6) | collective-permute-done | bytes 524320 | tf_op jit(solution)/shard_map/ppermute | solution.py:226
  95.0 12.7 %attend.1 = (bf16[128,4096]{1,0:T(8,128)(2,1)}, f32[1024,128]{1,0:T(8,128)}, f32[1024,128]{1,0:T(8,128)}, f32[4,2,512,128]{3,2,1,0:T(8,128)}, f32[4,2,1,512]{3,2,1,0:T(1,128)}) custom-call(s32[8]{0:T(128)S(1)} %pad_add_fusion.order, bf16[128,4096]{1,0:T(8,128)(2,1)} %bitcast.79, bf16[128,4096]{1,0:T(8,128)(2,1)} %bitcast.81, bf16[128,1024]{1,0:T(8,128)(2,1)} %bitcast.75, ...), custom_call_target="tpu_custom_call" | custom-call | tf_op jit(solution)/shard_map/attend/pallas_call | solution.py:388
  109.9 8.7 %collective-permute-start.26 = (f32[4,2,1,512]{3,2,1,0:T(1,128)S(1)}, f32[4,2,1,512]{3,2,1,0:T(1,128)S(1)}, u32[]{:S(2)}, u32[]{:S(2)}) collective-permute-start(f32[4,2,1,512]{3,2,1,0:T(1,128)S(1)} %reverse_add_fusion), channel_id=1, source_target_pairs={{0,2},{1,3},{2,0},{3,1},{4,6},{5,7},{6,4},{7,5},{8,10},{9,11},{10,... | collective-permute-start | bytes 49160 | tf_op jit(solution)/shard_map/ppermute | solution.py:226
  118.6 9.5 %collective-permute-done.26 = f32[4,2,1,512]{3,2,1,0:T(1,128)S(1)} collective-permute-done((f32[4,2,1,512]{3,2,1,0:T(1,128)S(1)}, f32[4,2,1,512]{3,2,1,0:T(1,128)S(1)}, u32[]{:S(2)}, u32[]{:S(2)}) %collective-permute-start.26) | collective-permute-done | bytes 16416 | tf_op jit(solution)/shard_map/ppermute | solution.py:226
  128.2 3.5 %collective-permute-done.27 = f32[4,2,1,512]{3,2,1,0:T(1,128)S(1)} collective-permute-done((f32[4,2,1,512]{3,2,1,0:T(1,128)S(1)}, f32[4,2,1,512]{3,2,1,0:T(1,128)S(1)}, u32[]{:S(2)}, u32[]{:S(2)}) %collective-permute-start.27) | collective-permute-done | bytes 16416 | tf_op jit(solution)/shard_map/ppermute | solution.py:226
  136.4 3.0 %collective-permute-done.12 = f32[1024,128]{1,0:T(8,128)S(1)} collective-permute-done((f32[1024,128]{1,0:T(8,128)S(1)}, f32[1024,128]{1,0:T(8,128)S(1)}, u32[]{:S(2)}, u32[]{:S(2)}) %collective-permute-start.12) | collective-permute-done | bytes 524320 | tf_op jit(solution)/shard_map/ppermute | solution.py:222
  140.5 6.1 %key_grads.1 = (f32[1024,128]{1,0:T(8,128)}, f32[1024,128]{1,0:T(8,128)}) custom-call(s32[8]{0:T(128)S(1)} %pad_add_fusion.order, bf16[128,1024]{1,0:T(8,128)(2,1)} %bitcast.84, bf16[128,1024]{1,0:T(8,128)(2,1)} %bitcast.76, bf16[128,1024]{1,0:T(8,128)(2,1)} %bitcast.85, bf16[128,1024]{1,0:T(8,128)(2,1)} %bitcast.77, ...), custom_call_target="tpu_custom_call" | custom-call | tf_op jit(solution)/shard_map/key_grads/pallas_call | solution.py:388
  149.7 2.3 %collective-permute-done.13 = f32[1,256,128]{2,1,0:T(8,128)S(1)} collective-permute-done((f32[1,256,128]{2,1,0:T(8,128)S(1)}, f32[1,256,128]{2,1,0:T(8,128)S(1)}, u32[]{:S(2)}, u32[]{:S(2)}) %collective-permute-start.13) | collective-permute-done | bytes 131104 | tf_op jit(solution)/shard_map/ppermute | solution.py:321
  152.9 2.7 %collective-permute-done.15 = f32[1,256,128]{2,1,0:T(8,128)S(1)} collective-permute-done((f32[1,256,128]{2,1,0:T(8,128)S(1)}, f32[1,256,128]{2,1,0:T(8,128)S(1)}, u32[]{:S(2)}, u32[]{:S(2)}) %collective-permute-start.15) | collective-permute-done | bytes 131104 | tf_op jit(solution)/shard_map/ppermute | solution.py:321
  170.5 4.0 %collective-permute-start.21 = (f32[1,256,128]{2,1,0:T(8,128)S(1)}, f32[1,256,128]{2,1,0:T(8,128)S(1)}, u32[]{:S(2)}, u32[]{:S(2)}) collective-permute-start(f32[1,256,128]{2,1,0:T(8,128)S(1)} %add.161), channel_id=1, source_target_pairs={{0,1},{1,0},{2,3},{3,2},{4,5},{5,4},{6,7},{7,6},{8,9},{9,8},{10,11... | collective-permute-start | bytes 393224 | tf_op jit(solution)/shard_map/ppermute | solution.py:222
  178.9 3.4 %collective-permute-start.24 = (f32[1,256,128]{2,1,0:T(8,128)S(1)}, f32[1,256,128]{2,1,0:T(8,128)S(1)}, u32[]{:S(2)}, u32[]{:S(2)}) collective-permute-start(f32[1,256,128]{2,1,0:T(8,128)S(1)} %collective-permute-done.20), channel_id=1, source_target_pairs={{0,1},{1,0},{2,3},{3,2},{4,5},{5,4},{6,7},{7,6},{8,9},{9,8},{10,11... | collective-permute-start | bytes 393224 | tf_op jit(solution)/shard_map/ppermute | solution.py:222
  (120 shorter events, 56.7 us)
Async XLA Ops:
  11.3 42.9 %collective-permute-start.4 = (f32[1024,128]{1,0:T(8,128)}, f32[1024,128]{1,0:T(8,128)S(1)}, u32[]{:S(2)}, u32[]{:S(2)}) collective-permute-start(f32[1024,128]{1,0:T(8,128)} %get-tuple-element.61), channel_id=1, source_target_pairs={{0,2},{1,3},{2,4},{3,5},{4,6},{5,7},{8,10},{9,11},{10,12},{11,13},... | collective-permute-start | bytes 1572872 | tf_op jit(solution)/shard_map/ppermute | solution.py:226
  15.7 38.5 %collective-permute-start.5 = (f32[1024,128]{1,0:T(8,128)}, f32[1024,128]{1,0:T(8,128)S(1)}, u32[]{:S(2)}, u32[]{:S(2)}) collective-permute-start(f32[1024,128]{1,0:T(8,128)} %get-tuple-element.42), channel_id=1, source_target_pairs={{0,4},{1,5},{8,12},{9,13},{16,20},{17,21},{24,28},{25,29}} | collective-permute-start | bytes 1572872 | tf_op jit(solution)/shard_map/ppermute | solution.py:226
  21.8 16.6 %collective-permute-start.2 = (f32[4,2,1,512]{3,2,1,0:T(1,128)S(1)}, f32[4,2,1,512]{3,2,1,0:T(1,128)S(1)}, u32[]{:S(2)}, u32[]{:S(2)}) collective-permute-start(f32[4,2,1,512]{3,2,1,0:T(1,128)S(1)} %reverse_add_fusion.1), channel_id=1, source_target_pairs={{0,2},{1,3},{2,0},{3,1},{4,6},{5,7},{6,4},{7,5},{8,10},{9,11},{10,... | collective-permute-start | bytes 49160 | tf_op jit(solution)/shard_map/ppermute | solution.py:226
  62.8 16.4 %collective-permute-start.8 = (f32[1024,128]{1,0:T(8,128)}, f32[1024,128]{1,0:T(8,128)}, u32[]{:S(2)}, u32[]{:S(2)}) collective-permute-start(f32[1024,128]{1,0:T(8,128)} %get-tuple-element.59), channel_id=1, source_target_pairs={{6,4},{7,5},{4,2},{5,3},{2,0},{3,1},{14,12},{15,13},{12,10},{13,11... | collective-permute-start | bytes 1572872 | tf_op jit(solution)/shard_map/ppermute | solution.py:226
  64.0 15.1 %collective-permute-start.9 = (f32[1024,128]{1,0:T(8,128)}, f32[1024,128]{1,0:T(8,128)}, u32[]{:S(2)}, u32[]{:S(2)}) collective-permute-start(f32[1024,128]{1,0:T(8,128)} %get-tuple-element.60), channel_id=1, source_target_pairs={{6,2},{7,3},{14,10},{15,11},{22,18},{23,19},{30,26},{31,27}} | collective-permute-start | bytes 1572872 | tf_op jit(solution)/shard_map/ppermute | solution.py:226
  65.5 16.0 %collective-permute-start.10 = (f32[1024,128]{1,0:T(8,128)}, f32[1024,128]{1,0:T(8,128)}, u32[]{:S(2)}, u32[]{:S(2)}) collective-permute-start(f32[1024,128]{1,0:T(8,128)} %select_select_fusion.1), channel_id=1, source_target_pairs={{2,6},{3,7},{10,14},{11,15},{18,22},{19,23},{26,30},{27,31}} | collective-permute-start | bytes 1572872 | tf_op jit(solution)/shard_map/ppermute | solution.py:226
  66.9 20.2 %collective-permute-start.6 = (f32[1024,128]{1,0:T(8,128)}, f32[1024,128]{1,0:T(8,128)}, u32[]{:S(2)}, u32[]{:S(2)}) collective-permute-start(f32[1024,128]{1,0:T(8,128)} %select_select_fusion.1), channel_id=1, source_target_pairs={{0,2},{1,3},{2,4},{3,5},{4,6},{5,7},{8,10},{9,11},{10,12},{11,13},... | collective-permute-start | bytes 1572872 | tf_op jit(solution)/shard_map/ppermute | solution.py:226
  91.4 40.9 %collective-permute-start.28 = (f32[1024,128]{1,0:T(8,128)}, f32[1024,128]{1,0:T(8,128)S(1)}, u32[]{:S(2)}, u32[]{:S(2)}) collective-permute-start(f32[1024,128]{1,0:T(8,128)} %select_select_fusion), channel_id=1, source_target_pairs={{6,4},{7,5},{4,2},{5,3},{2,0},{3,1},{14,12},{15,13},{12,10},{13,11... | collective-permute-start | bytes 1572872 | tf_op jit(solution)/shard_map/ppermute | solution.py:226
  92.7 39.6 %collective-permute-start.29 = (f32[1024,128]{1,0:T(8,128)}, f32[1024,128]{1,0:T(8,128)S(1)}, u32[]{:S(2)}, u32[]{:S(2)}) collective-permute-start(f32[1024,128]{1,0:T(8,128)} %select_select_fusion), channel_id=1, source_target_pairs={{4,0},{5,1},{12,8},{13,9},{20,16},{21,17},{28,24},{29,25}} | collective-permute-start | bytes 1572872 | tf_op jit(solution)/shard_map/ppermute | solution.py:226
  109.9 18.2 %collective-permute-start.26 = (f32[4,2,1,512]{3,2,1,0:T(1,128)S(1)}, f32[4,2,1,512]{3,2,1,0:T(1,128)S(1)}, u32[]{:S(2)}, u32[]{:S(2)}) collective-permute-start(f32[4,2,1,512]{3,2,1,0:T(1,128)S(1)} %reverse_add_fusion), channel_id=1, source_target_pairs={{0,2},{1,3},{2,0},{3,1},{4,6},{5,7},{6,4},{7,5},{8,10},{9,11},{10,... | collective-permute-start | bytes 49160 | tf_op jit(solution)/shard_map/ppermute | solution.py:226
  146.6 9.2 %collective-permute-start.31 = (f32[1024,128]{1,0:T(8,128)}, f32[1024,128]{1,0:T(8,128)S(1)}, u32[]{:S(2)}, u32[]{:S(2)}) collective-permute-start(f32[1024,128]{1,0:T(8,128)} %get-tuple-element.58), channel_id=1, source_target_pairs={{0,1},{1,0},{2,3},{3,2},{4,5},{5,4},{6,7},{7,6},{8,9},{9,8},{10,11... | collective-permute-start | bytes 1572872 | tf_op jit(solution)/shard_map/ppermute | solution.py:222
  149.5 6.1 %collective-permute-start.15 = (f32[1,256,128]{2,1,0:T(8,128)S(1)}, f32[1,256,128]{2,1,0:T(8,128)S(1)}, u32[]{:S(2)}, u32[]{:S(2)}) collective-permute-start(f32[1,256,128]{2,1,0:T(8,128)S(1)} %get-tuple-element.76), channel_id=1, source_target_pairs={{0,24},{8,16},{16,8},{24,0},{1,25},{9,17},{17,9},{25,1},{2,26},{10... | collective-permute-start | bytes 393224 | tf_op jit(solution)/shard_map/ppermute | solution.py:321
  159.7 6.5 %collective-permute-start.17 = (f32[1,256,128]{2,1,0:T(8,128)S(1)}, f32[1,256,128]{2,1,0:T(8,128)S(1)}, u32[]{:S(2)}, u32[]{:S(2)}) collective-permute-start(f32[1,256,128]{2,1,0:T(8,128)S(1)} %add.160), channel_id=1, source_target_pairs={{0,4},{1,5},{2,6},{3,7},{4,0},{5,1},{6,2},{7,3},{8,12},{9,13},{10,... | collective-permute-start | bytes 393224 | tf_op jit(solution)/shard_map/ppermute | solution.py:226
  166.2 8.3 %collective-permute-start.18 = (f32[1,256,128]{2,1,0:T(8,128)S(1)}, f32[1,256,128]{2,1,0:T(8,128)S(1)}, u32[]{:S(2)}, u32[]{:S(2)}) collective-permute-start(f32[1,256,128]{2,1,0:T(8,128)S(1)} %add.161), channel_id=1, source_target_pairs={{0,8},{8,0},{16,24},{24,16},{1,9},{9,1},{17,25},{25,17},{2,10},{10... | collective-permute-start | bytes 393224 | tf_op jit(solution)/shard_map/ppermute | solution.py:332
  167.7 6.8 %collective-permute-start.19 = (f32[1,256,128]{2,1,0:T(8,128)S(1)}, f32[1,256,128]{2,1,0:T(8,128)S(1)}, u32[]{:S(2)}, u32[]{:S(2)}) collective-permute-start(f32[1,256,128]{2,1,0:T(8,128)S(1)} %add.161), channel_id=1, source_target_pairs={{0,16},{8,24},{16,0},{24,8},{1,17},{9,25},{17,1},{25,9},{2,18},{10... | collective-permute-start | bytes 393224 | tf_op jit(solution)/shard_map/ppermute | solution.py:332
  168.8 7.4 %collective-permute-start.36 = (f32[1,256,128]{2,1,0:T(8,128)S(1)}, f32[1,256,128]{2,1,0:T(8,128)S(1)}, u32[]{:S(2)}, u32[]{:S(2)}) collective-permute-start(f32[1,256,128]{2,1,0:T(8,128)S(1)} %add.174), channel_id=1, source_target_pairs={{0,4},{1,5},{2,6},{3,7},{4,0},{5,1},{6,2},{7,3},{8,12},{9,13},{10,... | collective-permute-start | bytes 393224 | tf_op jit(solution)/shard_map/ppermute | solution.py:226
  169.0 8.2 %collective-permute-start.20 = (f32[1,256,128]{2,1,0:T(8,128)S(1)}, f32[1,256,128]{2,1,0:T(8,128)S(1)}, u32[]{:S(2)}, u32[]{:S(2)}) collective-permute-start(f32[1,256,128]{2,1,0:T(8,128)S(1)} %add.161), channel_id=1, source_target_pairs={{0,24},{8,16},{16,8},{24,0},{1,25},{9,17},{17,9},{25,1},{2,26},{10... | collective-permute-start | bytes 393224 | tf_op jit(solution)/shard_map/ppermute | solution.py:332
  170.5 7.5 %collective-permute-start.21 = (f32[1,256,128]{2,1,0:T(8,128)S(1)}, f32[1,256,128]{2,1,0:T(8,128)S(1)}, u32[]{:S(2)}, u32[]{:S(2)}) collective-permute-start(f32[1,256,128]{2,1,0:T(8,128)S(1)} %add.161), channel_id=1, source_target_pairs={{0,1},{1,0},{2,3},{3,2},{4,5},{5,4},{6,7},{7,6},{8,9},{9,8},{10,11... | collective-permute-start | bytes 393224 | tf_op jit(solution)/shard_map/ppermute | solution.py:222
  174.5 7.8 %collective-permute-start.23 = (f32[1,256,128]{2,1,0:T(8,128)S(1)}, f32[1,256,128]{2,1,0:T(8,128)S(1)}, u32[]{:S(2)}, u32[]{:S(2)}) collective-permute-start(f32[1,256,128]{2,1,0:T(8,128)S(1)} %collective-permute-done.19), channel_id=1, source_target_pairs={{0,1},{1,0},{2,3},{3,2},{4,5},{5,4},{6,7},{7,6},{8,9},{9,8},{10,11... | collective-permute-start | bytes 393224 | tf_op jit(solution)/shard_map/ppermute | solution.py:222
  176.2 6.2 %collective-permute-start.37 = (f32[1,256,128]{2,1,0:T(8,128)S(1)}, f32[1,256,128]{2,1,0:T(8,128)S(1)}, u32[]{:S(2)}, u32[]{:S(2)}) collective-permute-start(f32[1,256,128]{2,1,0:T(8,128)S(1)} %add.175), channel_id=1, source_target_pairs={{0,8},{8,0},{16,24},{24,16},{1,9},{9,1},{17,25},{25,17},{2,10},{10... | collective-permute-start | bytes 393224 | tf_op jit(solution)/shard_map/ppermute | solution.py:332
  177.2 7.1 %collective-permute-start.38 = (f32[1,256,128]{2,1,0:T(8,128)S(1)}, f32[1,256,128]{2,1,0:T(8,128)S(1)}, u32[]{:S(2)}, u32[]{:S(2)}) collective-permute-start(f32[1,256,128]{2,1,0:T(8,128)S(1)} %add.175), channel_id=1, source_target_pairs={{0,16},{8,24},{16,0},{24,8},{1,17},{9,25},{17,1},{25,9},{2,18},{10... | collective-permute-start | bytes 393224 | tf_op jit(solution)/shard_map/ppermute | solution.py:332
  177.9 7.2 %collective-permute-start.39 = (f32[1,256,128]{2,1,0:T(8,128)S(1)}, f32[1,256,128]{2,1,0:T(8,128)S(1)}, u32[]{:S(2)}, u32[]{:S(2)}) collective-permute-start(f32[1,256,128]{2,1,0:T(8,128)S(1)} %add.175), channel_id=1, source_target_pairs={{0,24},{8,16},{16,8},{24,0},{1,25},{9,17},{17,9},{25,1},{2,26},{10... | collective-permute-start | bytes 393224 | tf_op jit(solution)/shard_map/ppermute | solution.py:332
  178.9 7.9 %collective-permute-start.24 = (f32[1,256,128]{2,1,0:T(8,128)S(1)}, f32[1,256,128]{2,1,0:T(8,128)S(1)}, u32[]{:S(2)}, u32[]{:S(2)}) collective-permute-start(f32[1,256,128]{2,1,0:T(8,128)S(1)} %collective-permute-done.20), channel_id=1, source_target_pairs={{0,1},{1,0},{2,3},{3,2},{4,5},{5,4},{6,7},{7,6},{8,9},{9,8},{10,11... | collective-permute-start | bytes 393224 | tf_op jit(solution)/shard_map/ppermute | solution.py:222
  182.3 6.1 %collective-permute-start.40 = (f32[1,256,128]{2,1,0:T(8,128)S(1)}, f32[1,256,128]{2,1,0:T(8,128)S(1)}, u32[]{:S(2)}, u32[]{:S(2)}) collective-permute-start(f32[1,256,128]{2,1,0:T(8,128)S(1)} %add.175), channel_id=1, source_target_pairs={{0,1},{1,0},{2,3},{3,2},{4,5},{5,4},{6,7},{7,6},{8,9},{9,8},{10,11... | collective-permute-start | bytes 393224 | tf_op jit(solution)/shard_map/ppermute | solution.py:222
  (32 other events, 155.9 us)

commit v4 on v3

v4 whole, which is shorter than its diff:
```python
import jax
import jax.numpy as jnp
from jax import lax
from jax.experimental import pallas as pl
from jax.experimental.pallas import tpu as pltpu
from jax.sharding import PartitionSpec as P

BF = jnp.bfloat16
F32 = jnp.float32
VMEM_LIMIT = 32 * 1024 * 1024


def mm(a, b):
    return jnp.dot(a, b, preferred_element_type=F32)


def mm_nt(a, b):
    return lax.dot_general(a, b, (((1,), (1,)), ((), ())), preferred_element_type=F32)


def split(x):
    high = x.astype(BF)
    return high, (x - high.astype(F32)).astype(BF)


def cat(*pieces):
    return jnp.concatenate(pieces, axis=1)


def stack(*pieces):
    return jnp.concatenate(pieces, axis=0)


def soft(scores):
    top = jnp.max(scores, axis=0, keepdims=True)
    raised = jnp.exp(scores - top)
    return raised * (1.0 / jnp.sum(raised, axis=0, keepdims=True))


def both_soft(scores):
    return stack(soft(scores), soft(-scores))


def soft_back(probs, upstream):
    half = probs.shape[0] // 2
    p, n = probs[:half], probs[half:]
    gp, gn = upstream[:half], upstream[half:]
    result = p * (gp - jnp.sum(p * gp, axis=0, keepdims=True))
    result = result - n * (gn - jnp.sum(n * gn, axis=0, keepdims=True))
    return result.astype(BF)


def causal_mask(core, tokens):
    own = tokens // 2
    shift = core * own
    rows = lax.broadcasted_iota(jnp.int32, (tokens, tokens), 0)
    cols = lax.broadcasted_iota(jnp.int32, (tokens, tokens), 1)
    rows = rows + jnp.where(rows < own, shift, -shift)
    cols = cols + jnp.where(cols < own, shift, -shift)
    return rows >= cols


def column(row):
    return jnp.broadcast_to(row, (8, row.shape[1])).T[:, :1]


def three_lanes(wide, order):
    lane = lax.broadcasted_iota(jnp.int32, wide.shape, 1)
    high = wide.astype(BF).astype(F32)
    parts = {"h": high, "l": wide - high}
    result = jnp.where(lane == 2, parts[order[2]], 0.0)
    result = jnp.where(lane == 1, parts[order[1]], result)
    return jnp.where(lane == 0, parts[order[0]], result).astype(BF)


def tokens_of(own_ref, got_ref):
    return stack(own_ref[...], got_ref[...].astype(BF))


def put_parts(place, half, n, value, a_ref, b_ref, near_ref):
    i = pl.program_id(0)

    @pl.when(i < half)
    def _():
        a_ref[...] = value

    @pl.when(i >= half)
    def _():
        b_ref[...] = value

    @pl.when((i >= half) == (place == 1))
    def _():
        near_ref[...] = value


def before_of(place, half, near, far, near2, far2):
    first = jnp.where(place == 2, near2[...], near[...] + far2[...])
    second = jnp.where(place == 2, near[...] + far[...], near2[...])
    return jnp.where(pl.program_id(0) < half, first, second)


def pack_kernel(info, *refs):
    half = len(refs) // 2
    for x_ref, o_ref in zip(refs[:half], refs[half:]):
        o_ref[...] = x_ref[...].astype(F32)


def key_kernel(
    n, info, k_ref, kg_ref, v_ref, vg_ref, w_ref, kp_ref, kb_ref, norm_ref, a_ref, b_ref, near_ref
):
    group, width, dim = w_ref.shape
    keys = tokens_of(k_ref, kg_ref)
    values = tokens_of(v_ref, vg_ref)
    scores = mm_nt(w_ref[...].reshape(group * width, dim), keys)
    probs = stack(*[both_soft(scores[i * width : (i + 1) * width]) for i in range(group)])
    features = probs.astype(BF)
    kp_ref[0] = probs
    kb_ref[0] = features
    norm_ref[0] = mm_nt(jnp.ones((16, keys.shape[0]), BF), features)[:1]
    put_parts(info[2 * n + 1], n // 2, n, mm(features, values), a_ref, b_ref, near_ref)


def query_kernel(
    n, info, q_ref, qg_ref, c_ref, cg_ref, w_ref, kb_ref, pn_ref,
    qp_ref, qr_ref, wt_ref, a_ref, b_ref, near_ref,
):
    group, width, dim = w_ref.shape
    feats = 2 * width
    queries = tokens_of(q_ref, qg_ref)
    upstream = stack(c_ref[...].astype(F32), cg_ref[...])
    length = queries.shape[0]
    causal = causal_mask(info[2 * n], length)
    heads = range(group)
    cols = [slice(i * dim, (i + 1) * dim) for i in heads]
    rows = [slice(i * feats, (i + 1) * feats) for i in heads]
    scores = [mm_nt(w_ref[i], queries[:, cols[i]]) for i in heads]
    probs = [both_soft(x) for x in scores]
    query_t = [x.astype(BF) for x in probs]
    query_rows = [x.T for x in query_t]
    weights = [mm(query_rows[i], kb_ref[0, rows[i]]) for i in heads]
    weights = [jnp.where(causal, x, 0.0).astype(BF) for x in weights]
    norms = split(jnp.broadcast_to(pn_ref[0], (dim, group * feats)))
    ones = jnp.ones((dim, length), BF)
    den = [
        mm_nt(
            cat(weights[i], query_rows[i], query_rows[i]),
            cat(ones, norms[0][:, rows[i]], norms[1][:, rows[i]]),
        )
        for i in heads
    ]
    scaled = [(upstream[:, cols[i]] * (1.0 / den[i])).astype(BF) for i in heads]
    sums = [mm(query_t[i], scaled[i]) for i in heads]
    for i in heads:
        qp_ref[0, rows[i]] = probs[i]
        qr_ref[0, i] = query_rows[i]
        wt_ref[0, i] = weights[i]
    put_parts(info[2 * n + 2], n // 2, n, stack(*sums), a_ref, b_ref, near_ref)


def attend_kernel(
    n, info, c_ref, cg_ref, v_ref, vg_ref, qr_ref, wt_ref, pn_ref, near, far, near2, far2,
    att_ref, atg_ref, sc_ref, nl_ref, sn_ref,
):
    group, length, dim = qr_ref.shape[1:]
    feats = dim
    own = length // 2
    heads = range(group)
    cols = [slice(i * dim, (i + 1) * dim) for i in heads]
    rows = [slice(i * feats, (i + 1) * feats) for i in heads]
    upstream = stack(c_ref[...].astype(F32), cg_ref[...])
    values = tokens_of(v_ref, vg_ref)
    high, low = split(before_of(info[2 * n + 1], n // 2, near, far, near2, far2))
    norm_high, norm_low = split(jnp.broadcast_to(column(pn_ref[0]), (group * feats, dim)))
    high, low = cat(high, norm_high), cat(low, norm_low)
    values = cat(values, jnp.ones((length, dim), BF))
    query_rows = [qr_ref[0, i] for i in heads]
    both = [
        mm(cat(wt_ref[0, i], query_rows[i], query_rows[i]), stack(values, high[rows[i]], low[rows[i]]))
        for i in heads
    ]
    numerator = [x[:, :dim] for x in both]
    inverse = [1.0 / x[:, dim:] for x in both]
    scaled = [upstream[:, cols[i]] * inverse[i] for i in heads]
    products = [cat(*split(-(scaled[i] * inverse[i]) * numerator[i])) for i in heads]
    ones = jnp.ones((2 * dim, dim), BF)
    norm_grad = [mm(x, ones) for x in products]
    for i in heads:
        result = numerator[i] * inverse[i]
        att_ref[:, cols[i]] = result[:own].astype(BF)
        atg_ref[:, cols[i]] = result[own:]
        sc_ref[0, i] = scaled[i].astype(BF)
        nl_ref[0, i] = three_lanes(norm_grad[i], "hlh")
        sn_ref[0, :, rows[i]] = jnp.sum(
            query_rows[i].astype(F32) * norm_grad[i], axis=0, keepdims=True
        )


def query_grad_kernel(
    n, info, q_ref, qg_ref, v_ref, vg_ref, kb_ref, qp_ref, sc_ref, nl_ref, pn_ref,
    near, far, near2, far2, gq_ref, gk_ref,
):
    group, length, dim = sc_ref.shape[1:]
    feats = dim
    width = feats // 2
    heads = range(group)
    cols = [slice(i * dim, (i + 1) * dim) for i in heads]
    rows = [slice(i * feats, (i + 1) * feats) for i in heads]
    causal = causal_mask(info[2 * n], length)
    queries = tokens_of(q_ref, qg_ref)
    lane = lax.broadcasted_iota(jnp.int32, (length, dim), 1)
    values = cat(tokens_of(v_ref, vg_ref), jnp.where(lane < 2, 1.0, 0.0).astype(BF))
    high, low = split(before_of(info[2 * n + 1], n // 2, near, far, near2, far2))
    norm_cols = three_lanes(jnp.broadcast_to(column(pn_ref[0]), (group * feats, dim)), "hhl")
    scaled = [sc_ref[0, i] for i in heads]
    lanes = [nl_ref[0, i] for i in heads]
    mixed = [mm_nt(cat(scaled[i], lanes[i]), values) for i in heads]
    block = [jnp.where(causal, x, 0.0).astype(BF) for x in mixed]
    upstream = [
        mm_nt(
            cat(kb_ref[0, rows[i]], high[rows[i]], norm_cols[rows[i]], low[rows[i]]),
            cat(block[i], scaled[i], lanes[i], scaled[i]),
        )
        for i in heads
    ]
    probs = [qp_ref[0, r] for r in rows]
    back = [soft_back(probs[i], upstream[i]) for i in heads]
    for i in heads:
        gq_ref[0, i * width : (i + 1) * width] = mm(back[i], queries[:, cols[i]])
        gk_ref[0, rows[i]] = mm(probs[i].astype(BF), block[i])


def key_grad_kernel(
    n, info, k_ref, kg_ref, v_ref, vg_ref, kp_ref, gk_ref, sn_ref, near, far, near2, far2, out_ref
):
    rows, length = kp_ref.shape[1:]
    feats = k_ref.shape[1]
    values = tokens_of(v_ref, vg_ref)
    state = cat(*split(before_of(info[2 * n + 2], n // 2, near, far, near2, far2)))
    upstream = gk_ref[0] + mm_nt(state, cat(values, values))
    upstream = upstream + jnp.broadcast_to(column(sn_ref[0]), (rows, length))
    back = [
        soft_back(kp_ref[0, a : a + feats], upstream[a : a + feats])
        for a in range(0, rows, feats)
    ]
    out_ref[0] = mm(stack(*back), tokens_of(k_ref, kg_ref))


def attended_kernel(info, x_ref, kept_ref, o_ref):
    o_ref[...] = x_ref[...].astype(BF)


def out_kernel(info, *refs):
    out_ref = refs[-1]
    for i, ref in enumerate(refs[:-1]):
        out_ref[info[i]] = ref[...]


def core_swap(x):
    size = lax.axis_size("ctx")
    return lax.ppermute(x, "ctx", [(i, i ^ 1) for i in range(size)])


def chip_move(x, pairs):
    return lax.ppermute(x, "ctx", [(2 * a + c, 2 * b + c) for a, b in pairs for c in (0, 1)])


def after(values, *earlier):
    return lax.optimization_barrier((values, earlier))[0]


class Scan:
    def __init__(self, a, b, near, forward):
        self.chips = lax.axis_size("ctx") // 2
        chip = lax.axis_index("ctx") // 2
        self.forward = forward
        self.place = chip if forward else self.chips - 1 - chip
        self.a, self.b, self.payload = a, b, near

    def move(self, x, pairs):
        last = self.chips - 1
        turn = (lambda p: p) if self.forward else (lambda p: last - p)
        return chip_move(x, [(turn(p), turn(q)) for p, q in pairs])

    def first(self):
        if self.chips == 4:
            self.near = self.move(self.payload, [(0, 1), (1, 2), (2, 3)])
            self.far = self.move(self.b, [(0, 2)])

    def turn_around(self, *earlier):
        if self.chips == 4:
            a, b = after((self.a, self.b), *earlier) if earlier else (self.a, self.b)
            self.payload = jnp.where(
                self.place == 1,
                a + self.near,
                jnp.where(self.place == 2, b + self.near + self.far, b),
            )

    def second(self):
        if self.chips == 4:
            self.near2 = self.move(self.payload, [(0, 1), (1, 2), (2, 3)])
            self.far2 = self.move(self.payload, [(1, 3)])
            return self.near, self.far, self.near2, self.far2
        total = jnp.concatenate([self.a, self.b], axis=0)
        before = self.move(total, [(i, i + 1) for i in range(self.chips - 1)])
        step = 1
        while step < self.chips:
            pairs = [(i, i + step) for i in range(self.chips - step)]
            before = before + self.move(before, pairs)
            step *= 2
        rows = self.a.shape[0]
        zero = jnp.zeros_like(self.a)
        return before[:rows], zero, before[rows:], zero


def scan_norms(norm, chip, chips, forward, *earlier):
    base = jnp.zeros_like(norm)
    if earlier and chips <= 4:
        bits = range(1, chips)
        moved = [chip_move(norm, [(i, i ^ bit) for i in range(chips)]) for bit in bits]
        moved = after(moved, *earlier)
        for bit in bits:
            other = chip ^ bit
            base = base + jnp.where(other < chip if forward else other > chip, moved[bit - 1], 0.0)
        return base
    total = norm
    bit = 1
    while bit < chips:
        moved = chip_move(total, [(i, i ^ bit) for i in range(chips)])
        upper = (chip & bit) != 0 if forward else (chip & bit) == 0
        base = base + jnp.where(upper, moved, 0.0)
        total = total + moved
        bit *= 2
    return base


def sum_all(mine, chips):
    dp = lax.axis_size("dp")
    share = mine.shape[0] // dp
    got = [
        lax.ppermute(mine[k * share : (k + 1) * share], "dp", [(i, i ^ k) for i in range(dp)])
        for k in range(1, dp)
    ]
    total = mine[:share]
    for piece in got:
        total = total + piece
    bit = 1
    while bit < chips:
        total = total + chip_move(total, [(i, i ^ bit) for i in range(chips)])
        bit *= 2
    pieces = [total] + [
        lax.ppermute(total, "dp", [(i, i ^ k) for i in range(dp)]) for k in range(1, dp)
    ]
    pieces = pieces + [core_swap(x) for x in pieces]
    return [x[i] for x in pieces for i in range(share)]


def shards(queries, key_tokens, value_tokens, cotangent, query_map, key_map):
    own = queries.shape[1]
    length = 2 * own
    head_count, dim, width = query_map.shape
    shared = key_tokens.shape[2] // dim
    group = head_count // shared
    feats = 2 * width
    n = shared // 2
    wide = group * feats
    queries = queries.reshape(own, head_count * dim)
    cotangent = cotangent.reshape(own, head_count * dim)
    keys = key_tokens.reshape(own, shared * dim)
    values = value_tokens.reshape(own, shared * dim)
    query_map = jnp.swapaxes(query_map, 1, 2)
    key_map = jnp.swapaxes(key_map, 1, 2)

    ctx = lax.axis_index("ctx")
    chips = lax.axis_size("ctx") // 2
    chip, core = ctx // 2, ctx % 2
    dp = lax.axis_size("dp")
    part = jnp.arange(n, dtype=jnp.int32) ^ (lax.axis_index("dp") * (n // dp))
    places = jnp.stack([core, chip, chips - 1 - chip]) if chips == 4 else jnp.stack([core, core * 0 + 3, core * 0 + 3])
    info = jnp.concatenate([part + n * core, part + n * (1 - core), places]).astype(jnp.int32)

    def spec(shape, index):
        return pl.BlockSpec(shape, index)

    def own_cols(cols):
        return spec((own, cols), lambda i, info: (0, info[i]))

    def other_cols(cols):
        return spec((own, cols), lambda i, info: (0, info[n + i]))

    def got_cols(cols):
        return spec((own, cols), lambda i, info: (0, i))

    def per_head(*shape):
        return spec((1,) + shape, lambda i, info: (i,) + (0,) * len(shape))

    def shape_of(*shape, dtype=F32):
        return jax.ShapeDtypeStruct((n,) + shape, dtype)

    def call(name, body, in_specs, out_specs, out_shape, **options):
        run = pl.pallas_call(
            body,
            name=name,
            out_shape=[pltpu.HBM(x.shape, x.dtype) for x in out_shape],
            grid_spec=pltpu.PrefetchScalarGridSpec(
                num_scalar_prefetch=1, grid=(n,), in_specs=in_specs, out_specs=out_specs
            ),
            compiler_params=pltpu.CompilerParams(vmem_limit_bytes=VMEM_LIMIT),
            **options,
        )
        return lambda *arrays: run(
            info, *[pltpu.with_memory_space_constraint(x, pltpu.HBM) for x in arrays]
        )

    def part_body(body):
        return lambda *refs: body(n, *refs)

    one, four = dim, group * dim
    map_spec = spec((group, width, dim), lambda i, info: (info[i], 0, 0))
    row_spec, row = per_head(1, wide), shape_of(1, wide)
    flat_spec, flat = per_head(wide, length), shape_of(wide, length)
    half = n // 2
    half_state = jax.ShapeDtypeStruct((half * wide, dim), F32)
    a_spec = spec((wide, dim), lambda i, info: (jnp.minimum(i, half - 1), 0))
    b_spec = spec((wide, dim), lambda i, info: (jnp.maximum(i - half, 0), 0))
    moved_spec = spec((wide, dim), lambda i, info: (i % half, 0))

    def near_spec(which):
        def index(i, info):
            off = jnp.where(info[2 * n + which] == 1, half, 0)
            return (jnp.clip(i - off, 0, half - 1), 0)

        return spec((wide, dim), index)

    def pack(name, arrays, cols):
        packed = call(
            name,
            pack_kernel,
            [other_cols(cols)] * len(arrays),
            [got_cols(cols)] * len(arrays),
            [jax.ShapeDtypeStruct((own, n * cols), F32)] * len(arrays),
        )(*arrays)
        return packed

    packed_keys = pack("pack_keys", (keys, values), one)
    packed_queries = pack("pack_queries", after((queries, cotangent), *packed_keys), four)
    keys_got, values_got = [core_swap(x) for x in packed_keys]
    queries_got, cotangent_got = [core_swap(x) for x in packed_queries]

    key_probs, key_features, norm, a, b, near = call(
        "key_features",
        part_body(key_kernel),
        [own_cols(one), got_cols(one)] * 2 + [map_spec],
        [flat_spec, flat_spec, row_spec, a_spec, b_spec, near_spec(1)],
        [flat, shape_of(wide, length, dtype=BF), row] + [half_state] * 3,
    )(keys, keys_got, values, values_got, key_map)
    prefix_norm = scan_norms(norm, chip, chips, True)
    prefix = Scan(*after((a, b, near), prefix_norm), True)
    prefix.first()

    rows_spec = per_head(group, length, dim)
    rows_bf = shape_of(group, length, dim, dtype=BF)
    query_probs, query_rows, weights, a, b, near = call(
        "query_features",
        part_body(query_kernel),
        [own_cols(four), got_cols(four)] * 2 + [map_spec, flat_spec, row_spec],
        [flat_spec, rows_spec, per_head(group, length, length), a_spec, b_spec, near_spec(2)],
        [flat, rows_bf, shape_of(group, length, length, dtype=BF)] + [half_state] * 3,
    )(queries, queries_got, cotangent, cotangent_got, query_map, key_features, prefix_norm)
    suffix = Scan(a, b, near, False)
    suffix.first()
    prefix.turn_around(near)
    before = prefix.second()
    suffix.turn_around()
    before = after(before, suffix.payload)
    later = suffix.second()

    attended, attended_got, scaled, norm_lanes, norm = call(
        "attend",
        part_body(attend_kernel),
        [own_cols(four), got_cols(four), own_cols(one), got_cols(one)]
        + [rows_spec, per_head(group, length, length), row_spec]
        + [moved_spec] * 4,
        [own_cols(four), got_cols(four), rows_spec, rows_spec, row_spec],
        [
            jax.ShapeDtypeStruct((own, head_count * dim), BF),
            jax.ShapeDtypeStruct((own, n * four), F32),
            rows_bf,
            rows_bf,
            row,
        ],
    )(cotangent, cotangent_got, values, values_got, query_rows, weights, prefix_norm, *before)
    suffix_norm = scan_norms(norm, chip, chips, False, *later)
    grad_spec, grad = per_head(group * width, dim), shape_of(group * width, dim)
    query_part, key_up = call(
        "query_grads",
        part_body(query_grad_kernel),
        [own_cols(four), got_cols(four), own_cols(one), got_cols(one)]
        + [flat_spec, flat_spec, rows_spec, rows_spec, row_spec]
        + [moved_spec] * 4,
        [grad_spec, flat_spec],
        [grad, flat],
    )(
        queries, queries_got, values, values_got, key_features, query_probs, scaled, norm_lanes,
        prefix_norm, *before,
    )
    (key_part,) = call(
        "key_grads",
        part_body(key_grad_kernel),
        [own_cols(one), got_cols(one)] * 2 + [flat_spec, flat_spec, row_spec] + [moved_spec] * 4,
        [grad_spec],
        [grad],
    )(keys, keys_got, values, values_got, key_probs, key_up, suffix_norm, *later)
    (attended,) = call(
        "attended",
        attended_kernel,
        [got_cols(four), pl.BlockSpec(memory_space=pl.ANY)],
        [other_cols(four)],
        [jax.ShapeDtypeStruct((own, head_count * dim), BF)],
        input_output_aliases={2: 0},
    )(core_swap(attended_got), attended)

    def finish(name, mine):
        pieces = sum_all(mine, chips)
        whole = pl.BlockSpec(memory_space=pltpu.VMEM)
        natural = pl.pallas_call(
            out_kernel,
            name=name,
            out_shape=jax.ShapeDtypeStruct((shared, group * width, dim), F32),
            in_specs=[pl.BlockSpec(memory_space=pltpu.SMEM)] + [whole] * shared,
            out_specs=whole,
            compiler_params=pltpu.CompilerParams(vmem_limit_bytes=VMEM_LIMIT),
        )(info, *pieces)
        return jnp.swapaxes(natural.reshape(head_count, width, dim), 1, 2)

    query_grad = finish("query_out", query_part)
    key_grad = finish("key_out", key_part)
    return attended.reshape(1, own, head_count * dim), query_grad, key_grad


def solution(mesh):
    in_specs = (
        P("dp", "ctx", None),
        P("dp", "ctx", None),
        P("dp", "ctx", None),
        P("dp", "ctx", None),
        P(),
        P(),
    )
    out_specs = (P("dp", "ctx", None), P(), P())
    return jax.shard_map(shards, mesh=mesh, in_specs=in_specs, out_specs=out_specs, check_vma=False)
```

time: 191 us -> 162 us (0.85)
  waiting for transfers between devices: 62.8 us -> 20.9 us
  Pallas kernels: 38.7 us -> 51.1 us
  other arithmetic: 16.7 us -> 7.45 us
  starting transfers between devices: 68.7 us -> 74 us
  local copies, waits for them, and re-layouts: 2.03 us -> 6.26 us
    ppermute x16 -> x17, waiting for transfers between devices: 41.6 us -> 9.92 us  [chip_move(): lax.ppermute(x, 'ctx', [(2 * a + c, 2 * b + c) for a, b in pairs for c in...]
    pallas_call x4 -> x8, Pallas kernels: 35.5 us -> 48 us  [call(): run(info, *[pltpu.with_memory_space_constraint(x, pltpu.HBM) for x in arr...]
    ppermute x16 -> x13, waiting for transfers between devices: 10.5 us -> 3.16 us  [core_swap(): return lax.ppermute(x, 'ctx', [(i, i ^ 1) for i in range(size)])]
    ppermute x16 -> x17, starting transfers between devices: 36.3 us -> 42.9 us  [chip_move(): lax.ppermute(x, 'ctx', [(2 * a + c, 2 * b + c) for a, b in pairs for c in...]
    ppermute x6, waiting for transfers between devices: 10.7 us -> 4.22 us  [sum_all(): lax.ppermute(mine[k * share:(k + 1) * share], 'dp', [(i, i ^ k) for i in...]
    select_n x4 -> x0, other arithmetic: 6.25 us -> none  [the longest x2 3.57 us: __init__(): self.payload = (jnp.where(self.place == 1, self.b, self.a), self.b)]
    ppermute x6, waiting for transfers between devices: 0.02 us -> 3.63 us  [sum_all(): lax.ppermute(total, 'dp', [(i, i ^ k) for i in range(dp)])]
    add x6 -> x1, other arithmetic: 4.22 us -> 0.68 us  [scan_norms(): base + jnp.where(other < chip if forward else other > chip, moved[bit - 1...]
  transfers between devices with their start and end apart: 44 -> 42, of which waited for: 19 -> 14; matrix products, arithmetic and copies ran while one was open for 3% -> 6% of each run, Pallas kernels for 14% -> 26%
where the time goes in v4:
time: 162 us; the launch traced here: 161 us
  starting transfers between devices  74 us (46%)
  Pallas kernels  51.1 us (32%)
  waiting for transfers between devices  20.9 us (13%)
  other arithmetic  7.45 us (5%)
  local copies, waits for them, and re-layouts  6.26 us (4%)
    pallas_call x8, Pallas kernels, call(): run(info, *[pltpu.with_memory_space_constraint(x, pltpu.HBM) for x in arr...  48 us
    ppermute x17, starting transfers between devices, chip_move(): lax.ppermute(x, 'ctx', [(2 * a + c, 2 * b + c) for a, b in pairs for c in...  42.9 us
    ppermute x13, starting transfers between devices, core_swap(): return lax.ppermute(x, 'ctx', [(i, i ^ 1) for i in range(size)])  20.2 us
    ppermute x17, waiting for transfers between devices, chip_move(): lax.ppermute(x, 'ctx', [(2 * a + c, 2 * b + c) for a, b in pairs for c in...  9.92 us
    ppermute x6, starting transfers between devices, sum_all(): lax.ppermute(total, 'dp', [(i, i ^ k) for i in range(dp)])  5.43 us
    ppermute x6, starting transfers between devices, sum_all(): lax.ppermute(mine[k * share:(k + 1) * share], 'dp', [(i, i ^ k) for i in...  5.43 us
    ppermute x6, waiting for transfers between devices, sum_all(): lax.ppermute(mine[k * share:(k + 1) * share], 'dp', [(i, i ^ k) for i in...  4.22 us
    unnamed x36, local copies, waits for them, and re-layouts  4.06 us
  transfers between devices with their start and end apart: 42, of which 14 were waited for; matrix products, arithmetic and copies ran while one was open for 6% of the time, Pallas kernels for 26%

profile of v4, /device:TPU:1, one launch (start us, length us, event | category | flops | bytes accessed | tf_op | source)
XLA Modules:
  0.0 160.8 jit_solution(3630929431264544742)
XLA Ops:
  0.8 3.4 %pack_keys.1 = (f32[128,512]{1,0:T(8,128)}, f32[128,512]{1,0:T(8,128)}) custom-call(s32[11]{0:T(128)S(1)} %concatenate.3.info.refs_0_, bf16[128,1024]{1,0:T(8,128)(2,1)} %bitcast.59, bf16[128,1024]{1,0:T(8,128)(2,1)} %bitcast.54), custom_call_target="tpu_custom_call" | custom-call | tf_op jit(solution)/shard_map/pack_keys/pallas_call | solution.py:410
  4.2 4.1 %pack_queries.1 = (f32[128,2048]{1,0:T(8,128)}, f32[128,2048]{1,0:T(8,128)}) custom-call(s32[11]{0:T(128)S(1)} %concatenate.3.info.refs_0_, bf16[128,4096]{1,0:T(8,128)(2,1)} %bitcast.51, bf16[128,4096]{1,0:T(8,128)(2,1)} %bitcast.48), custom_call_target="tpu_custom_call" | custom-call | tf_op jit(solution)/shard_map/pack_queries/pallas_call | solution.py:410
  9.4 2.4 %collective-permute-done.1.refs_4_ = f32[128,512]{1,0:T(8,128)S(1)} collective-permute-done((f32[128,512]{1,0:T(8,128)S(1)}, f32[128,512]{1,0:T(8,128)S(1)}, u32[]{:S(2)}, u32[]{:S(2)}) %collective-permute-start.1) | collective-permute-done | bytes 262176 | tf_op jit(solution)/shard_map/ppermute | solution.py:260
  13.2 5.7 %key_features.1 = (f32[4,512,256]{2,1,0:T(8,128)}, bf16[4,512,256]{2,1,0:T(8,128)(2,1)}, f32[4,1,512]{2,1,0:T(1,128)}, f32[1024,128]{1,0:T(8,128)}, f32[1024,128]{1,0:T(8,128)}, /*index=5*/f32[1024,128]{1,0:T(8,128)}) custom-call(s32[11]{0:T(128)S(1)} %concatenate.3.info.refs_0_, bf16[128,1024]{1,0:T(8,128)(2,1)} %bitcast.60, f32[128,512]{1,0:T(8,128)} %copy-done.10, ...), custom_call_target="tpu_custom_call" | custom-call | tf_op jit(solution)/shard_map/key_features/pallas_call | solution.py:410
  18.9 2.4 %collective-permute-start.4 = (f32[4,1,512]{2,1,0:T(1,128)}, f32[4,1,512]{2,1,0:T(1,128)S(1)}, u32[]{:S(2)}, u32[]{:S(2)}) collective-permute-start(f32[4,1,512]{2,1,0:T(1,128)} %get-tuple-element.47), channel_id=1, source_target_pairs={{0,2},{1,3},{2,0},{3,1},{4,6},{5,7},{6,4},{7,5},{8,10},{9,11},{10,... | collective-permute-start | bytes 24584 | tf_op jit(solution)/shard_map/ppermute | solution.py:264
  23.3 2.5 %collective-permute-start.5 = (f32[4,1,512]{2,1,0:T(1,128)S(1)}, f32[4,1,512]{2,1,0:T(1,128)S(1)}, u32[]{:S(2)}, u32[]{:S(2)}) collective-permute-start(f32[4,1,512]{2,1,0:T(1,128)S(1)} %add.82), channel_id=1, source_target_pairs={{0,4},{1,5},{2,6},{3,7},{4,0},{5,1},{6,2},{7,3},{8,12},{9,13},{10,... | collective-permute-start | bytes 24584 | tf_op jit(solution)/shard_map/ppermute | solution.py:264
  27.5 3.3 %collective-permute-start.6 = (f32[1024,128]{1,0:T(8,128)}, f32[1024,128]{1,0:T(8,128)S(1)}, u32[]{:S(2)}, u32[]{:S(2)}) collective-permute-start(f32[1024,128]{1,0:T(8,128)} %get-tuple-element.53), channel_id=1, source_target_pairs={{0,2},{1,3},{2,4},{3,5},{4,6},{5,7},{8,10},{9,11},{10,12},{11,13},... | collective-permute-start | bytes 1572872 | tf_op jit(solution)/shard_map/ppermute | solution.py:264
  30.8 4.2 %collective-permute-start.7 = (f32[1024,128]{1,0:T(8,128)}, f32[1024,128]{1,0:T(8,128)S(1)}, u32[]{:S(2)}, u32[]{:S(2)}) collective-permute-start(f32[1024,128]{1,0:T(8,128)} %get-tuple-element.58), channel_id=1, source_target_pairs={{0,4},{1,5},{8,12},{9,13},{16,20},{17,21},{24,28},{25,29}} | collective-permute-start | bytes 1572872 | tf_op jit(solution)/shard_map/ppermute | solution.py:264
  36.4 8.3 %query_features.1 = (f32[4,512,256]{2,1,0:T(8,128)}, bf16[4,4,256,128]{3,2,1,0:T(8,128)(2,1)}, bf16[4,4,256,256]{3,2,1,0:T(8,128)(2,1)}, f32[1024,128]{1,0:T(8,1...) custom-call(s32[11]{0:T(128)S(1)} %concatenate.3.info.refs_0_, bf16[128,4096]{1,0:T(8,128)(2,1)} %bitcast.52, ...), custom_call_target="tpu_custom_call" | custom-call | tf_op jit(solution)/shard_map/query_features/pallas_call | solution.py:410
  46.7 4.2 %collective-permute-done.7.refs_9_.refs_11_ = f32[1024,128]{1,0:T(8,128)S(1)} collective-permute-done((f32[1024,128]{1,0:T(8,128)}, f32[1024,128]{1,0:T(8,128)S(1)}, u32[]{:S(2)}, u32[]{:S(2)}) %collective-permute-start.7) | collective-permute-done | bytes 524320 | tf_op jit(solution)/shard_map/ppermute | solution.py:264
  53.9 3.1 %collective-permute-done.10.refs_8_ = f32[1024,128]{1,0:T(8,128)S(1)} collective-permute-done((f32[1024,128]{1,0:T(8,128)}, f32[1024,128]{1,0:T(8,128)S(1)}, u32[]{:S(2)}, u32[]{:S(2)}) %collective-permute-start.10) | collective-permute-done | bytes 524320 | tf_op jit(solution)/shard_map/ppermute | solution.py:264
  57.0 2.6 %select_select_fusion = f32[1024,128]{1,0:T(8,128)} fusion(f32[1024,128]{1,0:T(8,128)} %get-tuple-element.60, f32[1024,128]{1,0:T(8,128)S(1)} %collective-permute-done.11.refs_9_, f32[1024,128]{1,0:T(8,128)S(1)} %collective-permute-done.10.refs_8_, f32[1024,128]{1,0:T(8,128)} %get-tuple-element.59, pred[]{:T(512)S(6)} %eq.17, pred[]{:T(512)S(6)} %eq.16), kind=kLoop, calls=%fused_computation | loop fusion | flops 655360 | bytes 2621442 | tf_op jit(solution)/shard_map/jit(_where)/select_n | solution.py:292
  63.1 7.6 %attend.1 = (bf16[128,4096]{1,0:T(8,128)(2,1)}, f32[128,2048]{1,0:T(8,128)}, bf16[4,4,256,128]{3,2,1,0:T(8,128)(2,1)}, bf16[4,4,256,128]{3,2,1,0:T(8,128)(2,1)}, f32[4,1,512]{2,1,0:T(1,128)}) custom-call(s32[11]{0:T(128)S(1)} %concatenate.3.info.refs_0_, bf16[128,4096]{1,0:T(8,128)(2,1)} %bitcast.50, f32[128,2048]{1,0:T(8,128)} %copy-done.4, ...), custom_call_target="tpu_custom_call" | custom-call | tf_op jit(solution)/shard_map/attend/pallas_call | solution.py:410
  70.8 8.4 %query_grads.1 = (f32[4,256,128]{2,1,0:T(8,128)}, f32[4,512,256]{2,1,0:T(8,128)}) custom-call(s32[11]{0:T(128)S(1)} %concatenate.3.info.refs_0_, bf16[128,4096]{1,0:T(8,128)(2,1)} %bitcast.53, f32[128,2048]{1,0:T(8,128)} %copy-done.3, bf16[128,1024]{1,0:T(8,128)(2,1)} %bitcast.57, f32[128,512]{1,0:T(8,128)} %copy-done.2, ...), custom_call_target="tpu_custom_call" | custom-call | tf_op jit(solution)/shard_map/query_grads/pallas_call | solution.py:410
  84.6 13.4 %collective-permute-start.25 = (f32[4,1,512]{2,1,0:T(1,128)S(1)}, f32[4,1,512]{2,1,0:T(1,128)S(1)}, u32[]{:S(2)}, u32[]{:S(2)}) collective-permute-start(f32[4,1,512]{2,1,0:T(1,128)S(1)} %copy-done.17), channel_id=1, source_target_pairs={{0,2},{1,3},{2,0},{3,1},{4,6},{5,7},{6,4},{7,5},{8,10},{9,11},{10,... | collective-permute-start | bytes 24584 | tf_op jit(solution)/shard_map/ppermute | solution.py:264
  98.0 3.0 %collective-permute-start.26 = (f32[4,1,512]{2,1,0:T(1,128)S(1)}, f32[4,1,512]{2,1,0:T(1,128)S(1)}, u32[]{:S(2)}, u32[]{:S(2)}) collective-permute-start(f32[4,1,512]{2,1,0:T(1,128)S(1)} %copy-done.17), channel_id=1, source_target_pairs={{0,4},{1,5},{2,6},{3,7},{4,0},{5,1},{6,2},{7,3},{8,12},{9,13},{10,... | collective-permute-start | bytes 24584 | tf_op jit(solution)/shard_map/ppermute | solution.py:264
  101.0 3.0 %collective-permute-start.27 = (f32[4,1,512]{2,1,0:T(1,128)S(1)}, f32[4,1,512]{2,1,0:T(1,128)S(1)}, u32[]{:S(2)}, u32[]{:S(2)}) collective-permute-start(f32[4,1,512]{2,1,0:T(1,128)S(1)} %copy-done.17), channel_id=1, source_target_pairs={{0,6},{1,7},{2,4},{3,5},{4,2},{5,3},{6,0},{7,1},{8,14},{9,15},{10,... | collective-permute-start | bytes 24584 | tf_op jit(solution)/shard_map/ppermute | solution.py:264
  105.0 6.7 %collective-permute-start.12 = (f32[128,2048]{1,0:T(8,128)S(1)}, f32[128,2048]{1,0:T(8,128)S(1)}, u32[]{:S(2)}, u32[]{:S(2)}) collective-permute-start(f32[128,2048]{1,0:T(8,128)S(1)} %copy-done.14), channel_id=1, source_target_pairs={{0,1},{1,0},{2,3},{3,2},{4,5},{5,4},{6,7},{7,6},{8,9},{9,8},{10,11... | collective-permute-start | bytes 3145736 | tf_op jit(solution)/shard_map/ppermute | solution.py:260
  112.5 6.5 %key_grads.1 = f32[4,256,128]{2,1,0:T(8,128)} custom-call(s32[11]{0:T(128)S(1)} %concatenate.3.info.refs_0_, bf16[128,1024]{1,0:T(8,128)(2,1)} %bitcast.61, f32[128,512]{1,0:T(8,128)} %copy-done.10, bf16[128,1024]{1,0:T(8,128)(2,1)} %bitcast.58, f32[128,512]{1,0:T(8,128)} %copy-done.2, f32[4,512,256]{2,1,0:T(8,128)} %get-tuple-element.71.refs_5_, ...), custom_call_target="tpu_custom_call" | custom-call | tf_op jit(solution)/shard_map/key_grads/pallas_call | solution.py:410
  120.6 2.1 %collective-permute-start.32 = (f32[1,256,128]{2,1,0:T(8,128)S(1)}, f32[1,256,128]{2,1,0:T(8,128)S(1)}, u32[]{:S(2)}, u32[]{:S(2)}) collective-permute-start(f32[1,256,128]{2,1,0:T(8,128)S(1)} %get-tuple-element.78), channel_id=1, source_target_pairs={{0,24},{8,16},{16,8},{24,0},{1,25},{9,17},{17,9},{25,1},{2,26},{10... | collective-permute-start | bytes 393224 | tf_op jit(solution)/shard_map/ppermute | solution.py:340
  126.9 3.2 %collective-permute-start.33 = (f32[1,256,128]{2,1,0:T(8,128)S(1)}, f32[1,256,128]{2,1,0:T(8,128)S(1)}, u32[]{:S(2)}, u32[]{:S(2)}) collective-permute-start(f32[1,256,128]{2,1,0:T(8,128)S(1)} %fusion.1), channel_id=1, source_target_pairs={{0,2},{1,3},{2,0},{3,1},{4,6},{5,7},{6,4},{7,5},{8,10},{9,11},{10,... | collective-permute-start | bytes 393224 | tf_op jit(solution)/shard_map/ppermute | solution.py:264
  134.3 4.1 %collective-permute-start.21 = (f32[1,256,128]{2,1,0:T(8,128)S(1)}, f32[1,256,128]{2,1,0:T(8,128)S(1)}, u32[]{:S(2)}, u32[]{:S(2)}) collective-permute-start(f32[1,256,128]{2,1,0:T(8,128)S(1)} %add.94), channel_id=1, source_target_pairs={{0,1},{1,0},{2,3},{3,2},{4,5},{5,4},{6,7},{7,6},{8,9},{9,8},{10,11... | collective-permute-start | bytes 393224 | tf_op jit(solution)/shard_map/ppermute | solution.py:260
  140.2 3.2 %collective-permute-start.24 = (f32[1,256,128]{2,1,0:T(8,128)S(1)}, f32[1,256,128]{2,1,0:T(8,128)S(1)}, u32[]{:S(2)}, u32[]{:S(2)}) collective-permute-start(f32[1,256,128]{2,1,0:T(8,128)S(1)} %collective-permute-done.20), channel_id=1, source_target_pairs={{0,1},{1,0},{2,3},{3,2},{4,5},{5,4},{6,7},{7,6},{8,9},{9,8},{10,11... | collective-permute-start | bytes 393224 | tf_op jit(solution)/shard_map/ppermute | solution.py:260
  155.3 3.8 %attended.1 = bf16[128,4096]{1,0:T(8,128)(2,1)} custom-call(s32[11]{0:T(128)S(1)} %concatenate.3.info.refs_0_, f32[128,2048]{1,0:T(8,128)} %copy-done.9, bf16[128,4096]{1,0:T(8,128)(2,1)} %get-tuple-element.66.kept_ref), custom_call_target="tpu_custom_call", output_to_operand_aliasing={{}: (2, {})} | custom-call | tf_op jit(solution)/shard_map/attended/pallas_call | solution.py:410
  (121 shorter events, 48.3 us)
Async XLA Ops:
  8.3 26.7 %collective-permute-start = (f32[128,2048]{1,0:T(8,128)}, f32[128,2048]{1,0:T(8,128)S(1)}, u32[]{:S(2)}, u32[]{:S(2)}) collective-permute-start(f32[128,2048]{1,0:T(8,128)} %get-tuple-element.44), channel_id=1, source_target_pairs={{0,1},{1,0},{2,3},{3,2},{4,5},{5,4},{6,7},{7,6},{8,9},{9,8},{10,11... | collective-permute-start | bytes 3145736 | tf_op jit(solution)/shard_map/ppermute | solution.py:260
  8.4 26.7 %collective-permute-start.2 = (f32[128,2048]{1,0:T(8,128)}, f32[128,2048]{1,0:T(8,128)S(1)}, u32[]{:S(2)}, u32[]{:S(2)}) collective-permute-start(f32[128,2048]{1,0:T(8,128)} %get-tuple-element.45), channel_id=1, source_target_pairs={{0,1},{1,0},{2,3},{3,2},{4,5},{5,4},{6,7},{7,6},{8,9},{9,8},{10,11... | collective-permute-start | bytes 3145736 | tf_op jit(solution)/shard_map/ppermute | solution.py:260
  27.5 19.1 %collective-permute-start.6 = (f32[1024,128]{1,0:T(8,128)}, f32[1024,128]{1,0:T(8,128)S(1)}, u32[]{:S(2)}, u32[]{:S(2)}) collective-permute-start(f32[1024,128]{1,0:T(8,128)} %get-tuple-element.53), channel_id=1, source_target_pairs={{0,2},{1,3},{2,4},{3,5},{4,6},{5,7},{8,10},{9,11},{10,12},{11,13},... | collective-permute-start | bytes 1572872 | tf_op jit(solution)/shard_map/ppermute | solution.py:264
  30.8 20.1 %collective-permute-start.7 = (f32[1024,128]{1,0:T(8,128)}, f32[1024,128]{1,0:T(8,128)S(1)}, u32[]{:S(2)}, u32[]{:S(2)}) collective-permute-start(f32[1024,128]{1,0:T(8,128)} %get-tuple-element.58), channel_id=1, source_target_pairs={{0,4},{1,5},{8,12},{9,13},{16,20},{17,21},{24,28},{25,29}} | collective-permute-start | bytes 1572872 | tf_op jit(solution)/shard_map/ppermute | solution.py:264
  44.7 12.3 %collective-permute-start.10 = (f32[1024,128]{1,0:T(8,128)}, f32[1024,128]{1,0:T(8,128)S(1)}, u32[]{:S(2)}, u32[]{:S(2)}) collective-permute-start(f32[1024,128]{1,0:T(8,128)} %get-tuple-element.56), channel_id=1, source_target_pairs={{6,4},{7,5},{4,2},{5,3},{2,0},{3,1},{14,12},{15,13},{12,10},{13,11... | collective-permute-start | bytes 1572872 | tf_op jit(solution)/shard_map/ppermute | solution.py:264
  46.0 11.0 %collective-permute-start.11 = (f32[1024,128]{1,0:T(8,128)}, f32[1024,128]{1,0:T(8,128)S(1)}, u32[]{:S(2)}, u32[]{:S(2)}) collective-permute-start(f32[1024,128]{1,0:T(8,128)} %get-tuple-element.60), channel_id=1, source_target_pairs={{6,2},{7,3},{14,10},{15,11},{22,18},{23,19},{30,26},{31,27}} | collective-permute-start | bytes 1572872 | tf_op jit(solution)/shard_map/ppermute | solution.py:264
  51.9 10.2 %collective-permute-start.8 = (f32[1024,128]{1,0:T(8,128)}, f32[1024,128]{1,0:T(8,128)S(1)}, u32[]{:S(2)}, u32[]{:S(2)}) collective-permute-start(f32[1024,128]{1,0:T(8,128)} %select_select_fusion.1), channel_id=1, source_target_pairs={{0,2},{1,3},{2,4},{3,5},{4,6},{5,7},{8,10},{9,11},{10,12},{11,13},... | collective-permute-start | bytes 1572872 | tf_op jit(solution)/shard_map/ppermute | solution.py:264
  53.2 9.0 %collective-permute-start.9 = (f32[1024,128]{1,0:T(8,128)}, f32[1024,128]{1,0:T(8,128)S(1)}, u32[]{:S(2)}, u32[]{:S(2)}) collective-permute-start(f32[1024,128]{1,0:T(8,128)} %select_select_fusion.1), channel_id=1, source_target_pairs={{2,6},{3,7},{10,14},{11,15},{18,22},{19,23},{26,30},{27,31}} | collective-permute-start | bytes 1572872 | tf_op jit(solution)/shard_map/ppermute | solution.py:264
  59.5 52.2 %collective-permute-start.28 = (f32[1024,128]{1,0:T(8,128)}, f32[1024,128]{1,0:T(8,128)}, u32[]{:S(2)}, u32[]{:S(2)}) collective-permute-start(f32[1024,128]{1,0:T(8,128)} %select_select_fusion), channel_id=1, source_target_pairs={{6,4},{7,5},{4,2},{5,3},{2,0},{3,1},{14,12},{15,13},{12,10},{13,11... | collective-permute-start | bytes 1572872 | tf_op jit(solution)/shard_map/ppermute | solution.py:264
  60.8 50.9 %collective-permute-start.29 = (f32[1024,128]{1,0:T(8,128)}, f32[1024,128]{1,0:T(8,128)S(1)}, u32[]{:S(2)}, u32[]{:S(2)}) collective-permute-start(f32[1024,128]{1,0:T(8,128)} %select_select_fusion), channel_id=1, source_target_pairs={{4,0},{5,1},{12,8},{13,9},{20,16},{21,17},{28,24},{29,25}} | collective-permute-start | bytes 1572872 | tf_op jit(solution)/shard_map/ppermute | solution.py:264
  81.6 16.4 %collective-permute-start.14 = (f32[1,256,128]{2,1,0:T(8,128)S(1)}, f32[1,256,128]{2,1,0:T(8,128)S(1)}, u32[]{:S(2)}, u32[]{:S(2)}) collective-permute-start(f32[1,256,128]{2,1,0:T(8,128)S(1)} %get-tuple-element.82), channel_id=1, source_target_pairs={{0,16},{8,24},{16,0},{24,8},{1,17},{9,25},{17,1},{25,9},{2,18},{10... | collective-permute-start | bytes 393224 | tf_op jit(solution)/shard_map/ppermute | solution.py:340
  82.8 18.2 %collective-permute-start.15 = (f32[1,256,128]{2,1,0:T(8,128)S(1)}, f32[1,256,128]{2,1,0:T(8,128)S(1)}, u32[]{:S(2)}, u32[]{:S(2)}) collective-permute-start(f32[1,256,128]{2,1,0:T(8,128)S(1)} %get-tuple-element.81), channel_id=1, source_target_pairs={{0,24},{8,16},{16,8},{24,0},{1,25},{9,17},{17,9},{25,1},{2,26},{10... | collective-permute-start | bytes 393224 | tf_op jit(solution)/shard_map/ppermute | solution.py:340
  84.6 20.4 %collective-permute-start.25 = (f32[4,1,512]{2,1,0:T(1,128)S(1)}, f32[4,1,512]{2,1,0:T(1,128)S(1)}, u32[]{:S(2)}, u32[]{:S(2)}) collective-permute-start(f32[4,1,512]{2,1,0:T(1,128)S(1)} %copy-done.17), channel_id=1, source_target_pairs={{0,2},{1,3},{2,0},{3,1},{4,6},{5,7},{6,4},{7,5},{8,10},{9,11},{10,... | collective-permute-start | bytes 24584 | tf_op jit(solution)/shard_map/ppermute | solution.py:264
  98.0 13.7 %collective-permute-start.26 = (f32[4,1,512]{2,1,0:T(1,128)S(1)}, f32[4,1,512]{2,1,0:T(1,128)S(1)}, u32[]{:S(2)}, u32[]{:S(2)}) collective-permute-start(f32[4,1,512]{2,1,0:T(1,128)S(1)} %copy-done.17), channel_id=1, source_target_pairs={{0,4},{1,5},{2,6},{3,7},{4,0},{5,1},{6,2},{7,3},{8,12},{9,13},{10,... | collective-permute-start | bytes 24584 | tf_op jit(solution)/shard_map/ppermute | solution.py:264
  101.0 10.7 %collective-permute-start.27 = (f32[4,1,512]{2,1,0:T(1,128)S(1)}, f32[4,1,512]{2,1,0:T(1,128)S(1)}, u32[]{:S(2)}, u32[]{:S(2)}) collective-permute-start(f32[4,1,512]{2,1,0:T(1,128)S(1)} %copy-done.17), channel_id=1, source_target_pairs={{0,6},{1,7},{2,4},{3,5},{4,2},{5,3},{6,0},{7,1},{8,14},{9,15},{10,... | collective-permute-start | bytes 24584 | tf_op jit(solution)/shard_map/ppermute | solution.py:264
  105.0 49.4 %collective-permute-start.12 = (f32[128,2048]{1,0:T(8,128)S(1)}, f32[128,2048]{1,0:T(8,128)S(1)}, u32[]{:S(2)}, u32[]{:S(2)}) collective-permute-start(f32[128,2048]{1,0:T(8,128)S(1)} %copy-done.14), channel_id=1, source_target_pairs={{0,1},{1,0},{2,3},{3,2},{4,5},{5,4},{6,7},{7,6},{8,9},{9,8},{10,11... | collective-permute-start | bytes 3145736 | tf_op jit(solution)/shard_map/ppermute | solution.py:260
  111.7 11.1 %collective-permute-start.16 = (f32[1,256,128]{2,1,0:T(8,128)S(1)}, f32[1,256,128]{2,1,0:T(8,128)S(1)}, u32[]{:S(2)}, u32[]{:S(2)}) collective-permute-start(f32[1,256,128]{2,1,0:T(8,128)S(1)} %add_add_fusion), channel_id=1, source_target_pairs={{0,2},{1,3},{2,0},{3,1},{4,6},{5,7},{6,4},{7,5},{8,10},{9,11},{10,... | collective-permute-start | bytes 393224 | tf_op jit(solution)/shard_map/ppermute | solution.py:264
  122.8 7.3 %collective-permute-start.17 = (f32[1,256,128]{2,1,0:T(8,128)S(1)}, f32[1,256,128]{2,1,0:T(8,128)S(1)}, u32[]{:S(2)}, u32[]{:S(2)}) collective-permute-start(f32[1,256,128]{2,1,0:T(8,128)S(1)} %add.93), channel_id=1, source_target_pairs={{0,4},{1,5},{2,6},{3,7},{4,0},{5,1},{6,2},{7,3},{8,12},{9,13},{10,... | collective-permute-start | bytes 393224 | tf_op jit(solution)/shard_map/ppermute | solution.py:264
  131.5 8.7 %collective-permute-start.20 = (f32[1,256,128]{2,1,0:T(8,128)S(1)}, f32[1,256,128]{2,1,0:T(8,128)S(1)}, u32[]{:S(2)}, u32[]{:S(2)}) collective-permute-start(f32[1,256,128]{2,1,0:T(8,128)S(1)} %add.94), channel_id=1, source_target_pairs={{0,24},{8,16},{16,8},{24,0},{1,25},{9,17},{17,9},{25,1},{2,26},{10... | collective-permute-start | bytes 393224 | tf_op jit(solution)/shard_map/ppermute | solution.py:351
  134.3 9.2 %collective-permute-start.21 = (f32[1,256,128]{2,1,0:T(8,128)S(1)}, f32[1,256,128]{2,1,0:T(8,128)S(1)}, u32[]{:S(2)}, u32[]{:S(2)}) collective-permute-start(f32[1,256,128]{2,1,0:T(8,128)S(1)} %add.94), channel_id=1, source_target_pairs={{0,1},{1,0},{2,3},{3,2},{4,5},{5,4},{6,7},{7,6},{8,9},{9,8},{10,11... | collective-permute-start | bytes 393224 | tf_op jit(solution)/shard_map/ppermute | solution.py:260
  146.2 12.9 %collective-permute-start.38 = (f32[1,256,128]{2,1,0:T(8,128)S(1)}, f32[1,256,128]{2,1,0:T(8,128)S(1)}, u32[]{:S(2)}, u32[]{:S(2)}) collective-permute-start(f32[1,256,128]{2,1,0:T(8,128)S(1)} %add.101), channel_id=1, source_target_pairs={{0,1},{1,0},{2,3},{3,2},{4,5},{5,4},{6,7},{7,6},{8,9},{9,8},{10,11... | collective-permute-start | bytes 393224 | tf_op jit(solution)/shard_map/ppermute | solution.py:260
  148.7 10.5 %collective-permute-start.39 = (f32[1,256,128]{2,1,0:T(8,128)S(1)}, f32[1,256,128]{2,1,0:T(8,128)S(1)}, u32[]{:S(2)}, u32[]{:S(2)}) collective-permute-start(f32[1,256,128]{2,1,0:T(8,128)S(1)} %collective-permute-done.35), channel_id=1, source_target_pairs={{0,1},{1,0},{2,3},{3,2},{4,5},{5,4},{6,7},{7,6},{8,9},{9,8},{10,11... | collective-permute-start | bytes 393224 | tf_op jit(solution)/shard_map/ppermute | solution.py:260
  149.9 9.3 %collective-permute-start.40 = (f32[1,256,128]{2,1,0:T(8,128)S(1)}, f32[1,256,128]{2,1,0:T(8,128)S(1)}, u32[]{:S(2)}, u32[]{:S(2)}) collective-permute-start(f32[1,256,128]{2,1,0:T(8,128)S(1)} %collective-permute-done.36), channel_id=1, source_target_pairs={{0,1},{1,0},{2,3},{3,2},{4,5},{5,4},{6,7},{7,6},{8,9},{9,8},{10,11... | collective-permute-start | bytes 393224 | tf_op jit(solution)/shard_map/ppermute | solution.py:260
  152.0 7.2 %collective-permute-start.41 = (f32[1,256,128]{2,1,0:T(8,128)S(1)}, f32[1,256,128]{2,1,0:T(8,128)S(1)}, u32[]{:S(2)}, u32[]{:S(2)}) collective-permute-start(f32[1,256,128]{2,1,0:T(8,128)S(1)} %collective-permute-done.37), channel_id=1, source_target_pairs={{0,1},{1,0},{2,3},{3,2},{4,5},{5,4},{6,7},{7,6},{8,9},{9,8},{10,11... | collective-permute-start | bytes 393224 | tf_op jit(solution)/shard_map/ppermute | solution.py:260
  (36 other events, 234.3 us)

commit v5 on v4

--- a/solution.py
+++ b/solution.py
@@ -99,10 +99,13 @@
     return jnp.where(pl.program_id(0) < half, first, second)
 
 
-def pack_kernel(info, *refs):
+def pack_kernel(n, info, *refs):
     half = len(refs) // 2
     for x_ref, o_ref in zip(refs[:half], refs[half:]):
-        o_ref[...] = x_ref[...].astype(F32)
+        cols = x_ref.shape[1] // n
+        for i in range(n):
+            start = pl.multiple_of((info[n + i] % n) * cols, cols)
+            o_ref[:, i * cols : (i + 1) * cols] = x_ref[:, pl.ds(start, cols)].astype(F32)
 
 
 def key_kernel(
@@ -245,8 +248,11 @@
     out_ref[0] = mm(stack(*back), tokens_of(k_ref, kg_ref))
 
 
-def attended_kernel(info, x_ref, kept_ref, o_ref):
-    o_ref[...] = x_ref[...].astype(BF)
+def attended_kernel(n, info, x_ref, kept_ref, o_ref):
+    cols = o_ref.shape[1] // n
+    for i in range(n):
+        start = pl.multiple_of((info[n + i] % n) * cols, cols)
+        o_ref[:, pl.ds(start, cols)] = x_ref[:, i * cols : (i + 1) * cols].astype(BF)
 
 
 def out_kernel(info, *refs):
@@ -333,13 +339,15 @@
     return base
 
 
-def sum_all(mine, chips):
+def sum_all(mine, chips, *earlier):
     dp = lax.axis_size("dp")
     share = mine.shape[0] // dp
     got = [
         lax.ppermute(mine[k * share : (k + 1) * share], "dp", [(i, i ^ k) for i in range(dp)])
         for k in range(1, dp)
     ]
+    if earlier:
+        got = after(got, *earlier)
     total = mine[:share]
     for piece in got:
         total = total + piece
@@ -396,13 +404,13 @@
     def shape_of(*shape, dtype=F32):
         return jax.ShapeDtypeStruct((n,) + shape, dtype)
 
-    def call(name, body, in_specs, out_specs, out_shape, **options):
+    def call(name, body, in_specs, out_specs, out_shape, steps=n, **options):
         run = pl.pallas_call(
             body,
             name=name,
             out_shape=[pltpu.HBM(x.shape, x.dtype) for x in out_shape],
             grid_spec=pltpu.PrefetchScalarGridSpec(
-                num_scalar_prefetch=1, grid=(n,), in_specs=in_specs, out_specs=out_specs
+                num_scalar_prefetch=1, grid=(steps,), in_specs=in_specs, out_specs=out_specs
             ),
             compiler_params=pltpu.CompilerParams(vmem_limit_bytes=VMEM_LIMIT),
             **options,
@@ -431,21 +439,20 @@
 
         return spec((wide, dim), index)
 
+    def other_half(cols):
+        return spec((own, n * cols), lambda i, info: (0, info[n] // n))
+
     def pack(name, arrays, cols):
-        packed = call(
+        return call(
             name,
-            pack_kernel,
-            [other_cols(cols)] * len(arrays),
-            [got_cols(cols)] * len(arrays),
+            part_body(pack_kernel),
+            [other_half(cols)] * len(arrays),
+            [spec((own, n * cols), lambda i, info: (0, 0))] * len(arrays),
             [jax.ShapeDtypeStruct((own, n * cols), F32)] * len(arrays),
+            steps=1,
         )(*arrays)
-        return packed
-
-    packed_keys = pack("pack_keys", (keys, values), one)
-    packed_queries = pack("pack_queries", after((queries, cotangent), *packed_keys), four)
-    keys_got, values_got = [core_swap(x) for x in packed_keys]
-    queries_got, cotangent_got = [core_swap(x) for x in packed_queries]
-
+
+    keys_got, values_got = [core_swap(x) for x in pack("pack_keys", (keys, values), one)]
     key_probs, key_features, norm, a, b, near = call(
         "key_features",
         part_body(key_kernel),
@@ -453,6 +460,8 @@
         [flat_spec, flat_spec, row_spec, a_spec, b_spec, near_spec(1)],
         [flat, shape_of(wide, length, dtype=BF), row] + [half_state] * 3,
     )(keys, keys_got, values, values_got, key_map)
+    packed = pack("pack_queries", after((queries, cotangent), norm), four)
+    queries_got, cotangent_got = [core_swap(x) for x in packed]
     prefix_norm = scan_norms(norm, chip, chips, True)
     prefix = Scan(*after((a, b, near), prefix_norm), True)
     prefix.first()
@@ -489,7 +498,6 @@
             row,
         ],
     )(cotangent, cotangent_got, values, values_got, query_rows, weights, prefix_norm, *before)
-    suffix_norm = scan_norms(norm, chip, chips, False, *later)
     grad_spec, grad = per_head(group * width, dim), shape_of(group * width, dim)
     query_part, key_up = call(
         "query_grads",
@@ -503,6 +511,8 @@
         queries, queries_got, values, values_got, key_features, query_probs, scaled, norm_lanes,
         prefix_norm, *before,
     )
+    suffix_norm = scan_norms(norm, chip, chips, False, query_part)
+    query_part = after(query_part, suffix_norm)
     (key_part,) = call(
         "key_grads",
         part_body(key_grad_kernel),
@@ -512,15 +522,16 @@
     )(keys, keys_got, values, values_got, key_probs, key_up, suffix_norm, *later)
     (attended,) = call(
         "attended",
-        attended_kernel,
-        [got_cols(four), pl.BlockSpec(memory_space=pl.ANY)],
-        [other_cols(four)],
+        part_body(attended_kernel),
+        [spec((own, n * four), lambda i, info: (0, 0)), pl.BlockSpec(memory_space=pl.ANY)],
+        [other_half(four)],
         [jax.ShapeDtypeStruct((own, head_count * dim), BF)],
+        steps=1,
         input_output_aliases={2: 0},
-    )(core_swap(attended_got), attended)
-
-    def finish(name, mine):
-        pieces = sum_all(mine, chips)
+    )(core_swap(after(attended_got, *later)), attended)
+
+    def finish(name, mine, *earlier):
+        pieces = sum_all(mine, chips, *earlier)
         whole = pl.BlockSpec(memory_space=pltpu.VMEM)
         natural = pl.pallas_call(
             out_kernel,
@@ -532,8 +543,8 @@
         )(info, *pieces)
         return jnp.swapaxes(natural.reshape(head_count, width, dim), 1, 2)
 
-    query_grad = finish("query_out", query_part)
-    key_grad = finish("key_out", key_part)
+    query_grad = finish("query_out", query_part, key_part)
+    key_grad = finish("key_out", key_part, attended)
     return attended.reshape(1, own, head_count * dim), query_grad, key_grad
 
 

time: 162 us -> 150 us (0.926)
  waiting for transfers between devices: 20.9 us -> 13.5 us
  Pallas kernels: 51.1 us -> 47.8 us
  other arithmetic: 7.45 us -> 4.85 us
    ppermute x6, waiting for transfers between devices: 4.22 us -> 0.02 us  [sum_all(): lax.ppermute(mine[k * share:(k + 1) * share], 'dp', [(i, i ^ k) for i in...]
    ppermute x6, waiting for transfers between devices: 3.63 us -> 0.02 us  [sum_all(): lax.ppermute(total, 'dp', [(i, i ^ k) for i in range(dp)])]
    pallas_call x8, Pallas kernels: 48 us -> 44.7 us  [call(): run(info, *[pltpu.with_memory_space_constraint(x, pltpu.HBM) for x in arr...]
    ppermute x17, waiting for transfers between devices: 9.92 us -> 11.8 us  [chip_move(): lax.ppermute(x, 'ctx', [(2 * a + c, 2 * b + c) for a, b in pairs for c in...]
    select_n x2, other arithmetic: 3.52 us -> 1.67 us  [turn_around(): jnp.where(self.place == 1, a + self.near, jnp.where(self.place == 2, b +...]
    unnamed x36 -> x32, local copies, waits for them, and re-layouts: 4.06 us -> 3.98 us
  transfers between devices with their start and end apart: 42 -> 42, of which waited for: 14 -> 9; matrix products, arithmetic and copies ran while one was open for 6% -> 5% of each run, Pallas kernels for 26% -> 24%
where the time goes in v5:
time: 150 us; the launch traced here: 149 us
  starting transfers between devices  75.3 us (50%)
  Pallas kernels  47.8 us (32%)
  waiting for transfers between devices  13.5 us (9%)
  local copies, waits for them, and re-layouts  6.17 us (4%)
  other arithmetic  4.85 us (3%)
    pallas_call x8, Pallas kernels, call(): run(info, *[pltpu.with_memory_space_constraint(x, pltpu.HBM) for x in arr...  44.7 us
    ppermute x17, starting transfers between devices, chip_move(): lax.ppermute(x, 'ctx', [(2 * a + c, 2 * b + c) for a, b in pairs for c in...  42.4 us
    ppermute x13, starting transfers between devices, core_swap(): return lax.ppermute(x, 'ctx', [(i, i ^ 1) for i in range(size)])  21.1 us
    ppermute x17, waiting for transfers between devices, chip_move(): lax.ppermute(x, 'ctx', [(2 * a + c, 2 * b + c) for a, b in pairs for c in...  11.8 us
    ppermute x6, starting transfers between devices, sum_all(): lax.ppermute(total, 'dp', [(i, i ^ k) for i in range(dp)])  6.46 us
    ppermute x6, starting transfers between devices, sum_all(): lax.ppermute(mine[k * share:(k + 1) * share], 'dp', [(i, i ^ k) for i in...  5.43 us
    unnamed x32, local copies, waits for them, and re-layouts  3.98 us
    pallas_call x2, Pallas kernels, finish(): pl.pallas_call(out_kernel, name=name, out_shape=jax.ShapeDtypeStruct((sha...  3.17 us
  transfers between devices with their start and end apart: 42, of which 9 were waited for; matrix products, arithmetic and copies ran while one was open for 5% of the time, Pallas kernels for 24%

profile of v5, /device:TPU:1, one launch (start us, length us, event | category | flops | bytes accessed | tf_op | source)
XLA Modules:
  0.0 148.7 jit_solution(8045048311457458286)
XLA Ops:
  0.8 2.4 %pack_keys.1 = (f32[128,512]{1,0:T(8,128)}, f32[128,512]{1,0:T(8,128)}) custom-call(s32[11]{0:T(128)S(1)} %concatenate.3.refs_0_.info, bf16[128,1024]{1,0:T(8,128)(2,1)} %bitcast.59, bf16[128,1024]{1,0:T(8,128)(2,1)} %bitcast.54), custom_call_target="tpu_custom_call" | custom-call | tf_op jit(solution)/shard_map/pack_keys/pallas_call | solution.py:418
  5.9 5.7 %key_features.1 = (f32[4,512,256]{2,1,0:T(8,128)}, bf16[4,512,256]{2,1,0:T(8,128)(2,1)}, f32[4,1,512]{2,1,0:T(1,128)}, f32[1024,128]{1,0:T(8,128)}, f32[1024,128]{1,0:T(8,128)}, /*index=5*/f32[1024,128]{1,0:T(8,128)}) custom-call(s32[11]{0:T(128)S(1)} %concatenate.3.refs_0_.info, bf16[128,1024]{1,0:T(8,128)(2,1)} %bitcast.60, f32[128,512]{1,0:T(8,128)} %copy-done.10, ...), custom_call_target="tpu_custom_call" | custom-call | tf_op jit(solution)/shard_map/key_features/pallas_call | solution.py:418
  11.7 3.1 %pack_queries.1 = (f32[128,2048]{1,0:T(8,128)}, f32[128,2048]{1,0:T(8,128)}) custom-call(s32[11]{0:T(128)S(1)} %concatenate.3.refs_0_.info, bf16[128,4096]{1,0:T(8,128)(2,1)} %bitcast.51, bf16[128,4096]{1,0:T(8,128)(2,1)} %bitcast.48), custom_call_target="tpu_custom_call" | custom-call | tf_op jit(solution)/shard_map/pack_queries/pallas_call | solution.py:418
  15.3 2.4 %collective-permute-start.4 = (f32[4,1,512]{2,1,0:T(1,128)S(1)}, f32[4,1,512]{2,1,0:T(1,128)S(1)}, u32[]{:S(2)}, u32[]{:S(2)}) collective-permute-start(f32[4,1,512]{2,1,0:T(1,128)S(1)} %copy-done.14), channel_id=1, source_target_pairs={{0,2},{1,3},{2,0},{3,1},{4,6},{5,7},{6,4},{7,5},{8,10},{9,11},{10,... | collective-permute-start | bytes 24584 | tf_op jit(solution)/shard_map/ppermute | solution.py:270
  18.8 2.5 %collective-permute-start.5 = (f32[4,1,512]{2,1,0:T(1,128)S(1)}, f32[4,1,512]{2,1,0:T(1,128)S(1)}, u32[]{:S(2)}, u32[]{:S(2)}) collective-permute-start(f32[4,1,512]{2,1,0:T(1,128)S(1)} %add.82), channel_id=1, source_target_pairs={{0,4},{1,5},{2,6},{3,7},{4,0},{5,1},{6,2},{7,3},{8,12},{9,13},{10,... | collective-permute-start | bytes 24584 | tf_op jit(solution)/shard_map/ppermute | solution.py:270
  23.0 3.3 %collective-permute-start.6 = (f32[1024,128]{1,0:T(8,128)}, f32[1024,128]{1,0:T(8,128)S(1)}, u32[]{:S(2)}, u32[]{:S(2)}) collective-permute-start(f32[1024,128]{1,0:T(8,128)} %get-tuple-element.61), channel_id=1, source_target_pairs={{0,2},{1,3},{2,4},{3,5},{4,6},{5,7},{8,10},{9,11},{10,12},{11,13},... | collective-permute-start | bytes 1572872 | tf_op jit(solution)/shard_map/ppermute | solution.py:270
  26.3 4.2 %collective-permute-start.7 = (f32[1024,128]{1,0:T(8,128)}, f32[1024,128]{1,0:T(8,128)S(1)}, u32[]{:S(2)}, u32[]{:S(2)}) collective-permute-start(f32[1024,128]{1,0:T(8,128)} %get-tuple-element.66), channel_id=1, source_target_pairs={{0,4},{1,5},{8,12},{9,13},{16,20},{17,21},{24,28},{25,29}} | collective-permute-start | bytes 1572872 | tf_op jit(solution)/shard_map/ppermute | solution.py:270
  31.8 8.3 %query_features.1 = (f32[4,512,256]{2,1,0:T(8,128)}, bf16[4,4,256,128]{3,2,1,0:T(8,128)(2,1)}, bf16[4,4,256,256]{3,2,1,0:T(8,128)(2,1)}, f32[1024,128]{1,0:T(8,1...) custom-call(s32[11]{0:T(128)S(1)} %concatenate.3.refs_0_.info, bf16[128,4096]{1,0:T(8,128)(2,1)} %bitcast.52, ...), custom_call_target="tpu_custom_call" | custom-call | tf_op jit(solution)/shard_map/query_features/pallas_call | solution.py:418
  42.3 4.0 %collective-permute-done.7.refs_9_.refs_11_ = f32[1024,128]{1,0:T(8,128)S(1)} collective-permute-done((f32[1024,128]{1,0:T(8,128)}, f32[1024,128]{1,0:T(8,128)S(1)}, u32[]{:S(2)}, u32[]{:S(2)}) %collective-permute-start.7) | collective-permute-done | bytes 524320 | tf_op jit(solution)/shard_map/ppermute | solution.py:270
  50.0 2.6 %collective-permute-done.10.refs_8_ = f32[1024,128]{1,0:T(8,128)S(1)} collective-permute-done((f32[1024,128]{1,0:T(8,128)}, f32[1024,128]{1,0:T(8,128)S(1)}, u32[]{:S(2)}, u32[]{:S(2)}) %collective-permute-start.10) | collective-permute-done | bytes 524320 | tf_op jit(solution)/shard_map/ppermute | solution.py:270
  55.3 1.8 %collective-permute-done.8.refs_10_.refs_12_ = f32[1024,128]{1,0:T(8,128)S(1)} collective-permute-done((f32[1024,128]{1,0:T(8,128)S(1)}, f32[1024,128]{1,0:T(8,128)S(1)}, u32[]{:S(2)}, u32[]{:S(2)}) %collective-permute-start.8) | collective-permute-done | bytes 524320 | tf_op jit(solution)/shard_map/ppermute | solution.py:270
  58.1 7.6 %attend.1 = (bf16[128,4096]{1,0:T(8,128)(2,1)}, f32[128,2048]{1,0:T(8,128)}, bf16[4,4,256,128]{3,2,1,0:T(8,128)(2,1)}, bf16[4,4,256,128]{3,2,1,0:T(8,128)(2,1)}, f32[4,1,512]{2,1,0:T(1,128)}) custom-call(s32[11]{0:T(128)S(1)} %concatenate.3.refs_0_.info, bf16[128,4096]{1,0:T(8,128)(2,1)} %bitcast.50, f32[128,2048]{1,0:T(8,128)} %copy-done.4, ...), custom_call_target="tpu_custom_call" | custom-call | tf_op jit(solution)/shard_map/attend/pallas_call | solution.py:418
  65.8 14.4 %collective-permute-start.15 = (f32[4,1,512]{2,1,0:T(1,128)}, f32[4,1,512]{2,1,0:T(1,128)S(1)}, u32[]{:S(2)}, u32[]{:S(2)}) collective-permute-start(f32[4,1,512]{2,1,0:T(1,128)} %get-tuple-element.80), channel_id=1, source_target_pairs={{0,2},{1,3},{2,0},{3,1},{4,6},{5,7},{6,4},{7,5},{8,10},{9,11},{10,... | collective-permute-start | bytes 24584 | tf_op jit(solution)/shard_map/ppermute | solution.py:270
  80.2 3.1 %collective-permute-start.16 = (f32[4,1,512]{2,1,0:T(1,128)}, f32[4,1,512]{2,1,0:T(1,128)S(1)}, u32[]{:S(2)}, u32[]{:S(2)}) collective-permute-start(f32[4,1,512]{2,1,0:T(1,128)} %get-tuple-element.80), channel_id=1, source_target_pairs={{0,4},{1,5},{2,6},{3,7},{4,0},{5,1},{6,2},{7,3},{8,12},{9,13},{10,... | collective-permute-start | bytes 24584 | tf_op jit(solution)/shard_map/ppermute | solution.py:270
  83.3 8.4 %query_grads.1 = (f32[4,256,128]{2,1,0:T(8,128)}, f32[4,512,256]{2,1,0:T(8,128)}) custom-call(s32[11]{0:T(128)S(1)} %concatenate.3.refs_0_.info, bf16[128,4096]{1,0:T(8,128)(2,1)} %bitcast.53, f32[128,2048]{1,0:T(8,128)} %copy-done.3, bf16[128,1024]{1,0:T(8,128)(2,1)} %bitcast.57, f32[128,512]{1,0:T(8,128)} %copy-done.2, ...), custom_call_target="tpu_custom_call" | custom-call | tf_op jit(solution)/shard_map/query_grads/pallas_call | solution.py:418
  91.8 5.4 %collective-permute-start.14 = (f32[128,2048]{1,0:T(8,128)S(1)}, f32[128,2048]{1,0:T(8,128)S(1)}, u32[]{:S(2)}, u32[]{:S(2)}) collective-permute-start(f32[128,2048]{1,0:T(8,128)S(1)} %copy-done.15), channel_id=1, source_target_pairs={{0,1},{1,0},{2,3},{3,2},{4,5},{5,4},{6,7},{7,6},{8,9},{9,8},{10,11... | collective-permute-start | bytes 3145736 | tf_op jit(solution)/shard_map/ppermute | solution.py:266
  101.7 6.5 %key_grads.1 = f32[4,256,128]{2,1,0:T(8,128)} custom-call(s32[11]{0:T(128)S(1)} %concatenate.3.refs_0_.info, bf16[128,1024]{1,0:T(8,128)(2,1)} %bitcast.61, f32[128,512]{1,0:T(8,128)} %copy-done.10, bf16[128,1024]{1,0:T(8,128)(2,1)} %bitcast.58, f32[128,512]{1,0:T(8,128)} %copy-done.2, f32[4,512,256]{2,1,0:T(8,128)} %get-tuple-element.85.refs_5_, ...), custom_call_target="tpu_custom_call" | custom-call | tf_op jit(solution)/shard_map/key_grads/pallas_call | solution.py:418
  113.2 3.6 %collective-permute-start.22 = (f32[1,256,128]{2,1,0:T(8,128)S(1)}, f32[1,256,128]{2,1,0:T(8,128)S(1)}, u32[]{:S(2)}, u32[]{:S(2)}) collective-permute-start(f32[1,256,128]{2,1,0:T(8,128)S(1)} %add.95), channel_id=1, source_target_pairs={{0,4},{1,5},{2,6},{3,7},{4,0},{5,1},{6,2},{7,3},{8,12},{9,13},{10,... | collective-permute-start | bytes 393224 | tf_op jit(solution)/shard_map/ppermute | solution.py:270
  117.8 2.6 %attended.1 = bf16[128,4096]{1,0:T(8,128)(2,1)} custom-call(s32[11]{0:T(128)S(1)} %concatenate.3.refs_0_.info, f32[128,2048]{1,0:T(8,128)} %copy-done.9, bf16[128,4096]{1,0:T(8,128)(2,1)} %get-tuple-element.75.refs_2_), custom_call_target="tpu_custom_call", output_to_operand_aliasing={{}: (2, {})} | custom-call | tf_op jit(solution)/shard_map/attended/pallas_call | solution.py:418
  127.6 4.4 %collective-permute-start.26 = (f32[1,256,128]{2,1,0:T(8,128)S(1)}, f32[1,256,128]{2,1,0:T(8,128)S(1)}, u32[]{:S(2)}, u32[]{:S(2)}) collective-permute-start(f32[1,256,128]{2,1,0:T(8,128)S(1)} %add.96), channel_id=1, source_target_pairs={{0,1},{1,0},{2,3},{3,2},{4,5},{5,4},{6,7},{7,6},{8,9},{9,8},{10,11... | collective-permute-start | bytes 393224 | tf_op jit(solution)/shard_map/ppermute | solution.py:266
  132.5 2.0 %collective-permute-start.35 = (f32[1,256,128]{2,1,0:T(8,128)S(1)}, f32[1,256,128]{2,1,0:T(8,128)S(1)}, u32[]{:S(2)}, u32[]{:S(2)}) collective-permute-start(f32[1,256,128]{2,1,0:T(8,128)S(1)} %add.101), channel_id=1, source_target_pairs={{0,8},{8,0},{16,24},{24,16},{1,9},{9,1},{17,25},{25,17},{2,10},{10... | collective-permute-start | bytes 393224 | tf_op jit(solution)/shard_map/ppermute | solution.py:359
  135.8 3.9 %collective-permute-start.29 = (f32[1,256,128]{2,1,0:T(8,128)S(1)}, f32[1,256,128]{2,1,0:T(8,128)S(1)}, u32[]{:S(2)}, u32[]{:S(2)}) collective-permute-start(f32[1,256,128]{2,1,0:T(8,128)S(1)} %collective-permute-done.25), channel_id=1, source_target_pairs={{0,1},{1,0},{2,3},{3,2},{4,5},{5,4},{6,7},{7,6},{8,9},{9,8},{10,11... | collective-permute-start | bytes 393224 | tf_op jit(solution)/shard_map/ppermute | solution.py:266
  139.8 1.8 %collective-permute-start.39 = (f32[1,256,128]{2,1,0:T(8,128)S(1)}, f32[1,256,128]{2,1,0:T(8,128)S(1)}, u32[]{:S(2)}, u32[]{:S(2)}) collective-permute-start(f32[1,256,128]{2,1,0:T(8,128)S(1)} %collective-permute-done.35), channel_id=1, source_target_pairs={{0,1},{1,0},{2,3},{3,2},{4,5},{5,4},{6,7},{7,6},{8,9},{9,8},{10,11... | collective-permute-start | bytes 393224 | tf_op jit(solution)/shard_map/ppermute | solution.py:266
  141.6 2.2 %collective-permute-start.40 = (f32[1,256,128]{2,1,0:T(8,128)S(1)}, f32[1,256,128]{2,1,0:T(8,128)S(1)}, u32[]{:S(2)}, u32[]{:S(2)}) collective-permute-start(f32[1,256,128]{2,1,0:T(8,128)S(1)} %collective-permute-done.36), channel_id=1, source_target_pairs={{0,1},{1,0},{2,3},{3,2},{4,5},{5,4},{6,7},{7,6},{8,9},{9,8},{10,11... | collective-permute-start | bytes 393224 | tf_op jit(solution)/shard_map/ppermute | solution.py:266
  (117 shorter events, 41.2 us)
Async XLA Ops:
  14.8 15.7 %collective-permute-start.2 = (f32[128,2048]{1,0:T(8,128)}, f32[128,2048]{1,0:T(8,128)S(1)}, u32[]{:S(2)}, u32[]{:S(2)}) collective-permute-start(f32[128,2048]{1,0:T(8,128)} %get-tuple-element.53), channel_id=1, source_target_pairs={{0,1},{1,0},{2,3},{3,2},{4,5},{5,4},{6,7},{7,6},{8,9},{9,8},{10,11... | collective-permute-start | bytes 3145736 | tf_op jit(solution)/shard_map/ppermute | solution.py:266
  15.0 15.6 %collective-permute-start.3 = (f32[128,2048]{1,0:T(8,128)}, f32[128,2048]{1,0:T(8,128)S(1)}, u32[]{:S(2)}, u32[]{:S(2)}) collective-permute-start(f32[128,2048]{1,0:T(8,128)} %get-tuple-element.54), channel_id=1, source_target_pairs={{0,1},{1,0},{2,3},{3,2},{4,5},{5,4},{6,7},{7,6},{8,9},{9,8},{10,11... | collective-permute-start | bytes 3145736 | tf_op jit(solution)/shard_map/ppermute | solution.py:266
  23.0 19.3 %collective-permute-start.6 = (f32[1024,128]{1,0:T(8,128)}, f32[1024,128]{1,0:T(8,128)S(1)}, u32[]{:S(2)}, u32[]{:S(2)}) collective-permute-start(f32[1024,128]{1,0:T(8,128)} %get-tuple-element.61), channel_id=1, source_target_pairs={{0,2},{1,3},{2,4},{3,5},{4,6},{5,7},{8,10},{9,11},{10,12},{11,13},... | collective-permute-start | bytes 1572872 | tf_op jit(solution)/shard_map/ppermute | solution.py:270
  26.3 20.1 %collective-permute-start.7 = (f32[1024,128]{1,0:T(8,128)}, f32[1024,128]{1,0:T(8,128)S(1)}, u32[]{:S(2)}, u32[]{:S(2)}) collective-permute-start(f32[1024,128]{1,0:T(8,128)} %get-tuple-element.66), channel_id=1, source_target_pairs={{0,4},{1,5},{8,12},{9,13},{16,20},{17,21},{24,28},{25,29}} | collective-permute-start | bytes 1572872 | tf_op jit(solution)/shard_map/ppermute | solution.py:270
  40.2 12.4 %collective-permute-start.10 = (f32[1024,128]{1,0:T(8,128)}, f32[1024,128]{1,0:T(8,128)S(1)}, u32[]{:S(2)}, u32[]{:S(2)}) collective-permute-start(f32[1024,128]{1,0:T(8,128)} %get-tuple-element.64), channel_id=1, source_target_pairs={{6,4},{7,5},{4,2},{5,3},{2,0},{3,1},{14,12},{15,13},{12,10},{13,11... | collective-permute-start | bytes 1572872 | tf_op jit(solution)/shard_map/ppermute | solution.py:270
  41.6 11.0 %collective-permute-start.11 = (f32[1024,128]{1,0:T(8,128)}, f32[1024,128]{1,0:T(8,128)S(1)}, u32[]{:S(2)}, u32[]{:S(2)}) collective-permute-start(f32[1024,128]{1,0:T(8,128)} %get-tuple-element.68), channel_id=1, source_target_pairs={{6,2},{7,3},{14,10},{15,11},{22,18},{23,19},{30,26},{31,27}} | collective-permute-start | bytes 1572872 | tf_op jit(solution)/shard_map/ppermute | solution.py:270
  48.0 9.2 %collective-permute-start.8 = (f32[1024,128]{1,0:T(8,128)S(1)}, f32[1024,128]{1,0:T(8,128)S(1)}, u32[]{:S(2)}, u32[]{:S(2)}) collective-permute-start(f32[1024,128]{1,0:T(8,128)S(1)} %select_select_fusion.1), channel_id=1, source_target_pairs={{0,2},{1,3},{2,4},{3,5},{4,6},{5,7},{8,10},{9,11},{10,12},{11,13},... | collective-permute-start | bytes 1572872 | tf_op jit(solution)/shard_map/ppermute | solution.py:270
  49.3 7.9 %collective-permute-start.9 = (f32[1024,128]{1,0:T(8,128)S(1)}, f32[1024,128]{1,0:T(8,128)S(1)}, u32[]{:S(2)}, u32[]{:S(2)}) collective-permute-start(f32[1024,128]{1,0:T(8,128)S(1)} %select_select_fusion.1), channel_id=1, source_target_pairs={{2,6},{3,7},{10,14},{11,15},{18,22},{19,23},{26,30},{27,31}} | collective-permute-start | bytes 1572872 | tf_op jit(solution)/shard_map/ppermute | solution.py:270
  52.7 39.1 %collective-permute-start.12 = (f32[1024,128]{1,0:T(8,128)S(1)}, f32[1024,128]{1,0:T(8,128)}, u32[]{:S(2)}, u32[]{:S(2)}) collective-permute-start(f32[1024,128]{1,0:T(8,128)S(1)} %select_select_fusion), channel_id=1, source_target_pairs={{6,4},{7,5},{4,2},{5,3},{2,0},{3,1},{14,12},{15,13},{12,10},{13,11... | collective-permute-start | bytes 1572872 | tf_op jit(solution)/shard_map/ppermute | solution.py:270
  54.0 37.8 %collective-permute-start.13 = (f32[1024,128]{1,0:T(8,128)S(1)}, f32[1024,128]{1,0:T(8,128)S(1)}, u32[]{:S(2)}, u32[]{:S(2)}) collective-permute-start(f32[1024,128]{1,0:T(8,128)S(1)} %select_select_fusion), channel_id=1, source_target_pairs={{4,0},{5,1},{12,8},{13,9},{20,16},{21,17},{28,24},{29,25}} | collective-permute-start | bytes 1572872 | tf_op jit(solution)/shard_map/ppermute | solution.py:270
  65.8 26.0 %collective-permute-start.15 = (f32[4,1,512]{2,1,0:T(1,128)}, f32[4,1,512]{2,1,0:T(1,128)S(1)}, u32[]{:S(2)}, u32[]{:S(2)}) collective-permute-start(f32[4,1,512]{2,1,0:T(1,128)} %get-tuple-element.80), channel_id=1, source_target_pairs={{0,2},{1,3},{2,0},{3,1},{4,6},{5,7},{6,4},{7,5},{8,10},{9,11},{10,... | collective-permute-start | bytes 24584 | tf_op jit(solution)/shard_map/ppermute | solution.py:270
  80.2 11.5 %collective-permute-start.16 = (f32[4,1,512]{2,1,0:T(1,128)}, f32[4,1,512]{2,1,0:T(1,128)S(1)}, u32[]{:S(2)}, u32[]{:S(2)}) collective-permute-start(f32[4,1,512]{2,1,0:T(1,128)} %get-tuple-element.80), channel_id=1, source_target_pairs={{0,4},{1,5},{2,6},{3,7},{4,0},{5,1},{6,2},{7,3},{8,12},{9,13},{10,... | collective-permute-start | bytes 24584 | tf_op jit(solution)/shard_map/ppermute | solution.py:270
  83.3 8.5 %collective-permute-start.17 = (f32[4,1,512]{2,1,0:T(1,128)}, f32[4,1,512]{2,1,0:T(1,128)S(1)}, u32[]{:S(2)}, u32[]{:S(2)}) collective-permute-start(f32[4,1,512]{2,1,0:T(1,128)} %get-tuple-element.80), channel_id=1, source_target_pairs={{0,6},{1,7},{2,4},{3,5},{4,2},{5,3},{6,0},{7,1},{8,14},{9,15},{10,... | collective-permute-start | bytes 24584 | tf_op jit(solution)/shard_map/ppermute | solution.py:270
  91.8 25.0 %collective-permute-start.14 = (f32[128,2048]{1,0:T(8,128)S(1)}, f32[128,2048]{1,0:T(8,128)S(1)}, u32[]{:S(2)}, u32[]{:S(2)}) collective-permute-start(f32[128,2048]{1,0:T(8,128)S(1)} %copy-done.15), channel_id=1, source_target_pairs={{0,1},{1,0},{2,3},{3,2},{4,5},{5,4},{6,7},{7,6},{8,9},{9,8},{10,11... | collective-permute-start | bytes 3145736 | tf_op jit(solution)/shard_map/ppermute | solution.py:266
  98.9 9.2 %collective-permute-start.18 = (f32[1,256,128]{2,1,0:T(8,128)S(1)}, f32[1,256,128]{2,1,0:T(8,128)S(1)}, u32[]{:S(2)}, u32[]{:S(2)}) collective-permute-start(f32[1,256,128]{2,1,0:T(8,128)S(1)} %get-tuple-element.98), channel_id=1, source_target_pairs={{0,8},{8,0},{16,24},{24,16},{1,9},{9,1},{17,25},{25,17},{2,10},{10... | collective-permute-start | bytes 393224 | tf_op jit(solution)/shard_map/ppermute | solution.py:346
  100.2 7.9 %collective-permute-start.19 = (f32[1,256,128]{2,1,0:T(8,128)S(1)}, f32[1,256,128]{2,1,0:T(8,128)S(1)}, u32[]{:S(2)}, u32[]{:S(2)}) collective-permute-start(f32[1,256,128]{2,1,0:T(8,128)S(1)} %get-tuple-element.97), channel_id=1, source_target_pairs={{0,16},{8,24},{16,0},{24,8},{1,17},{9,25},{17,1},{25,9},{2,18},{10... | collective-permute-start | bytes 393224 | tf_op jit(solution)/shard_map/ppermute | solution.py:346
  110.5 9.9 %collective-permute-start.30 = (f32[1,256,128]{2,1,0:T(8,128)S(1)}, f32[1,256,128]{2,1,0:T(8,128)S(1)}, u32[]{:S(2)}, u32[]{:S(2)}) collective-permute-start(f32[1,256,128]{2,1,0:T(8,128)S(1)} %get-tuple-element.95), channel_id=1, source_target_pairs={{0,8},{8,0},{16,24},{24,16},{1,9},{9,1},{17,25},{25,17},{2,10},{10... | collective-permute-start | bytes 393224 | tf_op jit(solution)/shard_map/ppermute | solution.py:346
  111.8 8.7 %collective-permute-start.31 = (f32[1,256,128]{2,1,0:T(8,128)S(1)}, f32[1,256,128]{2,1,0:T(8,128)S(1)}, u32[]{:S(2)}, u32[]{:S(2)}) collective-permute-start(f32[1,256,128]{2,1,0:T(8,128)S(1)} %get-tuple-element.94), channel_id=1, source_target_pairs={{0,16},{8,24},{16,0},{24,8},{1,17},{9,25},{17,1},{25,9},{2,18},{10... | collective-permute-start | bytes 393224 | tf_op jit(solution)/shard_map/ppermute | solution.py:346
  113.2 9.1 %collective-permute-start.22 = (f32[1,256,128]{2,1,0:T(8,128)S(1)}, f32[1,256,128]{2,1,0:T(8,128)S(1)}, u32[]{:S(2)}, u32[]{:S(2)}) collective-permute-start(f32[1,256,128]{2,1,0:T(8,128)S(1)} %add.95), channel_id=1, source_target_pairs={{0,4},{1,5},{2,6},{3,7},{4,0},{5,1},{6,2},{7,3},{8,12},{9,13},{10,... | collective-permute-start | bytes 393224 | tf_op jit(solution)/shard_map/ppermute | solution.py:270
  122.4 9.6 %collective-permute-start.23 = (f32[1,256,128]{2,1,0:T(8,128)S(1)}, f32[1,256,128]{2,1,0:T(8,128)S(1)}, u32[]{:S(2)}, u32[]{:S(2)}) collective-permute-start(f32[1,256,128]{2,1,0:T(8,128)S(1)} %add.96), channel_id=1, source_target_pairs={{0,8},{8,0},{16,24},{24,16},{1,9},{9,1},{17,25},{25,17},{2,10},{10... | collective-permute-start | bytes 393224 | tf_op jit(solution)/shard_map/ppermute | solution.py:359
  123.6 8.4 %collective-permute-start.24 = (f32[1,256,128]{2,1,0:T(8,128)S(1)}, f32[1,256,128]{2,1,0:T(8,128)S(1)}, u32[]{:S(2)}, u32[]{:S(2)}) collective-permute-start(f32[1,256,128]{2,1,0:T(8,128)S(1)} %add.96), channel_id=1, source_target_pairs={{0,16},{8,24},{16,0},{24,8},{1,17},{9,25},{17,1},{25,9},{2,18},{10... | collective-permute-start | bytes 393224 | tf_op jit(solution)/shard_map/ppermute | solution.py:359
  127.6 7.9 %collective-permute-start.26 = (f32[1,256,128]{2,1,0:T(8,128)S(1)}, f32[1,256,128]{2,1,0:T(8,128)S(1)}, u32[]{:S(2)}, u32[]{:S(2)}) collective-permute-start(f32[1,256,128]{2,1,0:T(8,128)S(1)} %add.96), channel_id=1, source_target_pairs={{0,1},{1,0},{2,3},{3,2},{4,5},{5,4},{6,7},{7,6},{8,9},{9,8},{10,11... | collective-permute-start | bytes 393224 | tf_op jit(solution)/shard_map/ppermute | solution.py:266
  135.5 8.3 %collective-permute-start.37 = (f32[1,256,128]{2,1,0:T(8,128)S(1)}, f32[1,256,128]{2,1,0:T(8,128)S(1)}, u32[]{:S(2)}, u32[]{:S(2)}) collective-permute-start(f32[1,256,128]{2,1,0:T(8,128)S(1)} %add.101), channel_id=1, source_target_pairs={{0,24},{8,16},{16,8},{24,0},{1,25},{9,17},{17,9},{25,1},{2,26},{10... | collective-permute-start | bytes 393224 | tf_op jit(solution)/shard_map/ppermute | solution.py:359
  135.8 9.7 %collective-permute-start.29 = (f32[1,256,128]{2,1,0:T(8,128)S(1)}, f32[1,256,128]{2,1,0:T(8,128)S(1)}, u32[]{:S(2)}, u32[]{:S(2)}) collective-permute-start(f32[1,256,128]{2,1,0:T(8,128)S(1)} %collective-permute-done.25), channel_id=1, source_target_pairs={{0,1},{1,0},{2,3},{3,2},{4,5},{5,4},{6,7},{7,6},{8,9},{9,8},{10,11... | collective-permute-start | bytes 393224 | tf_op jit(solution)/shard_map/ppermute | solution.py:266
  (34 other events, 191.5 us)

commit v6 on v5

--- a/solution.py
+++ b/solution.py
@@ -7,7 +7,7 @@
 
 BF = jnp.bfloat16
 F32 = jnp.float32
-VMEM_LIMIT = 32 * 1024 * 1024
+VMEM_LIMIT = 40 * 1024 * 1024
 
 
 def mm(a, b):
@@ -77,55 +77,36 @@
     return stack(own_ref[...], got_ref[...].astype(BF))
 
 
-def put_parts(place, half, n, value, a_ref, b_ref, near_ref):
-    i = pl.program_id(0)
-
-    @pl.when(i < half)
-    def _():
-        a_ref[...] = value
-
-    @pl.when(i >= half)
-    def _():
-        b_ref[...] = value
-
-    @pl.when((i >= half) == (place == 1))
-    def _():
-        near_ref[...] = value
-
-
-def before_of(place, half, near, far, near2, far2):
-    first = jnp.where(place == 2, near2[...], near[...] + far2[...])
-    second = jnp.where(place == 2, near[...] + far[...], near2[...])
-    return jnp.where(pl.program_id(0) < half, first, second)
-
-
-def pack_kernel(n, info, *refs):
+def before_of(place, first, near, far, near2, far2):
+    if first:
+        return jnp.where(place == 2, near2[...], near[...] + far2[...])
+    return jnp.where(place == 2, near[...] + far[...], near2[...])
+
+
+def pack_kernel(n, i, info, *refs):
     half = len(refs) // 2
     for x_ref, o_ref in zip(refs[:half], refs[half:]):
-        cols = x_ref.shape[1] // n
-        for i in range(n):
-            start = pl.multiple_of((info[n + i] % n) * cols, cols)
-            o_ref[:, i * cols : (i + 1) * cols] = x_ref[:, pl.ds(start, cols)].astype(F32)
+        o_ref[...] = x_ref[...].astype(F32)
 
 
 def key_kernel(
-    n, info, k_ref, kg_ref, v_ref, vg_ref, w_ref, kp_ref, kb_ref, norm_ref, a_ref, b_ref, near_ref
+    n, i, info, k_ref, kg_ref, v_ref, vg_ref, w_ref, kp_ref, kb_ref, norm_ref, state_ref
 ):
     group, width, dim = w_ref.shape
     keys = tokens_of(k_ref, kg_ref)
     values = tokens_of(v_ref, vg_ref)
     scores = mm_nt(w_ref[...].reshape(group * width, dim), keys)
-    probs = stack(*[both_soft(scores[i * width : (i + 1) * width]) for i in range(group)])
+    probs = stack(*[both_soft(scores[a : a + width]) for a in range(0, group * width, width)])
     features = probs.astype(BF)
     kp_ref[0] = probs
     kb_ref[0] = features
     norm_ref[0] = mm_nt(jnp.ones((16, keys.shape[0]), BF), features)[:1]
-    put_parts(info[2 * n + 1], n // 2, n, mm(features, values), a_ref, b_ref, near_ref)
+    state_ref[...] = mm(features, values)
 
 
 def query_kernel(
-    n, info, q_ref, qg_ref, c_ref, cg_ref, w_ref, kb_ref, pn_ref,
-    qp_ref, qr_ref, wt_ref, a_ref, b_ref, near_ref,
+    n, step, info, q_ref, qg_ref, c_ref, cg_ref, w_ref, kb_ref, pn_ref,
+    qp_ref, qr_ref, wt_ref, state_ref,
 ):
     group, width, dim = w_ref.shape
     feats = 2 * width
@@ -157,11 +138,11 @@
         qp_ref[0, rows[i]] = probs[i]
         qr_ref[0, i] = query_rows[i]
         wt_ref[0, i] = weights[i]
-    put_parts(info[2 * n + 2], n // 2, n, stack(*sums), a_ref, b_ref, near_ref)
+    state_ref[...] = stack(*sums)
 
 
 def attend_kernel(
-    n, info, c_ref, cg_ref, v_ref, vg_ref, qr_ref, wt_ref, pn_ref, near, far, near2, far2,
+    n, step, info, c_ref, cg_ref, v_ref, vg_ref, qr_ref, wt_ref, pn_ref, near, far, near2, far2,
     att_ref, atg_ref, sc_ref, nl_ref, sn_ref,
 ):
     group, length, dim = qr_ref.shape[1:]
@@ -172,7 +153,7 @@
     rows = [slice(i * feats, (i + 1) * feats) for i in heads]
     upstream = stack(c_ref[...].astype(F32), cg_ref[...])
     values = tokens_of(v_ref, vg_ref)
-    high, low = split(before_of(info[2 * n + 1], n // 2, near, far, near2, far2))
+    high, low = split(before_of(info[2 * n + 1], step < n // 2, near, far, near2, far2))
     norm_high, norm_low = split(jnp.broadcast_to(column(pn_ref[0]), (group * feats, dim)))
     high, low = cat(high, norm_high), cat(low, norm_low)
     values = cat(values, jnp.ones((length, dim), BF))
@@ -199,7 +180,7 @@
 
 
 def query_grad_kernel(
-    n, info, q_ref, qg_ref, v_ref, vg_ref, kb_ref, qp_ref, sc_ref, nl_ref, pn_ref,
+    n, step, info, q_ref, qg_ref, v_ref, vg_ref, kb_ref, qp_ref, sc_ref, nl_ref, pn_ref,
     near, far, near2, far2, gq_ref, gk_ref,
 ):
     group, length, dim = sc_ref.shape[1:]
@@ -212,7 +193,7 @@
     queries = tokens_of(q_ref, qg_ref)
     lane = lax.broadcasted_iota(jnp.int32, (length, dim), 1)
     values = cat(tokens_of(v_ref, vg_ref), jnp.where(lane < 2, 1.0, 0.0).astype(BF))
-    high, low = split(before_of(info[2 * n + 1], n // 2, near, far, near2, far2))
+    high, low = split(before_of(info[2 * n + 1], step < n // 2, near, far, near2, far2))
     norm_cols = three_lanes(jnp.broadcast_to(column(pn_ref[0]), (group * feats, dim)), "hhl")
     scaled = [sc_ref[0, i] for i in heads]
     lanes = [nl_ref[0, i] for i in heads]
@@ -233,12 +214,12 @@
 
 
 def key_grad_kernel(
-    n, info, k_ref, kg_ref, v_ref, vg_ref, kp_ref, gk_ref, sn_ref, near, far, near2, far2, out_ref
+    n, step, info, k_ref, kg_ref, v_ref, vg_ref, kp_ref, gk_ref, sn_ref, near, far, near2, far2, out_ref
 ):
     rows, length = kp_ref.shape[1:]
     feats = k_ref.shape[1]
     values = tokens_of(v_ref, vg_ref)
-    state = cat(*split(before_of(info[2 * n + 2], n // 2, near, far, near2, far2)))
+    state = cat(*split(before_of(info[2 * n + 2], step < n // 2, near, far, near2, far2)))
     upstream = gk_ref[0] + mm_nt(state, cat(values, values))
     upstream = upstream + jnp.broadcast_to(column(sn_ref[0]), (rows, length))
     back = [
@@ -248,11 +229,8 @@
     out_ref[0] = mm(stack(*back), tokens_of(k_ref, kg_ref))
 
 
-def attended_kernel(n, info, x_ref, kept_ref, o_ref):
-    cols = o_ref.shape[1] // n
-    for i in range(n):
-        start = pl.multiple_of((info[n + i] % n) * cols, cols)
-        o_ref[:, pl.ds(start, cols)] = x_ref[:, i * cols : (i + 1) * cols].astype(BF)
+def attended_kernel(n, i, info, x_ref, o_ref):
+    o_ref[...] = x_ref[...].astype(BF)
 
 
 def out_kernel(info, *refs):
@@ -404,23 +382,91 @@
     def shape_of(*shape, dtype=F32):
         return jax.ShapeDtypeStruct((n,) + shape, dtype)
 
-    def call(name, body, in_specs, out_specs, out_shape, steps=n, **options):
-        run = pl.pallas_call(
-            body,
-            name=name,
-            out_shape=[pltpu.HBM(x.shape, x.dtype) for x in out_shape],
-            grid_spec=pltpu.PrefetchScalarGridSpec(
-                num_scalar_prefetch=1, grid=(steps,), in_specs=in_specs, out_specs=out_specs
-            ),
-            compiler_params=pltpu.CompilerParams(vmem_limit_bytes=VMEM_LIMIT),
-            **options,
-        )
-        return lambda *arrays: run(
-            info, *[pltpu.with_memory_space_constraint(x, pltpu.HBM) for x in arrays]
-        )
-
-    def part_body(body):
-        return lambda *refs: body(n, *refs)
+    def block(ref, spec, i, info):
+        places = spec.index_map(i, info)
+        return ref.at[
+            tuple(
+                pl.ds(p * size if isinstance(p, int) else pl.multiple_of(p * size, size), size)
+                for p, size in zip(places, spec.block_shape)
+            )
+        ]
+
+    def call(name, body, in_specs, out_specs, out_shape, aliases=None):
+        in_specs = [x if isinstance(x, tuple) else (x, n) for x in in_specs]
+        kinds = [x.dtype for x in out_shape]
+        results = {}
+        for (spec_, which, _), kind in zip(out_specs, kinds):
+            results[which] = (spec_.block_shape, kind)
+        results = [results[k] for k in range(len(results))]
+        extra = len(aliases or {})
+
+        def kernel(info, *refs):
+            count = len(in_specs) + extra
+            ins, outs = refs[: len(in_specs)], refs[count : count + len(out_specs)]
+            rest = refs[count + len(out_specs) :]
+            in_bufs, out_bufs = rest[: len(in_specs)], rest[len(in_specs) : -2]
+            in_sem, out_sem = rest[-2:]
+
+            def incoming(i):
+                return [
+                    pltpu.make_async_copy(block(ref, spec_, i, info), buf.at[i], in_sem.at[k, i])
+                    for k, ((spec_, period), ref, buf) in enumerate(zip(in_specs, ins, in_bufs))
+                    if i < period
+                ]
+
+            def outgoing(i, act):
+                for k, ((spec_, which, when), ref) in enumerate(zip(out_specs, outs)):
+                    here = when(i, info)
+                    if here is False:
+                        continue
+                    copy = pltpu.make_async_copy(
+                        out_bufs[which].at[i], block(ref, spec_, i, info), out_sem.at[k, i]
+                    )
+                    if here is True:
+                        act(copy)
+                    else:
+                        pl.when(here)(lambda copy=copy: act(copy))
+
+            for i in range(n):
+                for copy in incoming(i):
+                    copy.start()
+            for i in range(n):
+                for copy in incoming(i):
+                    copy.wait()
+                blocks = [buf.at[i % period] for (_, period), buf in zip(in_specs, in_bufs)]
+                body(n, i, info, *blocks, *[buf.at[i] for buf in out_bufs])
+                outgoing(i, lambda copy: copy.start())
+            for i in range(n):
+                outgoing(i, lambda copy: copy.wait())
+
+        def run(*arrays):
+            anywhere = pl.BlockSpec(memory_space=pl.ANY)
+            buffers = [
+                pltpu.VMEM((period,) + tuple(x.block_shape), y.dtype)
+                for (x, period), y in zip(in_specs, arrays)
+            ] + [pltpu.VMEM((n,) + tuple(shape), kind) for shape, kind in results]
+            return pl.pallas_call(
+                kernel,
+                name=name,
+                out_shape=[pltpu.HBM(x.shape, x.dtype) for x in out_shape],
+                in_specs=[pl.BlockSpec(memory_space=pltpu.SMEM)] + [anywhere] * len(arrays),
+                out_specs=[anywhere] * len(out_shape),
+                scratch_shapes=buffers
+                + [
+                    pltpu.SemaphoreType.DMA((len(in_specs), n)),
+                    pltpu.SemaphoreType.DMA((len(out_specs), n)),
+                ],
+                input_output_aliases=aliases or {},
+                compiler_params=pltpu.CompilerParams(vmem_limit_bytes=VMEM_LIMIT),
+            )(info, *[pltpu.with_memory_space_constraint(x, pltpu.HBM) for x in arrays])
+
+        return run
+
+    def always(i, info):
+        return True
+
+    def each(*specs):
+        return [(x, k, always) for k, x in enumerate(specs)]
 
     one, four = dim, group * dim
     map_spec = spec((group, width, dim), lambda i, info: (info[i], 0, 0))
@@ -428,36 +474,31 @@
     flat_spec, flat = per_head(wide, length), shape_of(wide, length)
     half = n // 2
     half_state = jax.ShapeDtypeStruct((half * wide, dim), F32)
-    a_spec = spec((wide, dim), lambda i, info: (jnp.minimum(i, half - 1), 0))
-    b_spec = spec((wide, dim), lambda i, info: (jnp.maximum(i - half, 0), 0))
-    moved_spec = spec((wide, dim), lambda i, info: (i % half, 0))
-
-    def near_spec(which):
-        def index(i, info):
-            off = jnp.where(info[2 * n + which] == 1, half, 0)
-            return (jnp.clip(i - off, 0, half - 1), 0)
-
-        return spec((wide, dim), index)
-
-    def other_half(cols):
-        return spec((own, n * cols), lambda i, info: (0, info[n] // n))
+    moved_spec = (spec((wide, dim), lambda i, info: (i, 0)), half)
+    half_spec = spec((wide, dim), lambda i, info: (i % half, 0))
+
+    def states(which, place):
+        return [
+            (half_spec, which, lambda i, info: i < half),
+            (half_spec, which, lambda i, info: i >= half),
+            (half_spec, which, lambda i, info: (info[2 * n + place] == 1) == (i >= half)),
+        ]
 
     def pack(name, arrays, cols):
         return call(
             name,
-            part_body(pack_kernel),
-            [other_half(cols)] * len(arrays),
-            [spec((own, n * cols), lambda i, info: (0, 0))] * len(arrays),
+            pack_kernel,
+            [other_cols(cols)] * len(arrays),
+            each(*[got_cols(cols)] * len(arrays)),
             [jax.ShapeDtypeStruct((own, n * cols), F32)] * len(arrays),
-            steps=1,
         )(*arrays)
 
     keys_got, values_got = [core_swap(x) for x in pack("pack_keys", (keys, values), one)]
     key_probs, key_features, norm, a, b, near = call(
         "key_features",
-        part_body(key_kernel),
+        key_kernel,
         [own_cols(one), got_cols(one)] * 2 + [map_spec],
-        [flat_spec, flat_spec, row_spec, a_spec, b_spec, near_spec(1)],
+        each(flat_spec, flat_spec, row_spec) + states(3, 1),
         [flat, shape_of(wide, length, dtype=BF), row] + [half_state] * 3,
     )(keys, keys_got, values, values_got, key_map)
     packed = pack("pack_queries", after((queries, cotangent), norm), four)
@@ -470,9 +511,9 @@
     rows_bf = shape_of(group, length, dim, dtype=BF)
     query_probs, query_rows, weights, a, b, near = call(
         "query_features",
-        part_body(query_kernel),
+        query_kernel,
         [own_cols(four), got_cols(four)] * 2 + [map_spec, flat_spec, row_spec],
-        [flat_spec, rows_spec, per_head(group, length, length), a_spec, b_spec, near_spec(2)],
+        each(flat_spec, rows_spec, per_head(group, length, length)) + states(3, 2),
         [flat, rows_bf, shape_of(group, length, length, dtype=BF)] + [half_state] * 3,
     )(queries, queries_got, cotangent, cotangent_got, query_map, key_features, prefix_norm)
     suffix = Scan(a, b, near, False)
@@ -485,11 +526,11 @@
 
     attended, attended_got, scaled, norm_lanes, norm = call(
         "attend",
-        part_body(attend_kernel),
+        attend_kernel,
         [own_cols(four), got_cols(four), own_cols(one), got_cols(one)]
         + [rows_spec, per_head(group, length, length), row_spec]
         + [moved_spec] * 4,
-        [own_cols(four), got_cols(four), rows_spec, rows_spec, row_spec],
+        each(own_cols(four), got_cols(four), rows_spec, rows_spec, row_spec),
         [
             jax.ShapeDtypeStruct((own, head_count * dim), BF),
             jax.ShapeDtypeStruct((own, n * four), F32),
@@ -501,11 +542,11 @@
     grad_spec, grad = per_head(group * width, dim), shape_of(group * width, dim)
     query_part, key_up = call(
         "query_grads",
-        part_body(query_grad_kernel),
+        query_grad_kernel,
         [own_cols(four), got_cols(four), own_cols(one), got_cols(one)]
         + [flat_spec, flat_spec, rows_spec, rows_spec, row_spec]
         + [moved_spec] * 4,
-        [grad_spec, flat_spec],
+        each(grad_spec, flat_spec),
         [grad, flat],
     )(
         queries, queries_got, values, values_got, key_features, query_probs, scaled, norm_lanes,
@@ -515,19 +556,18 @@
     query_part = after(query_part, suffix_norm)
     (key_part,) = call(
         "key_grads",
-        part_body(key_grad_kernel),
+        key_grad_kernel,
         [own_cols(one), got_cols(one)] * 2 + [flat_spec, flat_spec, row_spec] + [moved_spec] * 4,
-        [grad_spec],
+        each(grad_spec),
         [grad],
     )(keys, keys_got, values, values_got, key_probs, key_up, suffix_norm, *later)
     (attended,) = call(
         "attended",
-        part_body(attended_kernel),
-        [spec((own, n * four), lambda i, info: (0, 0)), pl.BlockSpec(memory_space=pl.ANY)],
-        [other_half(four)],
+        attended_kernel,
+        [got_cols(four)],
+        each(other_cols(four)),
         [jax.ShapeDtypeStruct((own, head_count * dim), BF)],
-        steps=1,
-        input_output_aliases={2: 0},
+        aliases={2: 0},
     )(core_swap(after(attended_got, *later)), attended)
 
     def finish(name, mine, *earlier):

time: 150 us -> 147 us (0.980)
  Pallas kernels: 47.8 us -> 43.6 us
    pallas_call x8, Pallas kernels: 44.7 us -> 40.4 us  [run(): pl.pallas_call(kernel, name=name, out_shape=[pltpu.HBM(x.shape, x.dtype)...]
  transfers between devices with their start and end apart: 42 -> 42, of which waited for: 9 -> 9; matrix products, arithmetic and copies ran while one was open for 5% -> 5% of each run, Pallas kernels for 24% -> 22%
where the time goes in v6:
time: 147 us; the launch traced here: 146 us
  starting transfers between devices  76.3 us (52%)
  Pallas kernels  43.6 us (30%)
  waiting for transfers between devices  14.2 us (10%)
  local copies, waits for them, and re-layouts  6.18 us (4%)
  other arithmetic  4.85 us (3%)
    ppermute x17, starting transfers between devices, chip_move(): lax.ppermute(x, 'ctx', [(2 * a + c, 2 * b + c) for a, b in pairs for c in...  43.2 us
    pallas_call x8, Pallas kernels, run(): pl.pallas_call(kernel, name=name, out_shape=[pltpu.HBM(x.shape, x.dtype)...  40.4 us
    ppermute x13, starting transfers between devices, core_swap(): return lax.ppermute(x, 'ctx', [(i, i ^ 1) for i in range(size)])  21.3 us
    ppermute x17, waiting for transfers between devices, chip_move(): lax.ppermute(x, 'ctx', [(2 * a + c, 2 * b + c) for a, b in pairs for c in...  12.1 us
    ppermute x6, starting transfers between devices, sum_all(): lax.ppermute(total, 'dp', [(i, i ^ k) for i in range(dp)])  6.29 us
    ppermute x6, starting transfers between devices, sum_all(): lax.ppermute(mine[k * share:(k + 1) * share], 'dp', [(i, i ^ k) for i in...  5.43 us
    unnamed x32, local copies, waits for them, and re-layouts  3.98 us
    pallas_call x2, Pallas kernels, finish(): pl.pallas_call(out_kernel, name=name, out_shape=jax.ShapeDtypeStruct((sha...  3.17 us
  transfers between devices with their start and end apart: 42, of which 9 were waited for; matrix products, arithmetic and copies ran while one was open for 5% of the time, Pallas kernels for 22%

profile of v6, /device:TPU:1, one launch (start us, length us, event | category | flops | bytes accessed | tf_op | source)
XLA Modules:
  0.0 146.2 jit_solution(3552602753471270142)
XLA Ops:
  0.8 2.2 %pack_keys.1 = (f32[128,512]{1,0:T(8,128)}, f32[128,512]{1,0:T(8,128)}) custom-call(s32[11]{0:T(128)S(1)} %concatenate.3.info, bf16[128,1024]{1,0:T(8,128)(2,1)} %bitcast.59, bf16[128,1024]{1,0:T(8,128)(2,1)} %bitcast.54), custom_call_target="tpu_custom_call" | custom-call | tf_op jit(solution)/shard_map/pack_keys/pallas_call | solution.py:448
  5.9 5.0 %key_features.1 = (f32[4,512,256]{2,1,0:T(8,128)}, bf16[4,512,256]{2,1,0:T(8,128)(2,1)}, f32[4,1,512]{2,1,0:T(1,128)}, f32[1024,128]{1,0:T(8,128)}, f32[1024,128]{1,0:T(8,128)}, /*index=5*/f32[1024,128]{1,0:T(8,128)}) custom-call(s32[11]{0:T(128)S(1)} %concatenate.3.info, bf16[128,1024]{1,0:T(8,128)(2,1)} %bitcast.60, f32[128,512]{1,0:T(8,128)} %copy-done.10, ...), custom_call_target="tpu_custom_call" | custom-call | tf_op jit(solution)/shard_map/key_features/pallas_call | solution.py:448
  10.9 3.0 %pack_queries.1 = (f32[128,2048]{1,0:T(8,128)}, f32[128,2048]{1,0:T(8,128)}) custom-call(s32[11]{0:T(128)S(1)} %concatenate.3.info, bf16[128,4096]{1,0:T(8,128)(2,1)} %bitcast.51, bf16[128,4096]{1,0:T(8,128)(2,1)} %bitcast.48), custom_call_target="tpu_custom_call" | custom-call | tf_op jit(solution)/shard_map/pack_queries/pallas_call | solution.py:448
  14.5 2.5 %collective-permute-start.4 = (f32[4,1,512]{2,1,0:T(1,128)S(1)}, f32[4,1,512]{2,1,0:T(1,128)S(1)}, u32[]{:S(2)}, u32[]{:S(2)}) collective-permute-start(f32[4,1,512]{2,1,0:T(1,128)S(1)} %copy-done.14), channel_id=1, source_target_pairs={{0,2},{1,3},{2,0},{3,1},{4,6},{5,7},{6,4},{7,5},{8,10},{9,11},{10,... | collective-permute-start | bytes 24584 | tf_op jit(solution)/shard_map/ppermute | solution.py:248
  18.0 2.5 %collective-permute-start.5 = (f32[4,1,512]{2,1,0:T(1,128)S(1)}, f32[4,1,512]{2,1,0:T(1,128)S(1)}, u32[]{:S(2)}, u32[]{:S(2)}) collective-permute-start(f32[4,1,512]{2,1,0:T(1,128)S(1)} %add.82), channel_id=1, source_target_pairs={{0,4},{1,5},{2,6},{3,7},{4,0},{5,1},{6,2},{7,3},{8,12},{9,13},{10,... | collective-permute-start | bytes 24584 | tf_op jit(solution)/shard_map/ppermute | solution.py:248
  22.2 3.3 %collective-permute-start.6 = (f32[1024,128]{1,0:T(8,128)}, f32[1024,128]{1,0:T(8,128)S(1)}, u32[]{:S(2)}, u32[]{:S(2)}) collective-permute-start(f32[1024,128]{1,0:T(8,128)} %get-tuple-element.61), channel_id=1, source_target_pairs={{0,2},{1,3},{2,4},{3,5},{4,6},{5,7},{8,10},{9,11},{10,12},{11,13},... | collective-permute-start | bytes 1572872 | tf_op jit(solution)/shard_map/ppermute | solution.py:248
  25.5 4.2 %collective-permute-start.7 = (f32[1024,128]{1,0:T(8,128)}, f32[1024,128]{1,0:T(8,128)S(1)}, u32[]{:S(2)}, u32[]{:S(2)}) collective-permute-start(f32[1024,128]{1,0:T(8,128)} %get-tuple-element.66), channel_id=1, source_target_pairs={{0,4},{1,5},{8,12},{9,13},{16,20},{17,21},{24,28},{25,29}} | collective-permute-start | bytes 1572872 | tf_op jit(solution)/shard_map/ppermute | solution.py:248
  31.0 7.2 %query_features.1 = (f32[4,512,256]{2,1,0:T(8,128)}, bf16[4,4,256,128]{3,2,1,0:T(8,128)(2,1)}, bf16[4,4,256,256]{3,2,1,0:T(8,128)(2,1)}, f32[1024,128]{1,0:T(8,1...) custom-call(s32[11]{0:T(128)S(1)} %concatenate.3.info, bf16[128,4096]{1,0:T(8,128)(2,1)} %bitcast.52, ...), custom_call_target="tpu_custom_call" | custom-call | tf_op jit(solution)/shard_map/query_features/pallas_call | solution.py:448
  40.4 5.2 %collective-permute-done.7.refs_8_.refs_10_ = f32[1024,128]{1,0:T(8,128)S(1)} collective-permute-done((f32[1024,128]{1,0:T(8,128)}, f32[1024,128]{1,0:T(8,128)S(1)}, u32[]{:S(2)}, u32[]{:S(2)}) %collective-permute-start.7) | collective-permute-done | bytes 524320 | tf_op jit(solution)/shard_map/ppermute | solution.py:248
  53.5 2.8 %collective-permute-done.8.refs_9_.refs_11_ = f32[1024,128]{1,0:T(8,128)S(1)} collective-permute-done((f32[1024,128]{1,0:T(8,128)S(1)}, f32[1024,128]{1,0:T(8,128)S(1)}, u32[]{:S(2)}, u32[]{:S(2)}) %collective-permute-start.8) | collective-permute-done | bytes 524320 | tf_op jit(solution)/shard_map/ppermute | solution.py:248
  57.3 7.1 %attend.1 = (bf16[128,4096]{1,0:T(8,128)(2,1)}, f32[128,2048]{1,0:T(8,128)}, bf16[4,4,256,128]{3,2,1,0:T(8,128)(2,1)}, bf16[4,4,256,128]{3,2,1,0:T(8,128)(2,1)}, f32[4,1,512]{2,1,0:T(1,128)}) custom-call(s32[11]{0:T(128)S(1)} %concatenate.3.info, bf16[128,4096]{1,0:T(8,128)(2,1)} %bitcast.50, f32[128,2048]{1,0:T(8,128)} %copy-done.4, ...), custom_call_target="tpu_custom_call" | custom-call | tf_op jit(solution)/shard_map/attend/pallas_call | solution.py:448
  64.4 14.7 %collective-permute-start.15 = (f32[4,1,512]{2,1,0:T(1,128)}, f32[4,1,512]{2,1,0:T(1,128)S(1)}, u32[]{:S(2)}, u32[]{:S(2)}) collective-permute-start(f32[4,1,512]{2,1,0:T(1,128)} %get-tuple-element.80), channel_id=1, source_target_pairs={{0,2},{1,3},{2,0},{3,1},{4,6},{5,7},{6,4},{7,5},{8,10},{9,11},{10,... | collective-permute-start | bytes 24584 | tf_op jit(solution)/shard_map/ppermute | solution.py:248
  79.1 3.1 %collective-permute-start.16 = (f32[4,1,512]{2,1,0:T(1,128)}, f32[4,1,512]{2,1,0:T(1,128)S(1)}, u32[]{:S(2)}, u32[]{:S(2)}) collective-permute-start(f32[4,1,512]{2,1,0:T(1,128)} %get-tuple-element.80), channel_id=1, source_target_pairs={{0,4},{1,5},{2,6},{3,7},{4,0},{5,1},{6,2},{7,3},{8,12},{9,13},{10,... | collective-permute-start | bytes 24584 | tf_op jit(solution)/shard_map/ppermute | solution.py:248
  82.2 7.8 %query_grads.1 = (f32[4,256,128]{2,1,0:T(8,128)}, f32[4,512,256]{2,1,0:T(8,128)}) custom-call(s32[11]{0:T(128)S(1)} %concatenate.3.info, bf16[128,4096]{1,0:T(8,128)(2,1)} %bitcast.53, f32[128,2048]{1,0:T(8,128)} %copy-done.3, bf16[128,1024]{1,0:T(8,128)(2,1)} %bitcast.57, f32[128,512]{1,0:T(8,128)} %copy-done.2, ...), custom_call_target="tpu_custom_call" | custom-call | tf_op jit(solution)/shard_map/query_grads/pallas_call | solution.py:448
  90.1 5.2 %collective-permute-start.14 = (f32[128,2048]{1,0:T(8,128)S(1)}, f32[128,2048]{1,0:T(8,128)S(1)}, u32[]{:S(2)}, u32[]{:S(2)}) collective-permute-start(f32[128,2048]{1,0:T(8,128)S(1)} %copy-done.15), channel_id=1, source_target_pairs={{0,1},{1,0},{2,3},{3,2},{4,5},{5,4},{6,7},{7,6},{8,9},{9,8},{10,11... | collective-permute-start | bytes 3145736 | tf_op jit(solution)/shard_map/ppermute | solution.py:244
  99.7 5.6 %key_grads.1 = f32[4,256,128]{2,1,0:T(8,128)} custom-call(s32[11]{0:T(128)S(1)} %concatenate.3.info, bf16[128,1024]{1,0:T(8,128)(2,1)} %bitcast.61, f32[128,512]{1,0:T(8,128)} %copy-done.10, bf16[128,1024]{1,0:T(8,128)(2,1)} %bitcast.58, f32[128,512]{1,0:T(8,128)} %copy-done.2, f32[4,512,256]{2,1,0:T(8,128)} %get-tuple-element.85.refs_4_, ...), custom_call_target="tpu_custom_call" | custom-call | tf_op jit(solution)/shard_map/key_grads/pallas_call | solution.py:448
  110.8 3.6 %collective-permute-start.22 = (f32[1,256,128]{2,1,0:T(8,128)S(1)}, f32[1,256,128]{2,1,0:T(8,128)S(1)}, u32[]{:S(2)}, u32[]{:S(2)}) collective-permute-start(f32[1,256,128]{2,1,0:T(8,128)S(1)} %add.95), channel_id=1, source_target_pairs={{0,4},{1,5},{2,6},{3,7},{4,0},{5,1},{6,2},{7,3},{8,12},{9,13},{10,... | collective-permute-start | bytes 393224 | tf_op jit(solution)/shard_map/ppermute | solution.py:248
  115.4 2.5 %attended.1 = bf16[128,4096]{1,0:T(8,128)(2,1)} custom-call(s32[11]{0:T(128)S(1)} %concatenate.3.info, f32[128,2048]{1,0:T(8,128)} %copy-done.9, bf16[128,4096]{1,0:T(8,128)(2,1)} %get-tuple-element.75.refs_1_), custom_call_target="tpu_custom_call", output_to_operand_aliasing={{}: (2, {})} | custom-call | tf_op jit(solution)/shard_map/attended/pallas_call | solution.py:448
  118.9 3.0 %collective-permute-start.23 = (f32[1,256,128]{2,1,0:T(8,128)S(1)}, f32[1,256,128]{2,1,0:T(8,128)S(1)}, u32[]{:S(2)}, u32[]{:S(2)}) collective-permute-start(f32[1,256,128]{2,1,0:T(8,128)S(1)} %add.96), channel_id=1, source_target_pairs={{0,8},{8,0},{16,24},{24,16},{1,9},{9,1},{17,25},{25,17},{2,10},{10... | collective-permute-start | bytes 393224 | tf_op jit(solution)/shard_map/ppermute | solution.py:337
  122.7 2.0 %collective-permute-start.34 = (f32[1,256,128]{2,1,0:T(8,128)S(1)}, f32[1,256,128]{2,1,0:T(8,128)S(1)}, u32[]{:S(2)}, u32[]{:S(2)}) collective-permute-start(f32[1,256,128]{2,1,0:T(8,128)S(1)} %add.100), channel_id=1, source_target_pairs={{0,4},{1,5},{2,6},{3,7},{4,0},{5,1},{6,2},{7,3},{8,12},{9,13},{10,... | collective-permute-start | bytes 393224 | tf_op jit(solution)/shard_map/ppermute | solution.py:248
  125.2 4.9 %collective-permute-start.26 = (f32[1,256,128]{2,1,0:T(8,128)S(1)}, f32[1,256,128]{2,1,0:T(8,128)S(1)}, u32[]{:S(2)}, u32[]{:S(2)}) collective-permute-start(f32[1,256,128]{2,1,0:T(8,128)S(1)} %add.96), channel_id=1, source_target_pairs={{0,1},{1,0},{2,3},{3,2},{4,5},{5,4},{6,7},{7,6},{8,9},{9,8},{10,11... | collective-permute-start | bytes 393224 | tf_op jit(solution)/shard_map/ppermute | solution.py:244
  133.3 3.9 %collective-permute-start.29 = (f32[1,256,128]{2,1,0:T(8,128)S(1)}, f32[1,256,128]{2,1,0:T(8,128)S(1)}, u32[]{:S(2)}, u32[]{:S(2)}) collective-permute-start(f32[1,256,128]{2,1,0:T(8,128)S(1)} %collective-permute-done.25), channel_id=1, source_target_pairs={{0,1},{1,0},{2,3},{3,2},{4,5},{5,4},{6,7},{7,6},{8,9},{9,8},{10,11... | collective-permute-start | bytes 393224 | tf_op jit(solution)/shard_map/ppermute | solution.py:244
  137.3 1.7 %collective-permute-start.39 = (f32[1,256,128]{2,1,0:T(8,128)S(1)}, f32[1,256,128]{2,1,0:T(8,128)S(1)}, u32[]{:S(2)}, u32[]{:S(2)}) collective-permute-start(f32[1,256,128]{2,1,0:T(8,128)S(1)} %collective-permute-done.35), channel_id=1, source_target_pairs={{0,1},{1,0},{2,3},{3,2},{4,5},{5,4},{6,7},{7,6},{8,9},{9,8},{10,11... | collective-permute-start | bytes 393224 | tf_op jit(solution)/shard_map/ppermute | solution.py:244
  139.0 3.9 %collective-permute-start.40 = (f32[1,256,128]{2,1,0:T(8,128)S(1)}, f32[1,256,128]{2,1,0:T(8,128)S(1)}, u32[]{:S(2)}, u32[]{:S(2)}) collective-permute-start(f32[1,256,128]{2,1,0:T(8,128)S(1)} %collective-permute-done.36), channel_id=1, source_target_pairs={{0,1},{1,0},{2,3},{3,2},{4,5},{5,4},{6,7},{7,6},{8,9},{9,8},{10,11... | collective-permute-start | bytes 393224 | tf_op jit(solution)/shard_map/ppermute | solution.py:244
  (117 shorter events, 38.2 us)
Async XLA Ops:
  13.9 15.8 %collective-permute-start.2 = (f32[128,2048]{1,0:T(8,128)}, f32[128,2048]{1,0:T(8,128)S(1)}, u32[]{:S(2)}, u32[]{:S(2)}) collective-permute-start(f32[128,2048]{1,0:T(8,128)} %get-tuple-element.53), channel_id=1, source_target_pairs={{0,1},{1,0},{2,3},{3,2},{4,5},{5,4},{6,7},{7,6},{8,9},{9,8},{10,11... | collective-permute-start | bytes 3145736 | tf_op jit(solution)/shard_map/ppermute | solution.py:244
  14.1 15.6 %collective-permute-start.3 = (f32[128,2048]{1,0:T(8,128)}, f32[128,2048]{1,0:T(8,128)S(1)}, u32[]{:S(2)}, u32[]{:S(2)}) collective-permute-start(f32[128,2048]{1,0:T(8,128)} %get-tuple-element.54), channel_id=1, source_target_pairs={{0,1},{1,0},{2,3},{3,2},{4,5},{5,4},{6,7},{7,6},{8,9},{9,8},{10,11... | collective-permute-start | bytes 3145736 | tf_op jit(solution)/shard_map/ppermute | solution.py:244
  22.2 18.2 %collective-permute-start.6 = (f32[1024,128]{1,0:T(8,128)}, f32[1024,128]{1,0:T(8,128)S(1)}, u32[]{:S(2)}, u32[]{:S(2)}) collective-permute-start(f32[1024,128]{1,0:T(8,128)} %get-tuple-element.61), channel_id=1, source_target_pairs={{0,2},{1,3},{2,4},{3,5},{4,6},{5,7},{8,10},{9,11},{10,12},{11,13},... | collective-permute-start | bytes 1572872 | tf_op jit(solution)/shard_map/ppermute | solution.py:248
  25.5 20.0 %collective-permute-start.7 = (f32[1024,128]{1,0:T(8,128)}, f32[1024,128]{1,0:T(8,128)S(1)}, u32[]{:S(2)}, u32[]{:S(2)}) collective-permute-start(f32[1024,128]{1,0:T(8,128)} %get-tuple-element.66), channel_id=1, source_target_pairs={{0,4},{1,5},{8,12},{9,13},{16,20},{17,21},{24,28},{25,29}} | collective-permute-start | bytes 1572872 | tf_op jit(solution)/shard_map/ppermute | solution.py:248
  38.2 12.4 %collective-permute-start.10 = (f32[1024,128]{1,0:T(8,128)}, f32[1024,128]{1,0:T(8,128)S(1)}, u32[]{:S(2)}, u32[]{:S(2)}) collective-permute-start(f32[1024,128]{1,0:T(8,128)} %get-tuple-element.64), channel_id=1, source_target_pairs={{6,4},{7,5},{4,2},{5,3},{2,0},{3,1},{14,12},{15,13},{12,10},{13,11... | collective-permute-start | bytes 1572872 | tf_op jit(solution)/shard_map/ppermute | solution.py:248
  39.6 11.0 %collective-permute-start.11 = (f32[1024,128]{1,0:T(8,128)}, f32[1024,128]{1,0:T(8,128)S(1)}, u32[]{:S(2)}, u32[]{:S(2)}) collective-permute-start(f32[1024,128]{1,0:T(8,128)} %get-tuple-element.68), channel_id=1, source_target_pairs={{6,2},{7,3},{14,10},{15,11},{22,18},{23,19},{30,26},{31,27}} | collective-permute-start | bytes 1572872 | tf_op jit(solution)/shard_map/ppermute | solution.py:248
  47.1 9.2 %collective-permute-start.8 = (f32[1024,128]{1,0:T(8,128)S(1)}, f32[1024,128]{1,0:T(8,128)S(1)}, u32[]{:S(2)}, u32[]{:S(2)}) collective-permute-start(f32[1024,128]{1,0:T(8,128)S(1)} %select_select_fusion.1), channel_id=1, source_target_pairs={{0,2},{1,3},{2,4},{3,5},{4,6},{5,7},{8,10},{9,11},{10,12},{11,13},... | collective-permute-start | bytes 1572872 | tf_op jit(solution)/shard_map/ppermute | solution.py:248
  48.5 7.9 %collective-permute-start.9 = (f32[1024,128]{1,0:T(8,128)S(1)}, f32[1024,128]{1,0:T(8,128)S(1)}, u32[]{:S(2)}, u32[]{:S(2)}) collective-permute-start(f32[1024,128]{1,0:T(8,128)S(1)} %select_select_fusion.1), channel_id=1, source_target_pairs={{2,6},{3,7},{10,14},{11,15},{18,22},{19,23},{26,30},{27,31}} | collective-permute-start | bytes 1572872 | tf_op jit(solution)/shard_map/ppermute | solution.py:248
  50.8 39.3 %collective-permute-start.12 = (f32[1024,128]{1,0:T(8,128)S(1)}, f32[1024,128]{1,0:T(8,128)}, u32[]{:S(2)}, u32[]{:S(2)}) collective-permute-start(f32[1024,128]{1,0:T(8,128)S(1)} %select_select_fusion), channel_id=1, source_target_pairs={{6,4},{7,5},{4,2},{5,3},{2,0},{3,1},{14,12},{15,13},{12,10},{13,11... | collective-permute-start | bytes 1572872 | tf_op jit(solution)/shard_map/ppermute | solution.py:248
  52.1 38.0 %collective-permute-start.13 = (f32[1024,128]{1,0:T(8,128)S(1)}, f32[1024,128]{1,0:T(8,128)S(1)}, u32[]{:S(2)}, u32[]{:S(2)}) collective-permute-start(f32[1024,128]{1,0:T(8,128)S(1)} %select_select_fusion), channel_id=1, source_target_pairs={{4,0},{5,1},{12,8},{13,9},{20,16},{21,17},{28,24},{29,25}} | collective-permute-start | bytes 1572872 | tf_op jit(solution)/shard_map/ppermute | solution.py:248
  64.4 25.6 %collective-permute-start.15 = (f32[4,1,512]{2,1,0:T(1,128)}, f32[4,1,512]{2,1,0:T(1,128)S(1)}, u32[]{:S(2)}, u32[]{:S(2)}) collective-permute-start(f32[4,1,512]{2,1,0:T(1,128)} %get-tuple-element.80), channel_id=1, source_target_pairs={{0,2},{1,3},{2,0},{3,1},{4,6},{5,7},{6,4},{7,5},{8,10},{9,11},{10,... | collective-permute-start | bytes 24584 | tf_op jit(solution)/shard_map/ppermute | solution.py:248
  79.1 11.0 %collective-permute-start.16 = (f32[4,1,512]{2,1,0:T(1,128)}, f32[4,1,512]{2,1,0:T(1,128)S(1)}, u32[]{:S(2)}, u32[]{:S(2)}) collective-permute-start(f32[4,1,512]{2,1,0:T(1,128)} %get-tuple-element.80), channel_id=1, source_target_pairs={{0,4},{1,5},{2,6},{3,7},{4,0},{5,1},{6,2},{7,3},{8,12},{9,13},{10,... | collective-permute-start | bytes 24584 | tf_op jit(solution)/shard_map/ppermute | solution.py:248
  82.2 7.9 %collective-permute-start.17 = (f32[4,1,512]{2,1,0:T(1,128)}, f32[4,1,512]{2,1,0:T(1,128)S(1)}, u32[]{:S(2)}, u32[]{:S(2)}) collective-permute-start(f32[4,1,512]{2,1,0:T(1,128)} %get-tuple-element.80), channel_id=1, source_target_pairs={{0,6},{1,7},{2,4},{3,5},{4,2},{5,3},{6,0},{7,1},{8,14},{9,15},{10,... | collective-permute-start | bytes 24584 | tf_op jit(solution)/shard_map/ppermute | solution.py:248
  90.1 24.3 %collective-permute-start.14 = (f32[128,2048]{1,0:T(8,128)S(1)}, f32[128,2048]{1,0:T(8,128)S(1)}, u32[]{:S(2)}, u32[]{:S(2)}) collective-permute-start(f32[128,2048]{1,0:T(8,128)S(1)} %copy-done.15), channel_id=1, source_target_pairs={{0,1},{1,0},{2,3},{3,2},{4,5},{5,4},{6,7},{7,6},{8,9},{9,8},{10,11... | collective-permute-start | bytes 3145736 | tf_op jit(solution)/shard_map/ppermute | solution.py:244
  97.0 8.3 %collective-permute-start.18 = (f32[1,256,128]{2,1,0:T(8,128)S(1)}, f32[1,256,128]{2,1,0:T(8,128)S(1)}, u32[]{:S(2)}, u32[]{:S(2)}) collective-permute-start(f32[1,256,128]{2,1,0:T(8,128)S(1)} %get-tuple-element.98), channel_id=1, source_target_pairs={{0,8},{8,0},{16,24},{24,16},{1,9},{9,1},{17,25},{25,17},{2,10},{10... | collective-permute-start | bytes 393224 | tf_op jit(solution)/shard_map/ppermute | solution.py:324
  108.0 9.8 %collective-permute-start.30 = (f32[1,256,128]{2,1,0:T(8,128)S(1)}, f32[1,256,128]{2,1,0:T(8,128)S(1)}, u32[]{:S(2)}, u32[]{:S(2)}) collective-permute-start(f32[1,256,128]{2,1,0:T(8,128)S(1)} %get-tuple-element.95), channel_id=1, source_target_pairs={{0,8},{8,0},{16,24},{24,16},{1,9},{9,1},{17,25},{25,17},{2,10},{10... | collective-permute-start | bytes 393224 | tf_op jit(solution)/shard_map/ppermute | solution.py:324
  109.5 8.4 %collective-permute-start.31 = (f32[1,256,128]{2,1,0:T(8,128)S(1)}, f32[1,256,128]{2,1,0:T(8,128)S(1)}, u32[]{:S(2)}, u32[]{:S(2)}) collective-permute-start(f32[1,256,128]{2,1,0:T(8,128)S(1)} %get-tuple-element.94), channel_id=1, source_target_pairs={{0,16},{8,24},{16,0},{24,8},{1,17},{9,25},{17,1},{25,9},{2,18},{10... | collective-permute-start | bytes 393224 | tf_op jit(solution)/shard_map/ppermute | solution.py:324
  110.8 8.1 %collective-permute-start.22 = (f32[1,256,128]{2,1,0:T(8,128)S(1)}, f32[1,256,128]{2,1,0:T(8,128)S(1)}, u32[]{:S(2)}, u32[]{:S(2)}) collective-permute-start(f32[1,256,128]{2,1,0:T(8,128)S(1)} %add.95), channel_id=1, source_target_pairs={{0,4},{1,5},{2,6},{3,7},{4,0},{5,1},{6,2},{7,3},{8,12},{9,13},{10,... | collective-permute-start | bytes 393224 | tf_op jit(solution)/shard_map/ppermute | solution.py:248
  118.9 11.1 %collective-permute-start.23 = (f32[1,256,128]{2,1,0:T(8,128)S(1)}, f32[1,256,128]{2,1,0:T(8,128)S(1)}, u32[]{:S(2)}, u32[]{:S(2)}) collective-permute-start(f32[1,256,128]{2,1,0:T(8,128)S(1)} %add.96), channel_id=1, source_target_pairs={{0,8},{8,0},{16,24},{24,16},{1,9},{9,1},{17,25},{25,17},{2,10},{10... | collective-permute-start | bytes 393224 | tf_op jit(solution)/shard_map/ppermute | solution.py:337
  121.9 8.2 %collective-permute-start.24 = (f32[1,256,128]{2,1,0:T(8,128)S(1)}, f32[1,256,128]{2,1,0:T(8,128)S(1)}, u32[]{:S(2)}, u32[]{:S(2)}) collective-permute-start(f32[1,256,128]{2,1,0:T(8,128)S(1)} %add.96), channel_id=1, source_target_pairs={{0,16},{8,24},{16,0},{24,8},{1,17},{9,25},{17,1},{25,9},{2,18},{10... | collective-permute-start | bytes 393224 | tf_op jit(solution)/shard_map/ppermute | solution.py:337
  122.7 7.9 %collective-permute-start.34 = (f32[1,256,128]{2,1,0:T(8,128)S(1)}, f32[1,256,128]{2,1,0:T(8,128)S(1)}, u32[]{:S(2)}, u32[]{:S(2)}) collective-permute-start(f32[1,256,128]{2,1,0:T(8,128)S(1)} %add.100), channel_id=1, source_target_pairs={{0,4},{1,5},{2,6},{3,7},{4,0},{5,1},{6,2},{7,3},{8,12},{9,13},{10,... | collective-permute-start | bytes 393224 | tf_op jit(solution)/shard_map/ppermute | solution.py:248
  125.2 8.0 %collective-permute-start.26 = (f32[1,256,128]{2,1,0:T(8,128)S(1)}, f32[1,256,128]{2,1,0:T(8,128)S(1)}, u32[]{:S(2)}, u32[]{:S(2)}) collective-permute-start(f32[1,256,128]{2,1,0:T(8,128)S(1)} %add.96), channel_id=1, source_target_pairs={{0,1},{1,0},{2,3},{3,2},{4,5},{5,4},{6,7},{7,6},{8,9},{9,8},{10,11... | collective-permute-start | bytes 393224 | tf_op jit(solution)/shard_map/ppermute | solution.py:244
  133.2 9.8 %collective-permute-start.37 = (f32[1,256,128]{2,1,0:T(8,128)S(1)}, f32[1,256,128]{2,1,0:T(8,128)S(1)}, u32[]{:S(2)}, u32[]{:S(2)}) collective-permute-start(f32[1,256,128]{2,1,0:T(8,128)S(1)} %add.101), channel_id=1, source_target_pairs={{0,24},{8,16},{16,8},{24,0},{1,25},{9,17},{17,9},{25,1},{2,26},{10... | collective-permute-start | bytes 393224 | tf_op jit(solution)/shard_map/ppermute | solution.py:337
  133.3 9.6 %collective-permute-start.29 = (f32[1,256,128]{2,1,0:T(8,128)S(1)}, f32[1,256,128]{2,1,0:T(8,128)S(1)}, u32[]{:S(2)}, u32[]{:S(2)}) collective-permute-start(f32[1,256,128]{2,1,0:T(8,128)S(1)} %collective-permute-done.25), channel_id=1, source_target_pairs={{0,1},{1,0},{2,3},{3,2},{4,5},{5,4},{6,7},{7,6},{8,9},{9,8},{10,11... | collective-permute-start | bytes 393224 | tf_op jit(solution)/shard_map/ppermute | solution.py:244
  (34 other events, 186.5 us)

commit v7 on v6

--- a/solution.py
+++ b/solution.py
@@ -83,14 +83,9 @@
     return jnp.where(place == 2, near[...] + far[...], near2[...])
 
 
-def pack_kernel(n, i, info, *refs):
-    half = len(refs) // 2
-    for x_ref, o_ref in zip(refs[:half], refs[half:]):
-        o_ref[...] = x_ref[...].astype(F32)
-
-
 def key_kernel(
-    n, i, info, k_ref, kg_ref, v_ref, vg_ref, w_ref, kp_ref, kb_ref, norm_ref, state_ref
+    n, i, info, k_ref, kg_ref, v_ref, vg_ref, w_ref, q_ref, c_ref,
+    kp_ref, kb_ref, norm_ref, state_ref, qw_ref, cw_ref,
 ):
     group, width, dim = w_ref.shape
     keys = tokens_of(k_ref, kg_ref)
@@ -102,6 +97,8 @@
     kb_ref[0] = features
     norm_ref[0] = mm_nt(jnp.ones((16, keys.shape[0]), BF), features)[:1]
     state_ref[...] = mm(features, values)
+    qw_ref[...] = q_ref[...].astype(F32)
+    cw_ref[...] = c_ref[...].astype(F32)
 
 
 def query_kernel(
@@ -142,64 +139,57 @@
 
 
 def attend_kernel(
-    n, step, info, c_ref, cg_ref, v_ref, vg_ref, qr_ref, wt_ref, pn_ref, near, far, near2, far2,
-    att_ref, atg_ref, sc_ref, nl_ref, sn_ref,
+    n, step, info, q_ref, qg_ref, c_ref, cg_ref, v_ref, vg_ref, kb_ref, qp_ref, qr_ref, wt_ref, pn_ref,
+    near, far, near2, far2, att_ref, atg_ref, sn_ref, gq_ref, gk_ref,
 ):
     group, length, dim = qr_ref.shape[1:]
     feats = dim
+    width = feats // 2
     own = length // 2
     heads = range(group)
     cols = [slice(i * dim, (i + 1) * dim) for i in heads]
     rows = [slice(i * feats, (i + 1) * feats) for i in heads]
+    causal = causal_mask(info[2 * n], length)
+    queries = tokens_of(q_ref, qg_ref)
     upstream = stack(c_ref[...].astype(F32), cg_ref[...])
     values = tokens_of(v_ref, vg_ref)
     high, low = split(before_of(info[2 * n + 1], step < n // 2, near, far, near2, far2))
-    norm_high, norm_low = split(jnp.broadcast_to(column(pn_ref[0]), (group * feats, dim)))
-    high, low = cat(high, norm_high), cat(low, norm_low)
-    values = cat(values, jnp.ones((length, dim), BF))
+    norm_wide = jnp.broadcast_to(column(pn_ref[0]), (group * feats, dim))
+    norm_high, norm_low = split(norm_wide)
+    norm_cols = three_lanes(norm_wide, "hhl")
+    values_ones = cat(values, jnp.ones((length, dim), BF))
     query_rows = [qr_ref[0, i] for i in heads]
     both = [
-        mm(cat(wt_ref[0, i], query_rows[i], query_rows[i]), stack(values, high[rows[i]], low[rows[i]]))
+        mm(
+            cat(wt_ref[0, i], query_rows[i], query_rows[i]),
+            stack(
+                values_ones,
+                cat(high[rows[i]], norm_high[rows[i]]),
+                cat(low[rows[i]], norm_low[rows[i]]),
+            ),
+        )
         for i in heads
     ]
     numerator = [x[:, :dim] for x in both]
     inverse = [1.0 / x[:, dim:] for x in both]
-    scaled = [upstream[:, cols[i]] * inverse[i] for i in heads]
-    products = [cat(*split(-(scaled[i] * inverse[i]) * numerator[i])) for i in heads]
+    scaled_wide = [upstream[:, cols[i]] * inverse[i] for i in heads]
+    scaled = [x.astype(BF) for x in scaled_wide]
+    products = [cat(*split(-(scaled_wide[i] * inverse[i]) * numerator[i])) for i in heads]
     ones = jnp.ones((2 * dim, dim), BF)
     norm_grad = [mm(x, ones) for x in products]
     for i in heads:
         result = numerator[i] * inverse[i]
         att_ref[:, cols[i]] = result[:own].astype(BF)
         atg_ref[:, cols[i]] = result[own:]
-        sc_ref[0, i] = scaled[i].astype(BF)
-        nl_ref[0, i] = three_lanes(norm_grad[i], "hlh")
         sn_ref[0, :, rows[i]] = jnp.sum(
             query_rows[i].astype(F32) * norm_grad[i], axis=0, keepdims=True
         )
-
-
-def query_grad_kernel(
-    n, step, info, q_ref, qg_ref, v_ref, vg_ref, kb_ref, qp_ref, sc_ref, nl_ref, pn_ref,
-    near, far, near2, far2, gq_ref, gk_ref,
-):
-    group, length, dim = sc_ref.shape[1:]
-    feats = dim
-    width = feats // 2
-    heads = range(group)
-    cols = [slice(i * dim, (i + 1) * dim) for i in heads]
-    rows = [slice(i * feats, (i + 1) * feats) for i in heads]
-    causal = causal_mask(info[2 * n], length)
-    queries = tokens_of(q_ref, qg_ref)
+    lanes = [three_lanes(x, "hlh") for x in norm_grad]
     lane = lax.broadcasted_iota(jnp.int32, (length, dim), 1)
-    values = cat(tokens_of(v_ref, vg_ref), jnp.where(lane < 2, 1.0, 0.0).astype(BF))
-    high, low = split(before_of(info[2 * n + 1], step < n // 2, near, far, near2, far2))
-    norm_cols = three_lanes(jnp.broadcast_to(column(pn_ref[0]), (group * feats, dim)), "hhl")
-    scaled = [sc_ref[0, i] for i in heads]
-    lanes = [nl_ref[0, i] for i in heads]
-    mixed = [mm_nt(cat(scaled[i], lanes[i]), values) for i in heads]
+    values_lanes = cat(values, jnp.where(lane < 2, 1.0, 0.0).astype(BF))
+    mixed = [mm_nt(cat(scaled[i], lanes[i]), values_lanes) for i in heads]
     block = [jnp.where(causal, x, 0.0).astype(BF) for x in mixed]
-    upstream = [
+    upstream_q = [
         mm_nt(
             cat(kb_ref[0, rows[i]], high[rows[i]], norm_cols[rows[i]], low[rows[i]]),
             cat(block[i], scaled[i], lanes[i], scaled[i]),
@@ -207,7 +197,7 @@
         for i in heads
     ]
     probs = [qp_ref[0, r] for r in rows]
-    back = [soft_back(probs[i], upstream[i]) for i in heads]
+    back = [soft_back(probs[i], upstream_q[i]) for i in heads]
     for i in heads:
         gq_ref[0, i * width : (i + 1) * width] = mm(back[i], queries[:, cols[i]])
         gk_ref[0, rows[i]] = mm(probs[i].astype(BF), block[i])
@@ -484,24 +474,25 @@
             (half_spec, which, lambda i, info: (info[2 * n + place] == 1) == (i >= half)),
         ]
 
-    def pack(name, arrays, cols):
-        return call(
-            name,
-            pack_kernel,
-            [other_cols(cols)] * len(arrays),
-            each(*[got_cols(cols)] * len(arrays)),
-            [jax.ShapeDtypeStruct((own, n * cols), F32)] * len(arrays),
-        )(*arrays)
-
-    keys_got, values_got = [core_swap(x) for x in pack("pack_keys", (keys, values), one)]
-    key_probs, key_features, norm, a, b, near = call(
+    got_keys = spec((own, one), lambda i, info: (0, info[i] % n))
+    got_values = spec((own, one), lambda i, info: (1, info[i] % n))
+    half_cols = n * one
+    packed = jnp.concatenate(
+        [lax.dynamic_slice_in_dim(x, (1 - core) * half_cols, half_cols, axis=1) for x in (keys, values)]
+    )
+    swapped = core_swap(packed.astype(F32))
+    keys_got = values_got = swapped
+
+    wide_flat = jax.ShapeDtypeStruct((own, n * four), F32)
+    key_probs, key_features, norm, a, b, near, *packed = call(
         "key_features",
         key_kernel,
-        [own_cols(one), got_cols(one)] * 2 + [map_spec],
-        each(flat_spec, flat_spec, row_spec) + states(3, 1),
-        [flat, shape_of(wide, length, dtype=BF), row] + [half_state] * 3,
-    )(keys, keys_got, values, values_got, key_map)
-    packed = pack("pack_queries", after((queries, cotangent), norm), four)
+        [own_cols(one), got_keys, own_cols(one), got_values, map_spec] + [other_cols(four)] * 2,
+        each(flat_spec, flat_spec, row_spec)
+        + states(3, 1)
+        + [(got_cols(four), 4, always), (got_cols(four), 5, always)],
+        [flat, shape_of(wide, length, dtype=BF), row] + [half_state] * 3 + [wide_flat] * 2,
+    )(keys, keys_got, values, values_got, key_map, queries, cotangent)
     queries_got, cotangent_got = [core_swap(x) for x in packed]
     prefix_norm = scan_norms(norm, chip, chips, True)
     prefix = Scan(*after((a, b, near), prefix_norm), True)
@@ -524,40 +515,34 @@
     before = after(before, suffix.payload)
     later = suffix.second()
 
-    attended, attended_got, scaled, norm_lanes, norm = call(
+    grad_spec, grad = per_head(group * width, dim), shape_of(group * width, dim)
+    attended, attended_got, norm, query_part, key_up = call(
         "attend",
         attend_kernel,
-        [own_cols(four), got_cols(four), own_cols(one), got_cols(one)]
-        + [rows_spec, per_head(group, length, length), row_spec]
+        [own_cols(four), got_cols(four)] * 2
+        + [own_cols(one), got_values, flat_spec, flat_spec, rows_spec]
+        + [per_head(group, length, length), row_spec]
         + [moved_spec] * 4,
-        each(own_cols(four), got_cols(four), rows_spec, rows_spec, row_spec),
+        each(own_cols(four), got_cols(four), row_spec, grad_spec, flat_spec),
         [
             jax.ShapeDtypeStruct((own, head_count * dim), BF),
             jax.ShapeDtypeStruct((own, n * four), F32),
-            rows_bf,
-            rows_bf,
             row,
+            grad,
+            flat,
         ],
-    )(cotangent, cotangent_got, values, values_got, query_rows, weights, prefix_norm, *before)
-    grad_spec, grad = per_head(group * width, dim), shape_of(group * width, dim)
-    query_part, key_up = call(
-        "query_grads",
-        query_grad_kernel,
-        [own_cols(four), got_cols(four), own_cols(one), got_cols(one)]
-        + [flat_spec, flat_spec, rows_spec, rows_spec, row_spec]
-        + [moved_spec] * 4,
-        each(grad_spec, flat_spec),
-        [grad, flat],
     )(
-        queries, queries_got, values, values_got, key_features, query_probs, scaled, norm_lanes,
-        prefix_norm, *before,
+        queries, queries_got, cotangent, cotangent_got, values, values_got, key_features,
+        query_probs, query_rows, weights, prefix_norm, *before,
     )
     suffix_norm = scan_norms(norm, chip, chips, False, query_part)
     query_part = after(query_part, suffix_norm)
     (key_part,) = call(
         "key_grads",
         key_grad_kernel,
-        [own_cols(one), got_cols(one)] * 2 + [flat_spec, flat_spec, row_spec] + [moved_spec] * 4,
+        [own_cols(one), got_keys, own_cols(one), got_values]
+        + [flat_spec, flat_spec, row_spec]
+        + [moved_spec] * 4,
         each(grad_spec),
         [grad],
     )(keys, keys_got, values, values_got, key_probs, key_up, suffix_norm, *later)

time: 147 us -> 141 us (0.959)
  Pallas kernels: 43.6 us -> 34.4 us
  waiting for transfers between devices: 14.2 us -> 23 us
  starting transfers between devices: 76.3 us -> 68 us
  other arithmetic: 4.85 us -> 6.45 us
    pallas_call x8 -> x5, Pallas kernels: 40.4 us -> 31.2 us  [run(): pl.pallas_call(kernel, name=name, out_shape=[pltpu.HBM(x.shape, x.dtype)...]
    ppermute x17, waiting for transfers between devices: 12.1 us -> 18.6 us  [chip_move(): lax.ppermute(x, 'ctx', [(2 * a + c, 2 * b + c) for a, b in pairs for c in...]
    ppermute x17, starting transfers between devices: 43.2 us -> 38.6 us  [chip_move(): lax.ppermute(x, 'ctx', [(2 * a + c, 2 * b + c) for a, b in pairs for c in...]
    ppermute x13 -> x12, starting transfers between devices: 21.3 us -> 18.4 us  [core_swap(): return lax.ppermute(x, 'ctx', [(i, i ^ 1) for i in range(size)])]
    ppermute x6, waiting for transfers between devices: 0.39 us -> 2.59 us  [sum_all(): lax.ppermute(mine[k * share:(k + 1) * share], 'dp', [(i, i ^ k) for i in...]
    unnamed x32 -> x28, local copies, waits for them, and re-layouts: 3.98 us -> 4.1 us
  transfers between devices with their start and end apart: 42 -> 41, of which waited for: 9 -> 10; matrix products, arithmetic and copies ran while one was open for 5% -> 6% of each run, Pallas kernels for 22% -> 19%
where the time goes in v7:
time: 141 us; the launch traced here: 140 us
  starting transfers between devices  68 us (48%)
  Pallas kernels  34.4 us (24%)
  waiting for transfers between devices  23 us (16%)
  local copies, waits for them, and re-layouts  7.29 us (5%)
  other arithmetic  6.45 us (5%)
    ppermute x17, starting transfers between devices, chip_move(): lax.ppermute(x, 'ctx', [(2 * a + c, 2 * b + c) for a, b in pairs for c in...  38.6 us
    pallas_call x5, Pallas kernels, run(): pl.pallas_call(kernel, name=name, out_shape=[pltpu.HBM(x.shape, x.dtype)...  31.2 us
    ppermute x17, waiting for transfers between devices, chip_move(): lax.ppermute(x, 'ctx', [(2 * a + c, 2 * b + c) for a, b in pairs for c in...  18.6 us
    ppermute x12, starting transfers between devices, core_swap(): return lax.ppermute(x, 'ctx', [(i, i ^ 1) for i in range(size)])  18.4 us
    ppermute x6, starting transfers between devices, sum_all(): lax.ppermute(total, 'dp', [(i, i ^ k) for i in range(dp)])  5.59 us
    ppermute x6, starting transfers between devices, sum_all(): lax.ppermute(mine[k * share:(k + 1) * share], 'dp', [(i, i ^ k) for i in...  5.45 us
    unnamed x28, local copies, waits for them, and re-layouts  4.1 us
    pallas_call x2, Pallas kernels, finish(): pl.pallas_call(out_kernel, name=name, out_shape=jax.ShapeDtypeStruct((sha...  3.17 us
  transfers between devices with their start and end apart: 41, of which 10 were waited for; matrix products, arithmetic and copies ran while one was open for 6% of the time, Pallas kernels for 19%

profile of v7, /device:TPU:1, one launch (start us, length us, event | category | flops | bytes accessed | tf_op | source)
XLA Modules:
  0.0 140.1 jit_solution(2258761125515711998)
XLA Ops:
  1.9 1.8 %collective-permute-done.refs_1_.refs_3_.refs_5_ = f32[256,512]{1,0:T(8,128)S(1)} collective-permute-done((f32[256,512]{1,0:T(8,128)S(1)}, f32[256,512]{1,0:T(8,128)S(1)}, u32[]{:S(2)}, u32[]{:S(2)}) %collective-permute-start) | collective-permute-done | bytes 524320 | tf_op jit(solution)/shard_map/ppermute | solution.py:234
  4.5 5.5 %key_features.1 = (f32[4,512,256]{2,1,0:T(8,128)}, bf16[4,512,256]{2,1,0:T(8,128)(2,1)}, f32[4,1,512]{2,1,0:T(1,128)}, f32[1024,128]{1,0:T(8,128)}, f32[1024,128...) custom-call(s32[11]{0:T(128)S(1)} %concatenate.6.info, bf16[128,1024]{1,0:T(8,128)(2,1)} %bitcast.61, ...), custom_call_target="tpu_custom_call" | custom-call | tf_op jit(solution)/shard_map/key_features/pallas_call | solution.py:438
  10.6 2.5 %collective-permute-start.3 = (f32[4,1,512]{2,1,0:T(1,128)}, f32[4,1,512]{2,1,0:T(1,128)S(1)}, u32[]{:S(2)}, u32[]{:S(2)}) collective-permute-start(f32[4,1,512]{2,1,0:T(1,128)} %get-tuple-element.45), channel_id=1, source_target_pairs={{0,2},{1,3},{2,0},{3,1},{4,6},{5,7},{6,4},{7,5},{8,10},{9,11},{10,... | collective-permute-start | bytes 24584 | tf_op jit(solution)/shard_map/ppermute | solution.py:238
  15.1 2.5 %collective-permute-start.4 = (f32[4,1,512]{2,1,0:T(1,128)S(1)}, f32[4,1,512]{2,1,0:T(1,128)S(1)}, u32[]{:S(2)}, u32[]{:S(2)}) collective-permute-start(f32[4,1,512]{2,1,0:T(1,128)S(1)} %add.87), channel_id=1, source_target_pairs={{0,4},{1,5},{2,6},{3,7},{4,0},{5,1},{6,2},{7,3},{8,12},{9,13},{10,... | collective-permute-start | bytes 24584 | tf_op jit(solution)/shard_map/ppermute | solution.py:238
  19.2 3.3 %collective-permute-start.5 = (f32[1024,128]{1,0:T(8,128)}, f32[1024,128]{1,0:T(8,128)S(1)}, u32[]{:S(2)}, u32[]{:S(2)}) collective-permute-start(f32[1024,128]{1,0:T(8,128)} %get-tuple-element.52), channel_id=1, source_target_pairs={{0,2},{1,3},{2,4},{3,5},{4,6},{5,7},{8,10},{9,11},{10,12},{11,13},... | collective-permute-start | bytes 1572872 | tf_op jit(solution)/shard_map/ppermute | solution.py:238
  22.5 4.1 %collective-permute-start.6 = (f32[1024,128]{1,0:T(8,128)}, f32[1024,128]{1,0:T(8,128)S(1)}, u32[]{:S(2)}, u32[]{:S(2)}) collective-permute-start(f32[1024,128]{1,0:T(8,128)} %get-tuple-element.57), channel_id=1, source_target_pairs={{0,4},{1,5},{8,12},{9,13},{16,20},{17,21},{24,28},{25,29}} | collective-permute-start | bytes 1572872 | tf_op jit(solution)/shard_map/ppermute | solution.py:238
  28.0 7.2 %query_features.1 = (f32[4,512,256]{2,1,0:T(8,128)}, bf16[4,4,256,128]{3,2,1,0:T(8,128)(2,1)}, bf16[4,4,256,256]{3,2,1,0:T(8,128)(2,1)}, f32[1024,128]{1,0:T(8,1...) custom-call(s32[11]{0:T(128)S(1)} %concatenate.6.info, bf16[128,4096]{1,0:T(8,128)(2,1)} %bitcast.53, ...), custom_call_target="tpu_custom_call" | custom-call | tf_op jit(solution)/shard_map/query_features/pallas_call | solution.py:438
  37.4 5.2 %collective-permute-done.6.refs_12_ = f32[1024,128]{1,0:T(8,128)S(1)} collective-permute-done((f32[1024,128]{1,0:T(8,128)}, f32[1024,128]{1,0:T(8,128)S(1)}, u32[]{:S(2)}, u32[]{:S(2)}) %collective-permute-start.6) | collective-permute-done | bytes 524320 | tf_op jit(solution)/shard_map/ppermute | solution.py:238
  46.2 2.1 %collective-permute-done.9.refs_7_ = f32[1024,128]{1,0:T(8,128)S(1)} collective-permute-done((f32[1024,128]{1,0:T(8,128)}, f32[1024,128]{1,0:T(8,128)S(1)}, u32[]{:S(2)}, u32[]{:S(2)}) %collective-permute-start.9) | collective-permute-done | bytes 524320 | tf_op jit(solution)/shard_map/ppermute | solution.py:238
  54.3 10.5 %attend.1 = (bf16[128,4096]{1,0:T(8,128)(2,1)}, f32[128,2048]{1,0:T(8,128)}, f32[4,1,512]{2,1,0:T(1,128)}, f32[4,256,128]{2,1,0:T(8,128)}, f32[4,512,256]{2,1,0:T(8,128)}) custom-call(s32[11]{0:T(128)S(1)} %concatenate.6.info, bf16[128,4096]{1,0:T(8,128)(2,1)} %bitcast.54, f32[128,2048]{1,0:T(8,128)} %copy-done.1, bf16[128,4096]{1,0:T(8,128)(2,1)} %bitcast.57, ...), custom_call_target="tpu_custom_call" | custom-call | tf_op jit(solution)/shard_map/attend/pallas_call | solution.py:438
  64.8 14.7 %collective-permute-start.14 = (f32[4,1,512]{2,1,0:T(1,128)}, f32[4,1,512]{2,1,0:T(1,128)S(1)}, u32[]{:S(2)}, u32[]{:S(2)}) collective-permute-start(f32[4,1,512]{2,1,0:T(1,128)} %get-tuple-element.68), channel_id=1, source_target_pairs={{0,2},{1,3},{2,0},{3,1},{4,6},{5,7},{6,4},{7,5},{8,10},{9,11},{10,... | collective-permute-start | bytes 24584 | tf_op jit(solution)/shard_map/ppermute | solution.py:238
  79.5 3.1 %collective-permute-start.15 = (f32[4,1,512]{2,1,0:T(1,128)}, f32[4,1,512]{2,1,0:T(1,128)S(1)}, u32[]{:S(2)}, u32[]{:S(2)}) collective-permute-start(f32[4,1,512]{2,1,0:T(1,128)} %get-tuple-element.68), channel_id=1, source_target_pairs={{0,4},{1,5},{2,6},{3,7},{4,0},{5,1},{6,2},{7,3},{8,12},{9,13},{10,... | collective-permute-start | bytes 24584 | tf_op jit(solution)/shard_map/ppermute | solution.py:238
  82.6 6.0 %collective-permute-done.15 = f32[4,1,512]{2,1,0:T(1,128)S(1)} collective-permute-done((f32[4,1,512]{2,1,0:T(1,128)}, f32[4,1,512]{2,1,0:T(1,128)S(1)}, u32[]{:S(2)}, u32[]{:S(2)}) %collective-permute-start.15) | collective-permute-done | bytes 8224 | tf_op jit(solution)/shard_map/ppermute | solution.py:238
  88.6 4.9 %collective-permute-start.13 = (f32[128,2048]{1,0:T(8,128)}, f32[128,2048]{1,0:T(8,128)S(1)}, u32[]{:S(2)}, u32[]{:S(2)}) collective-permute-start(f32[128,2048]{1,0:T(8,128)} %get-tuple-element.65), channel_id=1, source_target_pairs={{0,1},{1,0},{2,3},{3,2},{4,5},{5,4},{6,7},{7,6},{8,9},{9,8},{10,11... | collective-permute-start | bytes 3145736 | tf_op jit(solution)/shard_map/ppermute | solution.py:234
  97.8 5.6 %key_grads.1 = f32[4,256,128]{2,1,0:T(8,128)} custom-call(s32[11]{0:T(128)S(1)} %concatenate.6.info, bf16[128,1024]{1,0:T(8,128)(2,1)} %bitcast.62, f32[256,512]{1,0:T(8,128)} %copy-done, bf16[128,1024]{1,0:T(8,128)(2,1)} %bitcast.60, f32[256,512]{1,0:T(8,128)} %copy-done, f32[4,512,256]{2,1,0:T(8,128)} %get-tuple-element.73.refs_4_, ...), custom_call_target="tpu_custom_call" | custom-call | tf_op jit(solution)/shard_map/key_grads/pallas_call | solution.py:438
  109.7 2.5 %attended.1 = bf16[128,4096]{1,0:T(8,128)(2,1)} custom-call(s32[11]{0:T(128)S(1)} %concatenate.6.info, f32[128,2048]{1,0:T(8,128)} %copy-done.7, bf16[128,4096]{1,0:T(8,128)(2,1)} %get-tuple-element.66.refs_1_), custom_call_target="tpu_custom_call", output_to_operand_aliasing={{}: (2, {})} | custom-call | tf_op jit(solution)/shard_map/attended/pallas_call | solution.py:438
  112.2 2.3 %collective-permute-done.31 = f32[1,256,128]{2,1,0:T(8,128)S(1)} collective-permute-done((f32[1,256,128]{2,1,0:T(8,128)S(1)}, f32[1,256,128]{2,1,0:T(8,128)S(1)}, u32[]{:S(2)}, u32[]{:S(2)}) %collective-permute-start.31) | collective-permute-done | bytes 131104 | tf_op jit(solution)/shard_map/ppermute | solution.py:314
  117.7 1.7 %collective-permute-done.32 = f32[1,256,128]{2,1,0:T(8,128)S(1)} collective-permute-done((f32[1,256,128]{2,1,0:T(8,128)S(1)}, f32[1,256,128]{2,1,0:T(8,128)S(1)}, u32[]{:S(2)}, u32[]{:S(2)}) %collective-permute-start.32) | collective-permute-done | bytes 131104 | tf_op jit(solution)/shard_map/ppermute | solution.py:238
  119.4 1.9 %collective-permute-start.24 = (f32[1,256,128]{2,1,0:T(8,128)S(1)}, f32[1,256,128]{2,1,0:T(8,128)S(1)}, u32[]{:S(2)}, u32[]{:S(2)}) collective-permute-start(f32[1,256,128]{2,1,0:T(8,128)S(1)} %add.101), channel_id=1, source_target_pairs={{0,24},{8,16},{16,8},{24,0},{1,25},{9,17},{17,9},{25,1},{2,26},{10... | collective-permute-start | bytes 393224 | tf_op jit(solution)/shard_map/ppermute | solution.py:327
  121.3 4.2 %collective-permute-start.25 = (f32[1,256,128]{2,1,0:T(8,128)S(1)}, f32[1,256,128]{2,1,0:T(8,128)S(1)}, u32[]{:S(2)}, u32[]{:S(2)}) collective-permute-start(f32[1,256,128]{2,1,0:T(8,128)S(1)} %add.101), channel_id=1, source_target_pairs={{0,1},{1,0},{2,3},{3,2},{4,5},{5,4},{6,7},{7,6},{8,9},{9,8},{10,11... | collective-permute-start | bytes 393224 | tf_op jit(solution)/shard_map/ppermute | solution.py:234
  129.1 3.4 %collective-permute-start.28 = (f32[1,256,128]{2,1,0:T(8,128)S(1)}, f32[1,256,128]{2,1,0:T(8,128)S(1)}, u32[]{:S(2)}, u32[]{:S(2)}) collective-permute-start(f32[1,256,128]{2,1,0:T(8,128)S(1)} %collective-permute-done.24), channel_id=1, source_target_pairs={{0,1},{1,0},{2,3},{3,2},{4,5},{5,4},{6,7},{7,6},{8,9},{9,8},{10,11... | collective-permute-start | bytes 393224 | tf_op jit(solution)/shard_map/ppermute | solution.py:234
  132.6 1.9 %collective-permute-start.38 = (f32[1,256,128]{2,1,0:T(8,128)S(1)}, f32[1,256,128]{2,1,0:T(8,128)S(1)}, u32[]{:S(2)}, u32[]{:S(2)}) collective-permute-start(f32[1,256,128]{2,1,0:T(8,128)S(1)} %collective-permute-done.34), channel_id=1, source_target_pairs={{0,1},{1,0},{2,3},{3,2},{4,5},{5,4},{6,7},{7,6},{8,9},{9,8},{10,11... | collective-permute-start | bytes 393224 | tf_op jit(solution)/shard_map/ppermute | solution.py:234
  135.3 1.6 %collective-permute-start.40 = (f32[1,256,128]{2,1,0:T(8,128)S(1)}, f32[1,256,128]{2,1,0:T(8,128)S(1)}, u32[]{:S(2)}, u32[]{:S(2)}) collective-permute-start(f32[1,256,128]{2,1,0:T(8,128)S(1)} %collective-permute-done.36), channel_id=1, source_target_pairs={{0,1},{1,0},{2,3},{3,2},{4,5},{5,4},{6,7},{7,6},{8,9},{9,8},{10,11... | collective-permute-start | bytes 393224 | tf_op jit(solution)/shard_map/ppermute | solution.py:234
  138.5 1.6 %key_out.1 = f32[8,256,128]{2,1,0:T(8,128)} custom-call(s32[11]{0:T(128)S(1)} %concatenate.6.info, f32[256,128]{1,0:T(8,128)S(1)} %bitcast.37, f32[256,128]{1,0:T(8,128)S(1)} %bitcast.42, f32[256,128]{1,0:T(8,128)S(1)} %bitcast.44, f32[256,128]{1,0:T(8,128)S(1)} %bitcast.46, f32[256,128]{1,0:T(8,128)S(1)} %bitcast.47, f32[256,128]{1,0:T(8,128)S(1)} %bitcast.48, ...), custom_call_target="tpu_custom_call" | custom-call | tf_op jit(solution)/shard_map/key_out/pallas_call | solution.py:561
  (110 shorter events, 39.1 us)
Async XLA Ops:
  10.0 16.7 %collective-permute-start.1 = (f32[128,2048]{1,0:T(8,128)}, f32[128,2048]{1,0:T(8,128)S(1)}, u32[]{:S(2)}, u32[]{:S(2)}) collective-permute-start(f32[128,2048]{1,0:T(8,128)} %get-tuple-element.42), channel_id=1, source_target_pairs={{0,1},{1,0},{2,3},{3,2},{4,5},{5,4},{6,7},{7,6},{8,9},{9,8},{10,11... | collective-permute-start | bytes 3145736 | tf_op jit(solution)/shard_map/ppermute | solution.py:234
  10.2 16.5 %collective-permute-start.2 = (f32[128,2048]{1,0:T(8,128)}, f32[128,2048]{1,0:T(8,128)S(1)}, u32[]{:S(2)}, u32[]{:S(2)}) collective-permute-start(f32[128,2048]{1,0:T(8,128)} %get-tuple-element.43), channel_id=1, source_target_pairs={{0,1},{1,0},{2,3},{3,2},{4,5},{5,4},{6,7},{7,6},{8,9},{9,8},{10,11... | collective-permute-start | bytes 3145736 | tf_op jit(solution)/shard_map/ppermute | solution.py:234
  19.2 18.2 %collective-permute-start.5 = (f32[1024,128]{1,0:T(8,128)}, f32[1024,128]{1,0:T(8,128)S(1)}, u32[]{:S(2)}, u32[]{:S(2)}) collective-permute-start(f32[1024,128]{1,0:T(8,128)} %get-tuple-element.52), channel_id=1, source_target_pairs={{0,2},{1,3},{2,4},{3,5},{4,6},{5,7},{8,10},{9,11},{10,12},{11,13},... | collective-permute-start | bytes 1572872 | tf_op jit(solution)/shard_map/ppermute | solution.py:238
  22.5 20.0 %collective-permute-start.6 = (f32[1024,128]{1,0:T(8,128)}, f32[1024,128]{1,0:T(8,128)S(1)}, u32[]{:S(2)}, u32[]{:S(2)}) collective-permute-start(f32[1024,128]{1,0:T(8,128)} %get-tuple-element.57), channel_id=1, source_target_pairs={{0,4},{1,5},{8,12},{9,13},{16,20},{17,21},{24,28},{25,29}} | collective-permute-start | bytes 1572872 | tf_op jit(solution)/shard_map/ppermute | solution.py:238
  35.2 11.0 %collective-permute-start.10 = (f32[1024,128]{1,0:T(8,128)}, f32[1024,128]{1,0:T(8,128)S(1)}, u32[]{:S(2)}, u32[]{:S(2)}) collective-permute-start(f32[1024,128]{1,0:T(8,128)} %get-tuple-element.59), channel_id=1, source_target_pairs={{6,2},{7,3},{14,10},{15,11},{22,18},{23,19},{30,26},{31,27}} | collective-permute-start | bytes 1572872 | tf_op jit(solution)/shard_map/ppermute | solution.py:238
  36.0 12.3 %collective-permute-start.9 = (f32[1024,128]{1,0:T(8,128)}, f32[1024,128]{1,0:T(8,128)S(1)}, u32[]{:S(2)}, u32[]{:S(2)}) collective-permute-start(f32[1024,128]{1,0:T(8,128)} %get-tuple-element.55), channel_id=1, source_target_pairs={{6,4},{7,5},{4,2},{5,3},{2,0},{3,1},{14,12},{15,13},{12,10},{13,11... | collective-permute-start | bytes 1572872 | tf_op jit(solution)/shard_map/ppermute | solution.py:238
  44.1 9.2 %collective-permute-start.7 = (f32[1024,128]{1,0:T(8,128)S(1)}, f32[1024,128]{1,0:T(8,128)S(1)}, u32[]{:S(2)}, u32[]{:S(2)}) collective-permute-start(f32[1024,128]{1,0:T(8,128)S(1)} %select_select_fusion.1), channel_id=1, source_target_pairs={{0,2},{1,3},{2,4},{3,5},{4,6},{5,7},{8,10},{9,11},{10,12},{11,13},... | collective-permute-start | bytes 1572872 | tf_op jit(solution)/shard_map/ppermute | solution.py:238
  45.5 7.9 %collective-permute-start.8 = (f32[1024,128]{1,0:T(8,128)S(1)}, f32[1024,128]{1,0:T(8,128)S(1)}, u32[]{:S(2)}, u32[]{:S(2)}) collective-permute-start(f32[1024,128]{1,0:T(8,128)S(1)} %select_select_fusion.1), channel_id=1, source_target_pairs={{2,6},{3,7},{10,14},{11,15},{18,22},{19,23},{26,30},{27,31}} | collective-permute-start | bytes 1572872 | tf_op jit(solution)/shard_map/ppermute | solution.py:238
  49.3 39.3 %collective-permute-start.11 = (f32[1024,128]{1,0:T(8,128)}, f32[1024,128]{1,0:T(8,128)S(1)}, u32[]{:S(2)}, u32[]{:S(2)}) collective-permute-start(f32[1024,128]{1,0:T(8,128)} %select_select_fusion), channel_id=1, source_target_pairs={{6,4},{7,5},{4,2},{5,3},{2,0},{3,1},{14,12},{15,13},{12,10},{13,11... | collective-permute-start | bytes 1572872 | tf_op jit(solution)/shard_map/ppermute | solution.py:238
  50.6 38.0 %collective-permute-start.12 = (f32[1024,128]{1,0:T(8,128)}, f32[1024,128]{1,0:T(8,128)S(1)}, u32[]{:S(2)}, u32[]{:S(2)}) collective-permute-start(f32[1024,128]{1,0:T(8,128)} %select_select_fusion), channel_id=1, source_target_pairs={{4,0},{5,1},{12,8},{13,9},{20,16},{21,17},{28,24},{29,25}} | collective-permute-start | bytes 1572872 | tf_op jit(solution)/shard_map/ppermute | solution.py:238
  64.8 17.8 %collective-permute-start.14 = (f32[4,1,512]{2,1,0:T(1,128)}, f32[4,1,512]{2,1,0:T(1,128)S(1)}, u32[]{:S(2)}, u32[]{:S(2)}) collective-permute-start(f32[4,1,512]{2,1,0:T(1,128)} %get-tuple-element.68), channel_id=1, source_target_pairs={{0,2},{1,3},{2,0},{3,1},{4,6},{5,7},{6,4},{7,5},{8,10},{9,11},{10,... | collective-permute-start | bytes 24584 | tf_op jit(solution)/shard_map/ppermute | solution.py:238
  79.5 9.1 %collective-permute-start.15 = (f32[4,1,512]{2,1,0:T(1,128)}, f32[4,1,512]{2,1,0:T(1,128)S(1)}, u32[]{:S(2)}, u32[]{:S(2)}) collective-permute-start(f32[4,1,512]{2,1,0:T(1,128)} %get-tuple-element.68), channel_id=1, source_target_pairs={{0,4},{1,5},{2,6},{3,7},{4,0},{5,1},{6,2},{7,3},{8,12},{9,13},{10,... | collective-permute-start | bytes 24584 | tf_op jit(solution)/shard_map/ppermute | solution.py:238
  88.6 20.1 %collective-permute-start.13 = (f32[128,2048]{1,0:T(8,128)}, f32[128,2048]{1,0:T(8,128)S(1)}, u32[]{:S(2)}, u32[]{:S(2)}) collective-permute-start(f32[128,2048]{1,0:T(8,128)} %get-tuple-element.65), channel_id=1, source_target_pairs={{0,1},{1,0},{2,3},{3,2},{4,5},{5,4},{6,7},{7,6},{8,9},{9,8},{10,11... | collective-permute-start | bytes 3145736 | tf_op jit(solution)/shard_map/ppermute | solution.py:234
  95.1 8.3 %collective-permute-start.17 = (f32[1,256,128]{2,1,0:T(8,128)S(1)}, f32[1,256,128]{2,1,0:T(8,128)S(1)}, u32[]{:S(2)}, u32[]{:S(2)}) collective-permute-start(f32[1,256,128]{2,1,0:T(8,128)S(1)} %get-tuple-element.86), channel_id=1, source_target_pairs={{0,8},{8,0},{16,24},{24,16},{1,9},{9,1},{17,25},{25,17},{2,10},{10... | collective-permute-start | bytes 393224 | tf_op jit(solution)/shard_map/ppermute | solution.py:314
  96.4 7.1 %collective-permute-start.18 = (f32[1,256,128]{2,1,0:T(8,128)S(1)}, f32[1,256,128]{2,1,0:T(8,128)S(1)}, u32[]{:S(2)}, u32[]{:S(2)}) collective-permute-start(f32[1,256,128]{2,1,0:T(8,128)S(1)} %get-tuple-element.85), channel_id=1, source_target_pairs={{0,16},{8,24},{16,0},{24,8},{1,17},{9,25},{17,1},{25,9},{2,18},{10... | collective-permute-start | bytes 393224 | tf_op jit(solution)/shard_map/ppermute | solution.py:314
  108.5 8.1 %collective-permute-start.21 = (f32[1,256,128]{2,1,0:T(8,128)S(1)}, f32[1,256,128]{2,1,0:T(8,128)S(1)}, u32[]{:S(2)}, u32[]{:S(2)}) collective-permute-start(f32[1,256,128]{2,1,0:T(8,128)S(1)} %add.100), channel_id=1, source_target_pairs={{0,4},{1,5},{2,6},{3,7},{4,0},{5,1},{6,2},{7,3},{8,12},{9,13},{10,... | collective-permute-start | bytes 393224 | tf_op jit(solution)/shard_map/ppermute | solution.py:238
  116.7 8.8 %collective-permute-start.22 = (f32[1,256,128]{2,1,0:T(8,128)S(1)}, f32[1,256,128]{2,1,0:T(8,128)S(1)}, u32[]{:S(2)}, u32[]{:S(2)}) collective-permute-start(f32[1,256,128]{2,1,0:T(8,128)S(1)} %add.101), channel_id=1, source_target_pairs={{0,8},{8,0},{16,24},{24,16},{1,9},{9,1},{17,25},{25,17},{2,10},{10... | collective-permute-start | bytes 393224 | tf_op jit(solution)/shard_map/ppermute | solution.py:327
  117.6 7.9 %collective-permute-start.23 = (f32[1,256,128]{2,1,0:T(8,128)S(1)}, f32[1,256,128]{2,1,0:T(8,128)S(1)}, u32[]{:S(2)}, u32[]{:S(2)}) collective-permute-start(f32[1,256,128]{2,1,0:T(8,128)S(1)} %add.101), channel_id=1, source_target_pairs={{0,16},{8,24},{16,0},{24,8},{1,17},{9,25},{17,1},{25,9},{2,18},{10... | collective-permute-start | bytes 393224 | tf_op jit(solution)/shard_map/ppermute | solution.py:327
  119.3 7.1 %collective-permute-start.33 = (f32[1,256,128]{2,1,0:T(8,128)S(1)}, f32[1,256,128]{2,1,0:T(8,128)S(1)}, u32[]{:S(2)}, u32[]{:S(2)}) collective-permute-start(f32[1,256,128]{2,1,0:T(8,128)S(1)} %add.105), channel_id=1, source_target_pairs={{0,4},{1,5},{2,6},{3,7},{4,0},{5,1},{6,2},{7,3},{8,12},{9,13},{10,... | collective-permute-start | bytes 393224 | tf_op jit(solution)/shard_map/ppermute | solution.py:238
  119.4 8.1 %collective-permute-start.24 = (f32[1,256,128]{2,1,0:T(8,128)S(1)}, f32[1,256,128]{2,1,0:T(8,128)S(1)}, u32[]{:S(2)}, u32[]{:S(2)}) collective-permute-start(f32[1,256,128]{2,1,0:T(8,128)S(1)} %add.101), channel_id=1, source_target_pairs={{0,24},{8,16},{16,8},{24,0},{1,25},{9,17},{17,9},{25,1},{2,26},{10... | collective-permute-start | bytes 393224 | tf_op jit(solution)/shard_map/ppermute | solution.py:327
  125.5 7.0 %collective-permute-start.27 = (f32[1,256,128]{2,1,0:T(8,128)S(1)}, f32[1,256,128]{2,1,0:T(8,128)S(1)}, u32[]{:S(2)}, u32[]{:S(2)}) collective-permute-start(f32[1,256,128]{2,1,0:T(8,128)S(1)} %collective-permute-done.23), channel_id=1, source_target_pairs={{0,1},{1,0},{2,3},{3,2},{4,5},{5,4},{6,7},{7,6},{8,9},{9,8},{10,11... | collective-permute-start | bytes 393224 | tf_op jit(solution)/shard_map/ppermute | solution.py:234
  127.5 7.1 %collective-permute-start.35 = (f32[1,256,128]{2,1,0:T(8,128)S(1)}, f32[1,256,128]{2,1,0:T(8,128)S(1)}, u32[]{:S(2)}, u32[]{:S(2)}) collective-permute-start(f32[1,256,128]{2,1,0:T(8,128)S(1)} %add.106), channel_id=1, source_target_pairs={{0,16},{8,24},{16,0},{24,8},{1,17},{9,25},{17,1},{25,9},{2,18},{10... | collective-permute-start | bytes 393224 | tf_op jit(solution)/shard_map/ppermute | solution.py:327
  128.2 7.1 %collective-permute-start.36 = (f32[1,256,128]{2,1,0:T(8,128)S(1)}, f32[1,256,128]{2,1,0:T(8,128)S(1)}, u32[]{:S(2)}, u32[]{:S(2)}) collective-permute-start(f32[1,256,128]{2,1,0:T(8,128)S(1)} %add.106), channel_id=1, source_target_pairs={{0,24},{8,16},{16,8},{24,0},{1,25},{9,17},{17,9},{25,1},{2,26},{10... | collective-permute-start | bytes 393224 | tf_op jit(solution)/shard_map/ppermute | solution.py:327
  129.1 7.8 %collective-permute-start.28 = (f32[1,256,128]{2,1,0:T(8,128)S(1)}, f32[1,256,128]{2,1,0:T(8,128)S(1)}, u32[]{:S(2)}, u32[]{:S(2)}) collective-permute-start(f32[1,256,128]{2,1,0:T(8,128)S(1)} %collective-permute-done.24), channel_id=1, source_target_pairs={{0,1},{1,0},{2,3},{3,2},{4,5},{5,4},{6,7},{7,6},{8,9},{9,8},{10,11... | collective-permute-start | bytes 393224 | tf_op jit(solution)/shard_map/ppermute | solution.py:234
  (31 other events, 186.8 us)

commit v8 on v7

--- a/solution.py
+++ b/solution.py
@@ -140,7 +140,7 @@
 
 def attend_kernel(
     n, step, info, q_ref, qg_ref, c_ref, cg_ref, v_ref, vg_ref, kb_ref, qp_ref, qr_ref, wt_ref, pn_ref,
-    near, far, near2, far2, att_ref, atg_ref, sn_ref, gq_ref, gk_ref,
+    near, far, near2, far2, att_ref, atg_ref, sn_ref, gk_ref, gq_ref,
 ):
     group, length, dim = qr_ref.shape[1:]
     feats = dim
@@ -199,7 +199,7 @@
     probs = [qp_ref[0, r] for r in rows]
     back = [soft_back(probs[i], upstream_q[i]) for i in heads]
     for i in heads:
-        gq_ref[0, i * width : (i + 1) * width] = mm(back[i], queries[:, cols[i]])
+        gq_ref[i * width : (i + 1) * width] = mm(back[i], queries[:, cols[i]])
         gk_ref[0, rows[i]] = mm(probs[i].astype(BF), block[i])
 
 
@@ -216,7 +216,7 @@
         soft_back(kp_ref[0, a : a + feats], upstream[a : a + feats])
         for a in range(0, rows, feats)
     ]
-    out_ref[0] = mm(stack(*back), tokens_of(k_ref, kg_ref))
+    out_ref[...] = mm(stack(*back), tokens_of(k_ref, kg_ref))
 
 
 def attended_kernel(n, i, info, x_ref, o_ref):
@@ -224,9 +224,10 @@
 
 
 def out_kernel(info, *refs):
-    out_ref = refs[-1]
-    for i, ref in enumerate(refs[:-1]):
-        out_ref[info[i]] = ref[...]
+    count = len(refs) // 2 - 1
+    for out_ref, pieces in zip(refs[-2:], (refs[:count], refs[count:-2])):
+        for i, ref in enumerate(pieces):
+            out_ref[info[i]] = ref[...]
 
 
 def core_swap(x):
@@ -309,14 +310,16 @@
 
 def sum_all(mine, chips, *earlier):
     dp = lax.axis_size("dp")
-    share = mine.shape[0] // dp
-    got = [
-        lax.ppermute(mine[k * share : (k + 1) * share], "dp", [(i, i ^ k) for i in range(dp)])
-        for k in range(1, dp)
+    share = len(mine) // dp
+    rows = mine[0].shape[0]
+    blocks = [
+        jnp.concatenate(mine[k * share : (k + 1) * share]) if share > 1 else mine[k]
+        for k in range(dp)
     ]
+    got = [lax.ppermute(blocks[k], "dp", [(i, i ^ k) for i in range(dp)]) for k in range(1, dp)]
     if earlier:
         got = after(got, *earlier)
-    total = mine[:share]
+    total = blocks[0]
     for piece in got:
         total = total + piece
     bit = 1
@@ -327,7 +330,7 @@
         lax.ppermute(total, "dp", [(i, i ^ k) for i in range(dp)]) for k in range(1, dp)
     ]
     pieces = pieces + [core_swap(x) for x in pieces]
-    return [x[i] for x in pieces for i in range(share)]
+    return [x[a : a + rows] if share > 1 else x for x in pieces for a in range(0, share * rows, rows)]
 
 
 def shards(queries, key_tokens, value_tokens, cotangent, query_map, key_map):
@@ -380,6 +383,13 @@
                 for p, size in zip(places, spec.block_shape)
             )
         ]
+
+    in_hbm = [queries, cotangent, keys, values, query_map, key_map]
+
+    def pinned(x):
+        if any(x is y for y in in_hbm):
+            return pltpu.with_memory_space_constraint(x, pltpu.HBM)
+        return x
 
     def call(name, body, in_specs, out_specs, out_shape, aliases=None):
         in_specs = [x if isinstance(x, tuple) else (x, n) for x in in_specs]
@@ -448,9 +458,18 @@
                 ],
                 input_output_aliases=aliases or {},
                 compiler_params=pltpu.CompilerParams(vmem_limit_bytes=VMEM_LIMIT),
-            )(info, *[pltpu.with_memory_space_constraint(x, pltpu.HBM) for x in arrays])
-
-        return run
+            )(info, *[pinned(x) for x in arrays])
+
+        def remember(*arrays):
+            made = run(*arrays)
+            in_hbm.extend(made)
+            return made
+
+        return remember
+
+    def spread(which):
+        whole = spec((group * width, dim), lambda i, info: (0, 0))
+        return [(whole, which, lambda i, info, k=k: i == k) for k in range(n)]
 
     def always(i, info):
         return True
@@ -515,36 +534,35 @@
     before = after(before, suffix.payload)
     later = suffix.second()
 
-    grad_spec, grad = per_head(group * width, dim), shape_of(group * width, dim)
-    attended, attended_got, norm, query_part, key_up = call(
+    grad = jax.ShapeDtypeStruct((group * width, dim), F32)
+    attended, attended_got, norm, key_up, *query_part = call(
         "attend",
         attend_kernel,
         [own_cols(four), got_cols(four)] * 2
         + [own_cols(one), got_values, flat_spec, flat_spec, rows_spec]
         + [per_head(group, length, length), row_spec]
         + [moved_spec] * 4,
-        each(own_cols(four), got_cols(four), row_spec, grad_spec, flat_spec),
+        each(own_cols(four), got_cols(four), row_spec, flat_spec) + spread(4),
         [
             jax.ShapeDtypeStruct((own, head_count * dim), BF),
             jax.ShapeDtypeStruct((own, n * four), F32),
             row,
-            grad,
             flat,
-        ],
+        ]
+        + [grad] * n,
     )(
         queries, queries_got, cotangent, cotangent_got, values, values_got, key_features,
         query_probs, query_rows, weights, prefix_norm, *before,
     )
-    suffix_norm = scan_norms(norm, chip, chips, False, query_part)
-    query_part = after(query_part, suffix_norm)
-    (key_part,) = call(
+    suffix_norm = scan_norms(norm, chip, chips, False, *query_part)
+    key_part = call(
         "key_grads",
         key_grad_kernel,
         [own_cols(one), got_keys, own_cols(one), got_values]
         + [flat_spec, flat_spec, row_spec]
         + [moved_spec] * 4,
-        each(grad_spec),
-        [grad],
+        spread(0),
+        [grad] * n,
     )(keys, keys_got, values, values_got, key_probs, key_up, suffix_norm, *later)
     (attended,) = call(
         "attended",
@@ -553,23 +571,22 @@
         each(other_cols(four)),
         [jax.ShapeDtypeStruct((own, head_count * dim), BF)],
         aliases={2: 0},
-    )(core_swap(after(attended_got, *later)), attended)
-
-    def finish(name, mine, *earlier):
-        pieces = sum_all(mine, chips, *earlier)
-        whole = pl.BlockSpec(memory_space=pltpu.VMEM)
-        natural = pl.pallas_call(
-            out_kernel,
-            name=name,
-            out_shape=jax.ShapeDtypeStruct((shared, group * width, dim), F32),
-            in_specs=[pl.BlockSpec(memory_space=pltpu.SMEM)] + [whole] * shared,
-            out_specs=whole,
-            compiler_params=pltpu.CompilerParams(vmem_limit_bytes=VMEM_LIMIT),
-        )(info, *pieces)
-        return jnp.swapaxes(natural.reshape(head_count, width, dim), 1, 2)
-
-    query_grad = finish("query_out", query_part, key_part)
-    key_grad = finish("key_out", key_part, attended)
+    )(core_swap(after(attended_got, suffix_norm, *later)), attended)
+
+    key_pieces = sum_all(key_part, chips, attended)
+    query_pieces = sum_all(after(query_part, suffix_norm), chips, *key_part)
+    whole = pl.BlockSpec(memory_space=pltpu.VMEM)
+    sums = pl.pallas_call(
+        out_kernel,
+        name="sums_out",
+        out_shape=[jax.ShapeDtypeStruct((shared, group * width, dim), F32)] * 2,
+        in_specs=[pl.BlockSpec(memory_space=pltpu.SMEM)] + [whole] * (2 * shared),
+        out_specs=[whole] * 2,
+        compiler_params=pltpu.CompilerParams(vmem_limit_bytes=VMEM_LIMIT),
+    )(info, *query_pieces, *key_pieces)
+    query_grad, key_grad = [
+        jnp.swapaxes(x.reshape(head_count, width, dim), 1, 2) for x in sums
+    ]
     return attended.reshape(1, own, head_count * dim), query_grad, key_grad
 
 

time: 141 us -> 137 us (0.972)
  local copies, waits for them, and re-layouts: 7.29 us -> 1.09 us
  waiting for transfers between devices: 23 us -> 27 us
  starting transfers between devices: 68 us -> 70.7 us
  Pallas kernels: 34.4 us -> 31.7 us
  other arithmetic: 6.45 us -> 4.59 us
    unnamed x28 -> x8, local copies, waits for them, and re-layouts: 4.1 us -> 0.02 us
    ppermute x6, starting transfers between devices: 5.59 us -> 8.08 us  [sum_all(): lax.ppermute(total, 'dp', [(i, i ^ k) for i in range(dp)])]
    slice x2 -> x0, local copies, waits for them, and re-layouts: 2.11 us -> none  [sum_all(): mine[k * share:(k + 1) * share]]
    add x2, other arithmetic: 1.89 us -> 0.07 us  [sum_all(): total = total + piece]
    pallas_call x5, Pallas kernels: 31.2 us -> 29.7 us  [run(): pl.pallas_call(kernel, name=name, out_shape=[pltpu.HBM(x.shape, x.dtype)...]
    pallas_call x2 -> x1, Pallas kernels: 3.17 us -> 2 us  [shards(): pl.pallas_call(out_kernel, name='sums_out', out_shape=[jax.ShapeDtypeStru...]
  transfers between devices with their start and end apart: 41 -> 41, of which waited for: 10 -> 15; matrix products, arithmetic and copies ran while one was open for 6% -> 3% of each run, Pallas kernels for 19% -> 18%
where the time goes in v8:
time: 137 us; the launch traced here: 136 us
  starting transfers between devices  70.7 us (52%)
  Pallas kernels  31.7 us (23%)
  waiting for transfers between devices  27 us (20%)
  other arithmetic  4.59 us (3%)
    ppermute x17, starting transfers between devices, chip_move(): lax.ppermute(x, 'ctx', [(2 * a + c, 2 * b + c) for a, b in pairs for c in...  39.5 us
    pallas_call x5, Pallas kernels, run(): pl.pallas_call(kernel, name=name, out_shape=[pltpu.HBM(x.shape, x.dtype)...  29.7 us
    ppermute x17, waiting for transfers between devices, chip_move(): lax.ppermute(x, 'ctx', [(2 * a + c, 2 * b + c) for a, b in pairs for c in...  19.8 us
    ppermute x12, starting transfers between devices, core_swap(): return lax.ppermute(x, 'ctx', [(i, i ^ 1) for i in range(size)])  17.8 us
    ppermute x6, starting transfers between devices, sum_all(): lax.ppermute(total, 'dp', [(i, i ^ k) for i in range(dp)])  8.08 us
    ppermute x6, starting transfers between devices, sum_all(): lax.ppermute(blocks[k], 'dp', [(i, i ^ k) for i in range(dp)])  5.38 us
    select_n x2, other arithmetic, turn_around(): jnp.where(self.place == 1, a + self.near, jnp.where(self.place == 2, b +...  3.66 us
    ppermute x6, waiting for transfers between devices, sum_all(): lax.ppermute(blocks[k], 'dp', [(i, i ^ k) for i in range(dp)])  3.4 us
  transfers between devices with their start and end apart: 41, of which 15 were waited for; matrix products, arithmetic and copies ran while one was open for 3% of the time, Pallas kernels for 18%

profile of v8, /device:TPU:1, one launch (start us, length us, event | category | flops | bytes accessed | tf_op | source)
XLA Modules:
  0.0 136.0 jit_solution(4197515712175615496)
XLA Ops:
  1.9 1.8 %collective-permute-done.refs_1_.refs_3_.refs_5_ = f32[256,512]{1,0:T(8,128)S(1)} collective-permute-done((f32[256,512]{1,0:T(8,128)S(1)}, f32[256,512]{1,0:T(8,128)S(1)}, u32[]{:S(2)}, u32[]{:S(2)}) %collective-permute-start) | collective-permute-done | bytes 524320 | tf_op jit(solution)/shard_map/ppermute | solution.py:235
  3.7 5.4 %key_features.1 = (f32[4,512,256]{2,1,0:T(8,128)}, bf16[4,512,256]{2,1,0:T(8,128)(2,1)}, f32[4,1,512]{2,1,0:T(1,128)}, f32[1024,128]{1,0:T(8,128)}, f32[1024,128...) custom-call(s32[11]{0:T(128)S(1)} %concatenate.6.info, bf16[128,1024]{1,0:T(8,128)(2,1)} %bitcast.29, ...), custom_call_target="tpu_custom_call" | custom-call | tf_op jit(solution)/shard_map/key_features/pallas_call | solution.py:448
  9.7 2.5 %collective-permute-start.3 = (f32[4,1,512]{2,1,0:T(1,128)}, f32[4,1,512]{2,1,0:T(1,128)S(1)}, u32[]{:S(2)}, u32[]{:S(2)}) collective-permute-start(f32[4,1,512]{2,1,0:T(1,128)} %get-tuple-element.57), channel_id=1, source_target_pairs={{0,2},{1,3},{2,0},{3,1},{4,6},{5,7},{6,4},{7,5},{8,10},{9,11},{10,... | collective-permute-start | bytes 24584 | tf_op jit(solution)/shard_map/ppermute | solution.py:239
  14.2 2.5 %collective-permute-start.4 = (f32[4,1,512]{2,1,0:T(1,128)S(1)}, f32[4,1,512]{2,1,0:T(1,128)S(1)}, u32[]{:S(2)}, u32[]{:S(2)}) collective-permute-start(f32[4,1,512]{2,1,0:T(1,128)S(1)} %add.87), channel_id=1, source_target_pairs={{0,4},{1,5},{2,6},{3,7},{4,0},{5,1},{6,2},{7,3},{8,12},{9,13},{10,... | collective-permute-start | bytes 24584 | tf_op jit(solution)/shard_map/ppermute | solution.py:239
  17.7 4.1 %collective-permute-start.5 = (f32[1024,128]{1,0:T(8,128)}, f32[1024,128]{1,0:T(8,128)}, u32[]{:S(2)}, u32[]{:S(2)}) collective-permute-start(f32[1024,128]{1,0:T(8,128)} %get-tuple-element.64), channel_id=1, source_target_pairs={{0,2},{1,3},{2,4},{3,5},{4,6},{5,7},{8,10},{9,11},{10,12},{11,13},... | collective-permute-start | bytes 1572872 | tf_op jit(solution)/shard_map/ppermute | solution.py:239
  21.8 4.1 %collective-permute-start.6 = (f32[1024,128]{1,0:T(8,128)}, f32[1024,128]{1,0:T(8,128)}, u32[]{:S(2)}, u32[]{:S(2)}) collective-permute-start(f32[1024,128]{1,0:T(8,128)} %get-tuple-element.69), channel_id=1, source_target_pairs={{0,4},{1,5},{8,12},{9,13},{16,20},{17,21},{24,28},{25,29}} | collective-permute-start | bytes 1572872 | tf_op jit(solution)/shard_map/ppermute | solution.py:239
  26.0 7.0 %query_features.1 = (f32[4,512,256]{2,1,0:T(8,128)}, bf16[4,4,256,128]{3,2,1,0:T(8,128)(2,1)}, bf16[4,4,256,256]{3,2,1,0:T(8,128)(2,1)}, f32[1024,128]{1,0:T(8,1...) custom-call(s32[11]{0:T(128)S(1)} %concatenate.6.info, bf16[128,4096]{1,0:T(8,128)(2,1)} %bitcast.21, ...), custom_call_target="tpu_custom_call" | custom-call | tf_op jit(solution)/shard_map/query_features/pallas_call | solution.py:448
  35.1 6.0 %collective-permute-done.6.refs_12_ = f32[1024,128]{1,0:T(8,128)} collective-permute-done((f32[1024,128]{1,0:T(8,128)}, f32[1024,128]{1,0:T(8,128)}, u32[]{:S(2)}, u32[]{:S(2)}) %collective-permute-start.6) | collective-permute-done | bytes 524320 | tf_op jit(solution)/shard_map/ppermute | solution.py:239
  41.1 1.6 %select_select_fusion.1 = f32[1024,128]{1,0:T(8,128)S(1)} fusion(f32[1024,128]{1,0:T(8,128)} %get-tuple-element.69, f32[1024,128]{1,0:T(8,128)} %collective-permute-done.6.refs_12_, f32[1024,128]{1,0:T(8,128)} %collective-permute-done.5.refs_11_, f32[1024,128]{1,0:T(8,128)} %get-tuple-element.68, pred[]{:T(512)S(6)} %eq.15, pred[]{:T(512)S(6)} %eq.14), kind=kLoop, calls=%fused_computation.1 | loop fusion | flops 655360 | bytes 2621442 | tf_op jit(solution)/shard_map/jit(_where)/select_n | solution.py:267
  46.1 2.0 %select_select_fusion = f32[1024,128]{1,0:T(8,128)} fusion(f32[1024,128]{1,0:T(8,128)S(1)} %copy-done.1, f32[1024,128]{1,0:T(8,128)S(1)} %collective-permute-done.10.refs_8_, f32[1024,128]{1,0:T(8,128)} %collective-permute-done.9.refs_7_, f32[1024,128]{1,0:T(8,128)S(1)} %copy-done, pred[]{:T(512)S(6)} %eq.17, pred[]{:T(512)S(6)} %eq.16), kind=kLoop, calls=%fused_computation | loop fusion | flops 655360 | bytes 2621442 | tf_op jit(solution)/shard_map/jit(_where)/select_n | solution.py:267
  51.9 10.3 %attend.1 = (bf16[128,4096]{1,0:T(8,128)(2,1)}, f32[128,2048]{1,0:T(8,128)}, f32[4,1,512]{2,1,0:T(1,128)}, f32[4,512,256]{2,1,0:T(8,128)}, f32[256,128]{1,0:T(8,...) custom-call(s32[11]{0:T(128)S(1)} %concatenate.6.info, bf16[128,4096]{1,0:T(8,128)(2,1)} %bitcast.22, ...), custom_call_target="tpu_custom_call" | custom-call | tf_op jit(solution)/shard_map/attend/pallas_call | solution.py:448
  62.2 15.0 %collective-permute-start.11 = (f32[4,1,512]{2,1,0:T(1,128)}, f32[4,1,512]{2,1,0:T(1,128)S(1)}, u32[]{:S(2)}, u32[]{:S(2)}) collective-permute-start(f32[4,1,512]{2,1,0:T(1,128)} %get-tuple-element.77), channel_id=1, source_target_pairs={{0,2},{1,3},{2,0},{3,1},{4,6},{5,7},{6,4},{7,5},{8,10},{9,11},{10,... | collective-permute-start | bytes 24584 | tf_op jit(solution)/shard_map/ppermute | solution.py:239
  77.2 3.1 %collective-permute-start.12 = (f32[4,1,512]{2,1,0:T(1,128)}, f32[4,1,512]{2,1,0:T(1,128)S(1)}, u32[]{:S(2)}, u32[]{:S(2)}) collective-permute-start(f32[4,1,512]{2,1,0:T(1,128)} %get-tuple-element.77), channel_id=1, source_target_pairs={{0,4},{1,5},{2,6},{3,7},{4,0},{5,1},{6,2},{7,3},{8,12},{9,13},{10,... | collective-permute-start | bytes 24584 | tf_op jit(solution)/shard_map/ppermute | solution.py:239
  80.3 7.3 %collective-permute-done.12 = f32[4,1,512]{2,1,0:T(1,128)S(1)} collective-permute-done((f32[4,1,512]{2,1,0:T(1,128)}, f32[4,1,512]{2,1,0:T(1,128)S(1)}, u32[]{:S(2)}, u32[]{:S(2)}) %collective-permute-start.12) | collective-permute-done | bytes 8224 | tf_op jit(solution)/shard_map/ppermute | solution.py:239
  87.7 3.5 %collective-permute-start.16 = (f32[128,2048]{1,0:T(8,128)}, f32[128,2048]{1,0:T(8,128)S(1)}, u32[]{:S(2)}, u32[]{:S(2)}) collective-permute-start(f32[128,2048]{1,0:T(8,128)} %get-tuple-element.85), channel_id=1, source_target_pairs={{0,1},{1,0},{2,3},{3,2},{4,5},{5,4},{6,7},{7,6},{8,9},{9,8},{10,11... | collective-permute-start | bytes 3145736 | tf_op jit(solution)/shard_map/ppermute | solution.py:235
  93.8 5.4 %key_grads.1 = (f32[256,128]{1,0:T(8,128)}, f32[256,128]{1,0:T(8,128)}, f32[256,128]{1,0:T(8,128)}, f32[256,128]{1,0:T(8,128)}) custom-call(s32[11]{0:T(128)S(1)} %concatenate.6.info, bf16[128,1024]{1,0:T(8,128)(2,1)} %bitcast.30, f32[256,512]{1,0:T(8,128)S(1)} %collective-permute-done.refs_1_.refs_3_.refs_5_, bf16[128,1024]{1,0:T(8,128)(2,1)} %bitcast.28, ...), custom_call_target="tpu_custom_call" | custom-call | tf_op jit(solution)/shard_map/key_grads/pallas_call | solution.py:448
  106.1 2.1 %collective-permute-done.31 = f32[256,128]{1,0:T(8,128)S(1)} collective-permute-done((f32[256,128]{1,0:T(8,128)}, f32[256,128]{1,0:T(8,128)S(1)}, u32[]{:S(2)}, u32[]{:S(2)}) %collective-permute-start.31) | collective-permute-done | bytes 131104 | tf_op jit(solution)/shard_map/ppermute | solution.py:319
  110.2 4.1 %collective-permute-start.22 = (f32[256,128]{1,0:T(8,128)S(1)}, f32[256,128]{1,0:T(8,128)S(1)}, u32[]{:S(2)}, u32[]{:S(2)}) collective-permute-start(f32[256,128]{1,0:T(8,128)S(1)} %add.101.refs_0_), channel_id=1, source_target_pairs={{0,8},{8,0},{16,24},{24,16},{1,9},{9,1},{17,25},{25,17},{2,10},{10... | collective-permute-start | bytes 393224 | tf_op jit(solution)/shard_map/ppermute | solution.py:330
  115.7 1.9 %collective-permute-start.25 = (f32[256,128]{1,0:T(8,128)S(1)}, f32[256,128]{1,0:T(8,128)S(1)}, u32[]{:S(2)}, u32[]{:S(2)}) collective-permute-start(f32[256,128]{1,0:T(8,128)S(1)} %add.101.refs_0_), channel_id=1, source_target_pairs={{0,1},{1,0},{2,3},{3,2},{4,5},{5,4},{6,7},{7,6},{8,9},{9,8},{10,11... | collective-permute-start | bytes 393224 | tf_op jit(solution)/shard_map/ppermute | solution.py:235
  117.6 1.8 %collective-permute-start.26 = (f32[256,128]{1,0:T(8,128)S(1)}, f32[256,128]{1,0:T(8,128)S(1)}, u32[]{:S(2)}, u32[]{:S(2)}) collective-permute-start(f32[256,128]{1,0:T(8,128)S(1)} %collective-permute-done.22.refs_1_), channel_id=1, source_target_pairs={{0,1},{1,0},{2,3},{3,2},{4,5},{5,4},{6,7},{7,6},{8,9},{9,8},{10,11... | collective-permute-start | bytes 393224 | tf_op jit(solution)/shard_map/ppermute | solution.py:235
  119.4 3.7 %collective-permute-start.27 = (f32[256,128]{1,0:T(8,128)S(1)}, f32[256,128]{1,0:T(8,128)S(1)}, u32[]{:S(2)}, u32[]{:S(2)}) collective-permute-start(f32[256,128]{1,0:T(8,128)S(1)} %collective-permute-done.23.refs_2_), channel_id=1, source_target_pairs={{0,1},{1,0},{2,3},{3,2},{4,5},{5,4},{6,7},{7,6},{8,9},{9,8},{10,11... | collective-permute-start | bytes 393224 | tf_op jit(solution)/shard_map/ppermute | solution.py:235
  127.8 2.1 %collective-permute-start.38 = (f32[256,128]{1,0:T(8,128)S(1)}, f32[256,128]{1,0:T(8,128)S(1)}, u32[]{:S(2)}, u32[]{:S(2)}) collective-permute-start(f32[256,128]{1,0:T(8,128)S(1)} %collective-permute-done.34.refs_9_), channel_id=1, source_target_pairs={{0,1},{1,0},{2,3},{3,2},{4,5},{5,4},{6,7},{7,6},{8,9},{9,8},{10,11... | collective-permute-start | bytes 393224 | tf_op jit(solution)/shard_map/ppermute | solution.py:235
  130.0 2.7 %collective-permute-start.39 = (f32[256,128]{1,0:T(8,128)S(1)}, f32[256,128]{1,0:T(8,128)S(1)}, u32[]{:S(2)}, u32[]{:S(2)}) collective-permute-start(f32[256,128]{1,0:T(8,128)S(1)} %collective-permute-done.35.refs_10_), channel_id=1, source_target_pairs={{0,1},{1,0},{2,3},{3,2},{4,5},{5,4},{6,7},{7,6},{8,9},{9,8},{10,11... | collective-permute-start | bytes 393224 | tf_op jit(solution)/shard_map/ppermute | solution.py:235
  134.0 2.0 %sums_out.1 = (f32[8,256,128]{2,1,0:T(8,128)}, f32[8,256,128]{2,1,0:T(8,128)}) custom-call(s32[11]{0:T(128)S(1)} %concatenate.6.info, f32[256,128]{1,0:T(8,128)S(1)} %add.101.refs_0_, f32[256,128]{1,0:T(8,128)S(1)} %collective-permute-done.22.refs_1_, f32[256,128]{1,0:T(8,128)S(1)} %collective-permute-done.23.refs_2_, ...), custom_call_target="tpu_custom_call" | custom-call | tf_op jit(solution)/shard_map/sums_out/pallas_call | solution.py:579
  (87 shorter events, 32.9 us)
Async XLA Ops:
  9.1 16.8 %collective-permute-start.1 = (f32[128,2048]{1,0:T(8,128)}, f32[128,2048]{1,0:T(8,128)S(1)}, u32[]{:S(2)}, u32[]{:S(2)}) collective-permute-start(f32[128,2048]{1,0:T(8,128)} %get-tuple-element.54), channel_id=1, source_target_pairs={{0,1},{1,0},{2,3},{3,2},{4,5},{5,4},{6,7},{7,6},{8,9},{9,8},{10,11... | collective-permute-start | bytes 3145736 | tf_op jit(solution)/shard_map/ppermute | solution.py:235
  9.3 16.6 %collective-permute-start.2 = (f32[128,2048]{1,0:T(8,128)}, f32[128,2048]{1,0:T(8,128)S(1)}, u32[]{:S(2)}, u32[]{:S(2)}) collective-permute-start(f32[128,2048]{1,0:T(8,128)} %get-tuple-element.55), channel_id=1, source_target_pairs={{0,1},{1,0},{2,3},{3,2},{4,5},{5,4},{6,7},{7,6},{8,9},{9,8},{10,11... | collective-permute-start | bytes 3145736 | tf_op jit(solution)/shard_map/ppermute | solution.py:235
  17.7 17.4 %collective-permute-start.5 = (f32[1024,128]{1,0:T(8,128)}, f32[1024,128]{1,0:T(8,128)}, u32[]{:S(2)}, u32[]{:S(2)}) collective-permute-start(f32[1024,128]{1,0:T(8,128)} %get-tuple-element.64), channel_id=1, source_target_pairs={{0,2},{1,3},{2,4},{3,5},{4,6},{5,7},{8,10},{9,11},{10,12},{11,13},... | collective-permute-start | bytes 1572872 | tf_op jit(solution)/shard_map/ppermute | solution.py:239
  21.8 19.3 %collective-permute-start.6 = (f32[1024,128]{1,0:T(8,128)}, f32[1024,128]{1,0:T(8,128)}, u32[]{:S(2)}, u32[]{:S(2)}) collective-permute-start(f32[1024,128]{1,0:T(8,128)} %get-tuple-element.69), channel_id=1, source_target_pairs={{0,4},{1,5},{8,12},{9,13},{16,20},{17,21},{24,28},{25,29}} | collective-permute-start | bytes 1572872 | tf_op jit(solution)/shard_map/ppermute | solution.py:239
  33.0 11.7 %collective-permute-start.10 = (f32[1024,128]{1,0:T(8,128)}, f32[1024,128]{1,0:T(8,128)S(1)}, u32[]{:S(2)}, u32[]{:S(2)}) collective-permute-start(f32[1024,128]{1,0:T(8,128)} %get-tuple-element.71), channel_id=1, source_target_pairs={{6,2},{7,3},{14,10},{15,11},{22,18},{23,19},{30,26},{31,27}} | collective-permute-start | bytes 1572872 | tf_op jit(solution)/shard_map/ppermute | solution.py:239
  33.7 12.4 %collective-permute-start.9 = (f32[1024,128]{1,0:T(8,128)}, f32[1024,128]{1,0:T(8,128)}, u32[]{:S(2)}, u32[]{:S(2)}) collective-permute-start(f32[1024,128]{1,0:T(8,128)} %get-tuple-element.67), channel_id=1, source_target_pairs={{6,4},{7,5},{4,2},{5,3},{2,0},{3,1},{14,12},{15,13},{12,10},{13,11... | collective-permute-start | bytes 1572872 | tf_op jit(solution)/shard_map/ppermute | solution.py:239
  42.7 9.2 %collective-permute-start.7 = (f32[1024,128]{1,0:T(8,128)S(1)}, f32[1024,128]{1,0:T(8,128)S(1)}, u32[]{:S(2)}, u32[]{:S(2)}) collective-permute-start(f32[1024,128]{1,0:T(8,128)S(1)} %select_select_fusion.1), channel_id=1, source_target_pairs={{0,2},{1,3},{2,4},{3,5},{4,6},{5,7},{8,10},{9,11},{10,12},{11,13},... | collective-permute-start | bytes 1572872 | tf_op jit(solution)/shard_map/ppermute | solution.py:239
  44.1 7.9 %collective-permute-start.8 = (f32[1024,128]{1,0:T(8,128)S(1)}, f32[1024,128]{1,0:T(8,128)S(1)}, u32[]{:S(2)}, u32[]{:S(2)}) collective-permute-start(f32[1024,128]{1,0:T(8,128)S(1)} %select_select_fusion.1), channel_id=1, source_target_pairs={{2,6},{3,7},{10,14},{11,15},{18,22},{19,23},{26,30},{27,31}} | collective-permute-start | bytes 1572872 | tf_op jit(solution)/shard_map/ppermute | solution.py:239
  48.2 39.5 %collective-permute-start.14 = (f32[1024,128]{1,0:T(8,128)}, f32[1024,128]{1,0:T(8,128)}, u32[]{:S(2)}, u32[]{:S(2)}) collective-permute-start(f32[1024,128]{1,0:T(8,128)} %select_select_fusion), channel_id=1, source_target_pairs={{6,4},{7,5},{4,2},{5,3},{2,0},{3,1},{14,12},{15,13},{12,10},{13,11... | collective-permute-start | bytes 1572872 | tf_op jit(solution)/shard_map/ppermute | solution.py:239
  49.5 38.2 %collective-permute-start.15 = (f32[1024,128]{1,0:T(8,128)}, f32[1024,128]{1,0:T(8,128)}, u32[]{:S(2)}, u32[]{:S(2)}) collective-permute-start(f32[1024,128]{1,0:T(8,128)} %select_select_fusion), channel_id=1, source_target_pairs={{4,0},{5,1},{12,8},{13,9},{20,16},{21,17},{28,24},{29,25}} | collective-permute-start | bytes 1572872 | tf_op jit(solution)/shard_map/ppermute | solution.py:239
  62.2 18.1 %collective-permute-start.11 = (f32[4,1,512]{2,1,0:T(1,128)}, f32[4,1,512]{2,1,0:T(1,128)S(1)}, u32[]{:S(2)}, u32[]{:S(2)}) collective-permute-start(f32[4,1,512]{2,1,0:T(1,128)} %get-tuple-element.77), channel_id=1, source_target_pairs={{0,2},{1,3},{2,0},{3,1},{4,6},{5,7},{6,4},{7,5},{8,10},{9,11},{10,... | collective-permute-start | bytes 24584 | tf_op jit(solution)/shard_map/ppermute | solution.py:239
  77.2 10.4 %collective-permute-start.12 = (f32[4,1,512]{2,1,0:T(1,128)}, f32[4,1,512]{2,1,0:T(1,128)S(1)}, u32[]{:S(2)}, u32[]{:S(2)}) collective-permute-start(f32[4,1,512]{2,1,0:T(1,128)} %get-tuple-element.77), channel_id=1, source_target_pairs={{0,4},{1,5},{2,6},{3,7},{4,0},{5,1},{6,2},{7,3},{8,12},{9,13},{10,... | collective-permute-start | bytes 24584 | tf_op jit(solution)/shard_map/ppermute | solution.py:239
  80.3 7.3 %collective-permute-start.13 = (f32[4,1,512]{2,1,0:T(1,128)}, f32[4,1,512]{2,1,0:T(1,128)S(1)}, u32[]{:S(2)}, u32[]{:S(2)}) collective-permute-start(f32[4,1,512]{2,1,0:T(1,128)} %get-tuple-element.77), channel_id=1, source_target_pairs={{0,6},{1,7},{2,4},{3,5},{4,2},{5,3},{6,0},{7,1},{8,14},{9,15},{10,... | collective-permute-start | bytes 24584 | tf_op jit(solution)/shard_map/ppermute | solution.py:239
  87.7 16.4 %collective-permute-start.16 = (f32[128,2048]{1,0:T(8,128)}, f32[128,2048]{1,0:T(8,128)S(1)}, u32[]{:S(2)}, u32[]{:S(2)}) collective-permute-start(f32[128,2048]{1,0:T(8,128)} %get-tuple-element.85), channel_id=1, source_target_pairs={{0,1},{1,0},{2,3},{3,2},{4,5},{5,4},{6,7},{7,6},{8,9},{9,8},{10,11... | collective-permute-start | bytes 3145736 | tf_op jit(solution)/shard_map/ppermute | solution.py:235
  91.2 8.1 %collective-permute-start.17 = (f32[256,128]{1,0:T(8,128)}, f32[256,128]{1,0:T(8,128)S(1)}, u32[]{:S(2)}, u32[]{:S(2)}) collective-permute-start(f32[256,128]{1,0:T(8,128)} %get-tuple-element.88), channel_id=1, source_target_pairs={{0,8},{8,0},{16,24},{24,16},{1,9},{9,1},{17,25},{25,17},{2,10},{10... | collective-permute-start | bytes 393224 | tf_op jit(solution)/shard_map/ppermute | solution.py:319
  92.4 6.9 %collective-permute-start.18 = (f32[256,128]{1,0:T(8,128)}, f32[256,128]{1,0:T(8,128)S(1)}, u32[]{:S(2)}, u32[]{:S(2)}) collective-permute-start(f32[256,128]{1,0:T(8,128)} %get-tuple-element.89), channel_id=1, source_target_pairs={{0,16},{8,24},{16,0},{24,8},{1,17},{9,25},{17,1},{25,9},{2,18},{10... | collective-permute-start | bytes 393224 | tf_op jit(solution)/shard_map/ppermute | solution.py:319
  110.2 7.4 %collective-permute-start.22 = (f32[256,128]{1,0:T(8,128)S(1)}, f32[256,128]{1,0:T(8,128)S(1)}, u32[]{:S(2)}, u32[]{:S(2)}) collective-permute-start(f32[256,128]{1,0:T(8,128)S(1)} %add.101.refs_0_), channel_id=1, source_target_pairs={{0,8},{8,0},{16,24},{24,16},{1,9},{9,1},{17,25},{25,17},{2,10},{10... | collective-permute-start | bytes 393224 | tf_op jit(solution)/shard_map/ppermute | solution.py:330
  114.3 8.8 %collective-permute-start.33 = (f32[256,128]{1,0:T(8,128)S(1)}, f32[256,128]{1,0:T(8,128)S(1)}, u32[]{:S(2)}, u32[]{:S(2)}) collective-permute-start(f32[256,128]{1,0:T(8,128)S(1)} %add.105), channel_id=1, source_target_pairs={{0,4},{1,5},{2,6},{3,7},{4,0},{5,1},{6,2},{7,3},{8,12},{9,13},{10,... | collective-permute-start | bytes 393224 | tf_op jit(solution)/shard_map/ppermute | solution.py:239
  114.3 8.9 %collective-permute-start.24 = (f32[256,128]{1,0:T(8,128)S(1)}, f32[256,128]{1,0:T(8,128)S(1)}, u32[]{:S(2)}, u32[]{:S(2)}) collective-permute-start(f32[256,128]{1,0:T(8,128)S(1)} %add.101.refs_0_), channel_id=1, source_target_pairs={{0,24},{8,16},{16,8},{24,0},{1,25},{9,17},{17,9},{25,1},{2,26},{10... | collective-permute-start | bytes 393224 | tf_op jit(solution)/shard_map/ppermute | solution.py:330
  115.7 8.7 %collective-permute-start.25 = (f32[256,128]{1,0:T(8,128)S(1)}, f32[256,128]{1,0:T(8,128)S(1)}, u32[]{:S(2)}, u32[]{:S(2)}) collective-permute-start(f32[256,128]{1,0:T(8,128)S(1)} %add.101.refs_0_), channel_id=1, source_target_pairs={{0,1},{1,0},{2,3},{3,2},{4,5},{5,4},{6,7},{7,6},{8,9},{9,8},{10,11... | collective-permute-start | bytes 393224 | tf_op jit(solution)/shard_map/ppermute | solution.py:235
  117.6 8.2 %collective-permute-start.26 = (f32[256,128]{1,0:T(8,128)S(1)}, f32[256,128]{1,0:T(8,128)S(1)}, u32[]{:S(2)}, u32[]{:S(2)}) collective-permute-start(f32[256,128]{1,0:T(8,128)S(1)} %collective-permute-done.22.refs_1_), channel_id=1, source_target_pairs={{0,1},{1,0},{2,3},{3,2},{4,5},{5,4},{6,7},{7,6},{8,9},{9,8},{10,11... | collective-permute-start | bytes 393224 | tf_op jit(solution)/shard_map/ppermute | solution.py:235
  119.4 7.7 %collective-permute-start.27 = (f32[256,128]{1,0:T(8,128)S(1)}, f32[256,128]{1,0:T(8,128)S(1)}, u32[]{:S(2)}, u32[]{:S(2)}) collective-permute-start(f32[256,128]{1,0:T(8,128)S(1)} %collective-permute-done.23.refs_2_), channel_id=1, source_target_pairs={{0,1},{1,0},{2,3},{3,2},{4,5},{5,4},{6,7},{7,6},{8,9},{9,8},{10,11... | collective-permute-start | bytes 393224 | tf_op jit(solution)/shard_map/ppermute | solution.py:235
  124.4 8.3 %collective-permute-start.36 = (f32[256,128]{1,0:T(8,128)S(1)}, f32[256,128]{1,0:T(8,128)S(1)}, u32[]{:S(2)}, u32[]{:S(2)}) collective-permute-start(f32[256,128]{1,0:T(8,128)S(1)} %add.106.refs_8_), channel_id=1, source_target_pairs={{0,24},{8,16},{16,8},{24,0},{1,25},{9,17},{17,9},{25,1},{2,26},{10... | collective-permute-start | bytes 393224 | tf_op jit(solution)/shard_map/ppermute | solution.py:330
  125.8 6.8 %collective-permute-start.28 = (f32[256,128]{1,0:T(8,128)S(1)}, f32[256,128]{1,0:T(8,128)S(1)}, u32[]{:S(2)}, u32[]{:S(2)}) collective-permute-start(f32[256,128]{1,0:T(8,128)S(1)} %collective-permute-done.24.refs_3_), channel_id=1, source_target_pairs={{0,1},{1,0},{2,3},{3,2},{4,5},{5,4},{6,7},{7,6},{8,9},{9,8},{10,11... | collective-permute-start | bytes 393224 | tf_op jit(solution)/shard_map/ppermute | solution.py:235
  (21 other events, 116.6 us)

commit v9 on v8

--- a/solution.py
+++ b/solution.py
@@ -77,10 +77,10 @@
     return stack(own_ref[...], got_ref[...].astype(BF))
 
 
-def before_of(place, first, near, far, near2, far2):
+def before_of(place, first, near, far, passed, passed_far, last):
     if first:
-        return jnp.where(place == 2, near2[...], near[...] + far2[...])
-    return jnp.where(place == 2, near[...] + far[...], near2[...])
+        return jnp.where(place == 2, passed[...], near[...] + passed_far[...])
+    return jnp.where(place == 2, near[...] + far[...], last[...])
 
 
 def key_kernel(
@@ -140,7 +140,7 @@
 
 def attend_kernel(
     n, step, info, q_ref, qg_ref, c_ref, cg_ref, v_ref, vg_ref, kb_ref, qp_ref, qr_ref, wt_ref, pn_ref,
-    near, far, near2, far2, att_ref, atg_ref, sn_ref, gk_ref, gq_ref,
+    near, far, passed, passed_far, last, att_ref, atg_ref, sn_ref, gk_ref, gq_ref,
 ):
     group, length, dim = qr_ref.shape[1:]
     feats = dim
@@ -153,7 +153,7 @@
     queries = tokens_of(q_ref, qg_ref)
     upstream = stack(c_ref[...].astype(F32), cg_ref[...])
     values = tokens_of(v_ref, vg_ref)
-    high, low = split(before_of(info[2 * n + 1], step < n // 2, near, far, near2, far2))
+    high, low = split(before_of(info[2 * n + 1], step < n // 2, near, far, passed, passed_far, last))
     norm_wide = jnp.broadcast_to(column(pn_ref[0]), (group * feats, dim))
     norm_high, norm_low = split(norm_wide)
     norm_cols = three_lanes(norm_wide, "hhl")
@@ -204,12 +204,13 @@
 
 
 def key_grad_kernel(
-    n, step, info, k_ref, kg_ref, v_ref, vg_ref, kp_ref, gk_ref, sn_ref, near, far, near2, far2, out_ref
+    n, step, info, k_ref, kg_ref, v_ref, vg_ref, kp_ref, gk_ref, sn_ref,
+    near, far, passed, passed_far, last, out_ref,
 ):
     rows, length = kp_ref.shape[1:]
     feats = k_ref.shape[1]
     values = tokens_of(v_ref, vg_ref)
-    state = cat(*split(before_of(info[2 * n + 2], step < n // 2, near, far, near2, far2)))
+    state = cat(*split(before_of(info[2 * n + 2], step < n // 2, near, far, passed, passed_far, last)))
     upstream = gk_ref[0] + mm_nt(state, cat(values, values))
     upstream = upstream + jnp.broadcast_to(column(sn_ref[0]), (rows, length))
     back = [
@@ -261,20 +262,19 @@
             self.near = self.move(self.payload, [(0, 1), (1, 2), (2, 3)])
             self.far = self.move(self.b, [(0, 2)])
 
-    def turn_around(self, *earlier):
+    def pass_on(self, *earlier):
         if self.chips == 4:
-            a, b = after((self.a, self.b), *earlier) if earlier else (self.a, self.b)
-            self.payload = jnp.where(
-                self.place == 1,
-                a + self.near,
-                jnp.where(self.place == 2, b + self.near + self.far, b),
-            )
-
-    def second(self):
+            a = after(self.a, *earlier) if earlier else self.a
+            self.payload = a + self.near
+            self.passed = self.move(self.payload, [(1, 2)])
+            self.passed_far = self.move(self.payload, [(1, 3)])
+
+    def finish(self, *earlier):
         if self.chips == 4:
-            self.near2 = self.move(self.payload, [(0, 1), (1, 2), (2, 3)])
-            self.far2 = self.move(self.payload, [(1, 3)])
-            return self.near, self.far, self.near2, self.far2
+            b = after(self.b, *earlier) if earlier else self.b
+            self.payload = jnp.where(self.place == 2, b + self.near + self.far, b)
+            last = self.move(self.payload, [(0, 1), (2, 3)])
+            return self.near, self.far, self.passed, self.passed_far, last
         total = jnp.concatenate([self.a, self.b], axis=0)
         before = self.move(total, [(i, i + 1) for i in range(self.chips - 1)])
         step = 1
@@ -284,7 +284,7 @@
             step *= 2
         rows = self.a.shape[0]
         zero = jnp.zeros_like(self.a)
-        return before[:rows], zero, before[rows:], zero
+        return before[:rows], zero, zero, zero, before[rows:]
 
 
 def scan_norms(norm, chip, chips, forward, *earlier):
@@ -392,7 +392,7 @@
         return x
 
     def call(name, body, in_specs, out_specs, out_shape, aliases=None):
-        in_specs = [x if isinstance(x, tuple) else (x, n) for x in in_specs]
+        in_specs = [x if isinstance(x, tuple) else (x, 0, n) for x in in_specs]
         kinds = [x.dtype for x in out_shape]
         results = {}
         for (spec_, which, _), kind in zip(out_specs, kinds):
@@ -409,9 +409,11 @@
 
             def incoming(i):
                 return [
-                    pltpu.make_async_copy(block(ref, spec_, i, info), buf.at[i], in_sem.at[k, i])
-                    for k, ((spec_, period), ref, buf) in enumerate(zip(in_specs, ins, in_bufs))
-                    if i < period
+                    pltpu.make_async_copy(
+                        block(ref, spec_, i, info), buf.at[i % period], in_sem.at[k, i]
+                    )
+                    for k, ((spec_, start, period), ref, buf) in enumerate(zip(in_specs, ins, in_bufs))
+                    if start <= i < start + period
                 ]
 
             def outgoing(i, act):
@@ -433,7 +435,7 @@
             for i in range(n):
                 for copy in incoming(i):
                     copy.wait()
-                blocks = [buf.at[i % period] for (_, period), buf in zip(in_specs, in_bufs)]
+                blocks = [buf.at[i % period] for (_, _, period), buf in zip(in_specs, in_bufs)]
                 body(n, i, info, *blocks, *[buf.at[i] for buf in out_bufs])
                 outgoing(i, lambda copy: copy.start())
             for i in range(n):
@@ -443,7 +445,7 @@
             anywhere = pl.BlockSpec(memory_space=pl.ANY)
             buffers = [
                 pltpu.VMEM((period,) + tuple(x.block_shape), y.dtype)
-                for (x, period), y in zip(in_specs, arrays)
+                for (x, _, period), y in zip(in_specs, arrays)
             ] + [pltpu.VMEM((n,) + tuple(shape), kind) for shape, kind in results]
             return pl.pallas_call(
                 kernel,
@@ -483,8 +485,8 @@
     flat_spec, flat = per_head(wide, length), shape_of(wide, length)
     half = n // 2
     half_state = jax.ShapeDtypeStruct((half * wide, dim), F32)
-    moved_spec = (spec((wide, dim), lambda i, info: (i, 0)), half)
     half_spec = spec((wide, dim), lambda i, info: (i % half, 0))
+    moved_specs = [(half_spec, start, half) for start in (0, half, 0, 0, half)]
 
     def states(which, place):
         return [
@@ -528,11 +530,11 @@
     )(queries, queries_got, cotangent, cotangent_got, query_map, key_features, prefix_norm)
     suffix = Scan(a, b, near, False)
     suffix.first()
-    prefix.turn_around(near)
-    before = prefix.second()
-    suffix.turn_around()
+    prefix.pass_on(near)
+    before = prefix.finish(prefix.payload)
+    suffix.pass_on()
     before = after(before, suffix.payload)
-    later = suffix.second()
+    later = suffix.finish(suffix.payload)
 
     grad = jax.ShapeDtypeStruct((group * width, dim), F32)
     attended, attended_got, norm, key_up, *query_part = call(
@@ -541,7 +543,7 @@
         [own_cols(four), got_cols(four)] * 2
         + [own_cols(one), got_values, flat_spec, flat_spec, rows_spec]
         + [per_head(group, length, length), row_spec]
-        + [moved_spec] * 4,
+        + moved_specs,
         each(own_cols(four), got_cols(four), row_spec, flat_spec) + spread(4),
         [
             jax.ShapeDtypeStruct((own, head_count * dim), BF),
@@ -560,7 +562,7 @@
         key_grad_kernel,
         [own_cols(one), got_keys, own_cols(one), got_values]
         + [flat_spec, flat_spec, row_spec]
-        + [moved_spec] * 4,
+        + moved_specs,
         spread(0),
         [grad] * n,
     )(keys, keys_got, values, values_got, key_probs, key_up, suffix_norm, *later)

time: 137 us -> 135 us (0.985)
  waiting for transfers between devices: 27 us -> 15.8 us
  starting transfers between devices: 70.7 us -> 79.2 us
    ppermute x17 -> x19, starting transfers between devices: 39.5 us -> 48.9 us  [chip_move(): lax.ppermute(x, 'ctx', [(2 * a + c, 2 * b + c) for a, b in pairs for c in...]
    ppermute x17 -> x19, waiting for transfers between devices: 19.8 us -> 11.8 us  [chip_move(): lax.ppermute(x, 'ctx', [(2 * a + c, 2 * b + c) for a, b in pairs for c in...]
    ppermute x6, waiting for transfers between devices: 3.4 us -> 1.26 us  [sum_all(): lax.ppermute(blocks[k], 'dp', [(i, i ^ k) for i in range(dp)])]
    add x0 -> x2, other arithmetic: none -> 2.03 us  [pass_on(): self.payload = a + self.near]
    select_n x2, other arithmetic: 3.66 us -> 2.28 us  [finish(): self.payload = jnp.where(self.place == 2, b + self.near + self.far, b)]
  transfers between devices with their start and end apart: 41 -> 43, of which waited for: 15 -> 13; matrix products, arithmetic and copies ran while one was open for 3% -> 4% of each run, Pallas kernels for 18% -> 18%
where the time goes in v9:
time: 135 us; the launch traced here: 134 us
  starting transfers between devices  79.2 us (59%)
  Pallas kernels  31.7 us (23%)
  waiting for transfers between devices  15.8 us (12%)
  other arithmetic  5.23 us (4%)
    ppermute x19, starting transfers between devices, chip_move(): lax.ppermute(x, 'ctx', [(2 * a + c, 2 * b + c) for a, b in pairs for c in...  48.9 us
    pallas_call x5, Pallas kernels, run(): pl.pallas_call(kernel, name=name, out_shape=[pltpu.HBM(x.shape, x.dtype)...  29.7 us
    ppermute x12, starting transfers between devices, core_swap(): return lax.ppermute(x, 'ctx', [(i, i ^ 1) for i in range(size)])  17 us
    ppermute x19, waiting for transfers between devices, chip_move(): lax.ppermute(x, 'ctx', [(2 * a + c, 2 * b + c) for a, b in pairs for c in...  11.8 us
    ppermute x6, starting transfers between devices, sum_all(): lax.ppermute(total, 'dp', [(i, i ^ k) for i in range(dp)])  7.97 us
    ppermute x6, starting transfers between devices, sum_all(): lax.ppermute(blocks[k], 'dp', [(i, i ^ k) for i in range(dp)])  5.38 us
    ppermute x12, waiting for transfers between devices, core_swap(): return lax.ppermute(x, 'ctx', [(i, i ^ 1) for i in range(size)])  2.75 us
  transfers between devices with their start and end apart: 43, of which 13 were waited for; matrix products, arithmetic and copies ran while one was open for 4% of the time, Pallas kernels for 18%

profile of v9, /device:TPU:1, one launch (start us, length us, event | category | flops | bytes accessed | tf_op | source)
XLA Modules:
  0.0 134.0 jit_solution(18165917143587609145)
XLA Ops:
  1.9 1.8 %collective-permute-done.refs_1_.refs_3_.refs_5_ = f32[256,512]{1,0:T(8,128)S(1)} collective-permute-done((f32[256,512]{1,0:T(8,128)S(1)}, f32[256,512]{1,0:T(8,128)S(1)}, u32[]{:S(2)}, u32[]{:S(2)}) %collective-permute-start) | collective-permute-done | bytes 524320 | tf_op jit(solution)/shard_map/ppermute | solution.py:236
  3.7 5.4 %key_features.1 = (f32[4,512,256]{2,1,0:T(8,128)}, bf16[4,512,256]{2,1,0:T(8,128)(2,1)}, f32[4,1,512]{2,1,0:T(1,128)}, f32[1024,128]{1,0:T(8,128)}, f32[1024,128...) custom-call(s32[11]{0:T(128)S(1)} %concatenate.6.info, bf16[128,1024]{1,0:T(8,128)(2,1)} %bitcast.29, ...), custom_call_target="tpu_custom_call" | custom-call | tf_op jit(solution)/shard_map/key_features/pallas_call | solution.py:450
  9.7 2.5 %collective-permute-start.3 = (f32[4,1,512]{2,1,0:T(1,128)}, f32[4,1,512]{2,1,0:T(1,128)S(1)}, u32[]{:S(2)}, u32[]{:S(2)}) collective-permute-start(f32[4,1,512]{2,1,0:T(1,128)} %get-tuple-element.59), channel_id=1, source_target_pairs={{0,2},{1,3},{2,0},{3,1},{4,6},{5,7},{6,4},{7,5},{8,10},{9,11},{10,... | collective-permute-start | bytes 24584 | tf_op jit(solution)/shard_map/ppermute | solution.py:240
  14.2 2.5 %collective-permute-start.4 = (f32[4,1,512]{2,1,0:T(1,128)S(1)}, f32[4,1,512]{2,1,0:T(1,128)S(1)}, u32[]{:S(2)}, u32[]{:S(2)}) collective-permute-start(f32[4,1,512]{2,1,0:T(1,128)S(1)} %add.87), channel_id=1, source_target_pairs={{0,4},{1,5},{2,6},{3,7},{4,0},{5,1},{6,2},{7,3},{8,12},{9,13},{10,... | collective-permute-start | bytes 24584 | tf_op jit(solution)/shard_map/ppermute | solution.py:240
  17.7 3.4 %collective-permute-start.5 = (f32[1024,128]{1,0:T(8,128)}, f32[1024,128]{1,0:T(8,128)S(1)}, u32[]{:S(2)}, u32[]{:S(2)}) collective-permute-start(f32[1024,128]{1,0:T(8,128)} %get-tuple-element.66), channel_id=1, source_target_pairs={{0,2},{1,3},{2,4},{3,5},{4,6},{5,7},{8,10},{9,11},{10,12},{11,13},... | collective-permute-start | bytes 1572872 | tf_op jit(solution)/shard_map/ppermute | solution.py:240
  21.1 4.9 %collective-permute-start.6 = (f32[1024,128]{1,0:T(8,128)}, f32[1024,128]{1,0:T(8,128)}, u32[]{:S(2)}, u32[]{:S(2)}) collective-permute-start(f32[1024,128]{1,0:T(8,128)} %get-tuple-element.71), channel_id=1, source_target_pairs={{0,4},{1,5},{8,12},{9,13},{16,20},{17,21},{24,28},{25,29}} | collective-permute-start | bytes 1572872 | tf_op jit(solution)/shard_map/ppermute | solution.py:240
  26.0 7.1 %query_features.1 = (f32[4,512,256]{2,1,0:T(8,128)}, bf16[4,4,256,128]{3,2,1,0:T(8,128)(2,1)}, bf16[4,4,256,256]{3,2,1,0:T(8,128)(2,1)}, f32[1024,128]{1,0:T(8,1...) custom-call(s32[11]{0:T(128)S(1)} %concatenate.6.info, bf16[128,4096]{1,0:T(8,128)(2,1)} %bitcast.21, ...), custom_call_target="tpu_custom_call" | custom-call | tf_op jit(solution)/shard_map/query_features/pallas_call | solution.py:450
  37.8 3.3 %collective-permute-done.6.refs_12_ = f32[1024,128]{1,0:T(8,128)} collective-permute-done((f32[1024,128]{1,0:T(8,128)}, f32[1024,128]{1,0:T(8,128)}, u32[]{:S(2)}, u32[]{:S(2)}) %collective-permute-start.6) | collective-permute-done | bytes 524320 | tf_op jit(solution)/shard_map/ppermute | solution.py:240
  42.5 5.6 %collective-permute-start.9 = (f32[1024,128]{1,0:T(8,128)S(1)}, f32[1024,128]{1,0:T(8,128)S(1)}, u32[]{:S(2)}, u32[]{:S(2)}) collective-permute-start(f32[1024,128]{1,0:T(8,128)S(1)} %add_select_fusion.1), channel_id=1, source_target_pairs={{0,2},{1,3},{4,6},{5,7},{8,10},{9,11},{12,14},{13,15},{16,18},{17,... | collective-permute-start | bytes 1572872 | tf_op jit(solution)/shard_map/ppermute | solution.py:240
  55.2 10.3 %attend.1 = (bf16[128,4096]{1,0:T(8,128)(2,1)}, f32[128,2048]{1,0:T(8,128)}, f32[4,1,512]{2,1,0:T(1,128)}, f32[4,512,256]{2,1,0:T(8,128)}, f32[256,128]{1,0:T(8,...) custom-call(s32[11]{0:T(128)S(1)} %concatenate.6.info, bf16[128,4096]{1,0:T(8,128)(2,1)} %bitcast.22, ...), custom_call_target="tpu_custom_call" | custom-call | tf_op jit(solution)/shard_map/attend/pallas_call | solution.py:450
  65.4 12.8 %collective-permute-start.11 = (f32[4,1,512]{2,1,0:T(1,128)}, f32[4,1,512]{2,1,0:T(1,128)S(1)}, u32[]{:S(2)}, u32[]{:S(2)}) collective-permute-start(f32[4,1,512]{2,1,0:T(1,128)} %get-tuple-element.79), channel_id=1, source_target_pairs={{0,2},{1,3},{2,0},{3,1},{4,6},{5,7},{6,4},{7,5},{8,10},{9,11},{10,... | collective-permute-start | bytes 24584 | tf_op jit(solution)/shard_map/ppermute | solution.py:240
  78.2 3.1 %collective-permute-start.12 = (f32[4,1,512]{2,1,0:T(1,128)}, f32[4,1,512]{2,1,0:T(1,128)S(1)}, u32[]{:S(2)}, u32[]{:S(2)}) collective-permute-start(f32[4,1,512]{2,1,0:T(1,128)} %get-tuple-element.79), channel_id=1, source_target_pairs={{0,4},{1,5},{2,6},{3,7},{4,0},{5,1},{6,2},{7,3},{8,12},{9,13},{10,... | collective-permute-start | bytes 24584 | tf_op jit(solution)/shard_map/ppermute | solution.py:240
  81.7 2.1 %collective-permute-start.13 = (f32[4,1,512]{2,1,0:T(1,128)}, f32[4,1,512]{2,1,0:T(1,128)S(1)}, u32[]{:S(2)}, u32[]{:S(2)}) collective-permute-start(f32[4,1,512]{2,1,0:T(1,128)} %get-tuple-element.79), channel_id=1, source_target_pairs={{0,6},{1,7},{2,4},{3,5},{4,2},{5,3},{6,0},{7,1},{8,14},{9,15},{10,... | collective-permute-start | bytes 24584 | tf_op jit(solution)/shard_map/ppermute | solution.py:240
  83.7 2.4 %collective-permute-done.13 = f32[4,1,512]{2,1,0:T(1,128)S(1)} collective-permute-done((f32[4,1,512]{2,1,0:T(1,128)}, f32[4,1,512]{2,1,0:T(1,128)S(1)}, u32[]{:S(2)}, u32[]{:S(2)}) %collective-permute-start.13) | collective-permute-done | bytes 8224 | tf_op jit(solution)/shard_map/ppermute | solution.py:240
  86.2 3.5 %collective-permute-start.18 = (f32[128,2048]{1,0:T(8,128)}, f32[128,2048]{1,0:T(8,128)S(1)}, u32[]{:S(2)}, u32[]{:S(2)}) collective-permute-start(f32[128,2048]{1,0:T(8,128)} %get-tuple-element.89), channel_id=1, source_target_pairs={{0,1},{1,0},{2,3},{3,2},{4,5},{5,4},{6,7},{7,6},{8,9},{9,8},{10,11... | collective-permute-start | bytes 3145736 | tf_op jit(solution)/shard_map/ppermute | solution.py:236
  92.4 5.4 %key_grads.1 = (f32[256,128]{1,0:T(8,128)}, f32[256,128]{1,0:T(8,128)}, f32[256,128]{1,0:T(8,128)}, f32[256,128]{1,0:T(8,128)}) custom-call(s32[11]{0:T(128)S(1)} %concatenate.6.info, bf16[128,1024]{1,0:T(8,128)(2,1)} %bitcast.30, f32[256,512]{1,0:T(8,128)S(1)} %collective-permute-done.refs_1_.refs_3_.refs_5_, bf16[128,1024]{1,0:T(8,128)(2,1)} %bitcast.28, ...), custom_call_target="tpu_custom_call" | custom-call | tf_op jit(solution)/shard_map/key_grads/pallas_call | solution.py:450
  102.5 2.1 %collective-permute-start.23 = (f32[256,128]{1,0:T(8,128)S(1)}, f32[256,128]{1,0:T(8,128)S(1)}, u32[]{:S(2)}, u32[]{:S(2)}) collective-permute-start(f32[256,128]{1,0:T(8,128)S(1)} %add.100), channel_id=1, source_target_pairs={{0,4},{1,5},{2,6},{3,7},{4,0},{5,1},{6,2},{7,3},{8,12},{9,13},{10,... | collective-permute-start | bytes 393224 | tf_op jit(solution)/shard_map/ppermute | solution.py:240
  104.6 1.5 %attended.1 = bf16[128,4096]{1,0:T(8,128)(2,1)} custom-call(s32[11]{0:T(128)S(1)} %concatenate.6.info, f32[128,2048]{1,0:T(8,128)S(1)} %collective-permute-done.18.refs_0_, bf16[128,4096]{1,0:T(8,128)(2,1)} %get-tuple-element.90.refs_1_), custom_call_target="tpu_custom_call", output_to_operand_aliasing={{}: (2, {})} | custom-call | tf_op jit(solution)/shard_map/attended/pallas_call | solution.py:450
  108.7 4.0 %collective-permute-start.24 = (f32[256,128]{1,0:T(8,128)S(1)}, f32[256,128]{1,0:T(8,128)S(1)}, u32[]{:S(2)}, u32[]{:S(2)}) collective-permute-start(f32[256,128]{1,0:T(8,128)S(1)} %add.101.refs_0_), channel_id=1, source_target_pairs={{0,8},{8,0},{16,24},{24,16},{1,9},{9,1},{17,25},{25,17},{2,10},{10... | collective-permute-start | bytes 393224 | tf_op jit(solution)/shard_map/ppermute | solution.py:330
  114.9 4.3 %collective-permute-start.27 = (f32[256,128]{1,0:T(8,128)S(1)}, f32[256,128]{1,0:T(8,128)S(1)}, u32[]{:S(2)}, u32[]{:S(2)}) collective-permute-start(f32[256,128]{1,0:T(8,128)S(1)} %add.101.refs_0_), channel_id=1, source_target_pairs={{0,1},{1,0},{2,3},{3,2},{4,5},{5,4},{6,7},{7,6},{8,9},{9,8},{10,11... | collective-permute-start | bytes 393224 | tf_op jit(solution)/shard_map/ppermute | solution.py:236
  121.2 1.5 %collective-permute-start.37 = (f32[256,128]{1,0:T(8,128)S(1)}, f32[256,128]{1,0:T(8,128)S(1)}, u32[]{:S(2)}, u32[]{:S(2)}) collective-permute-start(f32[256,128]{1,0:T(8,128)S(1)} %add.106.refs_8_), channel_id=1, source_target_pairs={{0,16},{8,24},{16,0},{24,8},{1,17},{9,25},{17,1},{25,9},{2,18},{10... | collective-permute-start | bytes 393224 | tf_op jit(solution)/shard_map/ppermute | solution.py:330
  123.8 2.8 %collective-permute-start.30 = (f32[256,128]{1,0:T(8,128)S(1)}, f32[256,128]{1,0:T(8,128)S(1)}, u32[]{:S(2)}, u32[]{:S(2)}) collective-permute-start(f32[256,128]{1,0:T(8,128)S(1)} %collective-permute-done.26.refs_3_), channel_id=1, source_target_pairs={{0,1},{1,0},{2,3},{3,2},{4,5},{5,4},{6,7},{7,6},{8,9},{9,8},{10,11... | collective-permute-start | bytes 393224 | tf_op jit(solution)/shard_map/ppermute | solution.py:236
  126.7 1.8 %collective-permute-start.40 = (f32[256,128]{1,0:T(8,128)S(1)}, f32[256,128]{1,0:T(8,128)S(1)}, u32[]{:S(2)}, u32[]{:S(2)}) collective-permute-start(f32[256,128]{1,0:T(8,128)S(1)} %collective-permute-done.36.refs_9_), channel_id=1, source_target_pairs={{0,1},{1,0},{2,3},{3,2},{4,5},{5,4},{6,7},{7,6},{8,9},{9,8},{10,11... | collective-permute-start | bytes 393224 | tf_op jit(solution)/shard_map/ppermute | solution.py:236
  132.0 2.0 %sums_out.1 = (f32[8,256,128]{2,1,0:T(8,128)}, f32[8,256,128]{2,1,0:T(8,128)}) custom-call(s32[11]{0:T(128)S(1)} %concatenate.6.info, f32[256,128]{1,0:T(8,128)S(1)} %add.101.refs_0_, f32[256,128]{1,0:T(8,128)S(1)} %collective-permute-done.24.refs_1_, f32[256,128]{1,0:T(8,128)S(1)} %collective-permute-done.25.refs_2_, ...), custom_call_target="tpu_custom_call" | custom-call | tf_op jit(solution)/shard_map/sums_out/pallas_call | solution.py:581
  (93 shorter events, 37.1 us)
Async XLA Ops:
  9.1 16.8 %collective-permute-start.1 = (f32[128,2048]{1,0:T(8,128)}, f32[128,2048]{1,0:T(8,128)S(1)}, u32[]{:S(2)}, u32[]{:S(2)}) collective-permute-start(f32[128,2048]{1,0:T(8,128)} %get-tuple-element.56), channel_id=1, source_target_pairs={{0,1},{1,0},{2,3},{3,2},{4,5},{5,4},{6,7},{7,6},{8,9},{9,8},{10,11... | collective-permute-start | bytes 3145736 | tf_op jit(solution)/shard_map/ppermute | solution.py:236
  9.3 16.6 %collective-permute-start.2 = (f32[128,2048]{1,0:T(8,128)}, f32[128,2048]{1,0:T(8,128)}, u32[]{:S(2)}, u32[]{:S(2)}) collective-permute-start(f32[128,2048]{1,0:T(8,128)} %get-tuple-element.57), channel_id=1, source_target_pairs={{0,1},{1,0},{2,3},{3,2},{4,5},{5,4},{6,7},{7,6},{8,9},{9,8},{10,11... | collective-permute-start | bytes 3145736 | tf_op jit(solution)/shard_map/ppermute | solution.py:236
  17.7 17.4 %collective-permute-start.5 = (f32[1024,128]{1,0:T(8,128)}, f32[1024,128]{1,0:T(8,128)S(1)}, u32[]{:S(2)}, u32[]{:S(2)}) collective-permute-start(f32[1024,128]{1,0:T(8,128)} %get-tuple-element.66), channel_id=1, source_target_pairs={{0,2},{1,3},{2,4},{3,5},{4,6},{5,7},{8,10},{9,11},{10,12},{11,13},... | collective-permute-start | bytes 1572872 | tf_op jit(solution)/shard_map/ppermute | solution.py:240
  21.1 20.1 %collective-permute-start.6 = (f32[1024,128]{1,0:T(8,128)}, f32[1024,128]{1,0:T(8,128)}, u32[]{:S(2)}, u32[]{:S(2)}) collective-permute-start(f32[1024,128]{1,0:T(8,128)} %get-tuple-element.71), channel_id=1, source_target_pairs={{0,4},{1,5},{8,12},{9,13},{16,20},{17,21},{24,28},{25,29}} | collective-permute-start | bytes 1572872 | tf_op jit(solution)/shard_map/ppermute | solution.py:240
  33.1 15.0 %collective-permute-start.10 = (f32[1024,128]{1,0:T(8,128)}, f32[1024,128]{1,0:T(8,128)S(1)}, u32[]{:S(2)}, u32[]{:S(2)}) collective-permute-start(f32[1024,128]{1,0:T(8,128)} %get-tuple-element.69), channel_id=1, source_target_pairs={{6,4},{7,5},{4,2},{5,3},{2,0},{3,1},{14,12},{15,13},{12,10},{13,11... | collective-permute-start | bytes 1572872 | tf_op jit(solution)/shard_map/ppermute | solution.py:240
  34.4 16.0 %collective-permute-start.14 = (f32[1024,128]{1,0:T(8,128)}, f32[1024,128]{1,0:T(8,128)S(1)}, u32[]{:S(2)}, u32[]{:S(2)}) collective-permute-start(f32[1024,128]{1,0:T(8,128)} %get-tuple-element.88), channel_id=1, source_target_pairs={{6,2},{7,3},{14,10},{15,11},{22,18},{23,19},{30,26},{31,27}} | collective-permute-start | bytes 1572872 | tf_op jit(solution)/shard_map/ppermute | solution.py:240
  36.3 16.4 %collective-permute-start.7 = (f32[1024,128]{1,0:T(8,128)S(1)}, f32[1024,128]{1,0:T(8,128)S(1)}, u32[]{:S(2)}, u32[]{:S(2)}) collective-permute-start(f32[1024,128]{1,0:T(8,128)S(1)} %add.89), channel_id=1, source_target_pairs={{2,4},{3,5},{10,12},{11,13},{18,20},{19,21},{26,28},{27,29}} | collective-permute-start | bytes 1572872 | tf_op jit(solution)/shard_map/ppermute | solution.py:240
  37.1 17.0 %collective-permute-start.8 = (f32[1024,128]{1,0:T(8,128)S(1)}, f32[1024,128]{1,0:T(8,128)S(1)}, u32[]{:S(2)}, u32[]{:S(2)}) collective-permute-start(f32[1024,128]{1,0:T(8,128)S(1)} %add.89), channel_id=1, source_target_pairs={{2,6},{3,7},{10,14},{11,15},{18,22},{19,23},{26,30},{27,31}} | collective-permute-start | bytes 1572872 | tf_op jit(solution)/shard_map/ppermute | solution.py:240
  42.5 12.7 %collective-permute-start.9 = (f32[1024,128]{1,0:T(8,128)S(1)}, f32[1024,128]{1,0:T(8,128)S(1)}, u32[]{:S(2)}, u32[]{:S(2)}) collective-permute-start(f32[1024,128]{1,0:T(8,128)S(1)} %add_select_fusion.1), channel_id=1, source_target_pairs={{0,2},{1,3},{4,6},{5,7},{8,10},{9,11},{12,14},{13,15},{16,18},{17,... | collective-permute-start | bytes 1572872 | tf_op jit(solution)/shard_map/ppermute | solution.py:240
  49.0 37.3 %collective-permute-start.15 = (f32[1024,128]{1,0:T(8,128)}, f32[1024,128]{1,0:T(8,128)}, u32[]{:S(2)}, u32[]{:S(2)}) collective-permute-start(f32[1024,128]{1,0:T(8,128)} %add.92), channel_id=1, source_target_pairs={{4,2},{5,3},{12,10},{13,11},{20,18},{21,19},{28,26},{29,27}} | collective-permute-start | bytes 1572872 | tf_op jit(solution)/shard_map/ppermute | solution.py:240
  50.4 35.8 %collective-permute-start.16 = (f32[1024,128]{1,0:T(8,128)}, f32[1024,128]{1,0:T(8,128)}, u32[]{:S(2)}, u32[]{:S(2)}) collective-permute-start(f32[1024,128]{1,0:T(8,128)} %add.92), channel_id=1, source_target_pairs={{4,0},{5,1},{12,8},{13,9},{20,16},{21,17},{28,24},{29,25}} | collective-permute-start | bytes 1572872 | tf_op jit(solution)/shard_map/ppermute | solution.py:240
  52.6 33.6 %collective-permute-start.17 = (f32[1024,128]{1,0:T(8,128)}, f32[1024,128]{1,0:T(8,128)}, u32[]{:S(2)}, u32[]{:S(2)}) collective-permute-start(f32[1024,128]{1,0:T(8,128)} %add_select_fusion), channel_id=1, source_target_pairs={{6,4},{7,5},{2,0},{3,1},{14,12},{15,13},{10,8},{11,9},{22,20},{23,... | collective-permute-start | bytes 1572872 | tf_op jit(solution)/shard_map/ppermute | solution.py:240
  65.4 16.2 %collective-permute-start.11 = (f32[4,1,512]{2,1,0:T(1,128)}, f32[4,1,512]{2,1,0:T(1,128)S(1)}, u32[]{:S(2)}, u32[]{:S(2)}) collective-permute-start(f32[4,1,512]{2,1,0:T(1,128)} %get-tuple-element.79), channel_id=1, source_target_pairs={{0,2},{1,3},{2,0},{3,1},{4,6},{5,7},{6,4},{7,5},{8,10},{9,11},{10,... | collective-permute-start | bytes 24584 | tf_op jit(solution)/shard_map/ppermute | solution.py:240
  86.2 18.4 %collective-permute-start.18 = (f32[128,2048]{1,0:T(8,128)}, f32[128,2048]{1,0:T(8,128)S(1)}, u32[]{:S(2)}, u32[]{:S(2)}) collective-permute-start(f32[128,2048]{1,0:T(8,128)} %get-tuple-element.89), channel_id=1, source_target_pairs={{0,1},{1,0},{2,3},{3,2},{4,5},{5,4},{6,7},{7,6},{8,9},{9,8},{10,11... | collective-permute-start | bytes 3145736 | tf_op jit(solution)/shard_map/ppermute | solution.py:236
  89.7 8.0 %collective-permute-start.19 = (f32[256,128]{1,0:T(8,128)}, f32[256,128]{1,0:T(8,128)S(1)}, u32[]{:S(2)}, u32[]{:S(2)}) collective-permute-start(f32[256,128]{1,0:T(8,128)} %get-tuple-element.92), channel_id=1, source_target_pairs={{0,8},{8,0},{16,24},{24,16},{1,9},{9,1},{17,25},{25,17},{2,10},{10... | collective-permute-start | bytes 393224 | tf_op jit(solution)/shard_map/ppermute | solution.py:319
  98.7 7.4 %collective-permute-start.31 = (f32[256,128]{1,0:T(8,128)}, f32[256,128]{1,0:T(8,128)S(1)}, u32[]{:S(2)}, u32[]{:S(2)}) collective-permute-start(f32[256,128]{1,0:T(8,128)} %get-tuple-element.98), channel_id=1, source_target_pairs={{0,8},{8,0},{16,24},{24,16},{1,9},{9,1},{17,25},{25,17},{2,10},{10... | collective-permute-start | bytes 393224 | tf_op jit(solution)/shard_map/ppermute | solution.py:319
  108.7 10.5 %collective-permute-start.24 = (f32[256,128]{1,0:T(8,128)S(1)}, f32[256,128]{1,0:T(8,128)S(1)}, u32[]{:S(2)}, u32[]{:S(2)}) collective-permute-start(f32[256,128]{1,0:T(8,128)S(1)} %add.101.refs_0_), channel_id=1, source_target_pairs={{0,8},{8,0},{16,24},{24,16},{1,9},{9,1},{17,25},{25,17},{2,10},{10... | collective-permute-start | bytes 393224 | tf_op jit(solution)/shard_map/ppermute | solution.py:330
  112.8 8.3 %collective-permute-start.35 = (f32[256,128]{1,0:T(8,128)S(1)}, f32[256,128]{1,0:T(8,128)S(1)}, u32[]{:S(2)}, u32[]{:S(2)}) collective-permute-start(f32[256,128]{1,0:T(8,128)S(1)} %add.105), channel_id=1, source_target_pairs={{0,4},{1,5},{2,6},{3,7},{4,0},{5,1},{6,2},{7,3},{8,12},{9,13},{10,... | collective-permute-start | bytes 393224 | tf_op jit(solution)/shard_map/ppermute | solution.py:240
  113.7 7.4 %collective-permute-start.26 = (f32[256,128]{1,0:T(8,128)S(1)}, f32[256,128]{1,0:T(8,128)S(1)}, u32[]{:S(2)}, u32[]{:S(2)}) collective-permute-start(f32[256,128]{1,0:T(8,128)S(1)} %add.101.refs_0_), channel_id=1, source_target_pairs={{0,24},{8,16},{16,8},{24,0},{1,25},{9,17},{17,9},{25,1},{2,26},{10... | collective-permute-start | bytes 393224 | tf_op jit(solution)/shard_map/ppermute | solution.py:330
  114.9 7.7 %collective-permute-start.27 = (f32[256,128]{1,0:T(8,128)S(1)}, f32[256,128]{1,0:T(8,128)S(1)}, u32[]{:S(2)}, u32[]{:S(2)}) collective-permute-start(f32[256,128]{1,0:T(8,128)S(1)} %add.101.refs_0_), channel_id=1, source_target_pairs={{0,1},{1,0},{2,3},{3,2},{4,5},{5,4},{6,7},{7,6},{8,9},{9,8},{10,11... | collective-permute-start | bytes 393224 | tf_op jit(solution)/shard_map/ppermute | solution.py:236
  119.2 7.4 %collective-permute-start.29 = (f32[256,128]{1,0:T(8,128)S(1)}, f32[256,128]{1,0:T(8,128)S(1)}, u32[]{:S(2)}, u32[]{:S(2)}) collective-permute-start(f32[256,128]{1,0:T(8,128)S(1)} %collective-permute-done.25.refs_2_), channel_id=1, source_target_pairs={{0,1},{1,0},{2,3},{3,2},{4,5},{5,4},{6,7},{7,6},{8,9},{9,8},{10,11... | collective-permute-start | bytes 393224 | tf_op jit(solution)/shard_map/ppermute | solution.py:236
  121.2 7.3 %collective-permute-start.37 = (f32[256,128]{1,0:T(8,128)S(1)}, f32[256,128]{1,0:T(8,128)S(1)}, u32[]{:S(2)}, u32[]{:S(2)}) collective-permute-start(f32[256,128]{1,0:T(8,128)S(1)} %add.106.refs_8_), channel_id=1, source_target_pairs={{0,16},{8,24},{16,0},{24,8},{1,17},{9,25},{17,1},{25,9},{2,18},{10... | collective-permute-start | bytes 393224 | tf_op jit(solution)/shard_map/ppermute | solution.py:330
  122.6 6.9 %collective-permute-start.38 = (f32[256,128]{1,0:T(8,128)S(1)}, f32[256,128]{1,0:T(8,128)S(1)}, u32[]{:S(2)}, u32[]{:S(2)}) collective-permute-start(f32[256,128]{1,0:T(8,128)S(1)} %add.106.refs_8_), channel_id=1, source_target_pairs={{0,24},{8,16},{16,8},{24,0},{1,25},{9,17},{17,9},{25,1},{2,26},{10... | collective-permute-start | bytes 393224 | tf_op jit(solution)/shard_map/ppermute | solution.py:330
  123.8 7.2 %collective-permute-start.30 = (f32[256,128]{1,0:T(8,128)S(1)}, f32[256,128]{1,0:T(8,128)S(1)}, u32[]{:S(2)}, u32[]{:S(2)}) collective-permute-start(f32[256,128]{1,0:T(8,128)S(1)} %collective-permute-done.26.refs_3_), channel_id=1, source_target_pairs={{0,1},{1,0},{2,3},{3,2},{4,5},{5,4},{6,7},{7,6},{8,9},{9,8},{10,11... | collective-permute-start | bytes 393224 | tf_op jit(solution)/shard_map/ppermute | solution.py:236
  (23 other events, 133.8 us)

commit v10 on v9

--- a/solution.py
+++ b/solution.py
@@ -91,8 +91,10 @@
     keys = tokens_of(k_ref, kg_ref)
     values = tokens_of(v_ref, vg_ref)
     scores = mm_nt(w_ref[...].reshape(group * width, dim), keys)
+    yield
     probs = stack(*[both_soft(scores[a : a + width]) for a in range(0, group * width, width)])
     features = probs.astype(BF)
+    yield
     kp_ref[0] = probs
     kb_ref[0] = features
     norm_ref[0] = mm_nt(jnp.ones((16, keys.shape[0]), BF), features)[:1]
@@ -115,11 +117,14 @@
     cols = [slice(i * dim, (i + 1) * dim) for i in heads]
     rows = [slice(i * feats, (i + 1) * feats) for i in heads]
     scores = [mm_nt(w_ref[i], queries[:, cols[i]]) for i in heads]
+    yield
     probs = [both_soft(x) for x in scores]
     query_t = [x.astype(BF) for x in probs]
     query_rows = [x.T for x in query_t]
+    yield
     weights = [mm(query_rows[i], kb_ref[0, rows[i]]) for i in heads]
     weights = [jnp.where(causal, x, 0.0).astype(BF) for x in weights]
+    yield
     norms = split(jnp.broadcast_to(pn_ref[0], (dim, group * feats)))
     ones = jnp.ones((dim, length), BF)
     den = [
@@ -129,7 +134,9 @@
         )
         for i in heads
     ]
+    yield
     scaled = [(upstream[:, cols[i]] * (1.0 / den[i])).astype(BF) for i in heads]
+    yield
     sums = [mm(query_t[i], scaled[i]) for i in heads]
     for i in heads:
         qp_ref[0, rows[i]] = probs[i]
@@ -170,13 +177,16 @@
         )
         for i in heads
     ]
+    yield
     numerator = [x[:, :dim] for x in both]
     inverse = [1.0 / x[:, dim:] for x in both]
     scaled_wide = [upstream[:, cols[i]] * inverse[i] for i in heads]
     scaled = [x.astype(BF) for x in scaled_wide]
     products = [cat(*split(-(scaled_wide[i] * inverse[i]) * numerator[i])) for i in heads]
     ones = jnp.ones((2 * dim, dim), BF)
+    yield
     norm_grad = [mm(x, ones) for x in products]
+    yield
     for i in heads:
         result = numerator[i] * inverse[i]
         att_ref[:, cols[i]] = result[:own].astype(BF)
@@ -188,7 +198,9 @@
     lane = lax.broadcasted_iota(jnp.int32, (length, dim), 1)
     values_lanes = cat(values, jnp.where(lane < 2, 1.0, 0.0).astype(BF))
     mixed = [mm_nt(cat(scaled[i], lanes[i]), values_lanes) for i in heads]
+    yield
     block = [jnp.where(causal, x, 0.0).astype(BF) for x in mixed]
+    yield
     upstream_q = [
         mm_nt(
             cat(kb_ref[0, rows[i]], high[rows[i]], norm_cols[rows[i]], low[rows[i]]),
@@ -196,8 +208,10 @@
         )
         for i in heads
     ]
+    yield
     probs = [qp_ref[0, r] for r in rows]
     back = [soft_back(probs[i], upstream_q[i]) for i in heads]
+    yield
     for i in heads:
         gq_ref[i * width : (i + 1) * width] = mm(back[i], queries[:, cols[i]])
         gk_ref[0, rows[i]] = mm(probs[i].astype(BF), block[i])
@@ -212,16 +226,19 @@
     values = tokens_of(v_ref, vg_ref)
     state = cat(*split(before_of(info[2 * n + 2], step < n // 2, near, far, passed, passed_far, last)))
     upstream = gk_ref[0] + mm_nt(state, cat(values, values))
+    yield
     upstream = upstream + jnp.broadcast_to(column(sn_ref[0]), (rows, length))
     back = [
         soft_back(kp_ref[0, a : a + feats], upstream[a : a + feats])
         for a in range(0, rows, feats)
     ]
+    yield
     out_ref[...] = mm(stack(*back), tokens_of(k_ref, kg_ref))
 
 
 def attended_kernel(n, i, info, x_ref, o_ref):
     o_ref[...] = x_ref[...].astype(BF)
+    yield
 
 
 def out_kernel(info, *refs):
@@ -289,6 +306,7 @@
 
 def scan_norms(norm, chip, chips, forward, *earlier):
     base = jnp.zeros_like(norm)
+    moved = norm
     if earlier and chips <= 4:
         bits = range(1, chips)
         moved = [chip_move(norm, [(i, i ^ bit) for i in range(chips)]) for bit in bits]
@@ -296,7 +314,7 @@
         for bit in bits:
             other = chip ^ bit
             base = base + jnp.where(other < chip if forward else other > chip, moved[bit - 1], 0.0)
-        return base
+        return base, moved[-1]
     total = norm
     bit = 1
     while bit < chips:
@@ -305,7 +323,7 @@
         base = base + jnp.where(upper, moved, 0.0)
         total = total + moved
         bit *= 2
-    return base
+    return base, moved
 
 
 def sum_all(mine, chips, *earlier):
@@ -391,7 +409,7 @@
             return pltpu.with_memory_space_constraint(x, pltpu.HBM)
         return x
 
-    def call(name, body, in_specs, out_specs, out_shape, aliases=None):
+    def call(name, body, in_specs, out_specs, out_shape, aliases=None, side_by_side=1):
         in_specs = [x if isinstance(x, tuple) else (x, 0, n) for x in in_specs]
         kinds = [x.dtype for x in out_shape]
         results = {}
@@ -432,12 +450,19 @@
             for i in range(n):
                 for copy in incoming(i):
                     copy.start()
-            for i in range(n):
-                for copy in incoming(i):
-                    copy.wait()
-                blocks = [buf.at[i % period] for (_, _, period), buf in zip(in_specs, in_bufs)]
-                body(n, i, info, *blocks, *[buf.at[i] for buf in out_bufs])
-                outgoing(i, lambda copy: copy.start())
+            for first in range(0, n, side_by_side):
+                steps = range(first, first + side_by_side)
+                for i in steps:
+                    for copy in incoming(i):
+                        copy.wait()
+                running = []
+                for i in steps:
+                    blocks = [buf.at[i % period] for (_, _, period), buf in zip(in_specs, in_bufs)]
+                    running.append(body(n, i, info, *blocks, *[buf.at[i] for buf in out_bufs]))
+                while running:
+                    running = [x for x in running if next(x, True) is None]
+                for i in steps:
+                    outgoing(i, lambda copy: copy.start())
             for i in range(n):
                 outgoing(i, lambda copy: copy.wait())
 
@@ -515,8 +540,8 @@
         [flat, shape_of(wide, length, dtype=BF), row] + [half_state] * 3 + [wide_flat] * 2,
     )(keys, keys_got, values, values_got, key_map, queries, cotangent)
     queries_got, cotangent_got = [core_swap(x) for x in packed]
-    prefix_norm = scan_norms(norm, chip, chips, True)
-    prefix = Scan(*after((a, b, near), prefix_norm), True)
+    prefix_norm, norm_moved = scan_norms(norm, chip, chips, True)
+    prefix = Scan(*after((a, b, near), norm_moved), True)
     prefix.first()
 
     rows_spec = per_head(group, length, dim)
@@ -527,6 +552,7 @@
         [own_cols(four), got_cols(four)] * 2 + [map_spec, flat_spec, row_spec],
         each(flat_spec, rows_spec, per_head(group, length, length)) + states(3, 2),
         [flat, rows_bf, shape_of(group, length, length, dtype=BF)] + [half_state] * 3,
+        side_by_side=2,
     )(queries, queries_got, cotangent, cotangent_got, query_map, key_features, prefix_norm)
     suffix = Scan(a, b, near, False)
     suffix.first()
@@ -556,7 +582,7 @@
         queries, queries_got, cotangent, cotangent_got, values, values_got, key_features,
         query_probs, query_rows, weights, prefix_norm, *before,
     )
-    suffix_norm = scan_norms(norm, chip, chips, False, *query_part)
+    suffix_norm, _ = scan_norms(norm, chip, chips, False, *query_part)
     key_part = call(
         "key_grads",
         key_grad_kernel,
@@ -565,6 +591,7 @@
         + moved_specs,
         spread(0),
         [grad] * n,
+        side_by_side=2,
     )(keys, keys_got, values, values_got, key_probs, key_up, suffix_norm, *later)
     (attended,) = call(
         "attended",

time: 135 us -> 135 us (level)
  no operation moved by 1% of the time
where the time goes in v10:
time: 135 us; the launch traced here: 134 us
  starting transfers between devices  79.2 us (59%)
  Pallas kernels  31.3 us (23%)
  waiting for transfers between devices  15.9 us (12%)
  other arithmetic  5.25 us (4%)
    ppermute x19, starting transfers between devices, chip_move(): lax.ppermute(x, 'ctx', [(2 * a + c, 2 * b + c) for a, b in pairs for c in...  48.9 us
    pallas_call x5, Pallas kernels, run(): pl.pallas_call(kernel, name=name, out_shape=[pltpu.HBM(x.shape, x.dtype)...  29.3 us
    ppermute x12, starting transfers between devices, core_swap(): return lax.ppermute(x, 'ctx', [(i, i ^ 1) for i in range(size)])  17 us
    ppermute x19, waiting for transfers between devices, chip_move(): lax.ppermute(x, 'ctx', [(2 * a + c, 2 * b + c) for a, b in pairs for c in...  11.7 us
    ppermute x6, starting transfers between devices, sum_all(): lax.ppermute(total, 'dp', [(i, i ^ k) for i in range(dp)])  7.93 us
    ppermute x6, starting transfers between devices, sum_all(): lax.ppermute(blocks[k], 'dp', [(i, i ^ k) for i in range(dp)])  5.38 us
    ppermute x12, waiting for transfers between devices, core_swap(): return lax.ppermute(x, 'ctx', [(i, i ^ 1) for i in range(size)])  2.75 us
  transfers between devices with their start and end apart: 43, of which 13 were waited for; matrix products, arithmetic and copies ran while one was open for 4% of the time, Pallas kernels for 18%

profile of v10, /device:TPU:1, one launch (start us, length us, event | category | flops | bytes accessed | tf_op | source)
XLA Modules:
  0.0 133.8 jit_solution(16691724458089644268)
XLA Ops:
  1.9 1.8 %collective-permute-done.refs_1_.refs_3_.refs_5_ = f32[256,512]{1,0:T(8,128)S(1)} collective-permute-done((f32[256,512]{1,0:T(8,128)S(1)}, f32[256,512]{1,0:T(8,128)S(1)}, u32[]{:S(2)}, u32[]{:S(2)}) %collective-permute-start) | collective-permute-done | bytes 524320 | tf_op jit(solution)/shard_map/ppermute | solution.py:253
  3.7 5.4 %key_features.1 = (f32[4,512,256]{2,1,0:T(8,128)}, bf16[4,512,256]{2,1,0:T(8,128)(2,1)}, f32[4,1,512]{2,1,0:T(1,128)}, f32[1024,128]{1,0:T(8,128)}, f32[1024,128...) custom-call(s32[11]{0:T(128)S(1)} %concatenate.6.info, bf16[128,1024]{1,0:T(8,128)(2,1)} %bitcast.29, ...), custom_call_target="tpu_custom_call" | custom-call | tf_op jit(solution)/shard_map/key_features/pallas_call | solution.py:475
  9.7 2.5 %collective-permute-start.3 = (f32[4,1,512]{2,1,0:T(1,128)}, f32[4,1,512]{2,1,0:T(1,128)S(1)}, u32[]{:S(2)}, u32[]{:S(2)}) collective-permute-start(f32[4,1,512]{2,1,0:T(1,128)} %get-tuple-element.59), channel_id=1, source_target_pairs={{0,2},{1,3},{2,0},{3,1},{4,6},{5,7},{6,4},{7,5},{8,10},{9,11},{10,... | collective-permute-start | bytes 24584 | tf_op jit(solution)/shard_map/ppermute | solution.py:257
  14.2 2.5 %collective-permute-start.4 = (f32[4,1,512]{2,1,0:T(1,128)S(1)}, f32[4,1,512]{2,1,0:T(1,128)S(1)}, u32[]{:S(2)}, u32[]{:S(2)}) collective-permute-start(f32[4,1,512]{2,1,0:T(1,128)S(1)} %add.87), channel_id=1, source_target_pairs={{0,4},{1,5},{2,6},{3,7},{4,0},{5,1},{6,2},{7,3},{8,12},{9,13},{10,... | collective-permute-start | bytes 24584 | tf_op jit(solution)/shard_map/ppermute | solution.py:257
  17.7 3.3 %collective-permute-start.5 = (f32[1024,128]{1,0:T(8,128)}, f32[1024,128]{1,0:T(8,128)S(1)}, u32[]{:S(2)}, u32[]{:S(2)}) collective-permute-start(f32[1024,128]{1,0:T(8,128)} %get-tuple-element.66), channel_id=1, source_target_pairs={{0,2},{1,3},{2,4},{3,5},{4,6},{5,7},{8,10},{9,11},{10,12},{11,13},... | collective-permute-start | bytes 1572872 | tf_op jit(solution)/shard_map/ppermute | solution.py:257
  21.0 4.9 %collective-permute-start.6 = (f32[1024,128]{1,0:T(8,128)}, f32[1024,128]{1,0:T(8,128)}, u32[]{:S(2)}, u32[]{:S(2)}) collective-permute-start(f32[1024,128]{1,0:T(8,128)} %get-tuple-element.71), channel_id=1, source_target_pairs={{0,4},{1,5},{8,12},{9,13},{16,20},{17,21},{24,28},{25,29}} | collective-permute-start | bytes 1572872 | tf_op jit(solution)/shard_map/ppermute | solution.py:257
  26.0 6.9 %query_features.1 = (f32[4,512,256]{2,1,0:T(8,128)}, bf16[4,4,256,128]{3,2,1,0:T(8,128)(2,1)}, bf16[4,4,256,256]{3,2,1,0:T(8,128)(2,1)}, f32[1024,128]{1,0:T(8,1...) custom-call(s32[11]{0:T(128)S(1)} %concatenate.6.info, bf16[128,4096]{1,0:T(8,128)(2,1)} %bitcast.21, ...), custom_call_target="tpu_custom_call" | custom-call | tf_op jit(solution)/shard_map/query_features/pallas_call | solution.py:475
  37.6 3.5 %collective-permute-done.6.refs_12_ = f32[1024,128]{1,0:T(8,128)} collective-permute-done((f32[1024,128]{1,0:T(8,128)}, f32[1024,128]{1,0:T(8,128)}, u32[]{:S(2)}, u32[]{:S(2)}) %collective-permute-start.6) | collective-permute-done | bytes 524320 | tf_op jit(solution)/shard_map/ppermute | solution.py:257
  42.5 5.4 %collective-permute-start.9 = (f32[1024,128]{1,0:T(8,128)S(1)}, f32[1024,128]{1,0:T(8,128)S(1)}, u32[]{:S(2)}, u32[]{:S(2)}) collective-permute-start(f32[1024,128]{1,0:T(8,128)S(1)} %add_select_fusion.1), channel_id=1, source_target_pairs={{0,2},{1,3},{4,6},{5,7},{8,10},{9,11},{12,14},{13,15},{16,18},{17,... | collective-permute-start | bytes 1572872 | tf_op jit(solution)/shard_map/ppermute | solution.py:257
  54.9 10.3 %attend.1 = (bf16[128,4096]{1,0:T(8,128)(2,1)}, f32[128,2048]{1,0:T(8,128)}, f32[4,1,512]{2,1,0:T(1,128)}, f32[4,512,256]{2,1,0:T(8,128)}, f32[256,128]{1,0:T(8,...) custom-call(s32[11]{0:T(128)S(1)} %concatenate.6.info, bf16[128,4096]{1,0:T(8,128)(2,1)} %bitcast.22, ...), custom_call_target="tpu_custom_call" | custom-call | tf_op jit(solution)/shard_map/attend/pallas_call | solution.py:475
  65.2 13.0 %collective-permute-start.11 = (f32[4,1,512]{2,1,0:T(1,128)}, f32[4,1,512]{2,1,0:T(1,128)S(1)}, u32[]{:S(2)}, u32[]{:S(2)}) collective-permute-start(f32[4,1,512]{2,1,0:T(1,128)} %get-tuple-element.79), channel_id=1, source_target_pairs={{0,2},{1,3},{2,0},{3,1},{4,6},{5,7},{6,4},{7,5},{8,10},{9,11},{10,... | collective-permute-start | bytes 24584 | tf_op jit(solution)/shard_map/ppermute | solution.py:257
  78.2 3.1 %collective-permute-start.12 = (f32[4,1,512]{2,1,0:T(1,128)}, f32[4,1,512]{2,1,0:T(1,128)S(1)}, u32[]{:S(2)}, u32[]{:S(2)}) collective-permute-start(f32[4,1,512]{2,1,0:T(1,128)} %get-tuple-element.79), channel_id=1, source_target_pairs={{0,4},{1,5},{2,6},{3,7},{4,0},{5,1},{6,2},{7,3},{8,12},{9,13},{10,... | collective-permute-start | bytes 24584 | tf_op jit(solution)/shard_map/ppermute | solution.py:257
  81.5 2.2 %collective-permute-start.13 = (f32[4,1,512]{2,1,0:T(1,128)}, f32[4,1,512]{2,1,0:T(1,128)S(1)}, u32[]{:S(2)}, u32[]{:S(2)}) collective-permute-start(f32[4,1,512]{2,1,0:T(1,128)} %get-tuple-element.79), channel_id=1, source_target_pairs={{0,6},{1,7},{2,4},{3,5},{4,2},{5,3},{6,0},{7,1},{8,14},{9,15},{10,... | collective-permute-start | bytes 24584 | tf_op jit(solution)/shard_map/ppermute | solution.py:257
  83.7 2.3 %collective-permute-done.13 = f32[4,1,512]{2,1,0:T(1,128)S(1)} collective-permute-done((f32[4,1,512]{2,1,0:T(1,128)}, f32[4,1,512]{2,1,0:T(1,128)S(1)}, u32[]{:S(2)}, u32[]{:S(2)}) %collective-permute-start.13) | collective-permute-done | bytes 8224 | tf_op jit(solution)/shard_map/ppermute | solution.py:257
  86.1 3.4 %collective-permute-start.18 = (f32[128,2048]{1,0:T(8,128)}, f32[128,2048]{1,0:T(8,128)S(1)}, u32[]{:S(2)}, u32[]{:S(2)}) collective-permute-start(f32[128,2048]{1,0:T(8,128)} %get-tuple-element.89), channel_id=1, source_target_pairs={{0,1},{1,0},{2,3},{3,2},{4,5},{5,4},{6,7},{7,6},{8,9},{9,8},{10,11... | collective-permute-start | bytes 3145736 | tf_op jit(solution)/shard_map/ppermute | solution.py:253
  92.2 5.3 %key_grads.1 = (f32[256,128]{1,0:T(8,128)}, f32[256,128]{1,0:T(8,128)}, f32[256,128]{1,0:T(8,128)}, f32[256,128]{1,0:T(8,128)}) custom-call(s32[11]{0:T(128)S(1)} %concatenate.6.info, bf16[128,1024]{1,0:T(8,128)(2,1)} %bitcast.30, f32[256,512]{1,0:T(8,128)S(1)} %collective-permute-done.refs_1_.refs_3_.refs_5_, bf16[128,1024]{1,0:T(8,128)(2,1)} %bitcast.28, ...), custom_call_target="tpu_custom_call" | custom-call | tf_op jit(solution)/shard_map/key_grads/pallas_call | solution.py:475
  102.3 2.1 %collective-permute-start.23 = (f32[256,128]{1,0:T(8,128)S(1)}, f32[256,128]{1,0:T(8,128)S(1)}, u32[]{:S(2)}, u32[]{:S(2)}) collective-permute-start(f32[256,128]{1,0:T(8,128)S(1)} %add.100), channel_id=1, source_target_pairs={{0,4},{1,5},{2,6},{3,7},{4,0},{5,1},{6,2},{7,3},{8,12},{9,13},{10,... | collective-permute-start | bytes 393224 | tf_op jit(solution)/shard_map/ppermute | solution.py:257
  104.4 1.5 %attended.1 = bf16[128,4096]{1,0:T(8,128)(2,1)} custom-call(s32[11]{0:T(128)S(1)} %concatenate.6.info, f32[128,2048]{1,0:T(8,128)S(1)} %collective-permute-done.18.refs_0_, bf16[128,4096]{1,0:T(8,128)(2,1)} %get-tuple-element.90.refs_1_), custom_call_target="tpu_custom_call", output_to_operand_aliasing={{}: (2, {})} | custom-call | tf_op jit(solution)/shard_map/attended/pallas_call | solution.py:475
  108.5 4.0 %collective-permute-start.24 = (f32[256,128]{1,0:T(8,128)S(1)}, f32[256,128]{1,0:T(8,128)S(1)}, u32[]{:S(2)}, u32[]{:S(2)}) collective-permute-start(f32[256,128]{1,0:T(8,128)S(1)} %add.101.refs_0_), channel_id=1, source_target_pairs={{0,8},{8,0},{16,24},{24,16},{1,9},{9,1},{17,25},{25,17},{2,10},{10... | collective-permute-start | bytes 393224 | tf_op jit(solution)/shard_map/ppermute | solution.py:348
  114.7 4.3 %collective-permute-start.27 = (f32[256,128]{1,0:T(8,128)S(1)}, f32[256,128]{1,0:T(8,128)S(1)}, u32[]{:S(2)}, u32[]{:S(2)}) collective-permute-start(f32[256,128]{1,0:T(8,128)S(1)} %add.101.refs_0_), channel_id=1, source_target_pairs={{0,1},{1,0},{2,3},{3,2},{4,5},{5,4},{6,7},{7,6},{8,9},{9,8},{10,11... | collective-permute-start | bytes 393224 | tf_op jit(solution)/shard_map/ppermute | solution.py:253
  121.0 1.5 %collective-permute-start.37 = (f32[256,128]{1,0:T(8,128)S(1)}, f32[256,128]{1,0:T(8,128)S(1)}, u32[]{:S(2)}, u32[]{:S(2)}) collective-permute-start(f32[256,128]{1,0:T(8,128)S(1)} %add.106.refs_8_), channel_id=1, source_target_pairs={{0,16},{8,24},{16,0},{24,8},{1,17},{9,25},{17,1},{25,9},{2,18},{10... | collective-permute-start | bytes 393224 | tf_op jit(solution)/shard_map/ppermute | solution.py:348
  123.6 2.7 %collective-permute-start.30 = (f32[256,128]{1,0:T(8,128)S(1)}, f32[256,128]{1,0:T(8,128)S(1)}, u32[]{:S(2)}, u32[]{:S(2)}) collective-permute-start(f32[256,128]{1,0:T(8,128)S(1)} %collective-permute-done.26.refs_3_), channel_id=1, source_target_pairs={{0,1},{1,0},{2,3},{3,2},{4,5},{5,4},{6,7},{7,6},{8,9},{9,8},{10,11... | collective-permute-start | bytes 393224 | tf_op jit(solution)/shard_map/ppermute | solution.py:253
  126.5 1.8 %collective-permute-start.40 = (f32[256,128]{1,0:T(8,128)S(1)}, f32[256,128]{1,0:T(8,128)S(1)}, u32[]{:S(2)}, u32[]{:S(2)}) collective-permute-start(f32[256,128]{1,0:T(8,128)S(1)} %collective-permute-done.36.refs_9_), channel_id=1, source_target_pairs={{0,1},{1,0},{2,3},{3,2},{4,5},{5,4},{6,7},{7,6},{8,9},{9,8},{10,11... | collective-permute-start | bytes 393224 | tf_op jit(solution)/shard_map/ppermute | solution.py:253
  131.8 2.0 %sums_out.1 = (f32[8,256,128]{2,1,0:T(8,128)}, f32[8,256,128]{2,1,0:T(8,128)}) custom-call(s32[11]{0:T(128)S(1)} %concatenate.6.info, f32[256,128]{1,0:T(8,128)S(1)} %add.101.refs_0_, f32[256,128]{1,0:T(8,128)S(1)} %collective-permute-done.24.refs_1_, f32[256,128]{1,0:T(8,128)S(1)} %collective-permute-done.25.refs_2_, ...), custom_call_target="tpu_custom_call" | custom-call | tf_op jit(solution)/shard_map/sums_out/pallas_call | solution.py:608
  (93 shorter events, 37.0 us)
Async XLA Ops:
  9.1 16.8 %collective-permute-start.1 = (f32[128,2048]{1,0:T(8,128)}, f32[128,2048]{1,0:T(8,128)S(1)}, u32[]{:S(2)}, u32[]{:S(2)}) collective-permute-start(f32[128,2048]{1,0:T(8,128)} %get-tuple-element.56), channel_id=1, source_target_pairs={{0,1},{1,0},{2,3},{3,2},{4,5},{5,4},{6,7},{7,6},{8,9},{9,8},{10,11... | collective-permute-start | bytes 3145736 | tf_op jit(solution)/shard_map/ppermute | solution.py:253
  9.3 16.6 %collective-permute-start.2 = (f32[128,2048]{1,0:T(8,128)}, f32[128,2048]{1,0:T(8,128)}, u32[]{:S(2)}, u32[]{:S(2)}) collective-permute-start(f32[128,2048]{1,0:T(8,128)} %get-tuple-element.57), channel_id=1, source_target_pairs={{0,1},{1,0},{2,3},{3,2},{4,5},{5,4},{6,7},{7,6},{8,9},{9,8},{10,11... | collective-permute-start | bytes 3145736 | tf_op jit(solution)/shard_map/ppermute | solution.py:253
  17.7 17.2 %collective-permute-start.5 = (f32[1024,128]{1,0:T(8,128)}, f32[1024,128]{1,0:T(8,128)S(1)}, u32[]{:S(2)}, u32[]{:S(2)}) collective-permute-start(f32[1024,128]{1,0:T(8,128)} %get-tuple-element.66), channel_id=1, source_target_pairs={{0,2},{1,3},{2,4},{3,5},{4,6},{5,7},{8,10},{9,11},{10,12},{11,13},... | collective-permute-start | bytes 1572872 | tf_op jit(solution)/shard_map/ppermute | solution.py:257
  21.0 20.1 %collective-permute-start.6 = (f32[1024,128]{1,0:T(8,128)}, f32[1024,128]{1,0:T(8,128)}, u32[]{:S(2)}, u32[]{:S(2)}) collective-permute-start(f32[1024,128]{1,0:T(8,128)} %get-tuple-element.71), channel_id=1, source_target_pairs={{0,4},{1,5},{8,12},{9,13},{16,20},{17,21},{24,28},{25,29}} | collective-permute-start | bytes 1572872 | tf_op jit(solution)/shard_map/ppermute | solution.py:257
  32.9 15.0 %collective-permute-start.10 = (f32[1024,128]{1,0:T(8,128)}, f32[1024,128]{1,0:T(8,128)S(1)}, u32[]{:S(2)}, u32[]{:S(2)}) collective-permute-start(f32[1024,128]{1,0:T(8,128)} %get-tuple-element.69), channel_id=1, source_target_pairs={{6,4},{7,5},{4,2},{5,3},{2,0},{3,1},{14,12},{15,13},{12,10},{13,11... | collective-permute-start | bytes 1572872 | tf_op jit(solution)/shard_map/ppermute | solution.py:257
  34.2 16.0 %collective-permute-start.14 = (f32[1024,128]{1,0:T(8,128)}, f32[1024,128]{1,0:T(8,128)S(1)}, u32[]{:S(2)}, u32[]{:S(2)}) collective-permute-start(f32[1024,128]{1,0:T(8,128)} %get-tuple-element.88), channel_id=1, source_target_pairs={{6,2},{7,3},{14,10},{15,11},{22,18},{23,19},{30,26},{31,27}} | collective-permute-start | bytes 1572872 | tf_op jit(solution)/shard_map/ppermute | solution.py:257
  36.1 16.4 %collective-permute-start.7 = (f32[1024,128]{1,0:T(8,128)S(1)}, f32[1024,128]{1,0:T(8,128)S(1)}, u32[]{:S(2)}, u32[]{:S(2)}) collective-permute-start(f32[1024,128]{1,0:T(8,128)S(1)} %add.89), channel_id=1, source_target_pairs={{2,4},{3,5},{10,12},{11,13},{18,20},{19,21},{26,28},{27,29}} | collective-permute-start | bytes 1572872 | tf_op jit(solution)/shard_map/ppermute | solution.py:257
  36.9 17.0 %collective-permute-start.8 = (f32[1024,128]{1,0:T(8,128)S(1)}, f32[1024,128]{1,0:T(8,128)S(1)}, u32[]{:S(2)}, u32[]{:S(2)}) collective-permute-start(f32[1024,128]{1,0:T(8,128)S(1)} %add.89), channel_id=1, source_target_pairs={{2,6},{3,7},{10,14},{11,15},{18,22},{19,23},{26,30},{27,31}} | collective-permute-start | bytes 1572872 | tf_op jit(solution)/shard_map/ppermute | solution.py:257
  42.5 12.5 %collective-permute-start.9 = (f32[1024,128]{1,0:T(8,128)S(1)}, f32[1024,128]{1,0:T(8,128)S(1)}, u32[]{:S(2)}, u32[]{:S(2)}) collective-permute-start(f32[1024,128]{1,0:T(8,128)S(1)} %add_select_fusion.1), channel_id=1, source_target_pairs={{0,2},{1,3},{4,6},{5,7},{8,10},{9,11},{12,14},{13,15},{16,18},{17,... | collective-permute-start | bytes 1572872 | tf_op jit(solution)/shard_map/ppermute | solution.py:257
  48.7 37.3 %collective-permute-start.15 = (f32[1024,128]{1,0:T(8,128)}, f32[1024,128]{1,0:T(8,128)}, u32[]{:S(2)}, u32[]{:S(2)}) collective-permute-start(f32[1024,128]{1,0:T(8,128)} %add.92), channel_id=1, source_target_pairs={{4,2},{5,3},{12,10},{13,11},{20,18},{21,19},{28,26},{29,27}} | collective-permute-start | bytes 1572872 | tf_op jit(solution)/shard_map/ppermute | solution.py:257
  50.2 35.9 %collective-permute-start.16 = (f32[1024,128]{1,0:T(8,128)}, f32[1024,128]{1,0:T(8,128)}, u32[]{:S(2)}, u32[]{:S(2)}) collective-permute-start(f32[1024,128]{1,0:T(8,128)} %add.92), channel_id=1, source_target_pairs={{4,0},{5,1},{12,8},{13,9},{20,16},{21,17},{28,24},{29,25}} | collective-permute-start | bytes 1572872 | tf_op jit(solution)/shard_map/ppermute | solution.py:257
  52.4 33.6 %collective-permute-start.17 = (f32[1024,128]{1,0:T(8,128)}, f32[1024,128]{1,0:T(8,128)}, u32[]{:S(2)}, u32[]{:S(2)}) collective-permute-start(f32[1024,128]{1,0:T(8,128)} %add_select_fusion), channel_id=1, source_target_pairs={{6,4},{7,5},{2,0},{3,1},{14,12},{15,13},{10,8},{11,9},{22,20},{23,... | collective-permute-start | bytes 1572872 | tf_op jit(solution)/shard_map/ppermute | solution.py:257
  65.2 16.3 %collective-permute-start.11 = (f32[4,1,512]{2,1,0:T(1,128)}, f32[4,1,512]{2,1,0:T(1,128)S(1)}, u32[]{:S(2)}, u32[]{:S(2)}) collective-permute-start(f32[4,1,512]{2,1,0:T(1,128)} %get-tuple-element.79), channel_id=1, source_target_pairs={{0,2},{1,3},{2,0},{3,1},{4,6},{5,7},{6,4},{7,5},{8,10},{9,11},{10,... | collective-permute-start | bytes 24584 | tf_op jit(solution)/shard_map/ppermute | solution.py:257
  86.1 18.3 %collective-permute-start.18 = (f32[128,2048]{1,0:T(8,128)}, f32[128,2048]{1,0:T(8,128)S(1)}, u32[]{:S(2)}, u32[]{:S(2)}) collective-permute-start(f32[128,2048]{1,0:T(8,128)} %get-tuple-element.89), channel_id=1, source_target_pairs={{0,1},{1,0},{2,3},{3,2},{4,5},{5,4},{6,7},{7,6},{8,9},{9,8},{10,11... | collective-permute-start | bytes 3145736 | tf_op jit(solution)/shard_map/ppermute | solution.py:253
  89.5 7.9 %collective-permute-start.19 = (f32[256,128]{1,0:T(8,128)}, f32[256,128]{1,0:T(8,128)S(1)}, u32[]{:S(2)}, u32[]{:S(2)}) collective-permute-start(f32[256,128]{1,0:T(8,128)} %get-tuple-element.92), channel_id=1, source_target_pairs={{0,8},{8,0},{16,24},{24,16},{1,9},{9,1},{17,25},{25,17},{2,10},{10... | collective-permute-start | bytes 393224 | tf_op jit(solution)/shard_map/ppermute | solution.py:337
  98.5 7.4 %collective-permute-start.31 = (f32[256,128]{1,0:T(8,128)}, f32[256,128]{1,0:T(8,128)S(1)}, u32[]{:S(2)}, u32[]{:S(2)}) collective-permute-start(f32[256,128]{1,0:T(8,128)} %get-tuple-element.98), channel_id=1, source_target_pairs={{0,8},{8,0},{16,24},{24,16},{1,9},{9,1},{17,25},{25,17},{2,10},{10... | collective-permute-start | bytes 393224 | tf_op jit(solution)/shard_map/ppermute | solution.py:337
  108.5 10.5 %collective-permute-start.24 = (f32[256,128]{1,0:T(8,128)S(1)}, f32[256,128]{1,0:T(8,128)S(1)}, u32[]{:S(2)}, u32[]{:S(2)}) collective-permute-start(f32[256,128]{1,0:T(8,128)S(1)} %add.101.refs_0_), channel_id=1, source_target_pairs={{0,8},{8,0},{16,24},{24,16},{1,9},{9,1},{17,25},{25,17},{2,10},{10... | collective-permute-start | bytes 393224 | tf_op jit(solution)/shard_map/ppermute | solution.py:348
  112.6 8.3 %collective-permute-start.35 = (f32[256,128]{1,0:T(8,128)S(1)}, f32[256,128]{1,0:T(8,128)S(1)}, u32[]{:S(2)}, u32[]{:S(2)}) collective-permute-start(f32[256,128]{1,0:T(8,128)S(1)} %add.105), channel_id=1, source_target_pairs={{0,4},{1,5},{2,6},{3,7},{4,0},{5,1},{6,2},{7,3},{8,12},{9,13},{10,... | collective-permute-start | bytes 393224 | tf_op jit(solution)/shard_map/ppermute | solution.py:257
  113.5 7.5 %collective-permute-start.26 = (f32[256,128]{1,0:T(8,128)S(1)}, f32[256,128]{1,0:T(8,128)S(1)}, u32[]{:S(2)}, u32[]{:S(2)}) collective-permute-start(f32[256,128]{1,0:T(8,128)S(1)} %add.101.refs_0_), channel_id=1, source_target_pairs={{0,24},{8,16},{16,8},{24,0},{1,25},{9,17},{17,9},{25,1},{2,26},{10... | collective-permute-start | bytes 393224 | tf_op jit(solution)/shard_map/ppermute | solution.py:348
  114.7 7.8 %collective-permute-start.27 = (f32[256,128]{1,0:T(8,128)S(1)}, f32[256,128]{1,0:T(8,128)S(1)}, u32[]{:S(2)}, u32[]{:S(2)}) collective-permute-start(f32[256,128]{1,0:T(8,128)S(1)} %add.101.refs_0_), channel_id=1, source_target_pairs={{0,1},{1,0},{2,3},{3,2},{4,5},{5,4},{6,7},{7,6},{8,9},{9,8},{10,11... | collective-permute-start | bytes 393224 | tf_op jit(solution)/shard_map/ppermute | solution.py:253
  119.0 7.4 %collective-permute-start.29 = (f32[256,128]{1,0:T(8,128)S(1)}, f32[256,128]{1,0:T(8,128)S(1)}, u32[]{:S(2)}, u32[]{:S(2)}) collective-permute-start(f32[256,128]{1,0:T(8,128)S(1)} %collective-permute-done.25.refs_2_), channel_id=1, source_target_pairs={{0,1},{1,0},{2,3},{3,2},{4,5},{5,4},{6,7},{7,6},{8,9},{9,8},{10,11... | collective-permute-start | bytes 393224 | tf_op jit(solution)/shard_map/ppermute | solution.py:253
  121.0 7.3 %collective-permute-start.37 = (f32[256,128]{1,0:T(8,128)S(1)}, f32[256,128]{1,0:T(8,128)S(1)}, u32[]{:S(2)}, u32[]{:S(2)}) collective-permute-start(f32[256,128]{1,0:T(8,128)S(1)} %add.106.refs_8_), channel_id=1, source_target_pairs={{0,16},{8,24},{16,0},{24,8},{1,17},{9,25},{17,1},{25,9},{2,18},{10... | collective-permute-start | bytes 393224 | tf_op jit(solution)/shard_map/ppermute | solution.py:348
  122.5 6.9 %collective-permute-start.38 = (f32[256,128]{1,0:T(8,128)S(1)}, f32[256,128]{1,0:T(8,128)S(1)}, u32[]{:S(2)}, u32[]{:S(2)}) collective-permute-start(f32[256,128]{1,0:T(8,128)S(1)} %add.106.refs_8_), channel_id=1, source_target_pairs={{0,24},{8,16},{16,8},{24,0},{1,25},{9,17},{17,9},{25,1},{2,26},{10... | collective-permute-start | bytes 393224 | tf_op jit(solution)/shard_map/ppermute | solution.py:348
  123.6 7.2 %collective-permute-start.30 = (f32[256,128]{1,0:T(8,128)S(1)}, f32[256,128]{1,0:T(8,128)S(1)}, u32[]{:S(2)}, u32[]{:S(2)}) collective-permute-start(f32[256,128]{1,0:T(8,128)S(1)} %collective-permute-done.26.refs_3_), channel_id=1, source_target_pairs={{0,1},{1,0},{2,3},{3,2},{4,5},{5,4},{6,7},{7,6},{8,9},{9,8},{10,11... | collective-permute-start | bytes 393224 | tf_op jit(solution)/shard_map/ppermute | solution.py:253
  (23 other events, 133.8 us)

commit v11 on v9

--- a/solution.py
+++ b/solution.py
@@ -43,11 +43,11 @@
 
 def soft_back(probs, upstream):
     half = probs.shape[0] // 2
-    p, n = probs[:half], probs[half:]
+    p, n = probs[:half].astype(F32), probs[half:].astype(F32)
     gp, gn = upstream[:half], upstream[half:]
-    result = p * (gp - jnp.sum(p * gp, axis=0, keepdims=True))
-    result = result - n * (gn - jnp.sum(n * gn, axis=0, keepdims=True))
-    return result.astype(BF)
+    mean_p = jnp.sum(p * gp, axis=0, keepdims=True) / jnp.sum(p, axis=0, keepdims=True)
+    mean_n = jnp.sum(n * gn, axis=0, keepdims=True) / jnp.sum(n, axis=0, keepdims=True)
+    return (p * (gp - mean_p) - n * (gn - mean_n)).astype(BF)
 
 
 def causal_mask(core, tokens):
@@ -85,7 +85,7 @@
 
 def key_kernel(
     n, i, info, k_ref, kg_ref, v_ref, vg_ref, w_ref, q_ref, c_ref,
-    kp_ref, kb_ref, norm_ref, state_ref, qw_ref, cw_ref,
+    kb_ref, norm_ref, state_ref, qw_ref, cw_ref,
 ):
     group, width, dim = w_ref.shape
     keys = tokens_of(k_ref, kg_ref)
@@ -93,7 +93,6 @@
     scores = mm_nt(w_ref[...].reshape(group * width, dim), keys)
     probs = stack(*[both_soft(scores[a : a + width]) for a in range(0, group * width, width)])
     features = probs.astype(BF)
-    kp_ref[0] = probs
     kb_ref[0] = features
     norm_ref[0] = mm_nt(jnp.ones((16, keys.shape[0]), BF), features)[:1]
     state_ref[...] = mm(features, values)
@@ -132,7 +131,7 @@
     scaled = [(upstream[:, cols[i]] * (1.0 / den[i])).astype(BF) for i in heads]
     sums = [mm(query_t[i], scaled[i]) for i in heads]
     for i in heads:
-        qp_ref[0, rows[i]] = probs[i]
+        qp_ref[0, rows[i]] = query_t[i]
         qr_ref[0, i] = query_rows[i]
         wt_ref[0, i] = weights[i]
     state_ref[...] = stack(*sums)
@@ -200,7 +199,7 @@
     back = [soft_back(probs[i], upstream_q[i]) for i in heads]
     for i in heads:
         gq_ref[i * width : (i + 1) * width] = mm(back[i], queries[:, cols[i]])
-        gk_ref[0, rows[i]] = mm(probs[i].astype(BF), block[i])
+        gk_ref[0, rows[i]] = mm(probs[i], block[i])
 
 
 def key_grad_kernel(
@@ -504,15 +503,16 @@
     swapped = core_swap(packed.astype(F32))
     keys_got = values_got = swapped
 
+    flat_bf = shape_of(wide, length, dtype=BF)
     wide_flat = jax.ShapeDtypeStruct((own, n * four), F32)
-    key_probs, key_features, norm, a, b, near, *packed = call(
+    key_features, norm, a, b, near, *packed = call(
         "key_features",
         key_kernel,
         [own_cols(one), got_keys, own_cols(one), got_values, map_spec] + [other_cols(four)] * 2,
-        each(flat_spec, flat_spec, row_spec)
-        + states(3, 1)
-        + [(got_cols(four), 4, always), (got_cols(four), 5, always)],
-        [flat, shape_of(wide, length, dtype=BF), row] + [half_state] * 3 + [wide_flat] * 2,
+        each(flat_spec, row_spec)
+        + states(2, 1)
+        + [(got_cols(four), 3, always), (got_cols(four), 4, always)],
+        [flat_bf, row] + [half_state] * 3 + [wide_flat] * 2,
     )(keys, keys_got, values, values_got, key_map, queries, cotangent)
     queries_got, cotangent_got = [core_swap(x) for x in packed]
     prefix_norm = scan_norms(norm, chip, chips, True)
@@ -526,7 +526,7 @@
         query_kernel,
         [own_cols(four), got_cols(four)] * 2 + [map_spec, flat_spec, row_spec],
         each(flat_spec, rows_spec, per_head(group, length, length)) + states(3, 2),
-        [flat, rows_bf, shape_of(group, length, length, dtype=BF)] + [half_state] * 3,
+        [flat_bf, rows_bf, shape_of(group, length, length, dtype=BF)] + [half_state] * 3,
     )(queries, queries_got, cotangent, cotangent_got, query_map, key_features, prefix_norm)
     suffix = Scan(a, b, near, False)
     suffix.first()
@@ -565,7 +565,7 @@
         + moved_specs,
         spread(0),
         [grad] * n,
-    )(keys, keys_got, values, values_got, key_probs, key_up, suffix_norm, *later)
+    )(keys, keys_got, values, values_got, key_features, key_up, suffix_norm, *later)
     (attended,) = call(
         "attended",
         attended_kernel,

time: 135 us -> 135 us (level)
  no operation moved by 1% of the time
where the time goes in v11:
time: 135 us; the launch traced here: 134 us
  starting transfers between devices  78.8 us (58%)
  Pallas kernels  31.4 us (23%)
  waiting for transfers between devices  16.6 us (12%)
  other arithmetic  5.24 us (4%)
    ppermute x19, starting transfers between devices, chip_move(): lax.ppermute(x, 'ctx', [(2 * a + c, 2 * b + c) for a, b in pairs for c in...  48.3 us
    pallas_call x5, Pallas kernels, run(): pl.pallas_call(kernel, name=name, out_shape=[pltpu.HBM(x.shape, x.dtype)...  29.4 us
    ppermute x12, starting transfers between devices, core_swap(): return lax.ppermute(x, 'ctx', [(i, i ^ 1) for i in range(size)])  17 us
    ppermute x19, waiting for transfers between devices, chip_move(): lax.ppermute(x, 'ctx', [(2 * a + c, 2 * b + c) for a, b in pairs for c in...  12.3 us
    ppermute x6, starting transfers between devices, sum_all(): lax.ppermute(total, 'dp', [(i, i ^ k) for i in range(dp)])  8.11 us
    ppermute x6, starting transfers between devices, sum_all(): lax.ppermute(blocks[k], 'dp', [(i, i ^ k) for i in range(dp)])  5.38 us
    ppermute x12, waiting for transfers between devices, core_swap(): return lax.ppermute(x, 'ctx', [(i, i ^ 1) for i in range(size)])  2.75 us
  transfers between devices with their start and end apart: 43, of which 13 were waited for; matrix products, arithmetic and copies ran while one was open for 4% of the time, Pallas kernels for 18%

profile of v11, /device:TPU:1, one launch (start us, length us, event | category | flops | bytes accessed | tf_op | source)
XLA Modules:
  0.0 134.1 jit_solution(16510898994021160522)
XLA Ops:
  1.9 1.8 %collective-permute-done.refs_1_.refs_3_.refs_5_ = f32[256,512]{1,0:T(8,128)S(1)} collective-permute-done((f32[256,512]{1,0:T(8,128)S(1)}, f32[256,512]{1,0:T(8,128)S(1)}, u32[]{:S(2)}, u32[]{:S(2)}) %collective-permute-start) | collective-permute-done | bytes 524320 | tf_op jit(solution)/shard_map/ppermute | solution.py:235
  3.7 5.4 %key_features.1 = (bf16[4,512,256]{2,1,0:T(8,128)(2,1)}, f32[4,1,512]{2,1,0:T(1,128)}, f32[1024,128]{1,0:T(8,128)}, f32[1024,128]{1,0:T(8,128)}, f32[1024,128]{1...) custom-call(s32[11]{0:T(128)S(1)} %concatenate.6.info, bf16[128,1024]{1,0:T(8,128)(2,1)} %bitcast.29, ...), custom_call_target="tpu_custom_call" | custom-call | tf_op jit(solution)/shard_map/key_features/pallas_call | solution.py:449
  9.7 2.5 %collective-permute-start.3 = (f32[4,1,512]{2,1,0:T(1,128)}, f32[4,1,512]{2,1,0:T(1,128)S(1)}, u32[]{:S(2)}, u32[]{:S(2)}) collective-permute-start(f32[4,1,512]{2,1,0:T(1,128)} %get-tuple-element.58), channel_id=1, source_target_pairs={{0,2},{1,3},{2,0},{3,1},{4,6},{5,7},{6,4},{7,5},{8,10},{9,11},{10,... | collective-permute-start | bytes 24584 | tf_op jit(solution)/shard_map/ppermute | solution.py:239
  14.2 2.5 %collective-permute-start.4 = (f32[4,1,512]{2,1,0:T(1,128)S(1)}, f32[4,1,512]{2,1,0:T(1,128)S(1)}, u32[]{:S(2)}, u32[]{:S(2)}) collective-permute-start(f32[4,1,512]{2,1,0:T(1,128)S(1)} %add.87), channel_id=1, source_target_pairs={{0,4},{1,5},{2,6},{3,7},{4,0},{5,1},{6,2},{7,3},{8,12},{9,13},{10,... | collective-permute-start | bytes 24584 | tf_op jit(solution)/shard_map/ppermute | solution.py:239
  17.7 3.4 %collective-permute-start.5 = (f32[1024,128]{1,0:T(8,128)}, f32[1024,128]{1,0:T(8,128)S(1)}, u32[]{:S(2)}, u32[]{:S(2)}) collective-permute-start(f32[1024,128]{1,0:T(8,128)} %get-tuple-element.65), channel_id=1, source_target_pairs={{0,2},{1,3},{2,4},{3,5},{4,6},{5,7},{8,10},{9,11},{10,12},{11,13},... | collective-permute-start | bytes 1572872 | tf_op jit(solution)/shard_map/ppermute | solution.py:239
  21.1 5.0 %collective-permute-start.6 = (f32[1024,128]{1,0:T(8,128)}, f32[1024,128]{1,0:T(8,128)}, u32[]{:S(2)}, u32[]{:S(2)}) collective-permute-start(f32[1024,128]{1,0:T(8,128)} %get-tuple-element.70), channel_id=1, source_target_pairs={{0,4},{1,5},{8,12},{9,13},{16,20},{17,21},{24,28},{25,29}} | collective-permute-start | bytes 1572872 | tf_op jit(solution)/shard_map/ppermute | solution.py:239
  26.0 7.1 %query_features.1 = (bf16[4,512,256]{2,1,0:T(8,128)(2,1)}, bf16[4,4,256,128]{3,2,1,0:T(8,128)(2,1)}, bf16[4,4,256,256]{3,2,1,0:T(8,128)(2,1)}, f32[1024,128]{1,0...) custom-call(s32[11]{0:T(128)S(1)} %concatenate.6.info, bf16[128,4096]{1,0:T(8,128)(2,1)} %bitcast.21, ...), custom_call_target="tpu_custom_call" | custom-call | tf_op jit(solution)/shard_map/query_features/pallas_call | solution.py:449
  37.9 3.2 %collective-permute-done.6.refs_12_ = f32[1024,128]{1,0:T(8,128)} collective-permute-done((f32[1024,128]{1,0:T(8,128)}, f32[1024,128]{1,0:T(8,128)}, u32[]{:S(2)}, u32[]{:S(2)}) %collective-permute-start.6) | collective-permute-done | bytes 524320 | tf_op jit(solution)/shard_map/ppermute | solution.py:239
  42.4 5.6 %collective-permute-start.9 = (f32[1024,128]{1,0:T(8,128)S(1)}, f32[1024,128]{1,0:T(8,128)S(1)}, u32[]{:S(2)}, u32[]{:S(2)}) collective-permute-start(f32[1024,128]{1,0:T(8,128)S(1)} %add_select_fusion.1), channel_id=1, source_target_pairs={{0,2},{1,3},{4,6},{5,7},{8,10},{9,11},{12,14},{13,15},{16,18},{17,... | collective-permute-start | bytes 1572872 | tf_op jit(solution)/shard_map/ppermute | solution.py:239
  49.0 1.5 %collective-permute-start.15 = (f32[1024,128]{1,0:T(8,128)}, f32[1024,128]{1,0:T(8,128)}, u32[]{:S(2)}, u32[]{:S(2)}) collective-permute-start(f32[1024,128]{1,0:T(8,128)} %add.92), channel_id=1, source_target_pairs={{4,2},{5,3},{12,10},{13,11},{20,18},{21,19},{28,26},{29,27}} | collective-permute-start | bytes 1572872 | tf_op jit(solution)/shard_map/ppermute | solution.py:239
  55.2 10.1 %attend.1 = (bf16[128,4096]{1,0:T(8,128)(2,1)}, f32[128,2048]{1,0:T(8,128)}, f32[4,1,512]{2,1,0:T(1,128)}, f32[4,512,256]{2,1,0:T(8,128)}, f32[256,128]{1,0:T(8,...) custom-call(s32[11]{0:T(128)S(1)} %concatenate.6.info, bf16[128,4096]{1,0:T(8,128)(2,1)} %bitcast.22, ...), custom_call_target="tpu_custom_call" | custom-call | tf_op jit(solution)/shard_map/attend/pallas_call | solution.py:449
  65.3 12.7 %collective-permute-start.11 = (f32[4,1,512]{2,1,0:T(1,128)}, f32[4,1,512]{2,1,0:T(1,128)S(1)}, u32[]{:S(2)}, u32[]{:S(2)}) collective-permute-start(f32[4,1,512]{2,1,0:T(1,128)} %get-tuple-element.78), channel_id=1, source_target_pairs={{0,2},{1,3},{2,0},{3,1},{4,6},{5,7},{6,4},{7,5},{8,10},{9,11},{10,... | collective-permute-start | bytes 24584 | tf_op jit(solution)/shard_map/ppermute | solution.py:239
  78.0 3.1 %collective-permute-start.12 = (f32[4,1,512]{2,1,0:T(1,128)}, f32[4,1,512]{2,1,0:T(1,128)S(1)}, u32[]{:S(2)}, u32[]{:S(2)}) collective-permute-start(f32[4,1,512]{2,1,0:T(1,128)} %get-tuple-element.78), channel_id=1, source_target_pairs={{0,4},{1,5},{2,6},{3,7},{4,0},{5,1},{6,2},{7,3},{8,12},{9,13},{10,... | collective-permute-start | bytes 24584 | tf_op jit(solution)/shard_map/ppermute | solution.py:239
  81.7 1.9 %collective-permute-start.13 = (f32[4,1,512]{2,1,0:T(1,128)}, f32[4,1,512]{2,1,0:T(1,128)S(1)}, u32[]{:S(2)}, u32[]{:S(2)}) collective-permute-start(f32[4,1,512]{2,1,0:T(1,128)} %get-tuple-element.78), channel_id=1, source_target_pairs={{0,6},{1,7},{2,4},{3,5},{4,2},{5,3},{6,0},{7,1},{8,14},{9,15},{10,... | collective-permute-start | bytes 24584 | tf_op jit(solution)/shard_map/ppermute | solution.py:239
  83.6 2.7 %collective-permute-done.13 = f32[4,1,512]{2,1,0:T(1,128)S(1)} collective-permute-done((f32[4,1,512]{2,1,0:T(1,128)}, f32[4,1,512]{2,1,0:T(1,128)S(1)}, u32[]{:S(2)}, u32[]{:S(2)}) %collective-permute-start.13) | collective-permute-done | bytes 8224 | tf_op jit(solution)/shard_map/ppermute | solution.py:239
  86.3 3.4 %collective-permute-start.18 = (f32[128,2048]{1,0:T(8,128)}, f32[128,2048]{1,0:T(8,128)S(1)}, u32[]{:S(2)}, u32[]{:S(2)}) collective-permute-start(f32[128,2048]{1,0:T(8,128)} %get-tuple-element.88), channel_id=1, source_target_pairs={{0,1},{1,0},{2,3},{3,2},{4,5},{5,4},{6,7},{7,6},{8,9},{9,8},{10,11... | collective-permute-start | bytes 3145736 | tf_op jit(solution)/shard_map/ppermute | solution.py:235
  92.4 5.3 %key_grads.1 = (f32[256,128]{1,0:T(8,128)}, f32[256,128]{1,0:T(8,128)}, f32[256,128]{1,0:T(8,128)}, f32[256,128]{1,0:T(8,128)}) custom-call(s32[11]{0:T(128)S(1)} %concatenate.6.info, bf16[128,1024]{1,0:T(8,128)(2,1)} %bitcast.30, f32[256,512]{1,0:T(8,128)S(1)} %collective-permute-done.refs_1_.refs_3_.refs_5_, bf16[128,1024]{1,0:T(8,128)(2,1)} %bitcast.28, ...), custom_call_target="tpu_custom_call" | custom-call | tf_op jit(solution)/shard_map/key_grads/pallas_call | solution.py:449
  102.5 2.0 %collective-permute-start.23 = (f32[256,128]{1,0:T(8,128)S(1)}, f32[256,128]{1,0:T(8,128)S(1)}, u32[]{:S(2)}, u32[]{:S(2)}) collective-permute-start(f32[256,128]{1,0:T(8,128)S(1)} %add.100), channel_id=1, source_target_pairs={{0,4},{1,5},{2,6},{3,7},{4,0},{5,1},{6,2},{7,3},{8,12},{9,13},{10,... | collective-permute-start | bytes 393224 | tf_op jit(solution)/shard_map/ppermute | solution.py:239
  108.7 4.1 %collective-permute-start.24 = (f32[256,128]{1,0:T(8,128)S(1)}, f32[256,128]{1,0:T(8,128)S(1)}, u32[]{:S(2)}, u32[]{:S(2)}) collective-permute-start(f32[256,128]{1,0:T(8,128)S(1)} %add.101.refs_0_), channel_id=1, source_target_pairs={{0,8},{8,0},{16,24},{24,16},{1,9},{9,1},{17,25},{25,17},{2,10},{10... | collective-permute-start | bytes 393224 | tf_op jit(solution)/shard_map/ppermute | solution.py:329
  114.8 4.3 %collective-permute-start.27 = (f32[256,128]{1,0:T(8,128)S(1)}, f32[256,128]{1,0:T(8,128)S(1)}, u32[]{:S(2)}, u32[]{:S(2)}) collective-permute-start(f32[256,128]{1,0:T(8,128)S(1)} %add.101.refs_0_), channel_id=1, source_target_pairs={{0,1},{1,0},{2,3},{3,2},{4,5},{5,4},{6,7},{7,6},{8,9},{9,8},{10,11... | collective-permute-start | bytes 393224 | tf_op jit(solution)/shard_map/ppermute | solution.py:235
  121.3 1.6 %collective-permute-start.37 = (f32[256,128]{1,0:T(8,128)S(1)}, f32[256,128]{1,0:T(8,128)S(1)}, u32[]{:S(2)}, u32[]{:S(2)}) collective-permute-start(f32[256,128]{1,0:T(8,128)S(1)} %add.106.refs_8_), channel_id=1, source_target_pairs={{0,16},{8,24},{16,0},{24,8},{1,17},{9,25},{17,1},{25,9},{2,18},{10... | collective-permute-start | bytes 393224 | tf_op jit(solution)/shard_map/ppermute | solution.py:329
  124.0 2.5 %collective-permute-start.30 = (f32[256,128]{1,0:T(8,128)S(1)}, f32[256,128]{1,0:T(8,128)S(1)}, u32[]{:S(2)}, u32[]{:S(2)}) collective-permute-start(f32[256,128]{1,0:T(8,128)S(1)} %collective-permute-done.26.refs_3_), channel_id=1, source_target_pairs={{0,1},{1,0},{2,3},{3,2},{4,5},{5,4},{6,7},{7,6},{8,9},{9,8},{10,11... | collective-permute-start | bytes 393224 | tf_op jit(solution)/shard_map/ppermute | solution.py:235
  126.6 2.1 %collective-permute-start.40 = (f32[256,128]{1,0:T(8,128)S(1)}, f32[256,128]{1,0:T(8,128)S(1)}, u32[]{:S(2)}, u32[]{:S(2)}) collective-permute-start(f32[256,128]{1,0:T(8,128)S(1)} %collective-permute-done.36.refs_9_), channel_id=1, source_target_pairs={{0,1},{1,0},{2,3},{3,2},{4,5},{5,4},{6,7},{7,6},{8,9},{9,8},{10,11... | collective-permute-start | bytes 393224 | tf_op jit(solution)/shard_map/ppermute | solution.py:235
  132.1 2.0 %sums_out.1 = (f32[8,256,128]{2,1,0:T(8,128)}, f32[8,256,128]{2,1,0:T(8,128)}) custom-call(s32[11]{0:T(128)S(1)} %concatenate.6.info, f32[256,128]{1,0:T(8,128)S(1)} %add.101.refs_0_, f32[256,128]{1,0:T(8,128)S(1)} %collective-permute-done.24.refs_1_, f32[256,128]{1,0:T(8,128)S(1)} %collective-permute-done.25.refs_2_, ...), custom_call_target="tpu_custom_call" | custom-call | tf_op jit(solution)/shard_map/sums_out/pallas_call | solution.py:581
  (93 shorter events, 37.4 us)
Async XLA Ops:
  9.1 16.9 %collective-permute-start.1 = (f32[128,2048]{1,0:T(8,128)}, f32[128,2048]{1,0:T(8,128)S(1)}, u32[]{:S(2)}, u32[]{:S(2)}) collective-permute-start(f32[128,2048]{1,0:T(8,128)} %get-tuple-element.55), channel_id=1, source_target_pairs={{0,1},{1,0},{2,3},{3,2},{4,5},{5,4},{6,7},{7,6},{8,9},{9,8},{10,11... | collective-permute-start | bytes 3145736 | tf_op jit(solution)/shard_map/ppermute | solution.py:235
  9.3 16.7 %collective-permute-start.2 = (f32[128,2048]{1,0:T(8,128)}, f32[128,2048]{1,0:T(8,128)}, u32[]{:S(2)}, u32[]{:S(2)}) collective-permute-start(f32[128,2048]{1,0:T(8,128)} %get-tuple-element.56), channel_id=1, source_target_pairs={{0,1},{1,0},{2,3},{3,2},{4,5},{5,4},{6,7},{7,6},{8,9},{9,8},{10,11... | collective-permute-start | bytes 3145736 | tf_op jit(solution)/shard_map/ppermute | solution.py:235
  17.7 17.5 %collective-permute-start.5 = (f32[1024,128]{1,0:T(8,128)}, f32[1024,128]{1,0:T(8,128)S(1)}, u32[]{:S(2)}, u32[]{:S(2)}) collective-permute-start(f32[1024,128]{1,0:T(8,128)} %get-tuple-element.65), channel_id=1, source_target_pairs={{0,2},{1,3},{2,4},{3,5},{4,6},{5,7},{8,10},{9,11},{10,12},{11,13},... | collective-permute-start | bytes 1572872 | tf_op jit(solution)/shard_map/ppermute | solution.py:239
  21.1 20.0 %collective-permute-start.6 = (f32[1024,128]{1,0:T(8,128)}, f32[1024,128]{1,0:T(8,128)}, u32[]{:S(2)}, u32[]{:S(2)}) collective-permute-start(f32[1024,128]{1,0:T(8,128)} %get-tuple-element.70), channel_id=1, source_target_pairs={{0,4},{1,5},{8,12},{9,13},{16,20},{17,21},{24,28},{25,29}} | collective-permute-start | bytes 1572872 | tf_op jit(solution)/shard_map/ppermute | solution.py:239
  33.1 15.0 %collective-permute-start.10 = (f32[1024,128]{1,0:T(8,128)}, f32[1024,128]{1,0:T(8,128)S(1)}, u32[]{:S(2)}, u32[]{:S(2)}) collective-permute-start(f32[1024,128]{1,0:T(8,128)} %get-tuple-element.68), channel_id=1, source_target_pairs={{6,4},{7,5},{4,2},{5,3},{2,0},{3,1},{14,12},{15,13},{12,10},{13,11... | collective-permute-start | bytes 1572872 | tf_op jit(solution)/shard_map/ppermute | solution.py:239
  34.4 16.1 %collective-permute-start.14 = (f32[1024,128]{1,0:T(8,128)}, f32[1024,128]{1,0:T(8,128)S(1)}, u32[]{:S(2)}, u32[]{:S(2)}) collective-permute-start(f32[1024,128]{1,0:T(8,128)} %get-tuple-element.87), channel_id=1, source_target_pairs={{6,2},{7,3},{14,10},{15,11},{22,18},{23,19},{30,26},{31,27}} | collective-permute-start | bytes 1572872 | tf_op jit(solution)/shard_map/ppermute | solution.py:239
  36.3 16.4 %collective-permute-start.7 = (f32[1024,128]{1,0:T(8,128)S(1)}, f32[1024,128]{1,0:T(8,128)S(1)}, u32[]{:S(2)}, u32[]{:S(2)}) collective-permute-start(f32[1024,128]{1,0:T(8,128)S(1)} %add.89), channel_id=1, source_target_pairs={{2,4},{3,5},{10,12},{11,13},{18,20},{19,21},{26,28},{27,29}} | collective-permute-start | bytes 1572872 | tf_op jit(solution)/shard_map/ppermute | solution.py:239
  37.2 17.1 %collective-permute-start.8 = (f32[1024,128]{1,0:T(8,128)S(1)}, f32[1024,128]{1,0:T(8,128)S(1)}, u32[]{:S(2)}, u32[]{:S(2)}) collective-permute-start(f32[1024,128]{1,0:T(8,128)S(1)} %add.89), channel_id=1, source_target_pairs={{2,6},{3,7},{10,14},{11,15},{18,22},{19,23},{26,30},{27,31}} | collective-permute-start | bytes 1572872 | tf_op jit(solution)/shard_map/ppermute | solution.py:239
  42.4 12.7 %collective-permute-start.9 = (f32[1024,128]{1,0:T(8,128)S(1)}, f32[1024,128]{1,0:T(8,128)S(1)}, u32[]{:S(2)}, u32[]{:S(2)}) collective-permute-start(f32[1024,128]{1,0:T(8,128)S(1)} %add_select_fusion.1), channel_id=1, source_target_pairs={{0,2},{1,3},{4,6},{5,7},{8,10},{9,11},{12,14},{13,15},{16,18},{17,... | collective-permute-start | bytes 1572872 | tf_op jit(solution)/shard_map/ppermute | solution.py:239
  49.0 37.2 %collective-permute-start.15 = (f32[1024,128]{1,0:T(8,128)}, f32[1024,128]{1,0:T(8,128)}, u32[]{:S(2)}, u32[]{:S(2)}) collective-permute-start(f32[1024,128]{1,0:T(8,128)} %add.92), channel_id=1, source_target_pairs={{4,2},{5,3},{12,10},{13,11},{20,18},{21,19},{28,26},{29,27}} | collective-permute-start | bytes 1572872 | tf_op jit(solution)/shard_map/ppermute | solution.py:239
  50.5 35.7 %collective-permute-start.16 = (f32[1024,128]{1,0:T(8,128)}, f32[1024,128]{1,0:T(8,128)}, u32[]{:S(2)}, u32[]{:S(2)}) collective-permute-start(f32[1024,128]{1,0:T(8,128)} %add.92), channel_id=1, source_target_pairs={{4,0},{5,1},{12,8},{13,9},{20,16},{21,17},{28,24},{29,25}} | collective-permute-start | bytes 1572872 | tf_op jit(solution)/shard_map/ppermute | solution.py:239
  52.8 33.5 %collective-permute-start.17 = (f32[1024,128]{1,0:T(8,128)}, f32[1024,128]{1,0:T(8,128)}, u32[]{:S(2)}, u32[]{:S(2)}) collective-permute-start(f32[1024,128]{1,0:T(8,128)} %add_select_fusion), channel_id=1, source_target_pairs={{6,4},{7,5},{2,0},{3,1},{14,12},{15,13},{10,8},{11,9},{22,20},{23,... | collective-permute-start | bytes 1572872 | tf_op jit(solution)/shard_map/ppermute | solution.py:239
  65.3 16.4 %collective-permute-start.11 = (f32[4,1,512]{2,1,0:T(1,128)}, f32[4,1,512]{2,1,0:T(1,128)S(1)}, u32[]{:S(2)}, u32[]{:S(2)}) collective-permute-start(f32[4,1,512]{2,1,0:T(1,128)} %get-tuple-element.78), channel_id=1, source_target_pairs={{0,2},{1,3},{2,0},{3,1},{4,6},{5,7},{6,4},{7,5},{8,10},{9,11},{10,... | collective-permute-start | bytes 24584 | tf_op jit(solution)/shard_map/ppermute | solution.py:239
  86.3 18.2 %collective-permute-start.18 = (f32[128,2048]{1,0:T(8,128)}, f32[128,2048]{1,0:T(8,128)S(1)}, u32[]{:S(2)}, u32[]{:S(2)}) collective-permute-start(f32[128,2048]{1,0:T(8,128)} %get-tuple-element.88), channel_id=1, source_target_pairs={{0,1},{1,0},{2,3},{3,2},{4,5},{5,4},{6,7},{7,6},{8,9},{9,8},{10,11... | collective-permute-start | bytes 3145736 | tf_op jit(solution)/shard_map/ppermute | solution.py:235
  89.7 7.9 %collective-permute-start.19 = (f32[256,128]{1,0:T(8,128)}, f32[256,128]{1,0:T(8,128)S(1)}, u32[]{:S(2)}, u32[]{:S(2)}) collective-permute-start(f32[256,128]{1,0:T(8,128)} %get-tuple-element.91), channel_id=1, source_target_pairs={{0,8},{8,0},{16,24},{24,16},{1,9},{9,1},{17,25},{25,17},{2,10},{10... | collective-permute-start | bytes 393224 | tf_op jit(solution)/shard_map/ppermute | solution.py:318
  98.7 7.3 %collective-permute-start.31 = (f32[256,128]{1,0:T(8,128)}, f32[256,128]{1,0:T(8,128)S(1)}, u32[]{:S(2)}, u32[]{:S(2)}) collective-permute-start(f32[256,128]{1,0:T(8,128)} %get-tuple-element.96), channel_id=1, source_target_pairs={{0,8},{8,0},{16,24},{24,16},{1,9},{9,1},{17,25},{25,17},{2,10},{10... | collective-permute-start | bytes 393224 | tf_op jit(solution)/shard_map/ppermute | solution.py:318
  108.7 10.4 %collective-permute-start.24 = (f32[256,128]{1,0:T(8,128)S(1)}, f32[256,128]{1,0:T(8,128)S(1)}, u32[]{:S(2)}, u32[]{:S(2)}) collective-permute-start(f32[256,128]{1,0:T(8,128)S(1)} %add.101.refs_0_), channel_id=1, source_target_pairs={{0,8},{8,0},{16,24},{24,16},{1,9},{9,1},{17,25},{25,17},{2,10},{10... | collective-permute-start | bytes 393224 | tf_op jit(solution)/shard_map/ppermute | solution.py:329
  112.8 8.4 %collective-permute-start.35 = (f32[256,128]{1,0:T(8,128)S(1)}, f32[256,128]{1,0:T(8,128)S(1)}, u32[]{:S(2)}, u32[]{:S(2)}) collective-permute-start(f32[256,128]{1,0:T(8,128)S(1)} %add.105), channel_id=1, source_target_pairs={{0,4},{1,5},{2,6},{3,7},{4,0},{5,1},{6,2},{7,3},{8,12},{9,13},{10,... | collective-permute-start | bytes 393224 | tf_op jit(solution)/shard_map/ppermute | solution.py:239
  113.4 7.9 %collective-permute-start.26 = (f32[256,128]{1,0:T(8,128)S(1)}, f32[256,128]{1,0:T(8,128)S(1)}, u32[]{:S(2)}, u32[]{:S(2)}) collective-permute-start(f32[256,128]{1,0:T(8,128)S(1)} %add.101.refs_0_), channel_id=1, source_target_pairs={{0,24},{8,16},{16,8},{24,0},{1,25},{9,17},{17,9},{25,1},{2,26},{10... | collective-permute-start | bytes 393224 | tf_op jit(solution)/shard_map/ppermute | solution.py:329
  114.8 8.1 %collective-permute-start.27 = (f32[256,128]{1,0:T(8,128)S(1)}, f32[256,128]{1,0:T(8,128)S(1)}, u32[]{:S(2)}, u32[]{:S(2)}) collective-permute-start(f32[256,128]{1,0:T(8,128)S(1)} %add.101.refs_0_), channel_id=1, source_target_pairs={{0,1},{1,0},{2,3},{3,2},{4,5},{5,4},{6,7},{7,6},{8,9},{9,8},{10,11... | collective-permute-start | bytes 393224 | tf_op jit(solution)/shard_map/ppermute | solution.py:235
  119.1 7.4 %collective-permute-start.29 = (f32[256,128]{1,0:T(8,128)S(1)}, f32[256,128]{1,0:T(8,128)S(1)}, u32[]{:S(2)}, u32[]{:S(2)}) collective-permute-start(f32[256,128]{1,0:T(8,128)S(1)} %collective-permute-done.25.refs_2_), channel_id=1, source_target_pairs={{0,1},{1,0},{2,3},{3,2},{4,5},{5,4},{6,7},{7,6},{8,9},{9,8},{10,11... | collective-permute-start | bytes 393224 | tf_op jit(solution)/shard_map/ppermute | solution.py:235
  121.3 7.3 %collective-permute-start.37 = (f32[256,128]{1,0:T(8,128)S(1)}, f32[256,128]{1,0:T(8,128)S(1)}, u32[]{:S(2)}, u32[]{:S(2)}) collective-permute-start(f32[256,128]{1,0:T(8,128)S(1)} %add.106.refs_8_), channel_id=1, source_target_pairs={{0,16},{8,24},{16,0},{24,8},{1,17},{9,25},{17,1},{25,9},{2,18},{10... | collective-permute-start | bytes 393224 | tf_op jit(solution)/shard_map/ppermute | solution.py:329
  122.9 6.8 %collective-permute-start.38 = (f32[256,128]{1,0:T(8,128)S(1)}, f32[256,128]{1,0:T(8,128)S(1)}, u32[]{:S(2)}, u32[]{:S(2)}) collective-permute-start(f32[256,128]{1,0:T(8,128)S(1)} %add.106.refs_8_), channel_id=1, source_target_pairs={{0,24},{8,16},{16,8},{24,0},{1,25},{9,17},{17,9},{25,1},{2,26},{10... | collective-permute-start | bytes 393224 | tf_op jit(solution)/shard_map/ppermute | solution.py:329
  124.0 7.2 %collective-permute-start.30 = (f32[256,128]{1,0:T(8,128)S(1)}, f32[256,128]{1,0:T(8,128)S(1)}, u32[]{:S(2)}, u32[]{:S(2)}) collective-permute-start(f32[256,128]{1,0:T(8,128)S(1)} %collective-permute-done.26.refs_3_), channel_id=1, source_target_pairs={{0,1},{1,0},{2,3},{3,2},{4,5},{5,4},{6,7},{7,6},{8,9},{9,8},{10,11... | collective-permute-start | bytes 393224 | tf_op jit(solution)/shard_map/ppermute | solution.py:235
  (23 other events, 134.0 us)
